TPU v7x, 32 devices: a whole 2x2x4 slice. The times are simulated.
32 devices in a mesh: groups: 2 (over y), patch: 4 (over z), head: 2 (over x), sub: 2 (over core).
Axes of the slice: x: 2, y: 2, z: 4, core: 2. Of those that a mesh axis runs over, the one named last changes fastest.
Arguments:
- queries: bfloat16 [768, 1024], P(('groups', 'patch'), ('head', 'sub')), parts along dimension 0, may hold values from -112 to 112
- held_keys: bfloat16 [768, 1024], P('groups', ('head', 'sub')), parts along dimension 0, may hold values from -4 to 4
- held_values: bfloat16 [768, 1024], P('groups', ('head', 'sub')), parts along dimension 0, may hold values from -4 to 4
- key_change: float32 [768, 1024], P(('groups', 'patch'), ('head', 'sub')), parts along dimension 0, may hold values from -0.6 to 0.6
- value_change: float32 [768, 1024], P(('groups', 'patch'), ('head', 'sub')), parts along dimension 0, may hold values from -1.8 to 1.8
- out_weight: bfloat16 [1024, 5120], P(('head', 'sub')), may hold values from -0.25 to 0.25
- hidden_in: bfloat16 [768, 5120], P(('groups', 'patch'), ('head', 'sub')), parts along dimension 0, may hold values from -3 to 3
- gate: float32 [10240], P(('groups', 'head', 'sub')), parts along dimension 0, may hold values from 0.5 to 2.5
Outputs:
- block_out: bfloat16 [768, 5120], P(('groups', 'patch'), ('head', 'sub')), parts along dimension 0
There are 2 independent parts, one for each index of `groups`. A program takes and returns all parts, laid end to end along the dimension named above; an argument that names none is the same for every part. Nothing has to cross between parts.
All inputs are finite; a program needn't handle non-finite values.
Results may differ from a plain program's by a relative error of at most 0.0044.
Values may be sent and summed in bfloat16 or wider, within the bound.
No kernel may reach another device: no remote copies, remote signals or barrier semaphores. Data moves between devices by JAX's collectives and lax.ppermute only.
A program may use at most 64 MiB of HBM per device.

v0:
```python
import math

import jax
import jax.numpy as jnp
from jax import lax
from jax.sharding import PartitionSpec as P

HD = 128


def split_heads(matrix, heads):
    return matrix.reshape(matrix.shape[0], heads, matrix.shape[1] // heads)


def decode(held_rows, residual_rows):
    return held_rows.astype(jnp.float32) + residual_rows.astype(jnp.float32)


def block_scores(query_heads, key_heads):
    scale = 1.0 / math.sqrt(query_heads.shape[2])
    products = jnp.einsum("qhd,khd->hqk", query_heads, key_heads, precision=lax.Precision.HIGHEST)
    return products * scale


def weighted_values(weights, value_heads):
    return jnp.einsum("hqk,khd->hqd", weights, value_heads, precision=lax.Precision.HIGHEST)


def per_device(
    queries, held_keys, held_values, key_change, value_change, out_weight, hidden_in, gate
):
    width = queries.shape[1]
    heads = width // HD
    own_rows = queries.shape[0]
    residual = jnp.concatenate(
        [key_change.astype(jnp.bfloat16), value_change.astype(jnp.bfloat16)], axis=1
    )
    query_heads = split_heads(queries.astype(jnp.float32), heads)
    gathered = lax.all_gather(residual, "patch", axis=0, tiled=True)
    key_heads = split_heads(decode(held_keys, gathered[:, :width]), heads)
    value_heads = split_heads(decode(held_values, gathered[:, width:]), heads)
    scores = block_scores(query_heads, key_heads)
    highest = jnp.max(scores, axis=2, keepdims=True)
    weights = jnp.exp(scores - highest)
    totals = jnp.sum(weights, axis=2, keepdims=True)
    attended_heads = weighted_values(weights, value_heads) / totals
    attended = attended_heads.transpose(1, 0, 2).reshape(own_rows, width)
    rounded = attended.astype(jnp.bfloat16)
    terms = jnp.dot(rounded, out_weight, preferred_element_type=jnp.float32)
    projected = lax.psum_scatter(terms, ("head", "sub"), scatter_dimension=1, tiled=True)
    return (hidden_in.astype(jnp.float32) + gate[None, :] * projected).astype(jnp.bfloat16)


def solution(mesh):
    in_specs = (
        P(("groups", "patch"), ("head", "sub")),
        P("groups", ("head", "sub")),
        P("groups", ("head", "sub")),
        P(("groups", "patch"), ("head", "sub")),
        P(("groups", "patch"), ("head", "sub")),
        P(("head", "sub"), None),
        P(("groups", "patch"), ("head", "sub")),
        P(("groups", "head", "sub")),
    )
    out_specs = P(("groups", "patch"), ("head", "sub"))
    return jax.shard_map(
        per_device, mesh=mesh, in_specs=in_specs, out_specs=out_specs, check_vma=False
    )
```

profile of v0, /device:TPU:0, one launch (start us, length us, event | category | flops | bytes accessed | tf_op | source)
XLA Modules:
  0.0 70.9 jit_solution(14638737851653690627)
XLA Ops:
  6.5 0.0 copy-start
  6.5 0.0 reduce-scatter.2.cloned.1.call-start
  6.5 1.0 %convert_element_type.33 = bf16[96,256]{1,0:T(8,128)(2,1)S(1)} convert(f32[96,256]{1,0:T(8,128)} %param.11) | non-fusion elementwise | flops 24576 | bytes 147456 | tf_op jit(solution)/shard_map/convert_element_type | solution.py:36
  7.6 0.9 %convert_element_type.34 = bf16[96,256]{1,0:T(8,128)(2,1)S(1)} convert(f32[96,256]{1,0:T(8,128)} %param.12) | non-fusion elementwise | flops 24576 | bytes 147456 | tf_op jit(solution)/shard_map/convert_element_type | solution.py:36
  8.5 16.2 %all_gather.3 = bf16[384,512]{1,0:T(8,128)(2,1)S(1)} all-gather(bf16[96,512]{1,0:T(8,128)(2,1)S(1)} %pad_maximum_fusion), channel_id=1, replica_groups=mesh['groups'=2,'patch'=4,'head'=2,'sub'=2] {'patch'}, dimensions={0}, use_global_device_ids=true | all-gather | bytes 491520 | tf_op jit(solution)/shard_map/all_gather | solution.py:39
  24.7 1.1 %add_bitcast_fusion.1 = (f32[48,2,8,128]{3,2,1,0:T(8,128)S(1)}, f32[48,2,8,128]{3,2,1,0:T(8,128)S(1)}) fusion(bf16[384,256]{1,0:T(8,128)(2,1)} %param.9, bf16[384,512]{1,0:T(8,128)(2,1)S(1)} %all_gather.3, bf16[384,256]{1,0:T(8,128)(2,1)} %param.10), kind=kLoop, calls=%fused_computation.12 | loop fusion | flops 589824 | bytes 1572864
  25.9 1.3 %fusion.15 = (f32[2,96]{1,0:T(2,128)S(1)}, f32[2,96,384]{2,1,0:T(8,128)S(1)}) fusion(f32[48,2,8,128]{3,2,1,0:T(8,128)S(1)} %get-tuple-element.5, bf16[96,256]{1,0:T(8,128)(2,1)} %param.8), kind=kOutput, calls=%fused_computation.22 | convolution fusion | flops 113393472 | bytes 738048 | tf_op jit(solution)/shard_map/qhd,khd->hqk/dot_general | solution.py:21
  27.1 0.2 fusion.8
  27.4 0.5 fusion.3
  27.9 0.0 copy-done
  27.9 0.0 copy-start.1
  27.9 0.0 copy-start.2
  27.9 1.8 %fusion.10 = f32[96,5120]{1,0:T(8,128)} fusion(bf16[256,5120]{1,0:T(8,128)(2,1)S(1)} %copy-done, bf16[2,12,8,128]{3,2,1,0:T(8,128)(2,1)S(1)} %fusion.3), kind=kOutput, calls=%fused_computation.17 | convolution fusion | flops 251658240 | bytes 4636672 | tf_op jit(solution)/shard_map/dot_general | solution.py:49
  29.7 0.0 reduce-scatter.2.cloned.1.call-update
  29.8 32.5 %reduce-scatter.2.cloned.1.call-done = f32[96,1280]{1,0:T(8,128)} async-done(((f32[96,5120]{1,0:T(8,128)}), f32[96,1280]{1,0:T(8,128)}) %reduce-scatter.2.cloned.1.call-update) | async-done | bytes 491536 | tf_op jit(solution)/shard_map/reduce_scatter | solution.py:50
  62.3 0.0 copy-done.1
  62.3 0.0 copy-done.2
  62.3 1.8 %add_convert_fusion = bf16[96,1280]{1,0:T(8,128)(2,1)} fusion(f32[96,1280]{1,0:T(8,128)} %reduce-scatter.2.cloned.1.call-done, bf16[96,1280]{1,0:T(8,128)(2,1)S(1)} %copy-done.1, f32[1280]{0:T(1024)S(1)} %copy-done.2), kind=kLoop, calls=%fused_computation.6 | loop fusion | flops 491520 | bytes 988160 | tf_op jit(solution)/shard_map/convert_element_type | solution.py:51
  (1 shorter events, 0.0 us)
Async XLA Ops:
  6.5 21.3 %copy-start = (bf16[256,5120]{1,0:T(8,128)(2,1)S(1)}, bf16[256,5120]{1,0:T(8,128)(2,1)}, u32[]{:S(2)}) copy-start(bf16[256,5120]{1,0:T(8,128)(2,1)} %param.13) | copy-start | bytes 7864324
  6.5 55.7 %reduce-scatter.2.cloned.1.call-start = ((), (), s32[]{:S(2)}) async-start(), calls=%async_computation.1 | async-start | bytes 2457600 | tf_op jit(solution)/shard_map/reduce_scatter | solution.py:50
  27.9 34.4 %copy-start.1 = (bf16[96,1280]{1,0:T(8,128)(2,1)S(1)}, bf16[96,1280]{1,0:T(8,128)(2,1)}, u32[]{:S(2)}) copy-start(bf16[96,1280]{1,0:T(8,128)(2,1)} %param.14) | copy-start | bytes 737284
  27.9 34.4 %copy-start.2 = (f32[1280]{0:T(1024)S(1)}, f32[1280]{0:T(1024)}, u32[]{:S(2)}) copy-start(f32[1280]{0:T(1024)} %param.15) | copy-start | bytes 15364
Sparse Core Ops, SparseCore 0:
  29.9 32.3 reduce-scatter.1
where the time goes:
time: 71.2 us; the launch traced here: 70.9 us
  waiting for transfers between devices  32.5 us (46%)
  blocking collectives  16.2 us (23%)
  between operations  13.4 us (19%)
  other arithmetic  5.07 us (7%)
  matrix products  3.63 us (5%)
    reduce_scatter x1, waiting for transfers between devices, per_device(): lax.psum_scatter(terms, ('head', 'sub'), scatter_dimension=1, tiled=True)  32.5 us
    all_gather x1, blocking collectives, per_device(): gathered = lax.all_gather(residual, 'patch', axis=0, tiled=True)  16.2 us
    dot_general x1, matrix products, per_device(): terms = jnp.dot(rounded, out_weight, preferred_element_type=jnp.float32)  1.84 us
    convert_element_type x1, other arithmetic, per_device(): (hidden_in.astype(jnp.float32) + gate[None, :] * projected).astype(jnp.bf...  1.78 us
  transfers between devices with their start and end apart: 1, of which 1 were waited for; matrix products, arithmetic and copies ran while one was open for 0% of the time, Pallas kernels for 0%

commit v1 on v0

v1 whole, which is shorter than its diff:
```python
import functools
import math

import jax
import jax.numpy as jnp
from jax import lax
from jax.experimental import pallas as pl
from jax.experimental.pallas import tpu as pltpu
from jax.sharding import PartitionSpec as P

HD = 128


def shift(array, axis, size, step):
    pairs = [(i, (i + step) % size) for i in range(size)]
    return lax.ppermute(array, axis, pairs)


def attention_kernel(scale, patch, patches, q_ref, held_k_ref, held_v_ref, *refs):
    residual_refs, out_ref = refs[:-1], refs[-1]
    rows, width = q_ref.shape
    me = lax.axis_index(patch)
    starts = [
        pl.multiple_of(lax.rem(me + patches - i, patches) * rows, rows) for i in range(patches)
    ]
    for head in range(width // HD):
        cols = slice(head * HD, (head + 1) * HD)
        value_cols = slice(width + head * HD, width + (head + 1) * HD)
        keys = jnp.concatenate(
            [
                jnp.concatenate([held_k_ref[pl.ds(at, rows), cols], ref[:, cols]], axis=1)
                for at, ref in zip(starts, residual_refs)
            ],
            axis=0,
        )
        values = jnp.concatenate(
            [
                jnp.concatenate([held_v_ref[pl.ds(at, rows), cols], ref[:, value_cols]], axis=1)
                for at, ref in zip(starts, residual_refs)
            ],
            axis=0,
        )
        q = q_ref[:, cols]
        products = lax.dot_general(
            jnp.concatenate([q, q], axis=1),
            keys,
            (((1,), (1,)), ((), ())),
            preferred_element_type=jnp.float32,
        )
        scores = products * scale
        weights = jnp.exp(scores - jnp.max(scores, axis=1, keepdims=True))
        totals = jnp.sum(weights, axis=1, keepdims=True)
        high = weights.astype(jnp.bfloat16)
        low = (weights - high.astype(jnp.float32)).astype(jnp.bfloat16)
        sums = jnp.dot(
            jnp.concatenate([high, low], axis=0), values, preferred_element_type=jnp.float32
        )
        sums = sums[:rows] + sums[rows:]
        sums = sums[:, :HD] + sums[:, HD:]
        out_ref[:, cols] = (sums / totals).astype(jnp.bfloat16)


def solution(mesh):
    patches, heads, subs = mesh.shape["patch"], mesh.shape["head"], mesh.shape["sub"]

    def per_device(
        queries, held_keys, held_values, key_change, value_change, out_weight, hidden_in, gate
    ):
        rows, width = queries.shape
        columns = hidden_in.shape[1]
        sub = lax.axis_index("sub")
        head = lax.axis_index("head")

        with jax.named_scope("residual_gather"):
            residual = jnp.concatenate(
                [key_change.astype(jnp.bfloat16), value_change.astype(jnp.bfloat16)], axis=1
            )
            residuals = [residual] + [
                shift(residual, "patch", patches, i) for i in range(1, patches)
            ]

        def weight_block(weight, of_head, of_sub):
            at = (of_head * subs + of_sub) * columns
            return lax.dynamic_slice(weight, (0, at), (width, columns))

        with jax.named_scope("weight_swap"):
            weights = []
            for step in range(heads):
                of_head = lax.rem(head + step, heads)
                parts = [weight_block(out_weight, of_head, sub)]
                for i in range(1, subs):
                    away = weight_block(out_weight, of_head, lax.rem(sub + i, subs))
                    parts.append(shift(away, "sub", subs, i))
                weights.append(parts)

        with jax.named_scope("attention"):
            attended = pl.pallas_call(
                functools.partial(attention_kernel, 1.0 / math.sqrt(HD), "patch", patches),
                out_shape=jax.ShapeDtypeStruct((rows, width), jnp.bfloat16),
                in_specs=[pl.BlockSpec(memory_space=pltpu.VMEM)] * (3 + patches),
                out_specs=pl.BlockSpec(memory_space=pltpu.VMEM),
                compiler_params=pltpu.CompilerParams(vmem_limit_bytes=8 * 1024 * 1024),
            )(queries, held_keys, held_values, *residuals)

        with jax.named_scope("attended_swap"):
            attended_parts = [attended] + [
                shift(attended, "sub", subs, i) for i in range(1, subs)
            ]

        def project(parts):
            total = 0.0
            for rows_of, weight in zip(attended_parts, parts):
                total = total + jnp.dot(rows_of, weight, preferred_element_type=jnp.float32)
            return total

        with jax.named_scope("projection"):
            arrived = []
            for step in range(1, heads):
                term = project(weights[step]).astype(jnp.bfloat16)
                arrived.append(shift(term, "head", heads, step))
            total = project(weights[0])
            for term in arrived:
                total = total + term.astype(jnp.float32)
            return (hidden_in.astype(jnp.float32) + gate[None, :] * total).astype(jnp.bfloat16)

    in_specs = (
        P(("groups", "patch"), ("head", "sub")),
        P("groups", ("head", "sub")),
        P("groups", ("head", "sub")),
        P(("groups", "patch"), ("head", "sub")),
        P(("groups", "patch"), ("head", "sub")),
        P(("head", "sub"), None),
        P(("groups", "patch"), ("head", "sub")),
        P(("groups", "head", "sub")),
    )
    out_specs = P(("groups", "patch"), ("head", "sub"))
    return jax.shard_map(
        per_device, mesh=mesh, in_specs=in_specs, out_specs=out_specs, check_vma=False
    )
```

time: 71.2 us -> 28.7 us (0.40)
  waiting for transfers between devices: 32.5 us -> 11.8 us
  blocking collectives: 16.2 us -> 0 us
  between operations: 13.4 us -> 0.15 us
  starting transfers between devices: 0.01 us -> 9.21 us
  other arithmetic: 5.07 us -> 0.02 us
  local copies, waits for them, and re-layouts: 0.02 us -> 2.61 us
  Pallas kernels: 0 us -> 0.83 us
    reduce_scatter x1 -> x0, waiting for transfers between devices: 32.5 us -> none  [per_device(): lax.psum_scatter(terms, ('head', 'sub'), scatter_dimension=1, tiled=True)]
    all_gather x1 -> x0, blocking collectives: 16.2 us -> none  [per_device(): gathered = lax.all_gather(residual, 'patch', axis=0, tiled=True)]
    ppermute x0 -> x7, waiting for transfers between devices: none -> 11.8 us  [shift(): return lax.ppermute(array, axis, pairs)]
    ppermute x0 -> x7, starting transfers between devices: none -> 9.21 us  [shift(): return lax.ppermute(array, axis, pairs)]
    dynamic_slice x0 -> x1, local copies, waits for them, and re-layouts: none -> 2.58 us  [weight_block(): return lax.dynamic_slice(weight, (0, at), (width, columns))]
    convert_element_type x1 -> x0, other arithmetic: 1.78 us -> none  [per_device(): (hidden_in.astype(jnp.float32) + gate[None, :] * projected).astype(jnp.bf...]
    unnamed x1 -> x0, other arithmetic: 1.12 us -> none
    convert_element_type x1, other arithmetic: 1.05 us -> 0.01 us  [per_device(): key_change.astype(jnp.bfloat16)]
  transfers between devices with their start and end apart: 1 -> 7, of which waited for: 1 -> 4; matrix products, arithmetic and copies ran while one was open for 0% -> 10% of each run, Pallas kernels for 0% -> 3%
where the time goes in v1:
time: 28.7 us; the launch traced here: 28.5 us
  waiting for transfers between devices  11.8 us (41%)
  starting transfers between devices  9.21 us (32%)
  matrix products  3.88 us (14%)
  local copies, waits for them, and re-layouts  2.61 us (9%)
  Pallas kernels  0.83 us (3%)
    ppermute x7, waiting for transfers between devices, shift(): return lax.ppermute(array, axis, pairs)  11.8 us
    ppermute x7, starting transfers between devices, shift(): return lax.ppermute(array, axis, pairs)  9.21 us
    dot_general x4, matrix products, project(): total = total + jnp.dot(rows_of, weight, preferred_element_type=jnp.float32)  3.88 us
    dynamic_slice x1, local copies, waits for them, and re-layouts, weight_block(): return lax.dynamic_slice(weight, (0, at), (width, columns))  2.58 us
    pallas_call x1, Pallas kernels, per_device(): pl.pallas_call(functools.partial(attention_kernel, 1.0 / math.sqrt(HD), '...  0.83 us
  transfers between devices with their start and end apart: 7, of which 4 were waited for; matrix products, arithmetic and copies ran while one was open for 10% of the time, Pallas kernels for 3%

profile of v1, /device:TPU:0, one launch (start us, length us, event | category | flops | bytes accessed | tf_op | source)
XLA Modules:
  0.0 28.5 jit_solution(15464093663914759621)
XLA Ops:
  0.0 0.0 copy-start.5
  0.0 0.0 copy-start.6
  0.0 0.0 copy-start.1
  0.0 0.0 copy-start.2
  0.0 0.0 copy-start
  0.0 0.0 copy-start.3
  0.0 2.6 %constant_dynamic-slice_fusion = (bf16[256,1280]{1,0:T(8,128)(2,1)}, bf16[256,1280]{1,0:T(8,128)(2,1)}) fusion(bf16[256,5120]{1,0:T(8,128)(2,1)} %param.13, s32[]{:T(128)S(6)} %select_n.15, s32[]{:T(128)S(6)} %select_n.13), kind=kLoop, calls=%fused_computation.10 | loop fusion | bytes 2621448 | tf_op jit(solution)/shard_map/weight_swap/dynamic_slice | solution.py:84
  2.6 0.0 copy-start.4
  2.6 0.0 copy-start.7
  2.6 0.5 %collective-permute-start.5 = (bf16[256,1280]{1,0:T(8,128)(2,1)}, bf16[256,1280]{1,0:T(8,128)(2,1)}, u32[]{:S(2)}, u32[]{:S(2)}) collective-permute-start(bf16[256,1280]{1,0:T(8,128)(2,1)} %get-tuple-element.5), channel_id=1, source_target_pairs={{0,1},{1,0},{2,3},{3,2},{4,5},{5,4},{6,7},{7,6},{8,9},{9,8},{10,11... | collective-permute-start | bytes 1966088 | tf_op jit(solution)/shard_map/weight_swap/ppermute | solution.py:16
  3.1 0.1 collective-permute-start.4
  3.2 0.0 copy-done.5
  3.2 0.0 copy-done.6
  3.2 3.1 %collective-permute-start = (bf16[96,512]{1,0:T(8,128)(2,1)S(1)}, bf16[96,512]{1,0:T(8,128)(2,1)S(1)}, u32[]{:S(2)}, u32[]{:S(2)}) collective-permute-start(bf16[96,512]{1,0:T(8,128)(2,1)S(1)} %pad_maximum_fusion.refs_0_), channel_id=1, source_target_pairs={{0,4},{4,8},{8,12},{12,0},{1,5},{5,9},{9,13},{13,1},{2,6},{6,10},{... | collective-permute-start | bytes 294920 | tf_op jit(solution)/shard_map/residual_gather/ppermute | solution.py:16
  6.3 2.6 %collective-permute-start.1 = (bf16[96,512]{1,0:T(8,128)(2,1)S(1)}, bf16[96,512]{1,0:T(8,128)(2,1)S(1)}, u32[]{:S(2)}, u32[]{:S(2)}) collective-permute-start(bf16[96,512]{1,0:T(8,128)(2,1)S(1)} %pad_maximum_fusion.refs_0_), channel_id=1, source_target_pairs={{0,8},{4,12},{8,0},{12,4},{1,9},{5,13},{9,1},{13,5},{2,10},{6,14},... | collective-permute-start | bytes 294920 | tf_op jit(solution)/shard_map/residual_gather/ppermute | solution.py:16
  8.9 1.3 %collective-permute-start.2 = (bf16[96,512]{1,0:T(8,128)(2,1)S(1)}, bf16[96,512]{1,0:T(8,128)(2,1)S(1)}, u32[]{:S(2)}, u32[]{:S(2)}) collective-permute-start(bf16[96,512]{1,0:T(8,128)(2,1)S(1)} %pad_maximum_fusion.refs_0_), channel_id=1, source_target_pairs={{0,12},{4,0},{8,4},{12,8},{1,13},{5,1},{9,5},{13,9},{2,14},{6,2},{... | collective-permute-start | bytes 294920 | tf_op jit(solution)/shard_map/residual_gather/ppermute | solution.py:16
  10.2 1.8 %collective-permute-done.refs_1_ = bf16[96,512]{1,0:T(8,128)(2,1)S(1)} collective-permute-done((bf16[96,512]{1,0:T(8,128)(2,1)S(1)}, bf16[96,512]{1,0:T(8,128)(2,1)S(1)}, u32[]{:S(2)}, u32[]{:S(2)}) %collective-permute-start) | collective-permute-done | bytes 98336 | tf_op jit(solution)/shard_map/residual_gather/ppermute | solution.py:16
  12.0 3.6 %collective-permute-done.1.refs_2_ = bf16[96,512]{1,0:T(8,128)(2,1)S(1)} collective-permute-done((bf16[96,512]{1,0:T(8,128)(2,1)S(1)}, bf16[96,512]{1,0:T(8,128)(2,1)S(1)}, u32[]{:S(2)}, u32[]{:S(2)}) %collective-permute-start.1) | collective-permute-done | bytes 98336 | tf_op jit(solution)/shard_map/residual_gather/ppermute | solution.py:16
  15.7 0.0 collective-permute-done.2.refs_3_
  15.7 0.0 copy-done.1
  15.7 0.0 copy-done.2
  15.7 0.0 copy-done
  15.7 0.8 %attention.1 = bf16[96,256]{1,0:T(8,128)(2,1)S(1)} custom-call(bf16[96,256]{1,0:T(8,128)(2,1)S(1)} %copy-done.2, bf16[384,256]{1,0:T(8,128)(2,1)S(1)} %copy-done, bf16[384,256]{1,0:T(8,128)(2,1)S(1)} %copy-done.1, bf16[96,512]{1,0:T(8,128)(2,1)S(1)} %pad_maximum_fusion.refs_0_, bf16[96,512]{1,0:T(8,128)(2,1)S(1)} %collective-permute-done.refs_1_, ...), custom_call_target="tpu_custom_call" | custom-call | tf_op jit(solution)/shard_map/attention/pallas_call | solution.py:97
  16.5 0.1 collective-permute-start.3
  16.6 1.2 %collective-permute-done.3 = bf16[96,256]{1,0:T(8,128)(2,1)S(1)} collective-permute-done((bf16[96,256]{1,0:T(8,128)(2,1)S(1)}, bf16[96,256]{1,0:T(8,128)(2,1)S(1)}, u32[]{:S(2)}, u32[]{:S(2)}) %collective-permute-start.3) | collective-permute-done | bytes 49184 | tf_op jit(solution)/shard_map/attended_swap/ppermute | solution.py:16
  17.8 0.0 collective-permute-done.5
  17.8 1.3 %fusion.10 = f32[96,1280]{1,0:T(8,128)S(1)} fusion(bf16[96,256]{1,0:T(8,128)(2,1)S(1)} %collective-permute-done.3, bf16[256,1280]{1,0:T(8,128)(2,1)} %collective-permute-done.5), kind=kOutput, calls=%fused_computation.15 | convolution fusion | flops 62914560 | bytes 1196032 | tf_op jit(solution)/shard_map/projection/dot_general | solution.py:113
  19.1 0.0 copy-done.3
  19.2 0.3 fusion.4
  19.4 1.6 %collective-permute-start.6 = (bf16[96,1280]{1,0:T(8,128)(2,1)S(1)}, bf16[96,1280]{1,0:T(8,128)(2,1)S(1)}, u32[]{:S(2)}, u32[]{:S(2)}) collective-permute-start(bf16[96,1280]{1,0:T(8,128)(2,1)S(1)} %fusion.4), channel_id=1, source_target_pairs={{0,2},{2,0},{1,3},{3,1},{4,6},{6,4},{5,7},{7,5},{8,10},{10,8},{9,1... | collective-permute-start | bytes 737288 | tf_op jit(solution)/shard_map/projection/ppermute | solution.py:16
  21.0 0.0 collective-permute-done.4
  21.0 1.3 %fusion.9 = f32[96,1280]{1,0:T(8,128)S(1)} fusion(bf16[96,256]{1,0:T(8,128)(2,1)S(1)} %collective-permute-done.3, bf16[256,1280]{1,0:T(8,128)(2,1)} %collective-permute-done.4), kind=kOutput, calls=%fused_computation.14 | convolution fusion | flops 62914560 | bytes 1196032 | tf_op jit(solution)/shard_map/projection/dot_general | solution.py:113
  22.4 5.1 %collective-permute-done.6 = bf16[96,1280]{1,0:T(8,128)(2,1)S(1)} collective-permute-done((bf16[96,1280]{1,0:T(8,128)(2,1)S(1)}, bf16[96,1280]{1,0:T(8,128)(2,1)S(1)}, u32[]{:S(2)}, u32[]{:S(2)}) %collective-permute-start.6) | collective-permute-done | bytes 245792 | tf_op jit(solution)/shard_map/projection/ppermute | solution.py:16
  27.5 0.0 copy-done.4
  27.5 0.0 copy-done.7
  27.5 1.0 %fusion.3 = bf16[96,1280]{1,0:T(8,128)(2,1)} fusion(f32[96,1280]{1,0:T(8,128)S(1)} %fusion.9, bf16[96,256]{1,0:T(8,128)(2,1)S(1)} %attention.1, bf16[256,5120]{1,0:T(8,128)(2,1)S(1)} %copy-done.3, s32[]{:T(128)S(6)} %select_n.12, bf16[96,1280]{1,0:T(8,128)(2,1)S(1)} %collective-permute-done.6, bf16[96,1280]{1,0:T(8,128)(2,1)S(1)} %copy-done.4, ...), kind=kOutput, calls=%fused_computation.5 | convolution fusion | flops 63774720 | bytes 1941508 | tf_op jit(solution)/shard_map/projection/dot_general | solution.py:113
  (3 shorter events, 0.0 us)
Async XLA Ops:
  0.0 3.2 %copy-start.5 = (f32[96,256]{1,0:T(8,128)S(1)}, f32[96,256]{1,0:T(8,128)}, u32[]{:S(2)}) copy-start(f32[96,256]{1,0:T(8,128)} %param.11) | copy-start | bytes 294916
  0.0 3.2 %copy-start.6 = (f32[96,256]{1,0:T(8,128)S(1)}, f32[96,256]{1,0:T(8,128)}, u32[]{:S(2)}) copy-start(f32[96,256]{1,0:T(8,128)} %param.12) | copy-start | bytes 294916
  0.0 15.7 %copy-start.1 = (bf16[384,256]{1,0:T(8,128)(2,1)S(1)}, bf16[384,256]{1,0:T(8,128)(2,1)}, u32[]{:S(2)}) copy-start(bf16[384,256]{1,0:T(8,128)(2,1)} %held_v_ref.1) | copy-start | bytes 589828
  0.0 15.7 %copy-start.2 = (bf16[96,256]{1,0:T(8,128)(2,1)S(1)}, bf16[96,256]{1,0:T(8,128)(2,1)}, u32[]{:S(2)}) copy-start(bf16[96,256]{1,0:T(8,128)(2,1)} %q_ref.1) | copy-start | bytes 147460
  0.0 15.7 %copy-start = (bf16[384,256]{1,0:T(8,128)(2,1)S(1)}, bf16[384,256]{1,0:T(8,128)(2,1)}, u32[]{:S(2)}) copy-start(bf16[384,256]{1,0:T(8,128)(2,1)} %held_k_ref.1) | copy-start | bytes 589828
  0.0 19.1 %copy-start.3 = (bf16[256,5120]{1,0:T(8,128)(2,1)S(1)}, bf16[256,5120]{1,0:T(8,128)(2,1)}, u32[]{:S(2)}) copy-start(bf16[256,5120]{1,0:T(8,128)(2,1)} %param.13) | copy-start | bytes 7864324
  2.6 24.9 %copy-start.4 = (bf16[96,1280]{1,0:T(8,128)(2,1)S(1)}, bf16[96,1280]{1,0:T(8,128)(2,1)}, u32[]{:S(2)}) copy-start(bf16[96,1280]{1,0:T(8,128)(2,1)} %param.14) | copy-start | bytes 737284
  2.6 24.9 %copy-start.7 = (f32[1280]{0:T(1024)S(1)}, f32[1280]{0:T(1024)}, u32[]{:S(2)}) copy-start(f32[1280]{0:T(1024)} %param.15) | copy-start | bytes 15364
  2.6 15.2 %collective-permute-start.5 = (bf16[256,1280]{1,0:T(8,128)(2,1)}, bf16[256,1280]{1,0:T(8,128)(2,1)}, u32[]{:S(2)}, u32[]{:S(2)}) collective-permute-start(bf16[256,1280]{1,0:T(8,128)(2,1)} %get-tuple-element.5), channel_id=1, source_target_pairs={{0,1},{1,0},{2,3},{3,2},{4,5},{5,4},{6,7},{7,6},{8,9},{9,8},{10,11... | collective-permute-start | bytes 1966088 | tf_op jit(solution)/shard_map/weight_swap/ppermute | solution.py:16
  3.1 17.9 %collective-permute-start.4 = (bf16[256,1280]{1,0:T(8,128)(2,1)}, bf16[256,1280]{1,0:T(8,128)(2,1)}, u32[]{:S(2)}, u32[]{:S(2)}) collective-permute-start(bf16[256,1280]{1,0:T(8,128)(2,1)} %get-tuple-element.6), channel_id=1, source_target_pairs={{0,1},{1,0},{2,3},{3,2},{4,5},{5,4},{6,7},{7,6},{8,9},{9,8},{10,11... | collective-permute-start | bytes 1966088 | tf_op jit(solution)/shard_map/weight_swap/ppermute | solution.py:16
  3.2 8.8 %collective-permute-start = (bf16[96,512]{1,0:T(8,128)(2,1)S(1)}, bf16[96,512]{1,0:T(8,128)(2,1)S(1)}, u32[]{:S(2)}, u32[]{:S(2)}) collective-permute-start(bf16[96,512]{1,0:T(8,128)(2,1)S(1)} %pad_maximum_fusion.refs_0_), channel_id=1, source_target_pairs={{0,4},{4,8},{8,12},{12,0},{1,5},{5,9},{9,13},{13,1},{2,6},{6,10},{... | collective-permute-start | bytes 294920 | tf_op jit(solution)/shard_map/residual_gather/ppermute | solution.py:16
  6.3 9.4 %collective-permute-start.1 = (bf16[96,512]{1,0:T(8,128)(2,1)S(1)}, bf16[96,512]{1,0:T(8,128)(2,1)S(1)}, u32[]{:S(2)}, u32[]{:S(2)}) collective-permute-start(bf16[96,512]{1,0:T(8,128)(2,1)S(1)} %pad_maximum_fusion.refs_0_), channel_id=1, source_target_pairs={{0,8},{4,12},{8,0},{12,4},{1,9},{5,13},{9,1},{13,5},{2,10},{6,14},... | collective-permute-start | bytes 294920 | tf_op jit(solution)/shard_map/residual_gather/ppermute | solution.py:16
  8.9 6.8 %collective-permute-start.2 = (bf16[96,512]{1,0:T(8,128)(2,1)S(1)}, bf16[96,512]{1,0:T(8,128)(2,1)S(1)}, u32[]{:S(2)}, u32[]{:S(2)}) collective-permute-start(bf16[96,512]{1,0:T(8,128)(2,1)S(1)} %pad_maximum_fusion.refs_0_), channel_id=1, source_target_pairs={{0,12},{4,0},{8,4},{12,8},{1,13},{5,1},{9,5},{13,9},{2,14},{6,2},{... | collective-permute-start | bytes 294920 | tf_op jit(solution)/shard_map/residual_gather/ppermute | solution.py:16
  16.5 1.3 %collective-permute-start.3 = (bf16[96,256]{1,0:T(8,128)(2,1)S(1)}, bf16[96,256]{1,0:T(8,128)(2,1)S(1)}, u32[]{:S(2)}, u32[]{:S(2)}) collective-permute-start(bf16[96,256]{1,0:T(8,128)(2,1)S(1)} %attention.1), channel_id=1, source_target_pairs={{0,1},{1,0},{2,3},{3,2},{4,5},{5,4},{6,7},{7,6},{8,9},{9,8},{10,11... | collective-permute-start | bytes 147464 | tf_op jit(solution)/shard_map/attended_swap/ppermute | solution.py:16
  19.4 8.1 %collective-permute-start.6 = (bf16[96,1280]{1,0:T(8,128)(2,1)S(1)}, bf16[96,1280]{1,0:T(8,128)(2,1)S(1)}, u32[]{:S(2)}, u32[]{:S(2)}) collective-permute-start(bf16[96,1280]{1,0:T(8,128)(2,1)S(1)} %fusion.4), channel_id=1, source_target_pairs={{0,2},{2,0},{1,3},{3,1},{4,6},{6,4},{5,7},{7,5},{8,10},{10,8},{9,1... | collective-permute-start | bytes 737288 | tf_op jit(solution)/shard_map/projection/ppermute | solution.py:16

commit v2 on v1

v2 whole, which is shorter than its diff:
```python
import functools
import math

import jax
import jax.numpy as jnp
from jax import lax
from jax.experimental import pallas as pl
from jax.experimental.pallas import tpu as pltpu
from jax.sharding import PartitionSpec as P

HD = 128
LANES = 128
VMEM_LIMIT = 12 * 1024 * 1024

IN_VMEM = pl.BlockSpec(memory_space=pltpu.VMEM)
ANYWHERE = pl.BlockSpec(memory_space=pl.ANY)


def call(kernel, out_shape, in_specs, out_specs, name, flops=0, moved=0, scratch_shapes=()):
    return pl.pallas_call(
        kernel,
        out_shape=out_shape,
        in_specs=in_specs,
        out_specs=out_specs,
        scratch_shapes=scratch_shapes,
        name=name,
        cost_estimate=pl.CostEstimate(flops=flops, bytes_accessed=moved, transcendentals=0),
        compiler_params=pltpu.CompilerParams(vmem_limit_bytes=VMEM_LIMIT),
    )


def shift(array, axis, size, step):
    return lax.ppermute(array, axis, [(i, (i + step) % size) for i in range(size)])


def gather_line_of_four(own):
    first = lax.ppermute(own, "patch", [(0, 2), (2, 3), (3, 1), (1, 0)])
    second = lax.ppermute(own, "patch", [(0, 1), (1, 3), (3, 2), (2, 0)])
    middle = lax.ppermute(own, "patch", [(1, 2), (2, 1)])
    ends = lax.ppermute(first, "patch", [(2, 3), (1, 0)])
    return [own, first, second, middle, ends]


def line_of_four_sources(place):
    def table(*entries):
        value = jnp.int32(entries[0])
        for i, entry in enumerate(entries[1:], 1):
            value = jnp.where(place == i, jnp.int32(entry), value)
        return value

    return [place, table(1, 3, 0, 2), table(2, 0, 3, 1), table(3, 2, 1, 0)]


def attention_kernel(scale, patches, q_ref, held_k_ref, held_v_ref, *refs):
    block_refs, out_ref = refs[:-1], refs[-1]
    rows, width = q_ref.shape
    me = lax.axis_index("patch")
    if patches == 4:
        sources = line_of_four_sources(me)
        inner = jnp.logical_and(me > 0, me < 3)
        last = jnp.where(inner, block_refs[3][...], block_refs[4][...])
        blocks = [ref[...] for ref in block_refs[:3]] + [last]
    else:
        sources = [lax.rem(me + patches - i, patches) for i in range(patches)]
        blocks = [ref[...] for ref in block_refs]
    starts = [pl.multiple_of(source * rows, rows) for source in sources]
    for head in range(width // HD):
        cols = slice(head * HD, (head + 1) * HD)
        value_cols = slice(width + head * HD, width + (head + 1) * HD)
        keys = jnp.concatenate(
            [
                jnp.concatenate([held_k_ref[pl.ds(at, rows), cols], block[:, cols]], axis=1)
                for at, block in zip(starts, blocks)
            ],
            axis=0,
        )
        values = jnp.concatenate(
            [
                jnp.concatenate([held_v_ref[pl.ds(at, rows), cols], block[:, value_cols]], axis=1)
                for at, block in zip(starts, blocks)
            ],
            axis=0,
        )
        q = q_ref[:, cols]
        products = lax.dot_general(
            jnp.concatenate([q, q], axis=1),
            keys,
            (((1,), (1,)), ((), ())),
            preferred_element_type=jnp.float32,
        )
        scores = products * scale
        weights = jnp.exp(scores - jnp.max(scores, axis=1, keepdims=True))
        totals = jnp.sum(weights, axis=1, keepdims=True)
        high = weights.astype(jnp.bfloat16)
        low = (weights - high.astype(jnp.float32)).astype(jnp.bfloat16)
        sums = jnp.dot(
            jnp.concatenate([high, low], axis=0), values, preferred_element_type=jnp.float32
        )
        sums = sums[:rows] + sums[rows:]
        sums = sums[:, :HD] + sums[:, HD:]
        out_ref[:, cols] = (sums / totals).astype(jnp.bfloat16)


def slices_kernel(heads, subs, columns, weight_ref, after_1_ref, after_2_ref, *refs):
    out_refs, sems = refs[:-1], refs[-1]
    head, sub = lax.axis_index("head"), lax.axis_index("sub")
    copies = []
    for n, out_ref in enumerate(out_refs):
        step, i = n // subs, n % subs
        block = lax.rem(head + step, heads) * subs + lax.rem(sub + i, subs)
        at = pl.multiple_of(block * columns, LANES)
        copies.append(
            pltpu.make_async_copy(weight_ref.at[:, pl.ds(at, columns)], out_ref, sems.at[n])
        )
    for copy in copies:
        copy.start()
    for copy in copies:
        copy.wait()


def dot(a_ref, b_ref):
    return jnp.dot(a_ref[...], b_ref[...], preferred_element_type=jnp.float32)


def own_term_kernel(attended_ref, weight_ref, out_ref):
    out_ref[...] = dot(attended_ref, weight_ref)


def sent_term_kernel(total_ref, *refs):
    out_ref = refs[-1]
    total = total_ref[...]
    for attended_ref, weight_ref in zip(refs[:-1:2], refs[1:-1:2]):
        total = total + dot(attended_ref, weight_ref)
    out_ref[...] = total.astype(jnp.bfloat16)


def base_kernel(hidden_ref, gate_ref, *refs):
    out_ref = refs[-1]
    total = 0.0
    for attended_ref, weight_ref in zip(refs[:-1:2], refs[1:-1:2]):
        total = total + dot(attended_ref, weight_ref)
    out_ref[...] = hidden_ref[...].astype(jnp.float32) + gate_ref[...] * total


def final_kernel(base_ref, gate_ref, *refs):
    arrived_refs, out_ref = refs[:-1], refs[-1]
    total = 0.0
    for ref in arrived_refs:
        total = total + ref[...].astype(jnp.float32)
    out_ref[...] = (base_ref[...] + gate_ref[...] * total).astype(jnp.bfloat16)


def solution(mesh):
    patches, heads, subs = mesh.shape["patch"], mesh.shape["head"], mesh.shape["sub"]

    def per_device(
        queries, held_keys, held_values, key_change, value_change, out_weight, hidden_in, gate
    ):
        rows, width = queries.shape
        columns = hidden_in.shape[1]

        with jax.named_scope("residual_gather"):
            residual = jnp.concatenate(
                [key_change.astype(jnp.bfloat16), value_change.astype(jnp.bfloat16)], axis=1
            )
            if patches == 4:
                blocks = gather_line_of_four(residual)
            else:
                blocks = [residual] + [
                    shift(residual, "patch", patches, i) for i in range(1, patches)
                ]

        with jax.named_scope("weight_swap"):
            if columns % LANES == 0:
                block_shape = jax.ShapeDtypeStruct((width, columns), jnp.bfloat16)
                count = heads * subs
                slices = call(
                    functools.partial(slices_kernel, heads, subs, columns),
                    [block_shape] * count,
                    [pl.BlockSpec(memory_space=pltpu.HBM), ANYWHERE, ANYWHERE],
                    [IN_VMEM] * count,
                    "weight_slices",
                    moved=2 * 2 * width * columns * count,
                    scratch_shapes=[pltpu.SemaphoreType.DMA((count,))],
                )(out_weight, *blocks[2:4])
            else:
                head, sub = lax.axis_index("head"), lax.axis_index("sub")
                slices = []
                for step in range(heads):
                    for i in range(subs):
                        block = lax.rem(head + step, heads) * subs + lax.rem(sub + i, subs)
                        slices.append(
                            lax.dynamic_slice(out_weight, (0, block * columns), (width, columns))
                        )
            weights = [
                [
                    slices[step * subs + i] if i == 0
                    else shift(slices[step * subs + i], "sub", subs, i)
                    for i in range(subs)
                ]
                for step in range(heads)
            ]

        with jax.named_scope("attention"):
            attended = call(
                functools.partial(attention_kernel, 1.0 / math.sqrt(HD), patches),
                jax.ShapeDtypeStruct((rows, width), jnp.bfloat16),
                [IN_VMEM] * (3 + len(blocks)),
                IN_VMEM,
                "attention",
                flops=20_000_000_000,
            )(queries, held_keys, held_values, *blocks)

        with jax.named_scope("attended_swap"):
            attended_parts = [attended] + [
                shift(attended, "sub", subs, i) for i in range(1, subs)
            ]

        term = jax.ShapeDtypeStruct((rows, columns), jnp.float32)
        sent = jax.ShapeDtypeStruct((rows, columns), jnp.bfloat16)
        product_flops = 2 * rows * width * columns
        with jax.named_scope("projection"):
            arrived = []
            for step in range(1, heads):
                own = call(
                    own_term_kernel, term, [IN_VMEM] * 2, IN_VMEM, "own_term", product_flops
                )(attended, weights[step][0])
                pairs = [
                    x for i in range(1, subs) for x in (attended_parts[i], weights[step][i])
                ]
                total = call(
                    sent_term_kernel,
                    sent,
                    [IN_VMEM] * (1 + len(pairs)),
                    IN_VMEM,
                    "sent_term",
                    product_flops,
                )(own, *pairs)
                arrived.append(shift(total, "head", heads, step))
            gate_row = gate.reshape(1, columns)
            pairs = [x for i in range(subs) for x in (attended_parts[i], weights[0][i])]
            base = call(
                base_kernel,
                term,
                [IN_VMEM] * (2 + len(pairs)),
                IN_VMEM,
                "base",
                2 * product_flops,
            )(hidden_in, gate_row, *pairs)
            return call(
                final_kernel,
                sent,
                [IN_VMEM] * (2 + len(arrived)),
                IN_VMEM,
                "final",
                moved=rows * columns * 8,
            )(base, gate_row, *arrived)

    in_specs = (
        P(("groups", "patch"), ("head", "sub")),
        P("groups", ("head", "sub")),
        P("groups", ("head", "sub")),
        P(("groups", "patch"), ("head", "sub")),
        P(("groups", "patch"), ("head", "sub")),
        P(("head", "sub"), None),
        P(("groups", "patch"), ("head", "sub")),
        P(("groups", "head", "sub")),
    )
    out_specs = P(("groups", "patch"), ("head", "sub"))
    return jax.shard_map(
        per_device, mesh=mesh, in_specs=in_specs, out_specs=out_specs, check_vma=False
    )
```

time: 28.7 us -> 27.2 us (0.948)
  matrix products: 3.88 us -> 0 us
  Pallas kernels: 0.83 us -> 2.68 us
  other arithmetic: 0.02 us -> 1.86 us
  starting transfers between devices: 9.21 us -> 8.23 us
  local copies, waits for them, and re-layouts: 2.61 us -> 1.77 us
  waiting for transfers between devices: 11.8 us -> 12.3 us
    dot_general x4 -> x0, matrix products: 3.88 us -> none  [project(): total = total + jnp.dot(rows_of, weight, preferred_element_type=jnp.float32)]
    dynamic_slice x1 -> x0, local copies, waits for them, and re-layouts: 2.58 us -> none  [weight_block(): return lax.dynamic_slice(weight, (0, at), (width, columns))]
    pallas_call x1 -> x6, Pallas kernels: 0.83 us -> 2.68 us  [the longest x1 0.83 us: per_device(): call(functools.partial(attention_kernel, 1.0 / math.sqrt(HD), patches), j...]
    unnamed x16 -> x12, local copies, waits for them, and re-layouts: 0.03 us -> 1.76 us
    ppermute x7 -> x8, starting transfers between devices: 9.21 us -> 8.23 us  [the longest x1 4.09 us: gather_line_of_four(): first = lax.ppermute(own, 'patch', [(0, 2), (2, 3), (3, 1), (1, 0)])]
    convert_element_type x1, other arithmetic: 0.01 us -> 0.95 us  [per_device(): key_change.astype(jnp.bfloat16)]
    convert_element_type x1, other arithmetic: 0.01 us -> 0.9 us  [per_device(): value_change.astype(jnp.bfloat16)]
    ppermute x7 -> x8, waiting for transfers between devices: 11.8 us -> 12.3 us  [the longest x4 7.26 us: shift(): lax.ppermute(array, axis, [(i, (i + step) % size) for i in range(size)])]
  transfers between devices with their start and end apart: 7 -> 8, of which waited for: 4 -> 5; matrix products, arithmetic and copies ran while one was open for 10% -> 0% of each run, Pallas kernels for 3% -> 7%
where the time goes in v2:
time: 27.2 us; the launch traced here: 27 us
  waiting for transfers between devices  12.3 us (45%)
  starting transfers between devices  8.23 us (30%)
  Pallas kernels  2.68 us (10%)
  other arithmetic  1.86 us (7%)
  local copies, waits for them, and re-layouts  1.77 us (7%)
    ppermute x4, waiting for transfers between devices, shift(): lax.ppermute(array, axis, [(i, (i + step) % size) for i in range(size)])  7.26 us
    ppermute x1, starting transfers between devices, gather_line_of_four(): first = lax.ppermute(own, 'patch', [(0, 2), (2, 3), (3, 1), (1, 0)])  4.09 us
    ppermute x1, waiting for transfers between devices, gather_line_of_four(): first = lax.ppermute(own, 'patch', [(0, 2), (2, 3), (3, 1), (1, 0)])  2.44 us
    ppermute x1, waiting for transfers between devices, gather_line_of_four(): second = lax.ppermute(own, 'patch', [(0, 1), (1, 3), (3, 2), (2, 0)])  2.35 us
    ppermute x4, starting transfers between devices, shift(): lax.ppermute(array, axis, [(i, (i + step) % size) for i in range(size)])  2.2 us
    unnamed x12, local copies, waits for them, and re-layouts  1.76 us
    ppermute x1, starting transfers between devices, gather_line_of_four(): ends = lax.ppermute(first, 'patch', [(2, 3), (1, 0)])  1.28 us
    convert_element_type x1, other arithmetic, per_device(): key_change.astype(jnp.bfloat16)  0.95 us
  transfers between devices with their start and end apart: 8, of which 5 were waited for; matrix products, arithmetic and copies ran while one was open for 0% of the time, Pallas kernels for 7%

profile of v2, /device:TPU:0, one launch (start us, length us, event | category | flops | bytes accessed | tf_op | source)
XLA Modules:
  0.0 27.0 jit_solution(1634421983360228737)
XLA Ops:
  0.0 0.0 copy-start.3
  0.0 0.0 copy-start.4
  0.0 0.0 copy-start.2
  0.0 0.9 %convert_element_type.6 = bf16[96,256]{1,0:T(8,128)(2,1)S(1)} convert(f32[96,256]{1,0:T(8,128)} %param.11) | non-fusion elementwise | flops 24576 | bytes 147456 | tf_op jit(solution)/shard_map/residual_gather/convert_element_type | solution.py:164
  1.0 0.9 %convert_element_type.7 = bf16[96,256]{1,0:T(8,128)(2,1)S(1)} convert(f32[96,256]{1,0:T(8,128)} %param.12) | non-fusion elementwise | flops 24576 | bytes 147456 | tf_op jit(solution)/shard_map/residual_gather/convert_element_type | solution.py:164
  1.9 4.1 %collective-permute-start = (bf16[96,512]{1,0:T(8,128)(2,1)S(1)}, bf16[96,512]{1,0:T(8,128)(2,1)S(1)}, u32[]{:S(2)}, u32[]{:S(2)}) collective-permute-start(bf16[96,512]{1,0:T(8,128)(2,1)S(1)} %pad_maximum_fusion.refs_0_), channel_id=1, source_target_pairs={{0,8},{8,12},{12,4},{4,0},{1,9},{9,13},{13,5},{5,1},{2,10},{10,14}... | collective-permute-start | bytes 294920 | tf_op jit(solution)/shard_map/residual_gather/ppermute | solution.py:37
  6.0 0.0 collective-permute-start.1
  6.0 0.7 %collective-permute-start.2 = (bf16[96,512]{1,0:T(8,128)(2,1)S(1)}, bf16[96,512]{1,0:T(8,128)(2,1)S(1)}, u32[]{:S(2)}, u32[]{:S(2)}) collective-permute-start(bf16[96,512]{1,0:T(8,128)(2,1)S(1)} %pad_maximum_fusion.refs_0_), channel_id=1, source_target_pairs={{4,8},{8,4},{5,9},{9,5},{6,10},{10,6},{7,11},{11,7},{20,24},{24,20... | collective-permute-start | bytes 294920 | tf_op jit(solution)/shard_map/residual_gather/ppermute | solution.py:39
  6.6 2.4 %collective-permute-done.refs_1_ = bf16[96,512]{1,0:T(8,128)(2,1)S(1)} collective-permute-done((bf16[96,512]{1,0:T(8,128)(2,1)S(1)}, bf16[96,512]{1,0:T(8,128)(2,1)S(1)}, u32[]{:S(2)}, u32[]{:S(2)}) %collective-permute-start) | collective-permute-done | bytes 98336 | tf_op jit(solution)/shard_map/residual_gather/ppermute | solution.py:37
  9.1 1.3 %collective-permute-start.3 = (bf16[96,512]{1,0:T(8,128)(2,1)S(1)}, bf16[96,512]{1,0:T(8,128)(2,1)S(1)}, u32[]{:S(2)}, u32[]{:S(2)}) collective-permute-start(bf16[96,512]{1,0:T(8,128)(2,1)S(1)} %collective-permute-done.refs_1_), channel_id=1, source_target_pairs={{8,12},{4,0},{9,13},{5,1},{10,14},{6,2},{11,15},{7,3},{24,28},{20,... | collective-permute-start | bytes 294920 | tf_op jit(solution)/shard_map/residual_gather/ppermute | solution.py:40
  10.4 2.4 %collective-permute-done.1.refs_2_.after_1_ref = bf16[96,512]{1,0:T(8,128)(2,1)S(1)} collective-permute-done((bf16[96,512]{1,0:T(8,128)(2,1)S(1)}, bf16[96,512]{1,0:T(8,128)(2,1)S(1)}, u32[]{:S(2)}, u32[]{:S(2)}) %collective-permute-start.1) | collective-permute-done | bytes 98336 | tf_op jit(solution)/shard_map/residual_gather/ppermute | solution.py:38
  12.7 0.0 collective-permute-done.2.refs_3_.after_2_ref
  12.7 0.0 copy-start
  12.7 1.7 %copy-done = bf16[256,5120]{1,0:T(8,128)(2,1)S(1)} copy-done((bf16[256,5120]{1,0:T(8,128)(2,1)S(1)}, bf16[256,5120]{1,0:T(8,128)(2,1)}, u32[]{:S(2)}) %copy-start) | copy-done | bytes 2621464
  14.5 0.3 weight_slices.1
  14.7 0.1 collective-permute-start.6
  14.8 0.5 %collective-permute-start.5 = (bf16[256,1280]{1,0:T(8,128)(2,1)S(1)}, bf16[256,1280]{1,0:T(8,128)(2,1)S(1)}, u32[]{:S(2)}, u32[]{:S(2)}) collective-permute-start(bf16[256,1280]{1,0:T(8,128)(2,1)S(1)} %get-tuple-element.10), channel_id=1, source_target_pairs={{0,1},{1,0},{2,3},{3,2},{4,5},{5,4},{6,7},{7,6},{8,9},{9,8},{10,11... | collective-permute-start | bytes 1966088 | tf_op jit(solution)/shard_map/weight_swap/ppermute | solution.py:33
  15.3 0.3 %collective-permute-done.3.refs_4_ = bf16[96,512]{1,0:T(8,128)(2,1)S(1)} collective-permute-done((bf16[96,512]{1,0:T(8,128)(2,1)S(1)}, bf16[96,512]{1,0:T(8,128)(2,1)S(1)}, u32[]{:S(2)}, u32[]{:S(2)}) %collective-permute-start.3) | collective-permute-done | bytes 98336 | tf_op jit(solution)/shard_map/residual_gather/ppermute | solution.py:40
  15.6 0.0 copy-done.3
  15.6 0.0 copy-done.4
  15.6 0.0 copy-done.2
  15.6 0.8 %attention.1.refs_0_.attended_ref = bf16[96,256]{1,0:T(8,128)(2,1)S(1)} custom-call(bf16[96,256]{1,0:T(8,128)(2,1)S(1)} %copy-done.4, bf16[384,256]{1,0:T(8,128)(2,1)S(1)} %copy-done.2, bf16[384,256]{1,0:T(8,128)(2,1)S(1)} %copy-done.3, bf16[96,512]{1,0:T(8,128)(2,1)S(1)} %pad_maximum_fusion.refs_0_, bf16[96,512]{1,0:T(8,128)(2,1)S(1)} %collective-permute-done.refs_1_, ...), custom_call_target="tpu_custom_call" | custom-call | flops 20000000000 | tf_op jit(solution)/shard_map/attention/attention/pallas_call | solution.py:205
  16.4 0.0 copy-start.5
  16.4 0.0 copy-start.1
  16.4 0.1 collective-permute-start.4
  16.5 0.2 own_term.1.total_ref
  16.8 1.1 %collective-permute-done.4.refs_2_.refs_0_ = bf16[96,256]{1,0:T(8,128)(2,1)S(1)} collective-permute-done((bf16[96,256]{1,0:T(8,128)(2,1)S(1)}, bf16[96,256]{1,0:T(8,128)(2,1)S(1)}, u32[]{:S(2)}, u32[]{:S(2)}) %collective-permute-start.4) | collective-permute-done | bytes 49184 | tf_op jit(solution)/shard_map/attended_swap/ppermute | solution.py:33
  17.9 0.0 collective-permute-done.6.refs_1_
  17.9 0.2 sent_term.1
  18.1 1.6 %collective-permute-start.7 = (bf16[96,1280]{1,0:T(8,128)(2,1)S(1)}, bf16[96,1280]{1,0:T(8,128)(2,1)S(1)}, u32[]{:S(2)}, u32[]{:S(2)}) collective-permute-start(bf16[96,1280]{1,0:T(8,128)(2,1)S(1)} %sent_term.1), channel_id=1, source_target_pairs={{0,2},{2,0},{1,3},{3,1},{4,6},{6,4},{5,7},{7,5},{8,10},{10,8},{9,1... | collective-permute-start | bytes 737288 | tf_op jit(solution)/shard_map/projection/ppermute | solution.py:33
  19.7 0.0 copy-done.5
  19.7 0.0 collective-permute-done.5.refs_3_
  19.7 0.0 copy-done.1
  19.7 0.3 %base.1.base_ref = f32[96,1280]{1,0:T(8,128)S(1)} custom-call(bf16[96,1280]{1,0:T(8,128)(2,1)S(1)} %copy-done.1, f32[1,1280]{1,0:T(1,128)S(1)} %reshape.3.gate_ref, bf16[96,256]{1,0:T(8,128)(2,1)S(1)} %attention.1.refs_0_.attended_ref, bf16[256,1280]{1,0:T(8,128)(2,1)S(1)} %get-tuple-element.9.refs_1_, ...), custom_call_target="tpu_custom_call" | custom-call | flops 125829120 | tf_op jit(solution)/shard_map/projection/base/pallas_call | solution.py:242
  20.1 6.1 %collective-permute-done.7.refs_0_ = bf16[96,1280]{1,0:T(8,128)(2,1)S(1)} collective-permute-done((bf16[96,1280]{1,0:T(8,128)(2,1)S(1)}, bf16[96,1280]{1,0:T(8,128)(2,1)S(1)}, u32[]{:S(2)}, u32[]{:S(2)}) %collective-permute-start.7) | collective-permute-done | bytes 245792 | tf_op jit(solution)/shard_map/projection/ppermute | solution.py:33
  26.2 0.8 %final.1 = bf16[96,1280]{1,0:T(8,128)(2,1)} custom-call(f32[96,1280]{1,0:T(8,128)S(1)} %base.1.base_ref, f32[1,1280]{1,0:T(1,128)S(1)} %reshape.3.gate_ref, bf16[96,1280]{1,0:T(8,128)(2,1)S(1)} %collective-permute-done.7.refs_0_), custom_call_target="tpu_custom_call" | custom-call | bytes 983040 | tf_op jit(solution)/shard_map/projection/final/pallas_call | solution.py:250
  (2 shorter events, 0.0 us)
Async XLA Ops:
  0.0 15.6 %copy-start.3 = (bf16[384,256]{1,0:T(8,128)(2,1)S(1)}, bf16[384,256]{1,0:T(8,128)(2,1)}, u32[]{:S(2)}) copy-start(bf16[384,256]{1,0:T(8,128)(2,1)} %held_v_ref.1) | copy-start | bytes 589828
  0.0 15.6 %copy-start.4 = (bf16[96,256]{1,0:T(8,128)(2,1)S(1)}, bf16[96,256]{1,0:T(8,128)(2,1)}, u32[]{:S(2)}) copy-start(bf16[96,256]{1,0:T(8,128)(2,1)} %q_ref.1) | copy-start | bytes 147460
  0.0 15.6 %copy-start.2 = (bf16[384,256]{1,0:T(8,128)(2,1)S(1)}, bf16[384,256]{1,0:T(8,128)(2,1)}, u32[]{:S(2)}) copy-start(bf16[384,256]{1,0:T(8,128)(2,1)} %held_k_ref.1) | copy-start | bytes 589828
  1.9 7.2 %collective-permute-start = (bf16[96,512]{1,0:T(8,128)(2,1)S(1)}, bf16[96,512]{1,0:T(8,128)(2,1)S(1)}, u32[]{:S(2)}, u32[]{:S(2)}) collective-permute-start(bf16[96,512]{1,0:T(8,128)(2,1)S(1)} %pad_maximum_fusion.refs_0_), channel_id=1, source_target_pairs={{0,8},{8,12},{12,4},{4,0},{1,9},{9,13},{13,5},{5,1},{2,10},{10,14}... | collective-permute-start | bytes 294920 | tf_op jit(solution)/shard_map/residual_gather/ppermute | solution.py:37
  6.0 6.7 %collective-permute-start.1 = (bf16[96,512]{1,0:T(8,128)(2,1)S(1)}, bf16[96,512]{1,0:T(8,128)(2,1)S(1)}, u32[]{:S(2)}, u32[]{:S(2)}) collective-permute-start(bf16[96,512]{1,0:T(8,128)(2,1)S(1)} %pad_maximum_fusion.refs_0_), channel_id=1, source_target_pairs={{0,4},{4,12},{12,8},{8,0},{1,5},{5,13},{13,9},{9,1},{2,6},{6,14},{... | collective-permute-start | bytes 294920 | tf_op jit(solution)/shard_map/residual_gather/ppermute | solution.py:38
  6.0 6.7 %collective-permute-start.2 = (bf16[96,512]{1,0:T(8,128)(2,1)S(1)}, bf16[96,512]{1,0:T(8,128)(2,1)S(1)}, u32[]{:S(2)}, u32[]{:S(2)}) collective-permute-start(bf16[96,512]{1,0:T(8,128)(2,1)S(1)} %pad_maximum_fusion.refs_0_), channel_id=1, source_target_pairs={{4,8},{8,4},{5,9},{9,5},{6,10},{10,6},{7,11},{11,7},{20,24},{24,20... | collective-permute-start | bytes 294920 | tf_op jit(solution)/shard_map/residual_gather/ppermute | solution.py:39
  9.1 6.5 %collective-permute-start.3 = (bf16[96,512]{1,0:T(8,128)(2,1)S(1)}, bf16[96,512]{1,0:T(8,128)(2,1)S(1)}, u32[]{:S(2)}, u32[]{:S(2)}) collective-permute-start(bf16[96,512]{1,0:T(8,128)(2,1)S(1)} %collective-permute-done.refs_1_), channel_id=1, source_target_pairs={{8,12},{4,0},{9,13},{5,1},{10,14},{6,2},{11,15},{7,3},{24,28},{20,... | collective-permute-start | bytes 294920 | tf_op jit(solution)/shard_map/residual_gather/ppermute | solution.py:40
  12.7 1.7 %copy-start = (bf16[256,5120]{1,0:T(8,128)(2,1)S(1)}, bf16[256,5120]{1,0:T(8,128)(2,1)}, u32[]{:S(2)}) copy-start(bf16[256,5120]{1,0:T(8,128)(2,1)} %weight_ref.1) | copy-start | bytes 7864324
  14.7 3.2 %collective-permute-start.6 = (bf16[256,1280]{1,0:T(8,128)(2,1)S(1)}, bf16[256,1280]{1,0:T(8,128)(2,1)S(1)}, u32[]{:S(2)}, u32[]{:S(2)}) collective-permute-start(bf16[256,1280]{1,0:T(8,128)(2,1)S(1)} %get-tuple-element.12), channel_id=1, source_target_pairs={{0,1},{1,0},{2,3},{3,2},{4,5},{5,4},{6,7},{7,6},{8,9},{9,8},{10,11... | collective-permute-start | bytes 1966088 | tf_op jit(solution)/shard_map/weight_swap/ppermute | solution.py:33
  14.8 4.9 %collective-permute-start.5 = (bf16[256,1280]{1,0:T(8,128)(2,1)S(1)}, bf16[256,1280]{1,0:T(8,128)(2,1)S(1)}, u32[]{:S(2)}, u32[]{:S(2)}) collective-permute-start(bf16[256,1280]{1,0:T(8,128)(2,1)S(1)} %get-tuple-element.10), channel_id=1, source_target_pairs={{0,1},{1,0},{2,3},{3,2},{4,5},{5,4},{6,7},{7,6},{8,9},{9,8},{10,11... | collective-permute-start | bytes 1966088 | tf_op jit(solution)/shard_map/weight_swap/ppermute | solution.py:33
  16.4 3.3 %copy-start.5 = (f32[1280]{0:T(1024)S(1)}, f32[1280]{0:T(1024)}, u32[]{:S(2)}) copy-start(f32[1280]{0:T(1024)} %param.15) | copy-start | bytes 15364
  16.4 3.3 %copy-start.1 = (bf16[96,1280]{1,0:T(8,128)(2,1)S(1)}, bf16[96,1280]{1,0:T(8,128)(2,1)}, u32[]{:S(2)}) copy-start(bf16[96,1280]{1,0:T(8,128)(2,1)} %hidden_ref.1) | copy-start | bytes 737284
  16.4 1.5 %collective-permute-start.4 = (bf16[96,256]{1,0:T(8,128)(2,1)S(1)}, bf16[96,256]{1,0:T(8,128)(2,1)S(1)}, u32[]{:S(2)}, u32[]{:S(2)}) collective-permute-start(bf16[96,256]{1,0:T(8,128)(2,1)S(1)} %attention.1.refs_0_.attended_ref), channel_id=1, source_target_pairs={{0,1},{1,0},{2,3},{3,2},{4,5},{5,4},{6,7},{7,6},{8,9},{9,8},{10,11... | collective-permute-start | bytes 147464 | tf_op jit(solution)/shard_map/attended_swap/ppermute | solution.py:33
  18.1 8.1 %collective-permute-start.7 = (bf16[96,1280]{1,0:T(8,128)(2,1)S(1)}, bf16[96,1280]{1,0:T(8,128)(2,1)S(1)}, u32[]{:S(2)}, u32[]{:S(2)}) collective-permute-start(bf16[96,1280]{1,0:T(8,128)(2,1)S(1)} %sent_term.1), channel_id=1, source_target_pairs={{0,2},{2,0},{1,3},{3,1},{4,6},{6,4},{5,7},{7,5},{8,10},{10,8},{9,1... | collective-permute-start | bytes 737288 | tf_op jit(solution)/shard_map/projection/ppermute | solution.py:33

commit v3 on v2

v3 whole, which is shorter than its diff:
```python
import functools
import math

import jax
import jax.numpy as jnp
from jax import lax
from jax.experimental import pallas as pl
from jax.experimental.pallas import tpu as pltpu
from jax.sharding import PartitionSpec as P

HD = 128
LANES = 128
VMEM_LIMIT = 12 * 1024 * 1024

IN_VMEM = pl.BlockSpec(memory_space=pltpu.VMEM)
ANYWHERE = pl.BlockSpec(memory_space=pl.ANY)


def call(
    kernel,
    out_shape,
    in_specs,
    out_specs,
    name,
    flops=0,
    moved=0,
    scratch_shapes=(),
    vmem=VMEM_LIMIT,
):
    return pl.pallas_call(
        kernel,
        out_shape=out_shape,
        in_specs=in_specs,
        out_specs=out_specs,
        scratch_shapes=scratch_shapes,
        name=name,
        cost_estimate=pl.CostEstimate(flops=flops, bytes_accessed=moved, transcendentals=0),
        compiler_params=pltpu.CompilerParams(vmem_limit_bytes=vmem),
    )


def shift(array, axis, size, step):
    return lax.ppermute(array, axis, [(i, (i + step) % size) for i in range(size)])


LINE_OF_FOUR = (
    ([(0, 2), (2, 3), (3, 1), (1, 0)], (1, 3, 0, 2)),
    ([(0, 1), (1, 3), (3, 2), (2, 0)], (2, 0, 3, 1)),
    ([(0, 3), (3, 0), (1, 2), (2, 1)], (3, 2, 1, 0)),
)


def gather_permutes(patches):
    if patches == 4:
        return [pairs for pairs, _ in LINE_OF_FOUR]
    return [
        [(i, (i + step) % patches) for i in range(patches)] for step in range(1, patches)
    ]


def gather_sources(patches, place):
    if patches == 4:
        sources = [place]
        for _, table in LINE_OF_FOUR:
            source = jnp.int32(table[0])
            for i in range(1, 4):
                source = jnp.where(place == i, jnp.int32(table[i]), source)
            sources.append(source)
        return sources
    return [lax.rem(place + patches - step, patches) for step in range(patches)]


def stage_kernel(patches, q_ref, held_k_ref, held_v_ref, products_ref, values_ref):
    rows, width = q_ref.shape
    sources = gather_sources(patches, lax.axis_index("patch"))
    starts = [pl.multiple_of(source * rows, rows) for source in sources]
    for i, at in enumerate(starts):
        values_ref[i * rows : (i + 1) * rows, :] = held_v_ref[pl.ds(at, rows), :]
    for head in range(width // HD):
        cols = slice(head * HD, (head + 1) * HD)
        keys = jnp.concatenate([held_k_ref[pl.ds(at, rows), cols] for at in starts], axis=0)
        products_ref[head] = dot_transposed(q_ref[:, cols], keys)


def dot_transposed(a, b):
    return lax.dot_general(
        a, b, (((1,), (1,)), ((), ())), preferred_element_type=jnp.float32
    )


def attention_kernel(scale, q_ref, products_ref, values_ref, *refs):
    block_refs, out_ref = refs[:-1], refs[-1]
    rows, width = q_ref.shape
    blocks = jnp.concatenate([ref[...] for ref in block_refs], axis=0)
    for head in range(width // HD):
        cols = slice(head * HD, (head + 1) * HD)
        value_cols = slice(width + head * HD, width + (head + 1) * HD)
        products = products_ref[head] + dot_transposed(q_ref[:, cols], blocks[:, cols])
        scores = products * scale
        weights = jnp.exp(scores - jnp.max(scores, axis=1, keepdims=True))
        totals = jnp.sum(weights, axis=1, keepdims=True)
        high = weights.astype(jnp.bfloat16)
        low = (weights - high.astype(jnp.float32)).astype(jnp.bfloat16)
        sums = jnp.dot(
            jnp.concatenate([high, low], axis=0),
            jnp.concatenate([values_ref[:, cols], blocks[:, value_cols]], axis=1),
            preferred_element_type=jnp.float32,
        )
        sums = sums[:rows] + sums[rows:]
        sums = sums[:, :HD] + sums[:, HD:]
        out_ref[:, cols] = (sums / totals).astype(jnp.bfloat16)


def block_dot(a_ref, weight_ref, block, columns):
    if block is None:
        weight = weight_ref[...]
    else:
        weight = weight_ref[:, pl.ds(pl.multiple_of(block * columns, LANES), columns)]
    return jnp.dot(a_ref[...], weight, preferred_element_type=jnp.float32)


def block_at(step, heads, subs):
    return lax.rem(lax.axis_index("head") + step, heads) * subs + lax.axis_index("sub")


def own_term_kernel(block_of, attended_ref, weight_ref, out_ref):
    out_ref[...] = block_dot(attended_ref, weight_ref, block_of(), out_ref.shape[1])


def sent_term_kernel(block_of, total_ref, *refs):
    out_ref = refs[-1]
    block, columns = block_of(), out_ref.shape[1]
    total = total_ref[...]
    for attended_ref, weight_ref in zip(refs[:-1:2], refs[1:-1:2]):
        total = total + block_dot(attended_ref, weight_ref, block, columns)
    out_ref[...] = total.astype(jnp.bfloat16)


def base_kernel(block_of, hidden_ref, gate_ref, *refs):
    out_ref = refs[-1]
    block, columns = block_of(), out_ref.shape[1]
    total = 0.0
    for attended_ref, weight_ref in zip(refs[:-1:2], refs[1:-1:2]):
        total = total + block_dot(attended_ref, weight_ref, block, columns)
    out_ref[...] = hidden_ref[...].astype(jnp.float32) + gate_ref[...] * total


def final_kernel(base_ref, gate_ref, *refs):
    arrived_refs, out_ref = refs[:-1], refs[-1]
    total = 0.0
    for ref in arrived_refs:
        total = total + ref[...].astype(jnp.float32)
    out_ref[...] = (base_ref[...] + gate_ref[...] * total).astype(jnp.bfloat16)


def solution(mesh):
    patches, heads, subs = mesh.shape["patch"], mesh.shape["head"], mesh.shape["sub"]

    def per_device(
        queries, held_keys, held_values, key_change, value_change, out_weight, hidden_in, gate
    ):
        rows, width = queries.shape
        columns = hidden_in.shape[1]

        with jax.named_scope("residual_gather"):
            low = jnp.float32(-jnp.inf)
            residual = jnp.maximum(
                lax.pad(key_change, low, ((0, 0, 0), (0, width, 0))),
                lax.pad(value_change, low, ((0, 0, 0), (width, 0, 0))),
            ).astype(jnp.bfloat16)
            blocks = [residual] + [
                lax.ppermute(residual, "patch", pairs) for pairs in gather_permutes(patches)
            ]

        with jax.named_scope("weight_swap"):
            weights = [out_weight] + [
                shift(out_weight, "sub", subs, i) for i in range(1, subs)
            ]

        def weight_and_block(i, step):
            if columns % LANES == 0:
                return weights[i], functools.partial(block_at, step, heads, subs)
            at = block_at(step, heads, subs) * columns
            return lax.dynamic_slice(weights[i], (0, at), (width, columns)), lambda: None

        tokens = rows * patches
        with jax.named_scope("attention"):
            products, values = call(
                functools.partial(stage_kernel, patches),
                [
                    jax.ShapeDtypeStruct((width // HD, rows, tokens), jnp.float32),
                    jax.ShapeDtypeStruct((tokens, width), jnp.bfloat16),
                ],
                [IN_VMEM] * 3,
                [IN_VMEM] * 2,
                "stage",
                flops=2_000_000_000,
            )(queries, held_keys, held_values)
            attended = call(
                functools.partial(attention_kernel, 1.0 / math.sqrt(HD)),
                jax.ShapeDtypeStruct((rows, width), jnp.bfloat16),
                [IN_VMEM] * (3 + len(blocks)),
                IN_VMEM,
                "attention",
                flops=2_000_000_000,
            )(queries, products, values, *blocks)

        with jax.named_scope("attended_swap"):
            attended_parts = [attended] + [
                shift(attended, "sub", subs, i) for i in range(1, subs)
            ]

        term = jax.ShapeDtypeStruct((rows, columns), jnp.float32)
        sent = jax.ShapeDtypeStruct((rows, columns), jnp.bfloat16)
        product_flops = 2 * rows * width * columns
        with jax.named_scope("projection"):
            arrived = []
            for step in range(1, heads):
                weight, block_of = weight_and_block(0, step)
                own = call(
                    functools.partial(own_term_kernel, block_of),
                    term,
                    [IN_VMEM] * 2,
                    IN_VMEM,
                    "own_term",
                    product_flops,
                )(attended, weight)
                pairs = [
                    x
                    for i in range(1, subs)
                    for x in (attended_parts[i], weight_and_block(i, step)[0])
                ]
                total = call(
                    functools.partial(sent_term_kernel, block_of),
                    sent,
                    [IN_VMEM] * (1 + len(pairs)),
                    IN_VMEM,
                    "sent_term",
                    product_flops,
                )(own, *pairs)
                arrived.append(shift(total, "head", heads, step))
            gate_row = gate.reshape(1, columns)
            pairs = [
                x for i in range(subs) for x in (attended_parts[i], weight_and_block(i, 0)[0])
            ]
            base = call(
                functools.partial(base_kernel, weight_and_block(0, 0)[1]),
                term,
                [IN_VMEM] * (2 + len(pairs)),
                IN_VMEM,
                "base",
                2 * product_flops,
            )(hidden_in, gate_row, *pairs)
            return call(
                final_kernel,
                sent,
                [IN_VMEM] * (2 + len(arrived)),
                IN_VMEM,
                "final",
                moved=rows * columns * 8,
            )(base, gate_row, *arrived)

    in_specs = (
        P(("groups", "patch"), ("head", "sub")),
        P("groups", ("head", "sub")),
        P("groups", ("head", "sub")),
        P(("groups", "patch"), ("head", "sub")),
        P(("groups", "patch"), ("head", "sub")),
        P(("head", "sub"), None),
        P(("groups", "patch"), ("head", "sub")),
        P(("groups", "head", "sub")),
    )
    out_specs = P(("groups", "patch"), ("head", "sub"))
    return jax.shard_map(
        per_device, mesh=mesh, in_specs=in_specs, out_specs=out_specs, check_vma=False
    )
```

time: 27.2 us -> 26.2 us (0.963)
  waiting for transfers between devices: 12.3 us -> 9.13 us
  local copies, waits for them, and re-layouts: 1.77 us -> 3.77 us
  starting transfers between devices: 8.23 us -> 9.67 us
  other arithmetic: 1.86 us -> 0.95 us
  Pallas kernels: 2.68 us -> 2.37 us
    unnamed x12, local copies, waits for them, and re-layouts: 1.76 us -> 3.77 us
    ppermute x4 -> x3, waiting for transfers between devices: 5.07 us -> 3.13 us  [per_device(): lax.ppermute(residual, 'patch', pairs)]
    ppermute x4 -> x3, starting transfers between devices: 6.03 us -> 7.59 us  [per_device(): lax.ppermute(residual, 'patch', pairs)]
    ppermute x4 -> x3, waiting for transfers between devices: 7.26 us -> 6 us  [shift(): lax.ppermute(array, axis, [(i, (i + step) % size) for i in range(size)])]
    convert_element_type x2 -> x1, other arithmetic: 1.85 us -> 0.95 us  [per_device(): residual = jnp.maximum(lax.pad(key_change, low, ((0, 0, 0), (0, width, 0)...]
    pallas_call x5, Pallas kernels: 1.92 us -> 1.62 us  [the longest x1 0.53 us: per_device(): call(functools.partial(attention_kernel, 1.0 / math.sqrt(HD)), jax.ShapeD...]
    ppermute x4 -> x3, starting transfers between devices: 2.2 us -> 2.08 us  [shift(): lax.ppermute(array, axis, [(i, (i + step) % size) for i in range(size)])]
  transfers between devices with their start and end apart: 8 -> 6, of which waited for: 5 -> 2; matrix products, arithmetic and copies ran while one was open for 0% -> 4% of each run, Pallas kernels for 7% -> 5%
where the time goes in v3:
time: 26.2 us; the launch traced here: 26 us
  starting transfers between devices  9.67 us (37%)
  waiting for transfers between devices  9.13 us (35%)
  local copies, waits for them, and re-layouts  3.77 us (14%)
  Pallas kernels  2.37 us (9%)
  other arithmetic  0.95 us (4%)
    ppermute x3, starting transfers between devices, per_device(): lax.ppermute(residual, 'patch', pairs)  7.59 us
    ppermute x3, waiting for transfers between devices, shift(): lax.ppermute(array, axis, [(i, (i + step) % size) for i in range(size)])  6 us
    unnamed x12, local copies, waits for them, and re-layouts  3.77 us
    ppermute x3, waiting for transfers between devices, per_device(): lax.ppermute(residual, 'patch', pairs)  3.13 us
    ppermute x3, starting transfers between devices, shift(): lax.ppermute(array, axis, [(i, (i + step) % size) for i in range(size)])  2.08 us
    convert_element_type x1, other arithmetic, per_device(): residual = jnp.maximum(lax.pad(key_change, low, ((0, 0, 0), (0, width, 0)...  0.95 us
    pallas_call x1, Pallas kernels, per_device(): call(final_kernel, sent, [IN_VMEM] * (2 + len(arrived)), IN_VMEM, 'final'...  0.75 us
    pallas_call x1, Pallas kernels, per_device(): call(functools.partial(attention_kernel, 1.0 / math.sqrt(HD)), jax.ShapeD...  0.53 us
  transfers between devices with their start and end apart: 6, of which 2 were waited for; matrix products, arithmetic and copies ran while one was open for 4% of the time, Pallas kernels for 5%

profile of v3, /device:TPU:0, one launch (start us, length us, event | category | flops | bytes accessed | tf_op | source)
XLA Modules:
  0.0 26.0 jit_solution(16951780848211444308)
XLA Ops:
  0.0 0.5 %collective-permute-start.4 = (bf16[256,5120]{1,0:T(8,128)(2,1)}, bf16[256,5120]{1,0:T(8,128)(2,1)S(1)}, u32[]{:S(2)}, u32[]{:S(2)}) collective-permute-start(bf16[256,5120]{1,0:T(8,128)(2,1)} %weight_ref.1), channel_id=1, source_target_pairs={{0,1},{1,0},{2,3},{3,2},{4,5},{5,4},{6,7},{7,6},{8,9},{9,8},{10,11... | collective-permute-start | bytes 7864328 | tf_op jit(solution)/shard_map/weight_swap/ppermute | solution.py:43
  0.5 1.0 %maximum_convert_fusion.refs_0_ = bf16[96,512]{1,0:T(8,128)(2,1)S(1)} fusion(f32[96,256]{1,0:T(8,128)} %param.12, f32[96,256]{1,0:T(8,128)} %param.11), kind=kLoop, calls=%fused_computation | loop fusion | flops 196608 | bytes 294912 | tf_op jit(solution)/shard_map/residual_gather/convert_element_type | solution.py:170
  1.4 4.7 %collective-permute-start.2 = (bf16[96,512]{1,0:T(8,128)(2,1)S(1)}, bf16[96,512]{1,0:T(8,128)(2,1)S(1)}, u32[]{:S(2)}, u32[]{:S(2)}) collective-permute-start(bf16[96,512]{1,0:T(8,128)(2,1)S(1)} %maximum_convert_fusion.refs_0_), channel_id=1, source_target_pairs={{0,12},{12,0},{4,8},{8,4},{1,13},{13,1},{5,9},{9,5},{2,14},{14,2},... | collective-permute-start | bytes 294920 | tf_op jit(solution)/shard_map/residual_gather/ppermute | solution.py:172
  6.1 0.0 collective-permute-start.1
  6.1 2.9 %collective-permute-start = (bf16[96,512]{1,0:T(8,128)(2,1)S(1)}, bf16[96,512]{1,0:T(8,128)(2,1)S(1)}, u32[]{:S(2)}, u32[]{:S(2)}) collective-permute-start(bf16[96,512]{1,0:T(8,128)(2,1)S(1)} %maximum_convert_fusion.refs_0_), channel_id=1, source_target_pairs={{0,8},{8,12},{12,4},{4,0},{1,9},{9,13},{13,5},{5,1},{2,10},{10,14}... | collective-permute-start | bytes 294920 | tf_op jit(solution)/shard_map/residual_gather/ppermute | solution.py:172
  9.0 0.0 copy-start.2
  9.0 0.9 %copy-done.2 = bf16[384,256]{1,0:T(8,128)(2,1)S(1)} copy-done((bf16[384,256]{1,0:T(8,128)(2,1)S(1)}, bf16[384,256]{1,0:T(8,128)(2,1)}, u32[]{:S(2)}) %copy-start.2) | copy-done | bytes 196632
  9.9 0.0 copy-start.3
  9.9 0.9 %copy-done.3 = bf16[384,256]{1,0:T(8,128)(2,1)S(1)} copy-done((bf16[384,256]{1,0:T(8,128)(2,1)S(1)}, bf16[384,256]{1,0:T(8,128)(2,1)}, u32[]{:S(2)}) %copy-start.3) | copy-done | bytes 196632
  10.9 0.0 copy-start.4
  10.9 0.8 %copy-done.4 = bf16[96,256]{1,0:T(8,128)(2,1)S(1)} copy-done((bf16[96,256]{1,0:T(8,128)(2,1)S(1)}, bf16[96,256]{1,0:T(8,128)(2,1)}, u32[]{:S(2)}) %copy-start.4) | copy-done | bytes 49176
  11.7 0.2 stage.1
  11.9 0.0 collective-permute-done.2.refs_3_
  11.9 3.1 %collective-permute-done.1.refs_2_ = bf16[96,512]{1,0:T(8,128)(2,1)S(1)} collective-permute-done((bf16[96,512]{1,0:T(8,128)(2,1)S(1)}, bf16[96,512]{1,0:T(8,128)(2,1)S(1)}, u32[]{:S(2)}, u32[]{:S(2)}) %collective-permute-start.1) | collective-permute-done | bytes 98336 | tf_op jit(solution)/shard_map/residual_gather/ppermute | solution.py:172
  15.0 0.0 collective-permute-done.refs_1_
  15.0 0.0 copy-start
  15.0 0.5 %attention.1.refs_0_.attended_ref = bf16[96,256]{1,0:T(8,128)(2,1)S(1)} custom-call(bf16[96,256]{1,0:T(8,128)(2,1)S(1)} %copy-done.4, f32[2,96,384]{2,1,0:T(8,128)S(1)} %get-tuple-element.7.products_ref, bf16[384,256]{1,0:T(8,128)(2,1)S(1)} %get-tuple-element.8.values_ref, bf16[96,512]{1,0:T(8,128)(2,1)S(1)} %maximum_convert_fusion.refs_0_, ...), custom_call_target="tpu_custom_call" | custom-call | flops 2000000000 | tf_op jit(solution)/shard_map/attention/attention/pallas_call | solution.py:199
  15.6 0.0 copy-start.5
  15.6 0.0 copy-start.1
  15.6 0.1 collective-permute-start.3
  15.7 1.1 %copy-done = bf16[256,5120]{1,0:T(8,128)(2,1)S(1)} copy-done((bf16[256,5120]{1,0:T(8,128)(2,1)S(1)}, bf16[256,5120]{1,0:T(8,128)(2,1)}, u32[]{:S(2)}) %copy-start) | copy-done | bytes 2621464
  16.8 0.2 own_term.1.total_ref
  17.0 0.0 collective-permute-done.3.refs_2_.refs_0_
  17.0 0.0 collective-permute-done.4.refs_3_.refs_1_
  17.0 0.3 %sent_term.1 = bf16[96,1280]{1,0:T(8,128)(2,1)S(1)} custom-call(f32[96,1280]{1,0:T(8,128)S(1)} %own_term.1.total_ref, bf16[96,256]{1,0:T(8,128)(2,1)S(1)} %collective-permute-done.3.refs_2_.refs_0_, bf16[256,5120]{1,0:T(8,128)(2,1)S(1)} %collective-permute-done.4.refs_3_.refs_1_), custom_call_target="tpu_custom_call" | custom-call | flops 62914560 | tf_op jit(solution)/shard_map/projection/sent_term/pallas_call | solution.py:233
  17.3 1.6 %collective-permute-start.5 = (bf16[96,1280]{1,0:T(8,128)(2,1)S(1)}, bf16[96,1280]{1,0:T(8,128)(2,1)S(1)}, u32[]{:S(2)}, u32[]{:S(2)}) collective-permute-start(bf16[96,1280]{1,0:T(8,128)(2,1)S(1)} %sent_term.1), channel_id=1, source_target_pairs={{0,2},{2,0},{1,3},{3,1},{4,6},{6,4},{5,7},{7,5},{8,10},{10,8},{9,1... | collective-permute-start | bytes 737288 | tf_op jit(solution)/shard_map/projection/ppermute | solution.py:43
  18.8 0.0 copy-done.5
  18.9 0.0 copy-done.1
  18.9 0.4 %base.1.base_ref = f32[96,1280]{1,0:T(8,128)S(1)} custom-call(bf16[96,1280]{1,0:T(8,128)(2,1)S(1)} %copy-done.1, f32[1,1280]{1,0:T(1,128)S(1)} %reshape.3.gate_ref, bf16[96,256]{1,0:T(8,128)(2,1)S(1)} %attention.1.refs_0_.attended_ref, bf16[256,5120]{1,0:T(8,128)(2,1)S(1)} %copy-done, bf16[96,256]{1,0:T(8,128)(2,1)S(1)} %collective-permute-done.3.refs_2_.refs_0_, ...), custom_call_target="tpu_custom_call" | custom-call | flops 125829120 | tf_op jit(solution)/shard_map/projection/base/pallas_call | solution.py:246
  19.2 6.0 %collective-permute-done.5.refs_0_ = bf16[96,1280]{1,0:T(8,128)(2,1)S(1)} collective-permute-done((bf16[96,1280]{1,0:T(8,128)(2,1)S(1)}, bf16[96,1280]{1,0:T(8,128)(2,1)S(1)}, u32[]{:S(2)}, u32[]{:S(2)}) %collective-permute-start.5) | collective-permute-done | bytes 245792 | tf_op jit(solution)/shard_map/projection/ppermute | solution.py:43
  25.2 0.8 %final.1 = bf16[96,1280]{1,0:T(8,128)(2,1)} custom-call(f32[96,1280]{1,0:T(8,128)S(1)} %base.1.base_ref, f32[1,1280]{1,0:T(1,128)S(1)} %reshape.3.gate_ref, bf16[96,1280]{1,0:T(8,128)(2,1)S(1)} %collective-permute-done.5.refs_0_), custom_call_target="tpu_custom_call" | custom-call | bytes 983040 | tf_op jit(solution)/shard_map/projection/final/pallas_call | solution.py:254
  (1 shorter events, 0.0 us)
Async XLA Ops:
  0.0 17.0 %collective-permute-start.4 = (bf16[256,5120]{1,0:T(8,128)(2,1)}, bf16[256,5120]{1,0:T(8,128)(2,1)S(1)}, u32[]{:S(2)}, u32[]{:S(2)}) collective-permute-start(bf16[256,5120]{1,0:T(8,128)(2,1)} %weight_ref.1), channel_id=1, source_target_pairs={{0,1},{1,0},{2,3},{3,2},{4,5},{5,4},{6,7},{7,6},{8,9},{9,8},{10,11... | collective-permute-start | bytes 7864328 | tf_op jit(solution)/shard_map/weight_swap/ppermute | solution.py:43
  1.4 10.5 %collective-permute-start.2 = (bf16[96,512]{1,0:T(8,128)(2,1)S(1)}, bf16[96,512]{1,0:T(8,128)(2,1)S(1)}, u32[]{:S(2)}, u32[]{:S(2)}) collective-permute-start(bf16[96,512]{1,0:T(8,128)(2,1)S(1)} %maximum_convert_fusion.refs_0_), channel_id=1, source_target_pairs={{0,12},{12,0},{4,8},{8,4},{1,13},{13,1},{5,9},{9,5},{2,14},{14,2},... | collective-permute-start | bytes 294920 | tf_op jit(solution)/shard_map/residual_gather/ppermute | solution.py:172
  6.1 8.9 %collective-permute-start.1 = (bf16[96,512]{1,0:T(8,128)(2,1)S(1)}, bf16[96,512]{1,0:T(8,128)(2,1)S(1)}, u32[]{:S(2)}, u32[]{:S(2)}) collective-permute-start(bf16[96,512]{1,0:T(8,128)(2,1)S(1)} %maximum_convert_fusion.refs_0_), channel_id=1, source_target_pairs={{0,4},{4,12},{12,8},{8,0},{1,5},{5,13},{13,9},{9,1},{2,6},{6,14},{... | collective-permute-start | bytes 294920 | tf_op jit(solution)/shard_map/residual_gather/ppermute | solution.py:172
  6.1 8.9 %collective-permute-start = (bf16[96,512]{1,0:T(8,128)(2,1)S(1)}, bf16[96,512]{1,0:T(8,128)(2,1)S(1)}, u32[]{:S(2)}, u32[]{:S(2)}) collective-permute-start(bf16[96,512]{1,0:T(8,128)(2,1)S(1)} %maximum_convert_fusion.refs_0_), channel_id=1, source_target_pairs={{0,8},{8,12},{12,4},{4,0},{1,9},{9,13},{13,5},{5,1},{2,10},{10,14}... | collective-permute-start | bytes 294920 | tf_op jit(solution)/shard_map/residual_gather/ppermute | solution.py:172
  9.0 0.9 %copy-start.2 = (bf16[384,256]{1,0:T(8,128)(2,1)S(1)}, bf16[384,256]{1,0:T(8,128)(2,1)}, u32[]{:S(2)}) copy-start(bf16[384,256]{1,0:T(8,128)(2,1)} %held_k_ref.1) | copy-start | bytes 589828
  9.9 0.9 %copy-start.3 = (bf16[384,256]{1,0:T(8,128)(2,1)S(1)}, bf16[384,256]{1,0:T(8,128)(2,1)}, u32[]{:S(2)}) copy-start(bf16[384,256]{1,0:T(8,128)(2,1)} %held_v_ref.1) | copy-start | bytes 589828
  10.9 0.8 %copy-start.4 = (bf16[96,256]{1,0:T(8,128)(2,1)S(1)}, bf16[96,256]{1,0:T(8,128)(2,1)}, u32[]{:S(2)}) copy-start(bf16[96,256]{1,0:T(8,128)(2,1)} %q_ref.3) | copy-start | bytes 147460
  15.0 1.7 %copy-start = (bf16[256,5120]{1,0:T(8,128)(2,1)S(1)}, bf16[256,5120]{1,0:T(8,128)(2,1)}, u32[]{:S(2)}) copy-start(bf16[256,5120]{1,0:T(8,128)(2,1)} %weight_ref.1) | copy-start | bytes 7864324
  15.6 3.3 %copy-start.5 = (f32[1280]{0:T(1024)S(1)}, f32[1280]{0:T(1024)}, u32[]{:S(2)}) copy-start(f32[1280]{0:T(1024)} %param.15) | copy-start | bytes 15364
  15.6 3.3 %copy-start.1 = (bf16[96,1280]{1,0:T(8,128)(2,1)S(1)}, bf16[96,1280]{1,0:T(8,128)(2,1)}, u32[]{:S(2)}) copy-start(bf16[96,1280]{1,0:T(8,128)(2,1)} %hidden_ref.1) | copy-start | bytes 737284
  15.6 1.4 %collective-permute-start.3 = (bf16[96,256]{1,0:T(8,128)(2,1)S(1)}, bf16[96,256]{1,0:T(8,128)(2,1)S(1)}, u32[]{:S(2)}, u32[]{:S(2)}) collective-permute-start(bf16[96,256]{1,0:T(8,128)(2,1)S(1)} %attention.1.refs_0_.attended_ref), channel_id=1, source_target_pairs={{0,1},{1,0},{2,3},{3,2},{4,5},{5,4},{6,7},{7,6},{8,9},{9,8},{10,11... | collective-permute-start | bytes 147464 | tf_op jit(solution)/shard_map/attended_swap/ppermute | solution.py:43
  17.3 7.9 %collective-permute-start.5 = (bf16[96,1280]{1,0:T(8,128)(2,1)S(1)}, bf16[96,1280]{1,0:T(8,128)(2,1)S(1)}, u32[]{:S(2)}, u32[]{:S(2)}) collective-permute-start(bf16[96,1280]{1,0:T(8,128)(2,1)S(1)} %sent_term.1), channel_id=1, source_target_pairs={{0,2},{2,0},{1,3},{3,1},{4,6},{6,4},{5,7},{7,5},{8,10},{10,8},{9,1... | collective-permute-start | bytes 737288 | tf_op jit(solution)/shard_map/projection/ppermute | solution.py:43

commit v4 on v3

--- a/solution.py
+++ b/solution.py
@@ -44,30 +44,59 @@
 
 
 LINE_OF_FOUR = (
-    ([(0, 2), (2, 3), (3, 1), (1, 0)], (1, 3, 0, 2)),
-    ([(0, 1), (1, 3), (3, 2), (2, 0)], (2, 0, 3, 1)),
-    ([(0, 3), (3, 0), (1, 2), (2, 1)], (3, 2, 1, 0)),
+    [(2, 1), (1, 3)],
+    [(1, 0), (0, 2), (3, 1)],
+    [(2, 0), (3, 2), (0, 3)],
+    [(0, 1), (1, 2), (2, 3), (3, 0)],
 )
 
 
 def gather_permutes(patches):
     if patches == 4:
-        return [pairs for pairs, _ in LINE_OF_FOUR]
+        return LINE_OF_FOUR
     return [
         [(i, (i + step) % patches) for i in range(patches)] for step in range(1, patches)
     ]
 
 
+def gather_slots(patches):
+    slots = []
+    for place in range(patches):
+        found = []
+        for n, pairs in enumerate(gather_permutes(patches)):
+            found += [(n, source) for source, target in pairs if target == place]
+        slots.append(found)
+    return slots
+
+
+def by_place(place, entries):
+    if all(entry is entries[0] for entry in entries):
+        return entries[0]
+    value = entries[0]
+    for i, entry in enumerate(entries[1:], 1):
+        if entry is not value:
+            value = jnp.where(place == i, entry, value)
+    return value
+
+
 def gather_sources(patches, place):
-    if patches == 4:
-        sources = [place]
-        for _, table in LINE_OF_FOUR:
-            source = jnp.int32(table[0])
-            for i in range(1, 4):
-                source = jnp.where(place == i, jnp.int32(table[i]), source)
-            sources.append(source)
-        return sources
-    return [lax.rem(place + patches - step, patches) for step in range(patches)]
+    if patches != 4:
+        return [lax.rem(place + patches - step, patches) for step in range(patches)]
+    slots = gather_slots(patches)
+    return [place] + [
+        by_place(place, [jnp.int32(found[i][1]) for found in slots]) for i in range(patches - 1)
+    ]
+
+
+def gathered_blocks(patches, refs):
+    if patches != 4:
+        return [ref[...] for ref in refs]
+    place = lax.axis_index("patch")
+    own, arrived = refs[0][...], [ref[...] for ref in refs[1:]]
+    slots = gather_slots(patches)
+    return [own] + [
+        by_place(place, [arrived[found[i][0]] for found in slots]) for i in range(patches - 1)
+    ]
 
 
 def stage_kernel(patches, q_ref, held_k_ref, held_v_ref, products_ref, values_ref):
@@ -88,10 +117,10 @@
     )
 
 
-def attention_kernel(scale, q_ref, products_ref, values_ref, *refs):
+def attention_kernel(scale, patches, q_ref, products_ref, values_ref, *refs):
     block_refs, out_ref = refs[:-1], refs[-1]
     rows, width = q_ref.shape
-    blocks = jnp.concatenate([ref[...] for ref in block_refs], axis=0)
+    blocks = jnp.concatenate(gathered_blocks(patches, block_refs), axis=0)
     for head in range(width // HD):
         cols = slice(head * HD, (head + 1) * HD)
         value_cols = slice(width + head * HD, width + (head + 1) * HD)
@@ -197,7 +226,7 @@
                 flops=2_000_000_000,
             )(queries, held_keys, held_values)
             attended = call(
-                functools.partial(attention_kernel, 1.0 / math.sqrt(HD)),
+                functools.partial(attention_kernel, 1.0 / math.sqrt(HD), patches),
                 jax.ShapeDtypeStruct((rows, width), jnp.bfloat16),
                 [IN_VMEM] * (3 + len(blocks)),
                 IN_VMEM,

time: 26.2 us -> 26.9 us (1.027)
  the two profiles are of different devices: /device:TPU:0 before, /device:TPU:14 now
where the time goes in v4:
time: 26.9 us; the launch traced here: 26.6 us
  starting transfers between devices  10.7 us (40%)
  waiting for transfers between devices  8.64 us (32%)
  local copies, waits for them, and re-layouts  3.76 us (14%)
  Pallas kernels  2.38 us (9%)
  other arithmetic  0.95 us (4%)
    ppermute x4, starting transfers between devices, per_device(): lax.ppermute(residual, 'patch', pairs)  10.1 us
    ppermute x3, waiting for transfers between devices, shift(): lax.ppermute(array, axis, [(i, (i + step) % size) for i in range(size)])  6.96 us
    unnamed x12, local copies, waits for them, and re-layouts  3.75 us
    ppermute x4, waiting for transfers between devices, per_device(): lax.ppermute(residual, 'patch', pairs)  1.68 us
    convert_element_type x1, other arithmetic, per_device(): residual = jnp.maximum(lax.pad(key_change, low, ((0, 0, 0), (0, width, 0)...  0.95 us
    pallas_call x1, Pallas kernels, per_device(): call(final_kernel, sent, [IN_VMEM] * (2 + len(arrived)), IN_VMEM, 'final'...  0.75 us
    ppermute x3, starting transfers between devices, shift(): lax.ppermute(array, axis, [(i, (i + step) % size) for i in range(size)])  0.67 us
  transfers between devices with their start and end apart: 7, of which 2 were waited for; matrix products, arithmetic and copies ran while one was open for 4% of the time, Pallas kernels for 5%

profile of v4, /device:TPU:14, one launch (start us, length us, event | category | flops | bytes accessed | tf_op | source)
XLA Modules:
  0.0 26.6 jit_solution(12174604264886710440)
XLA Ops:
  0.0 0.0 collective-permute-start.5
  0.0 1.0 %maximum_convert_fusion.refs_0_ = bf16[96,512]{1,0:T(8,128)(2,1)S(1)} fusion(f32[96,256]{1,0:T(8,128)} %param.12, f32[96,256]{1,0:T(8,128)} %param.11), kind=kLoop, calls=%fused_computation | loop fusion | flops 196608 | bytes 294912 | tf_op jit(solution)/shard_map/residual_gather/convert_element_type | solution.py:199
  1.0 1.6 %collective-permute-start.3 = (bf16[96,512]{1,0:T(8,128)(2,1)S(1)}, bf16[96,512]{1,0:T(8,128)(2,1)S(1)}, u32[]{:S(2)}, u32[]{:S(2)}) collective-permute-start(bf16[96,512]{1,0:T(8,128)(2,1)S(1)} %maximum_convert_fusion.refs_0_), channel_id=1, source_target_pairs={{0,4},{4,8},{8,12},{12,0},{1,5},{5,9},{9,13},{13,1},{2,6},{6,10},{... | collective-permute-start | bytes 294920 | tf_op jit(solution)/shard_map/residual_gather/ppermute | solution.py:201
  2.6 0.7 %collective-permute-start.2 = (bf16[96,512]{1,0:T(8,128)(2,1)S(1)}, bf16[96,512]{1,0:T(8,128)(2,1)S(1)}, u32[]{:S(2)}, u32[]{:S(2)}) collective-permute-start(bf16[96,512]{1,0:T(8,128)(2,1)S(1)} %maximum_convert_fusion.refs_0_), channel_id=1, source_target_pairs={{8,0},{12,8},{0,12},{9,1},{13,9},{1,13},{10,2},{14,10},{2,14},{11,... | collective-permute-start | bytes 294920 | tf_op jit(solution)/shard_map/residual_gather/ppermute | solution.py:201
  3.3 5.8 %collective-permute-start.1 = (bf16[96,512]{1,0:T(8,128)(2,1)S(1)}, bf16[96,512]{1,0:T(8,128)(2,1)S(1)}, u32[]{:S(2)}, u32[]{:S(2)}) collective-permute-start(bf16[96,512]{1,0:T(8,128)(2,1)S(1)} %maximum_convert_fusion.refs_0_), channel_id=1, source_target_pairs={{4,0},{0,8},{12,4},{5,1},{1,9},{13,5},{6,2},{2,10},{14,6},{7,3},{3... | collective-permute-start | bytes 294920 | tf_op jit(solution)/shard_map/residual_gather/ppermute | solution.py:201
  9.1 1.9 %collective-permute-start = (bf16[96,512]{1,0:T(8,128)(2,1)S(1)}, bf16[96,512]{1,0:T(8,128)(2,1)S(1)}, u32[]{:S(2)}, u32[]{:S(2)}) collective-permute-start(bf16[96,512]{1,0:T(8,128)(2,1)S(1)} %maximum_convert_fusion.refs_0_), channel_id=1, source_target_pairs={{8,4},{4,12},{9,5},{5,13},{10,6},{6,14},{11,7},{7,15},{24,20},{20,... | collective-permute-start | bytes 294920 | tf_op jit(solution)/shard_map/residual_gather/ppermute | solution.py:201
  11.0 0.0 copy-start.2
  11.0 0.9 %copy-done.2 = bf16[384,256]{1,0:T(8,128)(2,1)S(1)} copy-done((bf16[384,256]{1,0:T(8,128)(2,1)S(1)}, bf16[384,256]{1,0:T(8,128)(2,1)}, u32[]{:S(2)}) %copy-start.2) | copy-done | bytes 196632
  12.0 0.0 copy-start.3
  12.0 0.9 %copy-done.3 = bf16[384,256]{1,0:T(8,128)(2,1)S(1)} copy-done((bf16[384,256]{1,0:T(8,128)(2,1)S(1)}, bf16[384,256]{1,0:T(8,128)(2,1)}, u32[]{:S(2)}) %copy-start.3) | copy-done | bytes 196632
  12.9 0.0 copy-start.4
  12.9 0.8 %copy-done.4 = bf16[96,256]{1,0:T(8,128)(2,1)S(1)} copy-done((bf16[96,256]{1,0:T(8,128)(2,1)S(1)}, bf16[96,256]{1,0:T(8,128)(2,1)}, u32[]{:S(2)}) %copy-start.4) | copy-done | bytes 49176
  13.7 0.2 stage.1
  13.9 0.0 collective-permute-done.3.refs_4_
  13.9 0.0 collective-permute-done.2.refs_3_
  13.9 0.0 collective-permute-done.1.refs_2_
  13.9 1.7 %collective-permute-done.refs_1_ = bf16[96,512]{1,0:T(8,128)(2,1)S(1)} collective-permute-done((bf16[96,512]{1,0:T(8,128)(2,1)S(1)}, bf16[96,512]{1,0:T(8,128)(2,1)S(1)}, u32[]{:S(2)}, u32[]{:S(2)}) %collective-permute-start) | collective-permute-done | bytes 98336 | tf_op jit(solution)/shard_map/residual_gather/ppermute | solution.py:201
  15.6 0.0 copy-start
  15.6 0.5 %attention.1.refs_0_.attended_ref = bf16[96,256]{1,0:T(8,128)(2,1)S(1)} custom-call(bf16[96,256]{1,0:T(8,128)(2,1)S(1)} %copy-done.4, f32[2,96,384]{2,1,0:T(8,128)S(1)} %get-tuple-element.7.products_ref, bf16[384,256]{1,0:T(8,128)(2,1)S(1)} %get-tuple-element.8.values_ref, bf16[96,512]{1,0:T(8,128)(2,1)S(1)} %maximum_convert_fusion.refs_0_, ...), custom_call_target="tpu_custom_call" | custom-call | flops 2000000000 | tf_op jit(solution)/shard_map/attention/attention/pallas_call | solution.py:228
  16.2 0.0 copy-start.5
  16.2 0.0 copy-start.1
  16.2 0.1 collective-permute-start.4
  16.3 1.1 %copy-done = bf16[256,5120]{1,0:T(8,128)(2,1)S(1)} copy-done((bf16[256,5120]{1,0:T(8,128)(2,1)S(1)}, bf16[256,5120]{1,0:T(8,128)(2,1)}, u32[]{:S(2)}) %copy-start) | copy-done | bytes 2621464
  17.4 0.2 own_term.1.total_ref
  17.6 0.0 collective-permute-done.4.refs_2_.refs_0_
  17.6 0.0 collective-permute-done.5.refs_3_.refs_1_
  17.6 0.3 sent_term.1
  17.9 0.6 %collective-permute-start.6 = (bf16[96,1280]{1,0:T(8,128)(2,1)S(1)}, bf16[96,1280]{1,0:T(8,128)(2,1)S(1)}, u32[]{:S(2)}, u32[]{:S(2)}) collective-permute-start(bf16[96,1280]{1,0:T(8,128)(2,1)S(1)} %sent_term.1), channel_id=1, source_target_pairs={{0,2},{2,0},{1,3},{3,1},{4,6},{6,4},{5,7},{7,5},{8,10},{10,8},{9,1... | collective-permute-start | bytes 737288 | tf_op jit(solution)/shard_map/projection/ppermute | solution.py:43
  18.5 0.0 copy-done.5
  18.5 0.0 copy-done.1
  18.5 0.4 %base.1.base_ref = f32[96,1280]{1,0:T(8,128)S(1)} custom-call(bf16[96,1280]{1,0:T(8,128)(2,1)S(1)} %copy-done.1, f32[1,1280]{1,0:T(1,128)S(1)} %reshape.3.gate_ref, bf16[96,256]{1,0:T(8,128)(2,1)S(1)} %attention.1.refs_0_.attended_ref, bf16[256,5120]{1,0:T(8,128)(2,1)S(1)} %copy-done, bf16[96,256]{1,0:T(8,128)(2,1)S(1)} %collective-permute-done.4.refs_2_.refs_0_, ...), custom_call_target="tpu_custom_call" | custom-call | flops 125829120 | tf_op jit(solution)/shard_map/projection/base/pallas_call | solution.py:275
  18.9 7.0 %collective-permute-done.6.refs_0_ = bf16[96,1280]{1,0:T(8,128)(2,1)S(1)} collective-permute-done((bf16[96,1280]{1,0:T(8,128)(2,1)S(1)}, bf16[96,1280]{1,0:T(8,128)(2,1)S(1)}, u32[]{:S(2)}, u32[]{:S(2)}) %collective-permute-start.6) | collective-permute-done | bytes 245792 | tf_op jit(solution)/shard_map/projection/ppermute | solution.py:43
  25.8 0.8 %final.1 = bf16[96,1280]{1,0:T(8,128)(2,1)} custom-call(f32[96,1280]{1,0:T(8,128)S(1)} %base.1.base_ref, f32[1,1280]{1,0:T(1,128)S(1)} %reshape.3.gate_ref, bf16[96,1280]{1,0:T(8,128)(2,1)S(1)} %collective-permute-done.6.refs_0_), custom_call_target="tpu_custom_call" | custom-call | bytes 983040 | tf_op jit(solution)/shard_map/projection/final/pallas_call | solution.py:283
  (1 shorter events, 0.0 us)
Async XLA Ops:
  0.0 17.6 %collective-permute-start.5 = (bf16[256,5120]{1,0:T(8,128)(2,1)}, bf16[256,5120]{1,0:T(8,128)(2,1)S(1)}, u32[]{:S(2)}, u32[]{:S(2)}) collective-permute-start(bf16[256,5120]{1,0:T(8,128)(2,1)} %weight_ref.1), channel_id=1, source_target_pairs={{0,1},{1,0},{2,3},{3,2},{4,5},{5,4},{6,7},{7,6},{8,9},{9,8},{10,11... | collective-permute-start | bytes 7864328 | tf_op jit(solution)/shard_map/weight_swap/ppermute | solution.py:43
  1.0 13.0 %collective-permute-start.3 = (bf16[96,512]{1,0:T(8,128)(2,1)S(1)}, bf16[96,512]{1,0:T(8,128)(2,1)S(1)}, u32[]{:S(2)}, u32[]{:S(2)}) collective-permute-start(bf16[96,512]{1,0:T(8,128)(2,1)S(1)} %maximum_convert_fusion.refs_0_), channel_id=1, source_target_pairs={{0,4},{4,8},{8,12},{12,0},{1,5},{5,9},{9,13},{13,1},{2,6},{6,10},{... | collective-permute-start | bytes 294920 | tf_op jit(solution)/shard_map/residual_gather/ppermute | solution.py:201
  2.6 11.3 %collective-permute-start.2 = (bf16[96,512]{1,0:T(8,128)(2,1)S(1)}, bf16[96,512]{1,0:T(8,128)(2,1)S(1)}, u32[]{:S(2)}, u32[]{:S(2)}) collective-permute-start(bf16[96,512]{1,0:T(8,128)(2,1)S(1)} %maximum_convert_fusion.refs_0_), channel_id=1, source_target_pairs={{8,0},{12,8},{0,12},{9,1},{13,9},{1,13},{10,2},{14,10},{2,14},{11,... | collective-permute-start | bytes 294920 | tf_op jit(solution)/shard_map/residual_gather/ppermute | solution.py:201
  3.3 10.7 %collective-permute-start.1 = (bf16[96,512]{1,0:T(8,128)(2,1)S(1)}, bf16[96,512]{1,0:T(8,128)(2,1)S(1)}, u32[]{:S(2)}, u32[]{:S(2)}) collective-permute-start(bf16[96,512]{1,0:T(8,128)(2,1)S(1)} %maximum_convert_fusion.refs_0_), channel_id=1, source_target_pairs={{4,0},{0,8},{12,4},{5,1},{1,9},{13,5},{6,2},{2,10},{14,6},{7,3},{3... | collective-permute-start | bytes 294920 | tf_op jit(solution)/shard_map/residual_gather/ppermute | solution.py:201
  9.1 6.5 %collective-permute-start = (bf16[96,512]{1,0:T(8,128)(2,1)S(1)}, bf16[96,512]{1,0:T(8,128)(2,1)S(1)}, u32[]{:S(2)}, u32[]{:S(2)}) collective-permute-start(bf16[96,512]{1,0:T(8,128)(2,1)S(1)} %maximum_convert_fusion.refs_0_), channel_id=1, source_target_pairs={{8,4},{4,12},{9,5},{5,13},{10,6},{6,14},{11,7},{7,15},{24,20},{20,... | collective-permute-start | bytes 294920 | tf_op jit(solution)/shard_map/residual_gather/ppermute | solution.py:201
  11.0 0.9 %copy-start.2 = (bf16[384,256]{1,0:T(8,128)(2,1)S(1)}, bf16[384,256]{1,0:T(8,128)(2,1)}, u32[]{:S(2)}) copy-start(bf16[384,256]{1,0:T(8,128)(2,1)} %held_k_ref.1) | copy-start | bytes 589828
  12.0 0.9 %copy-start.3 = (bf16[384,256]{1,0:T(8,128)(2,1)S(1)}, bf16[384,256]{1,0:T(8,128)(2,1)}, u32[]{:S(2)}) copy-start(bf16[384,256]{1,0:T(8,128)(2,1)} %held_v_ref.1) | copy-start | bytes 589828
  12.9 0.8 %copy-start.4 = (bf16[96,256]{1,0:T(8,128)(2,1)S(1)}, bf16[96,256]{1,0:T(8,128)(2,1)}, u32[]{:S(2)}) copy-start(bf16[96,256]{1,0:T(8,128)(2,1)} %q_ref.3) | copy-start | bytes 147460
  15.6 1.7 %copy-start = (bf16[256,5120]{1,0:T(8,128)(2,1)S(1)}, bf16[256,5120]{1,0:T(8,128)(2,1)}, u32[]{:S(2)}) copy-start(bf16[256,5120]{1,0:T(8,128)(2,1)} %weight_ref.1) | copy-start | bytes 7864324
  16.2 2.3 %copy-start.5 = (f32[1280]{0:T(1024)S(1)}, f32[1280]{0:T(1024)}, u32[]{:S(2)}) copy-start(f32[1280]{0:T(1024)} %param.15) | copy-start | bytes 15364
  16.2 2.3 %copy-start.1 = (bf16[96,1280]{1,0:T(8,128)(2,1)S(1)}, bf16[96,1280]{1,0:T(8,128)(2,1)}, u32[]{:S(2)}) copy-start(bf16[96,1280]{1,0:T(8,128)(2,1)} %hidden_ref.1) | copy-start | bytes 737284
  16.2 1.4 %collective-permute-start.4 = (bf16[96,256]{1,0:T(8,128)(2,1)S(1)}, bf16[96,256]{1,0:T(8,128)(2,1)S(1)}, u32[]{:S(2)}, u32[]{:S(2)}) collective-permute-start(bf16[96,256]{1,0:T(8,128)(2,1)S(1)} %attention.1.refs_0_.attended_ref), channel_id=1, source_target_pairs={{0,1},{1,0},{2,3},{3,2},{4,5},{5,4},{6,7},{7,6},{8,9},{9,8},{10,11... | collective-permute-start | bytes 147464 | tf_op jit(solution)/shard_map/attended_swap/ppermute | solution.py:43
  17.9 7.9 %collective-permute-start.6 = (bf16[96,1280]{1,0:T(8,128)(2,1)S(1)}, bf16[96,1280]{1,0:T(8,128)(2,1)S(1)}, u32[]{:S(2)}, u32[]{:S(2)}) collective-permute-start(bf16[96,1280]{1,0:T(8,128)(2,1)S(1)} %sent_term.1), channel_id=1, source_target_pairs={{0,2},{2,0},{1,3},{3,1},{4,6},{6,4},{5,7},{7,5},{8,10},{10,8},{9,1... | collective-permute-start | bytes 737288 | tf_op jit(solution)/shard_map/projection/ppermute | solution.py:43

commit v5 on v3

--- a/solution.py
+++ b/solution.py
@@ -43,31 +43,12 @@
     return lax.ppermute(array, axis, [(i, (i + step) % size) for i in range(size)])
 
 
-LINE_OF_FOUR = (
-    ([(0, 2), (2, 3), (3, 1), (1, 0)], (1, 3, 0, 2)),
-    ([(0, 1), (1, 3), (3, 2), (2, 0)], (2, 0, 3, 1)),
-    ([(0, 3), (3, 0), (1, 2), (2, 1)], (3, 2, 1, 0)),
-)
-
-
-def gather_permutes(patches):
-    if patches == 4:
-        return [pairs for pairs, _ in LINE_OF_FOUR]
-    return [
-        [(i, (i + step) % patches) for i in range(patches)] for step in range(1, patches)
-    ]
+def gather_steps(patches):
+    return list(range(patches - 1, 0, -1))
 
 
 def gather_sources(patches, place):
-    if patches == 4:
-        sources = [place]
-        for _, table in LINE_OF_FOUR:
-            source = jnp.int32(table[0])
-            for i in range(1, 4):
-                source = jnp.where(place == i, jnp.int32(table[i]), source)
-            sources.append(source)
-        return sources
-    return [lax.rem(place + patches - step, patches) for step in range(patches)]
+    return [place] + [lax.rem(place + patches - step, patches) for step in gather_steps(patches)]
 
 
 def stage_kernel(patches, q_ref, held_k_ref, held_v_ref, products_ref, values_ref):
@@ -169,7 +150,7 @@
                 lax.pad(value_change, low, ((0, 0, 0), (width, 0, 0))),
             ).astype(jnp.bfloat16)
             blocks = [residual] + [
-                lax.ppermute(residual, "patch", pairs) for pairs in gather_permutes(patches)
+                shift(residual, "patch", patches, step) for step in gather_steps(patches)
             ]
 
         with jax.named_scope("weight_swap"):

time: 26.2 us -> 25 us (0.954)
  starting transfers between devices: 9.67 us -> 8.64 us
    ppermute x3 -> x0, starting transfers between devices: 7.59 us -> none  [per_device(): lax.ppermute(residual, 'patch', pairs)]
    ppermute x3 -> x6, starting transfers between devices: 2.08 us -> 8.64 us  [shift(): lax.ppermute(array, axis, [(i, (i + step) % size) for i in range(size)])]
    ppermute x3 -> x0, waiting for transfers between devices: 3.13 us -> none  [per_device(): lax.ppermute(residual, 'patch', pairs)]
    ppermute x3 -> x6, waiting for transfers between devices: 6 us -> 8.95 us  [shift(): lax.ppermute(array, axis, [(i, (i + step) % size) for i in range(size)])]
where the time goes in v5:
time: 25 us; the launch traced here: 24.8 us
  waiting for transfers between devices  8.95 us (36%)
  starting transfers between devices  8.64 us (35%)
  local copies, waits for them, and re-layouts  3.77 us (15%)
  Pallas kernels  2.37 us (9%)
  other arithmetic  0.95 us (4%)
    ppermute x6, waiting for transfers between devices, shift(): lax.ppermute(array, axis, [(i, (i + step) % size) for i in range(size)])  8.95 us
    ppermute x6, starting transfers between devices, shift(): lax.ppermute(array, axis, [(i, (i + step) % size) for i in range(size)])  8.64 us
    unnamed x12, local copies, waits for them, and re-layouts  3.77 us
    convert_element_type x1, other arithmetic, per_device(): residual = jnp.maximum(lax.pad(key_change, low, ((0, 0, 0), (0, width, 0)...  0.95 us
    pallas_call x1, Pallas kernels, per_device(): call(final_kernel, sent, [IN_VMEM] * (2 + len(arrived)), IN_VMEM, 'final'...  0.75 us
    pallas_call x1, Pallas kernels, per_device(): call(functools.partial(attention_kernel, 1.0 / math.sqrt(HD)), jax.ShapeD...  0.53 us
  transfers between devices with their start and end apart: 6, of which 2 were waited for; matrix products, arithmetic and copies ran while one was open for 4% of the time, Pallas kernels for 5%

profile of v5, /device:TPU:0, one launch (start us, length us, event | category | flops | bytes accessed | tf_op | source)
XLA Modules:
  0.0 24.8 jit_solution(11416725369584765052)
XLA Ops:
  0.0 0.5 %collective-permute-start.4 = (bf16[256,5120]{1,0:T(8,128)(2,1)}, bf16[256,5120]{1,0:T(8,128)(2,1)S(1)}, u32[]{:S(2)}, u32[]{:S(2)}) collective-permute-start(bf16[256,5120]{1,0:T(8,128)(2,1)} %weight_ref.1), channel_id=1, source_target_pairs={{0,1},{1,0},{2,3},{3,2},{4,5},{5,4},{6,7},{7,6},{8,9},{9,8},{10,11... | collective-permute-start | bytes 7864328 | tf_op jit(solution)/shard_map/weight_swap/ppermute | solution.py:43
  0.5 1.0 %maximum_convert_fusion.refs_0_ = bf16[96,512]{1,0:T(8,128)(2,1)S(1)} fusion(f32[96,256]{1,0:T(8,128)} %param.12, f32[96,256]{1,0:T(8,128)} %param.11), kind=kLoop, calls=%fused_computation | loop fusion | flops 196608 | bytes 294912 | tf_op jit(solution)/shard_map/residual_gather/convert_element_type | solution.py:151
  1.4 2.6 %collective-permute-start.2 = (bf16[96,512]{1,0:T(8,128)(2,1)S(1)}, bf16[96,512]{1,0:T(8,128)(2,1)S(1)}, u32[]{:S(2)}, u32[]{:S(2)}) collective-permute-start(bf16[96,512]{1,0:T(8,128)(2,1)S(1)} %maximum_convert_fusion.refs_0_), channel_id=1, source_target_pairs={{0,4},{4,8},{8,12},{12,0},{1,5},{5,9},{9,13},{13,1},{2,6},{6,10},{... | collective-permute-start | bytes 294920 | tf_op jit(solution)/shard_map/residual_gather/ppermute | solution.py:43
  4.0 2.6 %collective-permute-start.1 = (bf16[96,512]{1,0:T(8,128)(2,1)S(1)}, bf16[96,512]{1,0:T(8,128)(2,1)S(1)}, u32[]{:S(2)}, u32[]{:S(2)}) collective-permute-start(bf16[96,512]{1,0:T(8,128)(2,1)S(1)} %maximum_convert_fusion.refs_0_), channel_id=1, source_target_pairs={{0,8},{4,12},{8,0},{12,4},{1,9},{5,13},{9,1},{13,5},{2,10},{6,14},... | collective-permute-start | bytes 294920 | tf_op jit(solution)/shard_map/residual_gather/ppermute | solution.py:43
  6.6 1.3 %collective-permute-start = (bf16[96,512]{1,0:T(8,128)(2,1)S(1)}, bf16[96,512]{1,0:T(8,128)(2,1)S(1)}, u32[]{:S(2)}, u32[]{:S(2)}) collective-permute-start(bf16[96,512]{1,0:T(8,128)(2,1)S(1)} %maximum_convert_fusion.refs_0_), channel_id=1, source_target_pairs={{0,12},{4,0},{8,4},{12,8},{1,13},{5,1},{9,5},{13,9},{2,14},{6,2},{... | collective-permute-start | bytes 294920 | tf_op jit(solution)/shard_map/residual_gather/ppermute | solution.py:43
  8.0 0.0 copy-start.2
  8.0 0.9 %copy-done.2 = bf16[384,256]{1,0:T(8,128)(2,1)S(1)} copy-done((bf16[384,256]{1,0:T(8,128)(2,1)S(1)}, bf16[384,256]{1,0:T(8,128)(2,1)}, u32[]{:S(2)}) %copy-start.2) | copy-done | bytes 196632
  8.9 0.0 copy-start.3
  8.9 0.9 %copy-done.3 = bf16[384,256]{1,0:T(8,128)(2,1)S(1)} copy-done((bf16[384,256]{1,0:T(8,128)(2,1)S(1)}, bf16[384,256]{1,0:T(8,128)(2,1)}, u32[]{:S(2)}) %copy-start.3) | copy-done | bytes 196632
  9.8 0.0 copy-start.4
  9.8 0.8 %copy-done.4 = bf16[96,256]{1,0:T(8,128)(2,1)S(1)} copy-done((bf16[96,256]{1,0:T(8,128)(2,1)S(1)}, bf16[96,256]{1,0:T(8,128)(2,1)}, u32[]{:S(2)}) %copy-start.4) | copy-done | bytes 49176
  10.6 0.2 stage.1
  10.8 0.0 collective-permute-done.2.refs_3_
  10.9 2.9 %collective-permute-done.1.refs_2_ = bf16[96,512]{1,0:T(8,128)(2,1)S(1)} collective-permute-done((bf16[96,512]{1,0:T(8,128)(2,1)S(1)}, bf16[96,512]{1,0:T(8,128)(2,1)S(1)}, u32[]{:S(2)}, u32[]{:S(2)}) %collective-permute-start.1) | collective-permute-done | bytes 98336 | tf_op jit(solution)/shard_map/residual_gather/ppermute | solution.py:43
  13.8 0.0 collective-permute-done.refs_1_
  13.8 0.0 copy-start
  13.8 0.5 %attention.1.refs_0_.attended_ref = bf16[96,256]{1,0:T(8,128)(2,1)S(1)} custom-call(bf16[96,256]{1,0:T(8,128)(2,1)S(1)} %copy-done.4, f32[2,96,384]{2,1,0:T(8,128)S(1)} %get-tuple-element.7.products_ref, bf16[384,256]{1,0:T(8,128)(2,1)S(1)} %get-tuple-element.8.values_ref, bf16[96,512]{1,0:T(8,128)(2,1)S(1)} %maximum_convert_fusion.refs_0_, ...), custom_call_target="tpu_custom_call" | custom-call | flops 2000000000 | tf_op jit(solution)/shard_map/attention/attention/pallas_call | solution.py:180
  14.3 0.0 copy-start.5
  14.4 0.0 copy-start.1
  14.4 0.1 collective-permute-start.3
  14.5 1.1 %copy-done = bf16[256,5120]{1,0:T(8,128)(2,1)S(1)} copy-done((bf16[256,5120]{1,0:T(8,128)(2,1)S(1)}, bf16[256,5120]{1,0:T(8,128)(2,1)}, u32[]{:S(2)}) %copy-start) | copy-done | bytes 2621464
  15.6 0.2 own_term.1.total_ref
  15.8 0.0 collective-permute-done.3.refs_2_.refs_0_
  15.8 0.0 collective-permute-done.4.refs_3_.refs_1_
  15.8 0.3 %sent_term.1 = bf16[96,1280]{1,0:T(8,128)(2,1)S(1)} custom-call(f32[96,1280]{1,0:T(8,128)S(1)} %own_term.1.total_ref, bf16[96,256]{1,0:T(8,128)(2,1)S(1)} %collective-permute-done.3.refs_2_.refs_0_, bf16[256,5120]{1,0:T(8,128)(2,1)S(1)} %collective-permute-done.4.refs_3_.refs_1_), custom_call_target="tpu_custom_call" | custom-call | flops 62914560 | tf_op jit(solution)/shard_map/projection/sent_term/pallas_call | solution.py:214
  16.1 1.6 %collective-permute-start.5 = (bf16[96,1280]{1,0:T(8,128)(2,1)S(1)}, bf16[96,1280]{1,0:T(8,128)(2,1)S(1)}, u32[]{:S(2)}, u32[]{:S(2)}) collective-permute-start(bf16[96,1280]{1,0:T(8,128)(2,1)S(1)} %sent_term.1), channel_id=1, source_target_pairs={{0,2},{2,0},{1,3},{3,1},{4,6},{6,4},{5,7},{7,5},{8,10},{10,8},{9,1... | collective-permute-start | bytes 737288 | tf_op jit(solution)/shard_map/projection/ppermute | solution.py:43
  17.6 0.0 copy-done.5
  17.6 0.0 copy-done.1
  17.7 0.4 %base.1.base_ref = f32[96,1280]{1,0:T(8,128)S(1)} custom-call(bf16[96,1280]{1,0:T(8,128)(2,1)S(1)} %copy-done.1, f32[1,1280]{1,0:T(1,128)S(1)} %reshape.3.gate_ref, bf16[96,256]{1,0:T(8,128)(2,1)S(1)} %attention.1.refs_0_.attended_ref, bf16[256,5120]{1,0:T(8,128)(2,1)S(1)} %copy-done, bf16[96,256]{1,0:T(8,128)(2,1)S(1)} %collective-permute-done.3.refs_2_.refs_0_, ...), custom_call_target="tpu_custom_call" | custom-call | flops 125829120 | tf_op jit(solution)/shard_map/projection/base/pallas_call | solution.py:227
  18.0 6.0 %collective-permute-done.5.refs_0_ = bf16[96,1280]{1,0:T(8,128)(2,1)S(1)} collective-permute-done((bf16[96,1280]{1,0:T(8,128)(2,1)S(1)}, bf16[96,1280]{1,0:T(8,128)(2,1)S(1)}, u32[]{:S(2)}, u32[]{:S(2)}) %collective-permute-start.5) | collective-permute-done | bytes 245792 | tf_op jit(solution)/shard_map/projection/ppermute | solution.py:43
  24.0 0.8 %final.1 = bf16[96,1280]{1,0:T(8,128)(2,1)} custom-call(f32[96,1280]{1,0:T(8,128)S(1)} %base.1.base_ref, f32[1,1280]{1,0:T(1,128)S(1)} %reshape.3.gate_ref, bf16[96,1280]{1,0:T(8,128)(2,1)S(1)} %collective-permute-done.5.refs_0_), custom_call_target="tpu_custom_call" | custom-call | bytes 983040 | tf_op jit(solution)/shard_map/projection/final/pallas_call | solution.py:235
  (1 shorter events, 0.0 us)
Async XLA Ops:
  0.0 15.8 %collective-permute-start.4 = (bf16[256,5120]{1,0:T(8,128)(2,1)}, bf16[256,5120]{1,0:T(8,128)(2,1)S(1)}, u32[]{:S(2)}, u32[]{:S(2)}) collective-permute-start(bf16[256,5120]{1,0:T(8,128)(2,1)} %weight_ref.1), channel_id=1, source_target_pairs={{0,1},{1,0},{2,3},{3,2},{4,5},{5,4},{6,7},{7,6},{8,9},{9,8},{10,11... | collective-permute-start | bytes 7864328 | tf_op jit(solution)/shard_map/weight_swap/ppermute | solution.py:43
  1.4 9.4 %collective-permute-start.2 = (bf16[96,512]{1,0:T(8,128)(2,1)S(1)}, bf16[96,512]{1,0:T(8,128)(2,1)S(1)}, u32[]{:S(2)}, u32[]{:S(2)}) collective-permute-start(bf16[96,512]{1,0:T(8,128)(2,1)S(1)} %maximum_convert_fusion.refs_0_), channel_id=1, source_target_pairs={{0,4},{4,8},{8,12},{12,0},{1,5},{5,9},{9,13},{13,1},{2,6},{6,10},{... | collective-permute-start | bytes 294920 | tf_op jit(solution)/shard_map/residual_gather/ppermute | solution.py:43
  4.0 9.8 %collective-permute-start.1 = (bf16[96,512]{1,0:T(8,128)(2,1)S(1)}, bf16[96,512]{1,0:T(8,128)(2,1)S(1)}, u32[]{:S(2)}, u32[]{:S(2)}) collective-permute-start(bf16[96,512]{1,0:T(8,128)(2,1)S(1)} %maximum_convert_fusion.refs_0_), channel_id=1, source_target_pairs={{0,8},{4,12},{8,0},{12,4},{1,9},{5,13},{9,1},{13,5},{2,10},{6,14},... | collective-permute-start | bytes 294920 | tf_op jit(solution)/shard_map/residual_gather/ppermute | solution.py:43
  6.6 7.2 %collective-permute-start = (bf16[96,512]{1,0:T(8,128)(2,1)S(1)}, bf16[96,512]{1,0:T(8,128)(2,1)S(1)}, u32[]{:S(2)}, u32[]{:S(2)}) collective-permute-start(bf16[96,512]{1,0:T(8,128)(2,1)S(1)} %maximum_convert_fusion.refs_0_), channel_id=1, source_target_pairs={{0,12},{4,0},{8,4},{12,8},{1,13},{5,1},{9,5},{13,9},{2,14},{6,2},{... | collective-permute-start | bytes 294920 | tf_op jit(solution)/shard_map/residual_gather/ppermute | solution.py:43
  8.0 0.9 %copy-start.2 = (bf16[384,256]{1,0:T(8,128)(2,1)S(1)}, bf16[384,256]{1,0:T(8,128)(2,1)}, u32[]{:S(2)}) copy-start(bf16[384,256]{1,0:T(8,128)(2,1)} %held_k_ref.1) | copy-start | bytes 589828
  8.9 0.9 %copy-start.3 = (bf16[384,256]{1,0:T(8,128)(2,1)S(1)}, bf16[384,256]{1,0:T(8,128)(2,1)}, u32[]{:S(2)}) copy-start(bf16[384,256]{1,0:T(8,128)(2,1)} %held_v_ref.1) | copy-start | bytes 589828
  9.8 0.8 %copy-start.4 = (bf16[96,256]{1,0:T(8,128)(2,1)S(1)}, bf16[96,256]{1,0:T(8,128)(2,1)}, u32[]{:S(2)}) copy-start(bf16[96,256]{1,0:T(8,128)(2,1)} %q_ref.3) | copy-start | bytes 147460
  13.8 1.7 %copy-start = (bf16[256,5120]{1,0:T(8,128)(2,1)S(1)}, bf16[256,5120]{1,0:T(8,128)(2,1)}, u32[]{:S(2)}) copy-start(bf16[256,5120]{1,0:T(8,128)(2,1)} %weight_ref.1) | copy-start | bytes 7864324
  14.3 3.3 %copy-start.5 = (f32[1280]{0:T(1024)S(1)}, f32[1280]{0:T(1024)}, u32[]{:S(2)}) copy-start(f32[1280]{0:T(1024)} %param.15) | copy-start | bytes 15364
  14.4 3.3 %copy-start.1 = (bf16[96,1280]{1,0:T(8,128)(2,1)S(1)}, bf16[96,1280]{1,0:T(8,128)(2,1)}, u32[]{:S(2)}) copy-start(bf16[96,1280]{1,0:T(8,128)(2,1)} %hidden_ref.1) | copy-start | bytes 737284
  14.4 1.4 %collective-permute-start.3 = (bf16[96,256]{1,0:T(8,128)(2,1)S(1)}, bf16[96,256]{1,0:T(8,128)(2,1)S(1)}, u32[]{:S(2)}, u32[]{:S(2)}) collective-permute-start(bf16[96,256]{1,0:T(8,128)(2,1)S(1)} %attention.1.refs_0_.attended_ref), channel_id=1, source_target_pairs={{0,1},{1,0},{2,3},{3,2},{4,5},{5,4},{6,7},{7,6},{8,9},{9,8},{10,11... | collective-permute-start | bytes 147464 | tf_op jit(solution)/shard_map/attended_swap/ppermute | solution.py:43
  16.1 7.9 %collective-permute-start.5 = (bf16[96,1280]{1,0:T(8,128)(2,1)S(1)}, bf16[96,1280]{1,0:T(8,128)(2,1)S(1)}, u32[]{:S(2)}, u32[]{:S(2)}) collective-permute-start(bf16[96,1280]{1,0:T(8,128)(2,1)S(1)} %sent_term.1), channel_id=1, source_target_pairs={{0,2},{2,0},{1,3},{3,1},{4,6},{6,4},{5,7},{7,5},{8,10},{10,8},{9,1... | collective-permute-start | bytes 737288 | tf_op jit(solution)/shard_map/projection/ppermute | solution.py:43

commit v6 on v5

--- a/solution.py
+++ b/solution.py
@@ -25,7 +25,7 @@
     flops=0,
     moved=0,
     scratch_shapes=(),
-    vmem=VMEM_LIMIT,
+    aliases=None,
 ):
     return pl.pallas_call(
         kernel,
@@ -33,9 +33,10 @@
         in_specs=in_specs,
         out_specs=out_specs,
         scratch_shapes=scratch_shapes,
+        input_output_aliases=aliases or {},
         name=name,
         cost_estimate=pl.CostEstimate(flops=flops, bytes_accessed=moved, transcendentals=0),
-        compiler_params=pltpu.CompilerParams(vmem_limit_bytes=vmem),
+        compiler_params=pltpu.CompilerParams(vmem_limit_bytes=VMEM_LIMIT),
     )
 
 
@@ -43,12 +44,34 @@
     return lax.ppermute(array, axis, [(i, (i + step) % size) for i in range(size)])
 
 
-def gather_steps(patches):
-    return list(range(patches - 1, 0, -1))
+RING_OF_FOUR = ((0, 1), (1, 3), (3, 2), (2, 0))
+
+
+def gather(own, patches):
+    if patches != 4:
+        return [own] + [shift(own, "patch", patches, step) for step in range(1, patches)]
+    forth = lax.ppermute(own, "patch", RING_OF_FOUR)
+    back = lax.ppermute(own, "patch", [(target, source) for source, target in RING_OF_FOUR])
+    across = lax.ppermute(forth, "patch", RING_OF_FOUR)
+    return [own, across, back, forth]
 
 
 def gather_sources(patches, place):
-    return [place] + [lax.rem(place + patches - step, patches) for step in gather_steps(patches)]
+    if patches != 4:
+        return [lax.rem(place + patches - step, patches) for step in range(patches)]
+    before = {target: source for source, target in RING_OF_FOUR}
+    after = dict(RING_OF_FOUR)
+    return [place] + [
+        by_place(place, [table(i) for i in range(4)])
+        for table in (lambda i: before[before[i]], lambda i: after[i], lambda i: before[i])
+    ]
+
+
+def by_place(place, entries):
+    value = jnp.int32(entries[0])
+    for i, entry in enumerate(entries[1:], 1):
+        value = jnp.where(place == i, jnp.int32(entry), value)
+    return value
 
 
 def stage_kernel(patches, q_ref, held_k_ref, held_v_ref, products_ref, values_ref):
@@ -92,46 +115,47 @@
         out_ref[:, cols] = (sums / totals).astype(jnp.bfloat16)
 
 
-def block_dot(a_ref, weight_ref, block, columns):
-    if block is None:
+def block_dot(a_ref, weight_ref, start, columns):
+    if start is None:
         weight = weight_ref[...]
     else:
-        weight = weight_ref[:, pl.ds(pl.multiple_of(block * columns, LANES), columns)]
+        weight = weight_ref[:, pl.ds(pl.multiple_of(start(), LANES), columns)]
     return jnp.dot(a_ref[...], weight, preferred_element_type=jnp.float32)
 
 
-def block_at(step, heads, subs):
-    return lax.rem(lax.axis_index("head") + step, heads) * subs + lax.axis_index("sub")
-
-
-def own_term_kernel(block_of, attended_ref, weight_ref, out_ref):
-    out_ref[...] = block_dot(attended_ref, weight_ref, block_of(), out_ref.shape[1])
-
-
-def sent_term_kernel(block_of, total_ref, *refs):
+def own_term_kernel(starts, attended_ref, weight_ref, *out_refs):
+    for start, out_ref in zip(starts, out_refs):
+        out_ref[...] = block_dot(attended_ref, weight_ref, start, out_ref.shape[1])
+
+
+def sent_term_kernel(start, total_ref, *refs):
     out_ref = refs[-1]
-    block, columns = block_of(), out_ref.shape[1]
     total = total_ref[...]
     for attended_ref, weight_ref in zip(refs[:-1:2], refs[1:-1:2]):
-        total = total + block_dot(attended_ref, weight_ref, block, columns)
+        total = total + block_dot(attended_ref, weight_ref, start, out_ref.shape[1])
     out_ref[...] = total.astype(jnp.bfloat16)
 
 
-def base_kernel(block_of, hidden_ref, gate_ref, *refs):
+def base_kernel(start, hidden_ref, gate_ref, *refs):
     out_ref = refs[-1]
-    block, columns = block_of(), out_ref.shape[1]
     total = 0.0
     for attended_ref, weight_ref in zip(refs[:-1:2], refs[1:-1:2]):
-        total = total + block_dot(attended_ref, weight_ref, block, columns)
+        total = total + block_dot(attended_ref, weight_ref, start, out_ref.shape[1])
     out_ref[...] = hidden_ref[...].astype(jnp.float32) + gate_ref[...] * total
 
 
-def final_kernel(base_ref, gate_ref, *refs):
-    arrived_refs, out_ref = refs[:-1], refs[-1]
+def final_kernel(at, base_ref, gate_ref, *refs):
+    out_ref, result, sem = refs[-3:]
+    size = result.shape[1]
     total = 0.0
-    for ref in arrived_refs:
-        total = total + ref[...].astype(jnp.float32)
-    out_ref[...] = (base_ref[...] + gate_ref[...] * total).astype(jnp.bfloat16)
+    for ref in refs[:-3]:
+        if ref.shape == result.shape:
+            total = total + ref[...].astype(jnp.float32)
+    cols = slice(at, at + size)
+    result[...] = (base_ref[:, cols] + gate_ref[:, cols] * total).astype(jnp.bfloat16)
+    copy = pltpu.make_async_copy(result, out_ref.at[:, pl.ds(at, size)], sem)
+    copy.start()
+    copy.wait()
 
 
 def solution(mesh):
@@ -149,20 +173,25 @@
                 lax.pad(key_change, low, ((0, 0, 0), (0, width, 0))),
                 lax.pad(value_change, low, ((0, 0, 0), (width, 0, 0))),
             ).astype(jnp.bfloat16)
-            blocks = [residual] + [
-                shift(residual, "patch", patches, step) for step in gather_steps(patches)
-            ]
+            blocks = gather(residual, patches)
 
         with jax.named_scope("weight_swap"):
             weights = [out_weight] + [
                 shift(out_weight, "sub", subs, i) for i in range(1, subs)
             ]
 
-        def weight_and_block(i, step):
+        chunks = 2 if columns % (2 * LANES) == 0 else 1
+        size = columns // chunks
+
+        def block_start(step, chunk):
+            to = lax.rem(lax.axis_index("head") + step, heads) * subs + lax.axis_index("sub")
+            return to * columns + chunk * size
+
+        def weight_and_start(i, step, chunk=0, length=columns):
+            start = functools.partial(block_start, step, chunk)
             if columns % LANES == 0:
-                return weights[i], functools.partial(block_at, step, heads, subs)
-            at = block_at(step, heads, subs) * columns
-            return lax.dynamic_slice(weights[i], (0, at), (width, columns)), lambda: None
+                return weights[i], start
+            return lax.dynamic_slice(weights[i], (0, start()), (width, length)), None
 
         tokens = rows * patches
         with jax.named_scope("attention"):
@@ -192,54 +221,71 @@
             ]
 
         term = jax.ShapeDtypeStruct((rows, columns), jnp.float32)
-        sent = jax.ShapeDtypeStruct((rows, columns), jnp.bfloat16)
+        part = jax.ShapeDtypeStruct((rows, size), jnp.float32)
+        sent = jax.ShapeDtypeStruct((rows, size), jnp.bfloat16)
         product_flops = 2 * rows * width * columns
         with jax.named_scope("projection"):
-            arrived = []
+            arrived = [[] for _ in range(chunks)]
             for step in range(1, heads):
-                weight, block_of = weight_and_block(0, step)
-                own = call(
-                    functools.partial(own_term_kernel, block_of),
-                    term,
+                own_weight = weight_and_start(0, step, 0, size)[0]
+                own_terms = call(
+                    functools.partial(
+                        own_term_kernel,
+                        [weight_and_start(0, step, n, size)[1] for n in range(chunks)],
+                    ),
+                    [part] * chunks,
                     [IN_VMEM] * 2,
-                    IN_VMEM,
+                    [IN_VMEM] * chunks,
                     "own_term",
                     product_flops,
-                )(attended, weight)
-                pairs = [
-                    x
-                    for i in range(1, subs)
-                    for x in (attended_parts[i], weight_and_block(i, step)[0])
-                ]
-                total = call(
-                    functools.partial(sent_term_kernel, block_of),
-                    sent,
-                    [IN_VMEM] * (1 + len(pairs)),
-                    IN_VMEM,
-                    "sent_term",
-                    product_flops,
-                )(own, *pairs)
-                arrived.append(shift(total, "head", heads, step))
+                )(attended, own_weight)
+                for n in range(chunks):
+                    pairs = [
+                        x
+                        for i in range(1, subs)
+                        for x in (attended_parts[i], weight_and_start(i, step, n, size)[0])
+                    ]
+                    total = call(
+                        functools.partial(
+                            sent_term_kernel, weight_and_start(0, step, n, size)[1]
+                        ),
+                        sent,
+                        [IN_VMEM] * (1 + len(pairs)),
+                        IN_VMEM,
+                        "sent_term",
+                        product_flops // chunks,
+                    )(own_terms[n], *pairs)
+                    arrived[n].append(shift(total, "head", heads, step))
             gate_row = gate.reshape(1, columns)
             pairs = [
-                x for i in range(subs) for x in (attended_parts[i], weight_and_block(i, 0)[0])
+                x for i in range(subs) for x in (attended_parts[i], weight_and_start(i, 0)[0])
             ]
             base = call(
-                functools.partial(base_kernel, weight_and_block(0, 0)[1]),
+                functools.partial(base_kernel, weight_and_start(0, 0)[1]),
                 term,
                 [IN_VMEM] * (2 + len(pairs)),
                 IN_VMEM,
                 "base",
                 2 * product_flops,
             )(hidden_in, gate_row, *pairs)
-            return call(
-                final_kernel,
-                sent,
-                [IN_VMEM] * (2 + len(arrived)),
-                IN_VMEM,
-                "final",
-                moved=rows * columns * 8,
-            )(base, gate_row, *arrived)
+            out = None
+            for n in range(chunks):
+                before = [] if out is None else [out]
+                inputs = [base, gate_row, *arrived[n], *before]
+                out = call(
+                    functools.partial(final_kernel, n * size),
+                    jax.ShapeDtypeStruct((rows, columns), jnp.bfloat16),
+                    [IN_VMEM] * (2 + len(arrived[n])) + [ANYWHERE] * len(before),
+                    ANYWHERE,
+                    "final",
+                    moved=rows * size * 8,
+                    scratch_shapes=[
+                        pltpu.VMEM((rows, size), jnp.bfloat16),
+                        pltpu.SemaphoreType.DMA,
+                    ],
+                    aliases={len(inputs) - 1: 0} if before else {},
+                )(*inputs)
+            return out
 
     in_specs = (
         P(("groups", "patch"), ("head", "sub")),

time: 25 us -> 25.9 us (1.036)
  the two profiles are of different devices: /device:TPU:0 before, /device:TPU:28 now
where the time goes in v6:
time: 25.9 us; the launch traced here: 25.6 us
  waiting for transfers between devices  12.3 us (47%)
  starting transfers between devices  5.21 us (20%)
  local copies, waits for them, and re-layouts  3.8 us (15%)
  Pallas kernels  3.17 us (12%)
  other arithmetic  0.95 us (4%)
    ppermute x1, waiting for transfers between devices, gather(): forth = lax.ppermute(own, 'patch', RING_OF_FOUR)  5.29 us
    ppermute x4, waiting for transfers between devices, shift(): lax.ppermute(array, axis, [(i, (i + step) % size) for i in range(size)])  4.43 us
    unnamed x12, local copies, waits for them, and re-layouts  3.79 us
    ppermute x1, waiting for transfers between devices, gather(): across = lax.ppermute(forth, 'patch', RING_OF_FOUR)  2.62 us
    ppermute x1, starting transfers between devices, gather(): lax.ppermute(own, 'patch', [(target, source) for source, target in RING_O...  2.48 us
    ppermute x4, starting transfers between devices, shift(): lax.ppermute(array, axis, [(i, (i + step) % size) for i in range(size)])  2.23 us
    pallas_call x2, Pallas kernels, per_device(): call(functools.partial(final_kernel, n * size), jax.ShapeDtypeStruct((row...  1.39 us
    convert_element_type x1, other arithmetic, per_device(): residual = jnp.maximum(lax.pad(key_change, low, ((0, 0, 0), (0, width, 0)...  0.95 us
  transfers between devices with their start and end apart: 7, of which 4 were waited for; matrix products, arithmetic and copies ran while one was open for 4% of the time, Pallas kernels for 9%

profile of v6, /device:TPU:28, one launch (start us, length us, event | category | flops | bytes accessed | tf_op | source)
XLA Modules:
  0.0 25.6 jit_solution(6709594863059551297)
XLA Ops:
  0.0 0.0 collective-permute-start.4
  0.0 1.0 %maximum_convert_fusion.refs_0_ = bf16[96,512]{1,0:T(8,128)(2,1)S(1)} fusion(f32[96,256]{1,0:T(8,128)} %param.12, f32[96,256]{1,0:T(8,128)} %param.11), kind=kLoop, calls=%fused_computation | loop fusion | flops 196608 | bytes 294912 | tf_op jit(solution)/shard_map/residual_gather/convert_element_type | solution.py:175
  1.0 0.5 %collective-permute-start = (bf16[96,512]{1,0:T(8,128)(2,1)S(1)}, bf16[96,512]{1,0:T(8,128)(2,1)S(1)}, u32[]{:S(2)}, u32[]{:S(2)}) collective-permute-start(bf16[96,512]{1,0:T(8,128)(2,1)S(1)} %maximum_convert_fusion.refs_0_), channel_id=1, source_target_pairs={{0,4},{4,12},{12,8},{8,0},{1,5},{5,13},{13,9},{9,1},{2,6},{6,14},{... | collective-permute-start | bytes 294920 | tf_op jit(solution)/shard_map/residual_gather/ppermute | solution.py:53
  1.5 2.5 %collective-permute-start.2 = (bf16[96,512]{1,0:T(8,128)(2,1)S(1)}, bf16[96,512]{1,0:T(8,128)(2,1)S(1)}, u32[]{:S(2)}, u32[]{:S(2)}) collective-permute-start(bf16[96,512]{1,0:T(8,128)(2,1)S(1)} %maximum_convert_fusion.refs_0_), channel_id=1, source_target_pairs={{4,0},{12,4},{8,12},{0,8},{5,1},{13,5},{9,13},{1,9},{6,2},{14,6},{... | collective-permute-start | bytes 294920 | tf_op jit(solution)/shard_map/residual_gather/ppermute | solution.py:54
  3.9 5.3 %collective-permute-done.refs_3_ = bf16[96,512]{1,0:T(8,128)(2,1)S(1)} collective-permute-done((bf16[96,512]{1,0:T(8,128)(2,1)S(1)}, bf16[96,512]{1,0:T(8,128)(2,1)S(1)}, u32[]{:S(2)}, u32[]{:S(2)}) %collective-permute-start) | collective-permute-done | bytes 98336 | tf_op jit(solution)/shard_map/residual_gather/ppermute | solution.py:53
  9.2 0.0 collective-permute-start.1
  9.2 0.0 copy-start.2
  9.2 0.9 %copy-done.2 = bf16[384,256]{1,0:T(8,128)(2,1)S(1)} copy-done((bf16[384,256]{1,0:T(8,128)(2,1)S(1)}, bf16[384,256]{1,0:T(8,128)(2,1)}, u32[]{:S(2)}) %copy-start.2) | copy-done | bytes 196632
  10.2 0.0 copy-start.3
  10.2 0.9 %copy-done.3 = bf16[384,256]{1,0:T(8,128)(2,1)S(1)} copy-done((bf16[384,256]{1,0:T(8,128)(2,1)S(1)}, bf16[384,256]{1,0:T(8,128)(2,1)}, u32[]{:S(2)}) %copy-start.3) | copy-done | bytes 196632
  11.1 0.0 copy-start.4
  11.1 0.8 %copy-done.4 = bf16[96,256]{1,0:T(8,128)(2,1)S(1)} copy-done((bf16[96,256]{1,0:T(8,128)(2,1)S(1)}, bf16[96,256]{1,0:T(8,128)(2,1)}, u32[]{:S(2)}) %copy-start.4) | copy-done | bytes 49176
  11.9 0.2 stage.1
  12.1 0.0 collective-permute-done.2.refs_2_
  12.1 2.6 %collective-permute-done.1.refs_1_ = bf16[96,512]{1,0:T(8,128)(2,1)S(1)} collective-permute-done((bf16[96,512]{1,0:T(8,128)(2,1)S(1)}, bf16[96,512]{1,0:T(8,128)(2,1)S(1)}, u32[]{:S(2)}, u32[]{:S(2)}) %collective-permute-start.1) | collective-permute-done | bytes 98336 | tf_op jit(solution)/shard_map/residual_gather/ppermute | solution.py:55
  14.7 0.0 copy-start
  14.7 0.5 %attention.1.refs_0_.attended_ref = bf16[96,256]{1,0:T(8,128)(2,1)S(1)} custom-call(bf16[96,256]{1,0:T(8,128)(2,1)S(1)} %copy-done.4, f32[2,96,384]{2,1,0:T(8,128)S(1)} %get-tuple-element.9.products_ref, bf16[384,256]{1,0:T(8,128)(2,1)S(1)} %get-tuple-element.10.values_ref, bf16[96,512]{1,0:T(8,128)(2,1)S(1)} %maximum_convert_fusion.refs_0_, ...), custom_call_target="tpu_custom_call" | custom-call | flops 2000000000 | tf_op jit(solution)/shard_map/attention/attention/pallas_call | solution.py:209
  15.3 0.1 collective-permute-start.3
  15.4 1.1 %copy-done = bf16[256,5120]{1,0:T(8,128)(2,1)S(1)} copy-done((bf16[256,5120]{1,0:T(8,128)(2,1)S(1)}, bf16[256,5120]{1,0:T(8,128)(2,1)}, u32[]{:S(2)}) %copy-start) | copy-done | bytes 2621464
  16.5 0.2 own_term.1
  16.7 0.0 collective-permute-done.3.refs_2_.refs_0_
  16.8 0.0 collective-permute-done.4.refs_3_.refs_1_
  16.8 0.0 copy-start.5
  16.8 0.0 copy-start.1
  16.8 0.2 sent_term.3
  17.0 1.6 %collective-permute-start.6 = (bf16[96,640]{1,0:T(8,128)(2,1)S(1)}, bf16[96,640]{1,0:T(8,128)(2,1)S(1)}, u32[]{:S(2)}, u32[]{:S(2)}) collective-permute-start(bf16[96,640]{1,0:T(8,128)(2,1)S(1)} %sent_term.3), channel_id=1, source_target_pairs={{0,2},{2,0},{1,3},{3,1},{4,6},{6,4},{5,7},{7,5},{8,10},{10,8},{9,1... | collective-permute-start | bytes 368648 | tf_op jit(solution)/shard_map/projection/ppermute | solution.py:44
  18.6 0.2 sent_term.2
  18.8 0.6 %collective-permute-start.5 = (bf16[96,640]{1,0:T(8,128)(2,1)S(1)}, bf16[96,640]{1,0:T(8,128)(2,1)S(1)}, u32[]{:S(2)}, u32[]{:S(2)}) collective-permute-start(bf16[96,640]{1,0:T(8,128)(2,1)S(1)} %sent_term.2), channel_id=1, source_target_pairs={{0,2},{2,0},{1,3},{3,1},{4,6},{6,4},{5,7},{7,5},{8,10},{10,8},{9,1... | collective-permute-start | bytes 368648 | tf_op jit(solution)/shard_map/projection/ppermute | solution.py:44
  19.4 0.0 copy-done.5
  19.4 0.0 copy-done.1
  19.4 0.4 %base.1.base_ref = f32[96,1280]{1,0:T(8,128)S(1)} custom-call(bf16[96,1280]{1,0:T(8,128)(2,1)S(1)} %copy-done.1, f32[1,1280]{1,0:T(1,128)S(1)} %reshape.3.gate_ref, bf16[96,256]{1,0:T(8,128)(2,1)S(1)} %attention.1.refs_0_.attended_ref, bf16[256,5120]{1,0:T(8,128)(2,1)S(1)} %copy-done, bf16[96,256]{1,0:T(8,128)(2,1)S(1)} %collective-permute-done.3.refs_2_.refs_0_, ...), custom_call_target="tpu_custom_call" | custom-call | flops 125829120 | tf_op jit(solution)/shard_map/projection/base/pallas_call | solution.py:263
  19.8 3.5 %collective-permute-done.6.refs_0_ = bf16[96,640]{1,0:T(8,128)(2,1)S(1)} collective-permute-done((bf16[96,640]{1,0:T(8,128)(2,1)S(1)}, bf16[96,640]{1,0:T(8,128)(2,1)S(1)}, u32[]{:S(2)}, u32[]{:S(2)}) %collective-permute-start.6) | collective-permute-done | bytes 122912 | tf_op jit(solution)/shard_map/projection/ppermute | solution.py:44
  23.3 0.7 %final.2.refs_1_ = bf16[96,1280]{1,0:T(8,128)(2,1)} custom-call(f32[96,1280]{1,0:T(8,128)S(1)} %base.1.base_ref, f32[1,1280]{1,0:T(1,128)S(1)} %reshape.3.gate_ref, bf16[96,640]{1,0:T(8,128)(2,1)S(1)} %collective-permute-done.6.refs_0_), custom_call_target="tpu_custom_call" | custom-call | bytes 491520 | tf_op jit(solution)/shard_map/projection/final/pallas_call | solution.py:275
  24.0 0.9 %collective-permute-done.5.refs_0_ = bf16[96,640]{1,0:T(8,128)(2,1)S(1)} collective-permute-done((bf16[96,640]{1,0:T(8,128)(2,1)S(1)}, bf16[96,640]{1,0:T(8,128)(2,1)S(1)}, u32[]{:S(2)}, u32[]{:S(2)}) %collective-permute-start.5) | collective-permute-done | bytes 122912 | tf_op jit(solution)/shard_map/projection/ppermute | solution.py:44
  24.9 0.7 %final.3 = bf16[96,1280]{1,0:T(8,128)(2,1)} custom-call(f32[96,1280]{1,0:T(8,128)S(1)} %base.1.base_ref, f32[1,1280]{1,0:T(1,128)S(1)} %reshape.3.gate_ref, bf16[96,640]{1,0:T(8,128)(2,1)S(1)} %collective-permute-done.5.refs_0_, bf16[96,1280]{1,0:T(8,128)(2,1)} %final.2.refs_1_), custom_call_target="tpu_custom_call", output_to_operand_aliasing={{}: (3, {})} | custom-call | bytes 491520 | tf_op jit(solution)/shard_map/projection/final/pallas_call | solution.py:275
  (1 shorter events, 0.0 us)
Async XLA Ops:
  0.0 16.8 %collective-permute-start.4 = (bf16[256,5120]{1,0:T(8,128)(2,1)}, bf16[256,5120]{1,0:T(8,128)(2,1)S(1)}, u32[]{:S(2)}, u32[]{:S(2)}) collective-permute-start(bf16[256,5120]{1,0:T(8,128)(2,1)} %weight_ref.1), channel_id=1, source_target_pairs={{0,1},{1,0},{2,3},{3,2},{4,5},{5,4},{6,7},{7,6},{8,9},{9,8},{10,11... | collective-permute-start | bytes 7864328 | tf_op jit(solution)/shard_map/weight_swap/ppermute | solution.py:44
  1.0 8.3 %collective-permute-start = (bf16[96,512]{1,0:T(8,128)(2,1)S(1)}, bf16[96,512]{1,0:T(8,128)(2,1)S(1)}, u32[]{:S(2)}, u32[]{:S(2)}) collective-permute-start(bf16[96,512]{1,0:T(8,128)(2,1)S(1)} %maximum_convert_fusion.refs_0_), channel_id=1, source_target_pairs={{0,4},{4,12},{12,8},{8,0},{1,5},{5,13},{13,9},{9,1},{2,6},{6,14},{... | collective-permute-start | bytes 294920 | tf_op jit(solution)/shard_map/residual_gather/ppermute | solution.py:53
  1.5 10.6 %collective-permute-start.2 = (bf16[96,512]{1,0:T(8,128)(2,1)S(1)}, bf16[96,512]{1,0:T(8,128)(2,1)S(1)}, u32[]{:S(2)}, u32[]{:S(2)}) collective-permute-start(bf16[96,512]{1,0:T(8,128)(2,1)S(1)} %maximum_convert_fusion.refs_0_), channel_id=1, source_target_pairs={{4,0},{12,4},{8,12},{0,8},{5,1},{13,5},{9,13},{1,9},{6,2},{14,6},{... | collective-permute-start | bytes 294920 | tf_op jit(solution)/shard_map/residual_gather/ppermute | solution.py:54
  9.2 5.5 %collective-permute-start.1 = (bf16[96,512]{1,0:T(8,128)(2,1)S(1)}, bf16[96,512]{1,0:T(8,128)(2,1)S(1)}, u32[]{:S(2)}, u32[]{:S(2)}) collective-permute-start(bf16[96,512]{1,0:T(8,128)(2,1)S(1)} %collective-permute-done.refs_3_), channel_id=1, source_target_pairs={{0,4},{4,12},{12,8},{8,0},{1,5},{5,13},{13,9},{9,1},{2,6},{6,14},{... | collective-permute-start | bytes 294920 | tf_op jit(solution)/shard_map/residual_gather/ppermute | solution.py:55
  9.2 0.9 %copy-start.2 = (bf16[384,256]{1,0:T(8,128)(2,1)S(1)}, bf16[384,256]{1,0:T(8,128)(2,1)}, u32[]{:S(2)}) copy-start(bf16[384,256]{1,0:T(8,128)(2,1)} %held_k_ref.1) | copy-start | bytes 589828
  10.2 0.9 %copy-start.3 = (bf16[384,256]{1,0:T(8,128)(2,1)S(1)}, bf16[384,256]{1,0:T(8,128)(2,1)}, u32[]{:S(2)}) copy-start(bf16[384,256]{1,0:T(8,128)(2,1)} %held_v_ref.1) | copy-start | bytes 589828
  11.1 0.8 %copy-start.4 = (bf16[96,256]{1,0:T(8,128)(2,1)S(1)}, bf16[96,256]{1,0:T(8,128)(2,1)}, u32[]{:S(2)}) copy-start(bf16[96,256]{1,0:T(8,128)(2,1)} %q_ref.3) | copy-start | bytes 147460
  14.7 1.7 %copy-start = (bf16[256,5120]{1,0:T(8,128)(2,1)S(1)}, bf16[256,5120]{1,0:T(8,128)(2,1)}, u32[]{:S(2)}) copy-start(bf16[256,5120]{1,0:T(8,128)(2,1)} %weight_ref.1) | copy-start | bytes 7864324
  15.3 1.5 %collective-permute-start.3 = (bf16[96,256]{1,0:T(8,128)(2,1)S(1)}, bf16[96,256]{1,0:T(8,128)(2,1)S(1)}, u32[]{:S(2)}, u32[]{:S(2)}) collective-permute-start(bf16[96,256]{1,0:T(8,128)(2,1)S(1)} %attention.1.refs_0_.attended_ref), channel_id=1, source_target_pairs={{0,1},{1,0},{2,3},{3,2},{4,5},{5,4},{6,7},{7,6},{8,9},{9,8},{10,11... | collective-permute-start | bytes 147464 | tf_op jit(solution)/shard_map/attended_swap/ppermute | solution.py:44
  16.8 2.6 %copy-start.5 = (f32[1280]{0:T(1024)S(1)}, f32[1280]{0:T(1024)}, u32[]{:S(2)}) copy-start(f32[1280]{0:T(1024)} %param.15) | copy-start | bytes 15364
  16.8 2.6 %copy-start.1 = (bf16[96,1280]{1,0:T(8,128)(2,1)S(1)}, bf16[96,1280]{1,0:T(8,128)(2,1)}, u32[]{:S(2)}) copy-start(bf16[96,1280]{1,0:T(8,128)(2,1)} %hidden_ref.1) | copy-start | bytes 737284
  17.0 6.3 %collective-permute-start.6 = (bf16[96,640]{1,0:T(8,128)(2,1)S(1)}, bf16[96,640]{1,0:T(8,128)(2,1)S(1)}, u32[]{:S(2)}, u32[]{:S(2)}) collective-permute-start(bf16[96,640]{1,0:T(8,128)(2,1)S(1)} %sent_term.3), channel_id=1, source_target_pairs={{0,2},{2,0},{1,3},{3,1},{4,6},{6,4},{5,7},{7,5},{8,10},{10,8},{9,1... | collective-permute-start | bytes 368648 | tf_op jit(solution)/shard_map/projection/ppermute | solution.py:44
  18.8 6.1 %collective-permute-start.5 = (bf16[96,640]{1,0:T(8,128)(2,1)S(1)}, bf16[96,640]{1,0:T(8,128)(2,1)S(1)}, u32[]{:S(2)}, u32[]{:S(2)}) collective-permute-start(bf16[96,640]{1,0:T(8,128)(2,1)S(1)} %sent_term.2), channel_id=1, source_target_pairs={{0,2},{2,0},{1,3},{3,1},{4,6},{6,4},{5,7},{7,5},{8,10},{10,8},{9,1... | collective-permute-start | bytes 368648 | tf_op jit(solution)/shard_map/projection/ppermute | solution.py:44

commit v7 on v5

--- a/solution.py
+++ b/solution.py
@@ -92,46 +92,80 @@
         out_ref[:, cols] = (sums / totals).astype(jnp.bfloat16)
 
 
-def block_dot(a_ref, weight_ref, block, columns):
-    if block is None:
+def block_dot(a_ref, weight_ref, start, columns):
+    if start is None:
         weight = weight_ref[...]
     else:
-        weight = weight_ref[:, pl.ds(pl.multiple_of(block * columns, LANES), columns)]
+        weight = weight_ref[:, pl.ds(pl.multiple_of(start, LANES), columns)]
     return jnp.dot(a_ref[...], weight, preferred_element_type=jnp.float32)
 
 
-def block_at(step, heads, subs):
-    return lax.rem(lax.axis_index("head") + step, heads) * subs + lax.axis_index("sub")
-
-
-def own_term_kernel(block_of, attended_ref, weight_ref, out_ref):
-    out_ref[...] = block_dot(attended_ref, weight_ref, block_of(), out_ref.shape[1])
-
-
-def sent_term_kernel(block_of, total_ref, *refs):
+def products(start, columns, refs):
+    total = 0.0
+    for attended_ref, weight_ref in zip(refs[::2], refs[1::2]):
+        total = total + block_dot(attended_ref, weight_ref, start, columns)
+    return total
+
+
+def sent_term_kernel(start, *refs):
     out_ref = refs[-1]
-    block, columns = block_of(), out_ref.shape[1]
-    total = total_ref[...]
-    for attended_ref, weight_ref in zip(refs[:-1:2], refs[1:-1:2]):
-        total = total + block_dot(attended_ref, weight_ref, block, columns)
+    total = products(start(), out_ref.shape[1], refs[:-1])
     out_ref[...] = total.astype(jnp.bfloat16)
 
 
-def base_kernel(block_of, hidden_ref, gate_ref, *refs):
+def base_kernel(start, hidden_ref, gate_ref, *refs):
     out_ref = refs[-1]
-    block, columns = block_of(), out_ref.shape[1]
-    total = 0.0
-    for attended_ref, weight_ref in zip(refs[:-1:2], refs[1:-1:2]):
-        total = total + block_dot(attended_ref, weight_ref, block, columns)
+    total = products(start(), out_ref.shape[1], refs[:-1])
     out_ref[...] = hidden_ref[...].astype(jnp.float32) + gate_ref[...] * total
 
 
-def final_kernel(base_ref, gate_ref, *refs):
+def final_kernel(early, base_ref, gate_ref, *refs):
     arrived_refs, out_ref = refs[:-1], refs[-1]
     total = 0.0
     for ref in arrived_refs:
         total = total + ref[...].astype(jnp.float32)
-    out_ref[...] = (base_ref[...] + gate_ref[...] * total).astype(jnp.bfloat16)
+    if early:
+        out_ref[:, :early] = base_ref[:, :early].astype(jnp.bfloat16)
+    out_ref[:, early:] = (base_ref[:, early:] + gate_ref[:, early:] * total).astype(jnp.bfloat16)
+
+
+def early_weight_kernel(subs, columns, early, weight_ref, after_ref, out_ref, sems):
+    chip = (1 - lax.axis_index("head")) * subs
+    copies = []
+    for sub in range(subs):
+        at = pl.multiple_of((chip + sub) * columns, LANES)
+        copies.append(
+            pltpu.make_async_copy(
+                weight_ref.at[:, pl.ds(at, early)],
+                out_ref.at[:, pl.ds(sub * early, early)],
+                sems.at[sub],
+            )
+        )
+    for copy in copies:
+        copy.start()
+    for copy in copies:
+        copy.wait()
+
+
+def pack_kernel(early, attended_ref, weight_ref, out_ref):
+    rows = attended_ref.shape[0]
+    other = pl.multiple_of((1 - lax.axis_index("sub")) * early, LANES)
+    out_ref[:rows, :] = attended_ref[...]
+    out_ref[rows:, :] = weight_ref[:, pl.ds(other, early)]
+
+
+def early_kernel(early, base_ref, gate_ref, attended_ref, weight_ref, packed_ref, out_ref):
+    rows = attended_ref.shape[0]
+    mine = pl.multiple_of(lax.axis_index("sub") * early, LANES)
+    total = jnp.dot(
+        attended_ref[...],
+        weight_ref[:, pl.ds(mine, early)],
+        preferred_element_type=jnp.float32,
+    ) + jnp.dot(
+        packed_ref[:rows, :], packed_ref[rows:, :], preferred_element_type=jnp.float32
+    )
+    out_ref[...] = base_ref[...]
+    out_ref[:, :early] = base_ref[:, :early] + gate_ref[:, :early] * total
 
 
 def solution(mesh):
@@ -158,11 +192,37 @@
                 shift(out_weight, "sub", subs, i) for i in range(1, subs)
             ]
 
-        def weight_and_block(i, step):
+        early = 2 * LANES if heads == 2 and columns % LANES == 0 and columns > 4 * LANES else 0
+        if early:
+            with jax.named_scope("early_weight"):
+                early_weight = call(
+                    functools.partial(early_weight_kernel, subs, columns, early),
+                    jax.ShapeDtypeStruct((width, subs * early), jnp.bfloat16),
+                    [ANYWHERE] * 2,
+                    ANYWHERE,
+                    "early_weight",
+                    moved=4 * width * subs * early,
+                    scratch_shapes=[pltpu.SemaphoreType.DMA((subs,))],
+                    vmem=60 * 1024 * 1024,
+                )(out_weight, residual)
+                early_weight = shift(early_weight, "head", heads, 1)
+
+        def weight_and_start(i, step, skip=0):
+            def start():
+                to = lax.rem(lax.axis_index("head") + step, heads) * subs + lax.axis_index("sub")
+                return to * columns + skip
+
             if columns % LANES == 0:
-                return weights[i], functools.partial(block_at, step, heads, subs)
-            at = block_at(step, heads, subs) * columns
-            return lax.dynamic_slice(weights[i], (0, at), (width, columns)), lambda: None
+                return weights[i], start
+            return lax.dynamic_slice(weights[i], (0, start()), (width, columns)), lambda: None
+
+        def pairs_and_start(step, skip=0):
+            pairs = [
+                x
+                for i in range(subs)
+                for x in (attended_parts[i], weight_and_start(i, step, skip)[0])
+            ]
+            return pairs, weight_and_start(0, step, skip)[1]
 
         tokens = rows * patches
         with jax.named_scope("attention"):
@@ -190,51 +250,55 @@
             attended_parts = [attended] + [
                 shift(attended, "sub", subs, i) for i in range(1, subs)
             ]
+            if early:
+                other_attended = shift(attended, "head", heads, 1)
 
         term = jax.ShapeDtypeStruct((rows, columns), jnp.float32)
-        sent = jax.ShapeDtypeStruct((rows, columns), jnp.bfloat16)
+        sent = jax.ShapeDtypeStruct((rows, columns - early), jnp.bfloat16)
         product_flops = 2 * rows * width * columns
         with jax.named_scope("projection"):
             arrived = []
             for step in range(1, heads):
-                weight, block_of = weight_and_block(0, step)
-                own = call(
-                    functools.partial(own_term_kernel, block_of),
-                    term,
-                    [IN_VMEM] * 2,
-                    IN_VMEM,
-                    "own_term",
-                    product_flops,
-                )(attended, weight)
-                pairs = [
-                    x
-                    for i in range(1, subs)
-                    for x in (attended_parts[i], weight_and_block(i, step)[0])
-                ]
+                pairs, start = pairs_and_start(step, early)
                 total = call(
-                    functools.partial(sent_term_kernel, block_of),
+                    functools.partial(sent_term_kernel, start),
                     sent,
-                    [IN_VMEM] * (1 + len(pairs)),
+                    [IN_VMEM] * len(pairs),
                     IN_VMEM,
                     "sent_term",
-                    product_flops,
-                )(own, *pairs)
+                    2 * product_flops,
+                )(*pairs)
                 arrived.append(shift(total, "head", heads, step))
             gate_row = gate.reshape(1, columns)
-            pairs = [
-                x for i in range(subs) for x in (attended_parts[i], weight_and_block(i, 0)[0])
-            ]
+            pairs, start = pairs_and_start(0)
             base = call(
-                functools.partial(base_kernel, weight_and_block(0, 0)[1]),
+                functools.partial(base_kernel, start),
                 term,
                 [IN_VMEM] * (2 + len(pairs)),
                 IN_VMEM,
                 "base",
                 2 * product_flops,
             )(hidden_in, gate_row, *pairs)
+            if early:
+                packed = call(
+                    functools.partial(pack_kernel, early),
+                    jax.ShapeDtypeStruct((rows + width, early), jnp.bfloat16),
+                    [IN_VMEM] * 2,
+                    IN_VMEM,
+                    "pack",
+                )(other_attended, early_weight)
+                packed = shift(packed, "sub", subs, 1)
+                base = call(
+                    functools.partial(early_kernel, early),
+                    term,
+                    [IN_VMEM] * 5,
+                    IN_VMEM,
+                    "early",
+                    product_flops // 2,
+                )(base, gate_row, other_attended, early_weight, packed)
             return call(
-                final_kernel,
-                sent,
+                functools.partial(final_kernel, early),
+                jax.ShapeDtypeStruct((rows, columns), jnp.bfloat16),
                 [IN_VMEM] * (2 + len(arrived)),
                 IN_VMEM,
                 "final",

time: 25 us -> 31.5 us (1.26)
  Pallas kernels: 2.37 us -> 11.4 us
  local copies, waits for them, and re-layouts: 3.77 us -> 0.05 us
  starting transfers between devices: 8.64 us -> 10.5 us
  waiting for transfers between devices: 8.95 us -> 8.22 us
    pallas_call x4 -> x6, Pallas kernels: 1.62 us -> 10.7 us  [the longest x1 9.06 us: per_device(): call(functools.partial(early_weight_kernel, subs, columns, early), jax.Sh...]
    unnamed x12 -> x16, local copies, waits for them, and re-layouts: 3.77 us -> 0.04 us
    ppermute x6 -> x9, starting transfers between devices: 8.64 us -> 10.5 us  [shift(): lax.ppermute(array, axis, [(i, (i + step) % size) for i in range(size)])]
    ppermute x6 -> x9, waiting for transfers between devices: 8.95 us -> 8.22 us  [shift(): lax.ppermute(array, axis, [(i, (i + step) % size) for i in range(size)])]
  transfers between devices with their start and end apart: 6 -> 9, of which waited for: 2 -> 4; matrix products, arithmetic and copies ran while one was open for 4% -> 3% of each run, Pallas kernels for 5% -> 34%
where the time goes in v7:
time: 31.5 us; the launch traced here: 31.3 us
  Pallas kernels  11.4 us (36%)
  starting transfers between devices  10.5 us (33%)
  waiting for transfers between devices  8.22 us (26%)
  other arithmetic  0.95 us (3%)
    ppermute x9, starting transfers between devices, shift(): lax.ppermute(array, axis, [(i, (i + step) % size) for i in range(size)])  10.5 us
    pallas_call x1, Pallas kernels, per_device(): call(functools.partial(early_weight_kernel, subs, columns, early), jax.Sh...  9.06 us
    ppermute x9, waiting for transfers between devices, shift(): lax.ppermute(array, axis, [(i, (i + step) % size) for i in range(size)])  8.22 us
    convert_element_type x1, other arithmetic, per_device(): residual = jnp.maximum(lax.pad(key_change, low, ((0, 0, 0), (0, width, 0)...  0.95 us
    pallas_call x1, Pallas kernels, per_device(): call(functools.partial(final_kernel, early), jax.ShapeDtypeStruct((rows,...  0.75 us
  transfers between devices with their start and end apart: 9, of which 4 were waited for; matrix products, arithmetic and copies ran while one was open for 3% of the time, Pallas kernels for 34%

profile of v7, /device:TPU:0, one launch (start us, length us, event | category | flops | bytes accessed | tf_op | source)
XLA Modules:
  0.0 31.3 jit_solution(5911163669829069756)
XLA Ops:
  0.0 0.0 copy-start.6
  0.0 0.0 copy-start.5
  0.0 0.0 copy-start.4
  0.0 0.5 %collective-permute-start.4 = (bf16[256,5120]{1,0:T(8,128)(2,1)}, bf16[256,5120]{1,0:T(8,128)(2,1)S(1)}, u32[]{:S(2)}, u32[]{:S(2)}) collective-permute-start(bf16[256,5120]{1,0:T(8,128)(2,1)} %refs_1_.3), channel_id=1, source_target_pairs={{0,1},{1,0},{2,3},{3,2},{4,5},{5,4},{6,7},{7,6},{8,9},{9,8},{10,11... | collective-permute-start | bytes 7864328 | tf_op jit(solution)/shard_map/weight_swap/ppermute | solution.py:43
  0.5 1.0 %maximum_convert_fusion.refs_0_.after_ref = bf16[96,512]{1,0:T(8,128)(2,1)S(1)} fusion(f32[96,256]{1,0:T(8,128)} %param.12, f32[96,256]{1,0:T(8,128)} %param.11), kind=kLoop, calls=%fused_computation | loop fusion | flops 196608 | bytes 294912 | tf_op jit(solution)/shard_map/residual_gather/convert_element_type | solution.py:185
  1.5 0.0 copy-start.1
  1.5 2.8 %collective-permute-start.2 = (bf16[96,512]{1,0:T(8,128)(2,1)S(1)}, bf16[96,512]{1,0:T(8,128)(2,1)S(1)}, u32[]{:S(2)}, u32[]{:S(2)}) collective-permute-start(bf16[96,512]{1,0:T(8,128)(2,1)S(1)} %maximum_convert_fusion.refs_0_.after_ref), channel_id=1, source_target_pairs={{0,4},{4,8},{8,12},{12,0},{1,5},{5,9},{9,13},{13,1},{2,6},{6,10},{... | collective-permute-start | bytes 294920 | tf_op jit(solution)/shard_map/residual_gather/ppermute | solution.py:43
  4.3 2.6 %collective-permute-start.1 = (bf16[96,512]{1,0:T(8,128)(2,1)S(1)}, bf16[96,512]{1,0:T(8,128)(2,1)S(1)}, u32[]{:S(2)}, u32[]{:S(2)}) collective-permute-start(bf16[96,512]{1,0:T(8,128)(2,1)S(1)} %maximum_convert_fusion.refs_0_.after_ref), channel_id=1, source_target_pairs={{0,8},{4,12},{8,0},{12,4},{1,9},{5,13},{9,1},{13,5},{2,10},{6,14},... | collective-permute-start | bytes 294920 | tf_op jit(solution)/shard_map/residual_gather/ppermute | solution.py:43
  6.9 1.3 %collective-permute-start = (bf16[96,512]{1,0:T(8,128)(2,1)S(1)}, bf16[96,512]{1,0:T(8,128)(2,1)S(1)}, u32[]{:S(2)}, u32[]{:S(2)}) collective-permute-start(bf16[96,512]{1,0:T(8,128)(2,1)S(1)} %maximum_convert_fusion.refs_0_.after_ref), channel_id=1, source_target_pairs={{0,12},{4,0},{8,4},{12,8},{1,13},{5,1},{9,5},{13,9},{2,14},{6,2},{... | collective-permute-start | bytes 294920 | tf_op jit(solution)/shard_map/residual_gather/ppermute | solution.py:43
  8.2 0.0 copy-done.1
  8.2 9.1 %early_weight.1 = bf16[256,512]{1,0:T(8,128)(2,1)} custom-call(bf16[256,5120]{1,0:T(8,128)(2,1)} %refs_1_.3, bf16[96,512]{1,0:T(8,128)(2,1)} %copy-done.1), custom_call_target="tpu_custom_call" | custom-call | bytes 524288 | tf_op jit(solution)/shard_map/early_weight/early_weight/pallas_call | solution.py:198
  17.3 0.0 copy-start.2
  17.3 1.6 %collective-permute-start.6 = (bf16[256,512]{1,0:T(8,128)(2,1)}, bf16[256,512]{1,0:T(8,128)(2,1)S(1)}, u32[]{:S(2)}, u32[]{:S(2)}) collective-permute-start(bf16[256,512]{1,0:T(8,128)(2,1)} %early_weight.1), channel_id=1, source_target_pairs={{0,2},{2,0},{1,3},{3,1},{4,6},{6,4},{5,7},{7,5},{8,10},{10,8},{9,1... | collective-permute-start | bytes 786440 | tf_op jit(solution)/shard_map/early_weight/ppermute | solution.py:43
  18.8 0.0 copy-done.6
  18.8 0.0 copy-done.5
  18.9 0.0 copy-done.4
  18.9 0.2 stage.1
  19.1 0.0 collective-permute-done.2.refs_3_
  19.1 0.0 collective-permute-done.1.refs_2_
  19.1 0.0 collective-permute-done.refs_1_
  19.1 0.0 copy-done.2
  19.1 0.0 copy-start
  19.1 0.5 %attention.1.refs_0_ = bf16[96,256]{1,0:T(8,128)(2,1)S(1)} custom-call(bf16[96,256]{1,0:T(8,128)(2,1)S(1)} %copy-done.6, f32[2,96,384]{2,1,0:T(8,128)S(1)} %get-tuple-element.7.products_ref, bf16[384,256]{1,0:T(8,128)(2,1)S(1)} %get-tuple-element.8.values_ref, bf16[96,512]{1,0:T(8,128)(2,1)S(1)} %copy-done.2, ...), custom_call_target="tpu_custom_call" | custom-call | flops 2000000000 | tf_op jit(solution)/shard_map/attention/attention/pallas_call | solution.py:240
  19.7 0.0 copy-start.7
  19.7 0.0 copy-start.3
  19.7 0.1 collective-permute-start.3
  19.8 0.6 %collective-permute-start.5 = (bf16[96,256]{1,0:T(8,128)(2,1)S(1)}, bf16[96,256]{1,0:T(8,128)(2,1)S(1)}, u32[]{:S(2)}, u32[]{:S(2)}) collective-permute-start(bf16[96,256]{1,0:T(8,128)(2,1)S(1)} %attention.1.refs_0_), channel_id=1, source_target_pairs={{0,2},{2,0},{1,3},{3,1},{4,6},{6,4},{5,7},{7,5},{8,10},{10,8},{9,1... | collective-permute-start | bytes 147464 | tf_op jit(solution)/shard_map/attended_swap/ppermute | solution.py:43
  20.4 0.6 %collective-permute-done.3.refs_2_ = bf16[96,256]{1,0:T(8,128)(2,1)S(1)} collective-permute-done((bf16[96,256]{1,0:T(8,128)(2,1)S(1)}, bf16[96,256]{1,0:T(8,128)(2,1)S(1)}, u32[]{:S(2)}, u32[]{:S(2)}) %collective-permute-start.3) | collective-permute-done | bytes 49184 | tf_op jit(solution)/shard_map/attended_swap/ppermute | solution.py:43
  21.0 0.0 collective-permute-done.4.refs_3_
  21.0 0.0 copy-done
  21.0 0.3 sent_term.1
  21.3 1.0 %collective-permute-start.8 = (bf16[96,1024]{1,0:T(8,128)(2,1)S(1)}, bf16[96,1024]{1,0:T(8,128)(2,1)S(1)}, u32[]{:S(2)}, u32[]{:S(2)}) collective-permute-start(bf16[96,1024]{1,0:T(8,128)(2,1)S(1)} %sent_term.1), channel_id=1, source_target_pairs={{0,2},{2,0},{1,3},{3,1},{4,6},{6,4},{5,7},{7,5},{8,10},{10,8},{9,1... | collective-permute-start | bytes 589832 | tf_op jit(solution)/shard_map/projection/ppermute | solution.py:43
  22.3 5.6 %collective-permute-done.5.attended_ref = bf16[96,256]{1,0:T(8,128)(2,1)S(1)} collective-permute-done((bf16[96,256]{1,0:T(8,128)(2,1)S(1)}, bf16[96,256]{1,0:T(8,128)(2,1)S(1)}, u32[]{:S(2)}, u32[]{:S(2)}) %collective-permute-start.5) | collective-permute-done | bytes 49184 | tf_op jit(solution)/shard_map/attended_swap/ppermute | solution.py:43
  27.9 0.0 collective-permute-done.6.weight_ref
  27.9 0.1 collective-permute-start.7
  28.0 0.0 copy-done.7
  28.0 0.0 copy-done.3
  28.0 0.4 %base.1.base_ref = f32[96,1280]{1,0:T(8,128)S(1)} custom-call(bf16[96,1280]{1,0:T(8,128)(2,1)S(1)} %copy-done.3, f32[1,1280]{1,0:T(1,128)S(1)} %reshape.3.gate_ref, bf16[96,256]{1,0:T(8,128)(2,1)S(1)} %attention.1.refs_0_, bf16[256,5120]{1,0:T(8,128)(2,1)S(1)} %copy-done, bf16[96,256]{1,0:T(8,128)(2,1)S(1)} %collective-permute-done.3.refs_2_, ...), custom_call_target="tpu_custom_call" | custom-call | flops 125829120 | tf_op jit(solution)/shard_map/projection/base/pallas_call | solution.py:274
  28.4 1.0 %collective-permute-done.7.packed_ref = bf16[352,256]{1,0:T(8,128)(2,1)S(1)} collective-permute-done((bf16[352,256]{1,0:T(8,128)(2,1)S(1)}, bf16[352,256]{1,0:T(8,128)(2,1)S(1)}, u32[]{:S(2)}, u32[]{:S(2)}) %collective-permute-start.7) | collective-permute-done | bytes 180256 | tf_op jit(solution)/shard_map/projection/ppermute | solution.py:43
  29.4 0.2 early.1.base_ref
  29.6 1.0 %collective-permute-done.8.refs_0_ = bf16[96,1024]{1,0:T(8,128)(2,1)S(1)} collective-permute-done((bf16[96,1024]{1,0:T(8,128)(2,1)S(1)}, bf16[96,1024]{1,0:T(8,128)(2,1)S(1)}, u32[]{:S(2)}, u32[]{:S(2)}) %collective-permute-start.8) | collective-permute-done | bytes 196640 | tf_op jit(solution)/shard_map/projection/ppermute | solution.py:43
  30.6 0.7 %final.1 = bf16[96,1280]{1,0:T(8,128)(2,1)} custom-call(f32[96,1280]{1,0:T(8,128)S(1)} %early.1.base_ref, f32[1,1280]{1,0:T(1,128)S(1)} %reshape.3.gate_ref, bf16[96,1024]{1,0:T(8,128)(2,1)S(1)} %collective-permute-done.8.refs_0_), custom_call_target="tpu_custom_call" | custom-call | bytes 983040 | tf_op jit(solution)/shard_map/projection/final/pallas_call | solution.py:299
  (2 shorter events, 0.0 us)
Async XLA Ops:
  0.0 18.8 %copy-start.6 = (bf16[96,256]{1,0:T(8,128)(2,1)S(1)}, bf16[96,256]{1,0:T(8,128)(2,1)}, u32[]{:S(2)}) copy-start(bf16[96,256]{1,0:T(8,128)(2,1)} %q_ref.3) | copy-start | bytes 147460
  0.0 18.8 %copy-start.5 = (bf16[384,256]{1,0:T(8,128)(2,1)S(1)}, bf16[384,256]{1,0:T(8,128)(2,1)}, u32[]{:S(2)}) copy-start(bf16[384,256]{1,0:T(8,128)(2,1)} %held_v_ref.1) | copy-start | bytes 589828
  0.0 18.8 %copy-start.4 = (bf16[384,256]{1,0:T(8,128)(2,1)S(1)}, bf16[384,256]{1,0:T(8,128)(2,1)}, u32[]{:S(2)}) copy-start(bf16[384,256]{1,0:T(8,128)(2,1)} %held_k_ref.1) | copy-start | bytes 589828
  0.0 21.0 %collective-permute-start.4 = (bf16[256,5120]{1,0:T(8,128)(2,1)}, bf16[256,5120]{1,0:T(8,128)(2,1)S(1)}, u32[]{:S(2)}, u32[]{:S(2)}) collective-permute-start(bf16[256,5120]{1,0:T(8,128)(2,1)} %refs_1_.3), channel_id=1, source_target_pairs={{0,1},{1,0},{2,3},{3,2},{4,5},{5,4},{6,7},{7,6},{8,9},{9,8},{10,11... | collective-permute-start | bytes 7864328 | tf_op jit(solution)/shard_map/weight_swap/ppermute | solution.py:43
  1.5 6.7 %copy-start.1 = (bf16[96,512]{1,0:T(8,128)(2,1)}, bf16[96,512]{1,0:T(8,128)(2,1)S(1)}, u32[]{:S(2)}) copy-start(bf16[96,512]{1,0:T(8,128)(2,1)S(1)} %maximum_convert_fusion.refs_0_.after_ref) | copy-start | bytes 294916
  1.5 17.6 %collective-permute-start.2 = (bf16[96,512]{1,0:T(8,128)(2,1)S(1)}, bf16[96,512]{1,0:T(8,128)(2,1)S(1)}, u32[]{:S(2)}, u32[]{:S(2)}) collective-permute-start(bf16[96,512]{1,0:T(8,128)(2,1)S(1)} %maximum_convert_fusion.refs_0_.after_ref), channel_id=1, source_target_pairs={{0,4},{4,8},{8,12},{12,0},{1,5},{5,9},{9,13},{13,1},{2,6},{6,10},{... | collective-permute-start | bytes 294920 | tf_op jit(solution)/shard_map/residual_gather/ppermute | solution.py:43
  4.3 14.8 %collective-permute-start.1 = (bf16[96,512]{1,0:T(8,128)(2,1)S(1)}, bf16[96,512]{1,0:T(8,128)(2,1)S(1)}, u32[]{:S(2)}, u32[]{:S(2)}) collective-permute-start(bf16[96,512]{1,0:T(8,128)(2,1)S(1)} %maximum_convert_fusion.refs_0_.after_ref), channel_id=1, source_target_pairs={{0,8},{4,12},{8,0},{12,4},{1,9},{5,13},{9,1},{13,5},{2,10},{6,14},... | collective-permute-start | bytes 294920 | tf_op jit(solution)/shard_map/residual_gather/ppermute | solution.py:43
  6.9 12.2 %collective-permute-start = (bf16[96,512]{1,0:T(8,128)(2,1)S(1)}, bf16[96,512]{1,0:T(8,128)(2,1)S(1)}, u32[]{:S(2)}, u32[]{:S(2)}) collective-permute-start(bf16[96,512]{1,0:T(8,128)(2,1)S(1)} %maximum_convert_fusion.refs_0_.after_ref), channel_id=1, source_target_pairs={{0,12},{4,0},{8,4},{12,8},{1,13},{5,1},{9,5},{13,9},{2,14},{6,2},{... | collective-permute-start | bytes 294920 | tf_op jit(solution)/shard_map/residual_gather/ppermute | solution.py:43
  17.3 1.8 %copy-start.2 = (bf16[96,512]{1,0:T(8,128)(2,1)S(1)}, bf16[96,512]{1,0:T(8,128)(2,1)}, u32[]{:S(2)}) copy-start(bf16[96,512]{1,0:T(8,128)(2,1)} %copy-done.1) | copy-start | bytes 294916
  17.3 10.6 %collective-permute-start.6 = (bf16[256,512]{1,0:T(8,128)(2,1)}, bf16[256,512]{1,0:T(8,128)(2,1)S(1)}, u32[]{:S(2)}, u32[]{:S(2)}) collective-permute-start(bf16[256,512]{1,0:T(8,128)(2,1)} %early_weight.1), channel_id=1, source_target_pairs={{0,2},{2,0},{1,3},{3,1},{4,6},{6,4},{5,7},{7,5},{8,10},{10,8},{9,1... | collective-permute-start | bytes 786440 | tf_op jit(solution)/shard_map/early_weight/ppermute | solution.py:43
  19.1 1.9 %copy-start = (bf16[256,5120]{1,0:T(8,128)(2,1)S(1)}, bf16[256,5120]{1,0:T(8,128)(2,1)}, u32[]{:S(2)}) copy-start(bf16[256,5120]{1,0:T(8,128)(2,1)} %refs_1_.3) | copy-start | bytes 7864324
  19.7 8.3 %copy-start.7 = (f32[1280]{0:T(1024)S(1)}, f32[1280]{0:T(1024)}, u32[]{:S(2)}) copy-start(f32[1280]{0:T(1024)} %param.15) | copy-start | bytes 15364
  19.7 8.3 %copy-start.3 = (bf16[96,1280]{1,0:T(8,128)(2,1)S(1)}, bf16[96,1280]{1,0:T(8,128)(2,1)}, u32[]{:S(2)}) copy-start(bf16[96,1280]{1,0:T(8,128)(2,1)} %hidden_ref.1) | copy-start | bytes 737284
  19.7 1.3 %collective-permute-start.3 = (bf16[96,256]{1,0:T(8,128)(2,1)S(1)}, bf16[96,256]{1,0:T(8,128)(2,1)S(1)}, u32[]{:S(2)}, u32[]{:S(2)}) collective-permute-start(bf16[96,256]{1,0:T(8,128)(2,1)S(1)} %attention.1.refs_0_), channel_id=1, source_target_pairs={{0,1},{1,0},{2,3},{3,2},{4,5},{5,4},{6,7},{7,6},{8,9},{9,8},{10,11... | collective-permute-start | bytes 147464 | tf_op jit(solution)/shard_map/attended_swap/ppermute | solution.py:43
  19.8 8.1 %collective-permute-start.5 = (bf16[96,256]{1,0:T(8,128)(2,1)S(1)}, bf16[96,256]{1,0:T(8,128)(2,1)S(1)}, u32[]{:S(2)}, u32[]{:S(2)}) collective-permute-start(bf16[96,256]{1,0:T(8,128)(2,1)S(1)} %attention.1.refs_0_), channel_id=1, source_target_pairs={{0,2},{2,0},{1,3},{3,1},{4,6},{6,4},{5,7},{7,5},{8,10},{10,8},{9,1... | collective-permute-start | bytes 147464 | tf_op jit(solution)/shard_map/attended_swap/ppermute | solution.py:43
  21.3 9.3 %collective-permute-start.8 = (bf16[96,1024]{1,0:T(8,128)(2,1)S(1)}, bf16[96,1024]{1,0:T(8,128)(2,1)S(1)}, u32[]{:S(2)}, u32[]{:S(2)}) collective-permute-start(bf16[96,1024]{1,0:T(8,128)(2,1)S(1)} %sent_term.1), channel_id=1, source_target_pairs={{0,2},{2,0},{1,3},{3,1},{4,6},{6,4},{5,7},{7,5},{8,10},{10,8},{9,1... | collective-permute-start | bytes 589832 | tf_op jit(solution)/shard_map/projection/ppermute | solution.py:43
  27.9 1.5 %collective-permute-start.7 = (bf16[352,256]{1,0:T(8,128)(2,1)S(1)}, bf16[352,256]{1,0:T(8,128)(2,1)S(1)}, u32[]{:S(2)}, u32[]{:S(2)}) collective-permute-start(bf16[352,256]{1,0:T(8,128)(2,1)S(1)} %pack.1), channel_id=1, source_target_pairs={{0,1},{1,0},{2,3},{3,2},{4,5},{5,4},{6,7},{7,6},{8,9},{9,8},{10,11... | collective-permute-start | bytes 540680 | tf_op jit(solution)/shard_map/projection/ppermute | solution.py:43

commit v8 on v7

--- a/solution.py
+++ b/solution.py
@@ -148,21 +148,27 @@
 
 
 def pack_kernel(early, attended_ref, weight_ref, out_ref):
-    rows = attended_ref.shape[0]
+    rows, width = attended_ref.shape
+    for i in range(width // early):
+        out_ref[i * rows : (i + 1) * rows, :] = attended_ref[:, i * early : (i + 1) * early]
     other = pl.multiple_of((1 - lax.axis_index("sub")) * early, LANES)
-    out_ref[:rows, :] = attended_ref[...]
-    out_ref[rows:, :] = weight_ref[:, pl.ds(other, early)]
+    out_ref[rows * (width // early) :, :] = weight_ref[:, pl.ds(other, early)]
 
 
 def early_kernel(early, base_ref, gate_ref, attended_ref, weight_ref, packed_ref, out_ref):
-    rows = attended_ref.shape[0]
+    rows, width = attended_ref.shape
+    pieces = width // early
     mine = pl.multiple_of(lax.axis_index("sub") * early, LANES)
     total = jnp.dot(
         attended_ref[...],
         weight_ref[:, pl.ds(mine, early)],
         preferred_element_type=jnp.float32,
     ) + jnp.dot(
-        packed_ref[:rows, :], packed_ref[rows:, :], preferred_element_type=jnp.float32
+        jnp.concatenate(
+            [packed_ref[i * rows : (i + 1) * rows, :] for i in range(pieces)], axis=1
+        ),
+        packed_ref[pieces * rows :, :],
+        preferred_element_type=jnp.float32,
     )
     out_ref[...] = base_ref[...]
     out_ref[:, :early] = base_ref[:, :early] + gate_ref[:, :early] * total
@@ -192,14 +198,14 @@
                 shift(out_weight, "sub", subs, i) for i in range(1, subs)
             ]
 
-        early = 2 * LANES if heads == 2 and columns % LANES == 0 and columns > 4 * LANES else 0
+        early = LANES if heads == 2 and columns % LANES == 0 and columns > 4 * LANES else 0
         if early:
             with jax.named_scope("early_weight"):
                 early_weight = call(
                     functools.partial(early_weight_kernel, subs, columns, early),
                     jax.ShapeDtypeStruct((width, subs * early), jnp.bfloat16),
                     [ANYWHERE] * 2,
-                    ANYWHERE,
+                    IN_VMEM,
                     "early_weight",
                     moved=4 * width * subs * early,
                     scratch_shapes=[pltpu.SemaphoreType.DMA((subs,))],
@@ -282,7 +288,7 @@
             if early:
                 packed = call(
                     functools.partial(pack_kernel, early),
-                    jax.ShapeDtypeStruct((rows + width, early), jnp.bfloat16),
+                    jax.ShapeDtypeStruct((rows * (width // early) + width, early), jnp.bfloat16),
                     [IN_VMEM] * 2,
                     IN_VMEM,
                     "pack",

time: 31.5 us -> 32.4 us (1.029); the launches traced: 31.3 us -> 31.7 us
  Pallas kernels: 11.4 us -> 7.58 us
  local copies, waits for them, and re-layouts: 0.05 us -> 2.68 us
  waiting for transfers between devices: 8.22 us -> 9.56 us
    pallas_call x1, Pallas kernels: 9.06 us -> 1.71 us  [per_device(): call(functools.partial(early_weight_kernel, subs, columns, early), jax.Sh...]
    unnamed x16 -> x14, local copies, waits for them, and re-layouts: 0.04 us -> 2.67 us
    pallas_call x1, Pallas kernels: 0.31 us -> 2.08 us  [per_device(): call(functools.partial(sent_term_kernel, start), sent, [IN_VMEM] * len(pa...]
    pallas_call x1, Pallas kernels: 0.36 us -> 2.09 us  [per_device(): call(functools.partial(base_kernel, start), term, [IN_VMEM] * (2 + len(pa...]
    ppermute x9, waiting for transfers between devices: 8.22 us -> 9.56 us  [shift(): lax.ppermute(array, axis, [(i, (i + step) % size) for i in range(size)])]
  transfers between devices with their start and end apart: 9 -> 9, of which waited for: 4 -> 3; matrix products, arithmetic and copies ran while one was open for 3% -> 3% of each run, Pallas kernels for 34% -> 22%
where the time goes in v8:
time: 32.4 us; the launch traced here: 31.7 us
  starting transfers between devices  10.8 us (33%)
  waiting for transfers between devices  9.56 us (30%)
  Pallas kernels  7.58 us (23%)
  local copies, waits for them, and re-layouts  2.68 us (8%)
  other arithmetic  0.95 us (3%)
    ppermute x9, starting transfers between devices, shift(): lax.ppermute(array, axis, [(i, (i + step) % size) for i in range(size)])  10.8 us
    ppermute x9, waiting for transfers between devices, shift(): lax.ppermute(array, axis, [(i, (i + step) % size) for i in range(size)])  9.56 us
    unnamed x14, local copies, waits for them, and re-layouts  2.67 us
    pallas_call x1, Pallas kernels, per_device(): call(functools.partial(base_kernel, start), term, [IN_VMEM] * (2 + len(pa...  2.09 us
    pallas_call x1, Pallas kernels, per_device(): call(functools.partial(sent_term_kernel, start), sent, [IN_VMEM] * len(pa...  2.08 us
    pallas_call x1, Pallas kernels, per_device(): call(functools.partial(early_weight_kernel, subs, columns, early), jax.Sh...  1.71 us
    convert_element_type x1, other arithmetic, per_device(): residual = jnp.maximum(lax.pad(key_change, low, ((0, 0, 0), (0, width, 0)...  0.95 us
    pallas_call x1, Pallas kernels, per_device(): call(functools.partial(final_kernel, early), jax.ShapeDtypeStruct((rows,...  0.77 us
  transfers between devices with their start and end apart: 9, of which 3 were waited for; matrix products, arithmetic and copies ran while one was open for 3% of the time, Pallas kernels for 22%

profile of v8, /device:TPU:0, one launch (start us, length us, event | category | flops | bytes accessed | tf_op | source)
XLA Modules:
  0.0 31.7 jit_solution(4672071891728702312)
XLA Ops:
  0.0 0.5 %collective-permute-start.4 = (bf16[256,5120]{1,0:T(8,128)(2,1)}, bf16[256,5120]{1,0:T(8,128)(2,1)}, u32[]{:S(2)}, u32[]{:S(2)}) collective-permute-start(bf16[256,5120]{1,0:T(8,128)(2,1)} %refs_1_.3), channel_id=1, source_target_pairs={{0,1},{1,0},{2,3},{3,2},{4,5},{5,4},{6,7},{7,6},{8,9},{9,8},{10,11... | collective-permute-start | bytes 7864328 | tf_op jit(solution)/shard_map/weight_swap/ppermute | solution.py:43
  0.5 1.0 %maximum_convert_fusion.refs_0_.after_ref = bf16[96,512]{1,0:T(8,128)(2,1)S(1)} fusion(f32[96,256]{1,0:T(8,128)} %param.12, f32[96,256]{1,0:T(8,128)} %param.11), kind=kLoop, calls=%fused_computation | loop fusion | flops 196608 | bytes 294912 | tf_op jit(solution)/shard_map/residual_gather/convert_element_type | solution.py:191
  1.4 0.0 copy-start.1
  1.4 2.6 %collective-permute-start.2 = (bf16[96,512]{1,0:T(8,128)(2,1)S(1)}, bf16[96,512]{1,0:T(8,128)(2,1)S(1)}, u32[]{:S(2)}, u32[]{:S(2)}) collective-permute-start(bf16[96,512]{1,0:T(8,128)(2,1)S(1)} %maximum_convert_fusion.refs_0_.after_ref), channel_id=1, source_target_pairs={{0,4},{4,8},{8,12},{12,0},{1,5},{5,9},{9,13},{13,1},{2,6},{6,10},{... | collective-permute-start | bytes 294920 | tf_op jit(solution)/shard_map/residual_gather/ppermute | solution.py:43
  4.0 2.6 %collective-permute-start.1 = (bf16[96,512]{1,0:T(8,128)(2,1)S(1)}, bf16[96,512]{1,0:T(8,128)(2,1)S(1)}, u32[]{:S(2)}, u32[]{:S(2)}) collective-permute-start(bf16[96,512]{1,0:T(8,128)(2,1)S(1)} %maximum_convert_fusion.refs_0_.after_ref), channel_id=1, source_target_pairs={{0,8},{4,12},{8,0},{12,4},{1,9},{5,13},{9,1},{13,5},{2,10},{6,14},... | collective-permute-start | bytes 294920 | tf_op jit(solution)/shard_map/residual_gather/ppermute | solution.py:43
  6.6 1.3 %collective-permute-start = (bf16[96,512]{1,0:T(8,128)(2,1)S(1)}, bf16[96,512]{1,0:T(8,128)(2,1)S(1)}, u32[]{:S(2)}, u32[]{:S(2)}) collective-permute-start(bf16[96,512]{1,0:T(8,128)(2,1)S(1)} %maximum_convert_fusion.refs_0_.after_ref), channel_id=1, source_target_pairs={{0,12},{4,0},{8,4},{12,8},{1,13},{5,1},{9,5},{13,9},{2,14},{6,2},{... | collective-permute-start | bytes 294920 | tf_op jit(solution)/shard_map/residual_gather/ppermute | solution.py:43
  8.0 0.0 copy-start.3
  8.0 0.9 %copy-done.3 = bf16[384,256]{1,0:T(8,128)(2,1)S(1)} copy-done((bf16[384,256]{1,0:T(8,128)(2,1)S(1)}, bf16[384,256]{1,0:T(8,128)(2,1)}, u32[]{:S(2)}) %copy-start.3) | copy-done | bytes 196632
  8.9 0.0 copy-start.4
  8.9 0.9 %copy-done.4 = bf16[384,256]{1,0:T(8,128)(2,1)S(1)} copy-done((bf16[384,256]{1,0:T(8,128)(2,1)S(1)}, bf16[384,256]{1,0:T(8,128)(2,1)}, u32[]{:S(2)}) %copy-start.4) | copy-done | bytes 196632
  9.8 0.0 copy-start.5
  9.8 0.8 %copy-done.5 = bf16[96,256]{1,0:T(8,128)(2,1)S(1)} copy-done((bf16[96,256]{1,0:T(8,128)(2,1)S(1)}, bf16[96,256]{1,0:T(8,128)(2,1)}, u32[]{:S(2)}) %copy-start.5) | copy-done | bytes 49176
  10.6 0.2 stage.1
  10.9 0.0 collective-permute-done.2.refs_3_
  10.9 2.9 %collective-permute-done.1.refs_2_ = bf16[96,512]{1,0:T(8,128)(2,1)S(1)} collective-permute-done((bf16[96,512]{1,0:T(8,128)(2,1)S(1)}, bf16[96,512]{1,0:T(8,128)(2,1)S(1)}, u32[]{:S(2)}, u32[]{:S(2)}) %collective-permute-start.1) | collective-permute-done | bytes 98336 | tf_op jit(solution)/shard_map/residual_gather/ppermute | solution.py:43
  13.8 0.0 collective-permute-done.refs_1_
  13.8 0.0 copy-done.1
  13.8 0.5 %attention.1.refs_0_ = bf16[96,256]{1,0:T(8,128)(2,1)S(1)} custom-call(bf16[96,256]{1,0:T(8,128)(2,1)S(1)} %copy-done.5, f32[2,96,384]{2,1,0:T(8,128)S(1)} %get-tuple-element.7.products_ref, bf16[384,256]{1,0:T(8,128)(2,1)S(1)} %get-tuple-element.8.values_ref, bf16[96,512]{1,0:T(8,128)(2,1)S(1)} %maximum_convert_fusion.refs_0_.after_ref, ...), custom_call_target="tpu_custom_call" | custom-call | flops 2000000000 | tf_op jit(solution)/shard_map/attention/attention/pallas_call | solution.py:246
  14.4 0.0 copy-start
  14.4 0.1 collective-permute-start.3
  14.4 1.7 %early_weight.1 = bf16[256,256]{1,0:T(8,128)(2,1)} custom-call(bf16[256,5120]{1,0:T(8,128)(2,1)} %refs_1_.3, bf16[96,512]{1,0:T(8,128)(2,1)} %copy-done.1), custom_call_target="tpu_custom_call" | custom-call | bytes 262144 | tf_op jit(solution)/shard_map/early_weight/early_weight/pallas_call | solution.py:204
  16.2 0.0 copy-start.6
  16.2 0.0 copy-start.2
  16.2 1.6 %collective-permute-start.6 = (bf16[256,256]{1,0:T(8,128)(2,1)}, bf16[256,256]{1,0:T(8,128)(2,1)S(1)}, u32[]{:S(2)}, u32[]{:S(2)}) collective-permute-start(bf16[256,256]{1,0:T(8,128)(2,1)} %early_weight.1), channel_id=1, source_target_pairs={{0,2},{2,0},{1,3},{3,1},{4,6},{6,4},{5,7},{7,5},{8,10},{10,8},{9,1... | collective-permute-start | bytes 393224 | tf_op jit(solution)/shard_map/early_weight/ppermute | solution.py:43
  17.7 0.0 collective-permute-done.3.refs_2_
  17.7 0.0 collective-permute-done.4.refs_3_
  17.8 0.0 copy-done
  17.8 2.1 %sent_term.1 = bf16[96,1152]{1,0:T(8,128)(2,1)S(1)} custom-call(bf16[96,256]{1,0:T(8,128)(2,1)S(1)} %attention.1.refs_0_, bf16[256,5120]{1,0:T(8,128)(2,1)S(1)} %copy-done, bf16[96,256]{1,0:T(8,128)(2,1)S(1)} %collective-permute-done.3.refs_2_, bf16[256,5120]{1,0:T(8,128)(2,1)} %collective-permute-done.4.refs_3_), custom_call_target="tpu_custom_call" | custom-call | flops 125829120 | tf_op jit(solution)/shard_map/projection/sent_term/pallas_call | solution.py:269
  19.8 0.6 %collective-permute-start.8 = (bf16[96,1152]{1,0:T(8,128)(2,1)S(1)}, bf16[96,1152]{1,0:T(8,128)(2,1)S(1)}, u32[]{:S(2)}, u32[]{:S(2)}) collective-permute-start(bf16[96,1152]{1,0:T(8,128)(2,1)S(1)} %sent_term.1), channel_id=1, source_target_pairs={{0,2},{2,0},{1,3},{3,1},{4,6},{6,4},{5,7},{7,5},{8,10},{10,8},{9,1... | collective-permute-start | bytes 663560 | tf_op jit(solution)/shard_map/projection/ppermute | solution.py:43
  20.4 1.5 %collective-permute-start.5 = (bf16[96,256]{1,0:T(8,128)(2,1)S(1)}, bf16[96,256]{1,0:T(8,128)(2,1)S(1)}, u32[]{:S(2)}, u32[]{:S(2)}) collective-permute-start(bf16[96,256]{1,0:T(8,128)(2,1)S(1)} %attention.1.refs_0_), channel_id=1, source_target_pairs={{0,2},{2,0},{1,3},{3,1},{4,6},{6,4},{5,7},{7,5},{8,10},{10,8},{9,1... | collective-permute-start | bytes 147464 | tf_op jit(solution)/shard_map/attended_swap/ppermute | solution.py:43
  21.9 0.4 %collective-permute-done.6.weight_ref = bf16[256,256]{1,0:T(8,128)(2,1)S(1)} collective-permute-done((bf16[256,256]{1,0:T(8,128)(2,1)}, bf16[256,256]{1,0:T(8,128)(2,1)S(1)}, u32[]{:S(2)}, u32[]{:S(2)}) %collective-permute-start.6) | collective-permute-done | bytes 131104 | tf_op jit(solution)/shard_map/early_weight/ppermute | solution.py:43
  22.4 6.2 %collective-permute-done.5.attended_ref = bf16[96,256]{1,0:T(8,128)(2,1)S(1)} collective-permute-done((bf16[96,256]{1,0:T(8,128)(2,1)S(1)}, bf16[96,256]{1,0:T(8,128)(2,1)S(1)}, u32[]{:S(2)}, u32[]{:S(2)}) %collective-permute-start.5) | collective-permute-done | bytes 49184 | tf_op jit(solution)/shard_map/attended_swap/ppermute | solution.py:43
  28.6 0.1 collective-permute-start.7
  28.6 0.0 copy-done.6
  28.7 0.0 copy-done.2
  28.7 2.1 %base.1.base_ref = f32[96,1280]{1,0:T(8,128)S(1)} custom-call(bf16[96,1280]{1,0:T(8,128)(2,1)S(1)} %copy-done.2, f32[1,1280]{1,0:T(1,128)S(1)} %reshape.3.gate_ref, bf16[96,256]{1,0:T(8,128)(2,1)S(1)} %attention.1.refs_0_, bf16[256,5120]{1,0:T(8,128)(2,1)S(1)} %copy-done, bf16[96,256]{1,0:T(8,128)(2,1)S(1)} %collective-permute-done.3.refs_2_, ...), custom_call_target="tpu_custom_call" | custom-call | flops 125829120 | tf_op jit(solution)/shard_map/projection/base/pallas_call | solution.py:280
  30.8 0.0 collective-permute-done.7.packed_ref
  30.8 0.2 early.1.base_ref
  31.0 0.0 collective-permute-done.8.refs_0_
  31.0 0.8 %final.1 = bf16[96,1280]{1,0:T(8,128)(2,1)} custom-call(f32[96,1280]{1,0:T(8,128)S(1)} %early.1.base_ref, f32[1,1280]{1,0:T(1,128)S(1)} %reshape.3.gate_ref, bf16[96,1152]{1,0:T(8,128)(2,1)S(1)} %collective-permute-done.8.refs_0_), custom_call_target="tpu_custom_call" | custom-call | bytes 983040 | tf_op jit(solution)/shard_map/projection/final/pallas_call | solution.py:305
  (2 shorter events, 0.0 us)
Async XLA Ops:
  0.0 17.8 %collective-permute-start.4 = (bf16[256,5120]{1,0:T(8,128)(2,1)}, bf16[256,5120]{1,0:T(8,128)(2,1)}, u32[]{:S(2)}, u32[]{:S(2)}) collective-permute-start(bf16[256,5120]{1,0:T(8,128)(2,1)} %refs_1_.3), channel_id=1, source_target_pairs={{0,1},{1,0},{2,3},{3,2},{4,5},{5,4},{6,7},{7,6},{8,9},{9,8},{10,11... | collective-permute-start | bytes 7864328 | tf_op jit(solution)/shard_map/weight_swap/ppermute | solution.py:43
  1.4 12.4 %copy-start.1 = (bf16[96,512]{1,0:T(8,128)(2,1)}, bf16[96,512]{1,0:T(8,128)(2,1)S(1)}, u32[]{:S(2)}) copy-start(bf16[96,512]{1,0:T(8,128)(2,1)S(1)} %maximum_convert_fusion.refs_0_.after_ref) | copy-start | bytes 294916
  1.4 9.4 %collective-permute-start.2 = (bf16[96,512]{1,0:T(8,128)(2,1)S(1)}, bf16[96,512]{1,0:T(8,128)(2,1)S(1)}, u32[]{:S(2)}, u32[]{:S(2)}) collective-permute-start(bf16[96,512]{1,0:T(8,128)(2,1)S(1)} %maximum_convert_fusion.refs_0_.after_ref), channel_id=1, source_target_pairs={{0,4},{4,8},{8,12},{12,0},{1,5},{5,9},{9,13},{13,1},{2,6},{6,10},{... | collective-permute-start | bytes 294920 | tf_op jit(solution)/shard_map/residual_gather/ppermute | solution.py:43
  4.0 9.8 %collective-permute-start.1 = (bf16[96,512]{1,0:T(8,128)(2,1)S(1)}, bf16[96,512]{1,0:T(8,128)(2,1)S(1)}, u32[]{:S(2)}, u32[]{:S(2)}) collective-permute-start(bf16[96,512]{1,0:T(8,128)(2,1)S(1)} %maximum_convert_fusion.refs_0_.after_ref), channel_id=1, source_target_pairs={{0,8},{4,12},{8,0},{12,4},{1,9},{5,13},{9,1},{13,5},{2,10},{6,14},... | collective-permute-start | bytes 294920 | tf_op jit(solution)/shard_map/residual_gather/ppermute | solution.py:43
  6.6 7.2 %collective-permute-start = (bf16[96,512]{1,0:T(8,128)(2,1)S(1)}, bf16[96,512]{1,0:T(8,128)(2,1)S(1)}, u32[]{:S(2)}, u32[]{:S(2)}) collective-permute-start(bf16[96,512]{1,0:T(8,128)(2,1)S(1)} %maximum_convert_fusion.refs_0_.after_ref), channel_id=1, source_target_pairs={{0,12},{4,0},{8,4},{12,8},{1,13},{5,1},{9,5},{13,9},{2,14},{6,2},{... | collective-permute-start | bytes 294920 | tf_op jit(solution)/shard_map/residual_gather/ppermute | solution.py:43
  8.0 0.9 %copy-start.3 = (bf16[384,256]{1,0:T(8,128)(2,1)S(1)}, bf16[384,256]{1,0:T(8,128)(2,1)}, u32[]{:S(2)}) copy-start(bf16[384,256]{1,0:T(8,128)(2,1)} %held_k_ref.1) | copy-start | bytes 589828
  8.9 0.9 %copy-start.4 = (bf16[384,256]{1,0:T(8,128)(2,1)S(1)}, bf16[384,256]{1,0:T(8,128)(2,1)}, u32[]{:S(2)}) copy-start(bf16[384,256]{1,0:T(8,128)(2,1)} %held_v_ref.1) | copy-start | bytes 589828
  9.8 0.8 %copy-start.5 = (bf16[96,256]{1,0:T(8,128)(2,1)S(1)}, bf16[96,256]{1,0:T(8,128)(2,1)}, u32[]{:S(2)}) copy-start(bf16[96,256]{1,0:T(8,128)(2,1)} %q_ref.3) | copy-start | bytes 147460
  14.4 3.4 %copy-start = (bf16[256,5120]{1,0:T(8,128)(2,1)S(1)}, bf16[256,5120]{1,0:T(8,128)(2,1)}, u32[]{:S(2)}) copy-start(bf16[256,5120]{1,0:T(8,128)(2,1)} %refs_1_.3) | copy-start | bytes 7864324
  14.4 3.4 %collective-permute-start.3 = (bf16[96,256]{1,0:T(8,128)(2,1)S(1)}, bf16[96,256]{1,0:T(8,128)(2,1)S(1)}, u32[]{:S(2)}, u32[]{:S(2)}) collective-permute-start(bf16[96,256]{1,0:T(8,128)(2,1)S(1)} %attention.1.refs_0_), channel_id=1, source_target_pairs={{0,1},{1,0},{2,3},{3,2},{4,5},{5,4},{6,7},{7,6},{8,9},{9,8},{10,11... | collective-permute-start | bytes 147464 | tf_op jit(solution)/shard_map/attended_swap/ppermute | solution.py:43
  16.2 12.5 %copy-start.6 = (f32[1280]{0:T(1024)S(1)}, f32[1280]{0:T(1024)}, u32[]{:S(2)}) copy-start(f32[1280]{0:T(1024)} %param.15) | copy-start | bytes 15364
  16.2 12.5 %copy-start.2 = (bf16[96,1280]{1,0:T(8,128)(2,1)S(1)}, bf16[96,1280]{1,0:T(8,128)(2,1)}, u32[]{:S(2)}) copy-start(bf16[96,1280]{1,0:T(8,128)(2,1)} %hidden_ref.1) | copy-start | bytes 737284
  16.2 6.2 %collective-permute-start.6 = (bf16[256,256]{1,0:T(8,128)(2,1)}, bf16[256,256]{1,0:T(8,128)(2,1)S(1)}, u32[]{:S(2)}, u32[]{:S(2)}) collective-permute-start(bf16[256,256]{1,0:T(8,128)(2,1)} %early_weight.1), channel_id=1, source_target_pairs={{0,2},{2,0},{1,3},{3,1},{4,6},{6,4},{5,7},{7,5},{8,10},{10,8},{9,1... | collective-permute-start | bytes 393224 | tf_op jit(solution)/shard_map/early_weight/ppermute | solution.py:43
  19.8 11.1 %collective-permute-start.8 = (bf16[96,1152]{1,0:T(8,128)(2,1)S(1)}, bf16[96,1152]{1,0:T(8,128)(2,1)S(1)}, u32[]{:S(2)}, u32[]{:S(2)}) collective-permute-start(bf16[96,1152]{1,0:T(8,128)(2,1)S(1)} %sent_term.1), channel_id=1, source_target_pairs={{0,2},{2,0},{1,3},{3,1},{4,6},{6,4},{5,7},{7,5},{8,10},{10,8},{9,1... | collective-permute-start | bytes 663560 | tf_op jit(solution)/shard_map/projection/ppermute | solution.py:43
  20.4 8.1 %collective-permute-start.5 = (bf16[96,256]{1,0:T(8,128)(2,1)S(1)}, bf16[96,256]{1,0:T(8,128)(2,1)S(1)}, u32[]{:S(2)}, u32[]{:S(2)}) collective-permute-start(bf16[96,256]{1,0:T(8,128)(2,1)S(1)} %attention.1.refs_0_), channel_id=1, source_target_pairs={{0,2},{2,0},{1,3},{3,1},{4,6},{6,4},{5,7},{7,5},{8,10},{10,8},{9,1... | collective-permute-start | bytes 147464 | tf_op jit(solution)/shard_map/attended_swap/ppermute | solution.py:43
  28.6 2.2 %collective-permute-start.7 = (bf16[448,128]{1,0:T(8,128)(2,1)S(1)}, bf16[448,128]{1,0:T(8,128)(2,1)S(1)}, u32[]{:S(2)}, u32[]{:S(2)}) collective-permute-start(bf16[448,128]{1,0:T(8,128)(2,1)S(1)} %pack.1), channel_id=1, source_target_pairs={{0,1},{1,0},{2,3},{3,2},{4,5},{5,4},{6,7},{7,6},{8,9},{9,8},{10,11... | collective-permute-start | bytes 344072 | tf_op jit(solution)/shard_map/projection/ppermute | solution.py:43

commit v9 on v8

--- a/solution.py
+++ b/solution.py
@@ -11,6 +11,7 @@
 HD = 128
 LANES = 128
 VMEM_LIMIT = 12 * 1024 * 1024
+EARLY = 256
 
 IN_VMEM = pl.BlockSpec(memory_space=pltpu.VMEM)
 ANYWHERE = pl.BlockSpec(memory_space=pl.ANY)
@@ -129,24 +130,6 @@
     out_ref[:, early:] = (base_ref[:, early:] + gate_ref[:, early:] * total).astype(jnp.bfloat16)
 
 
-def early_weight_kernel(subs, columns, early, weight_ref, after_ref, out_ref, sems):
-    chip = (1 - lax.axis_index("head")) * subs
-    copies = []
-    for sub in range(subs):
-        at = pl.multiple_of((chip + sub) * columns, LANES)
-        copies.append(
-            pltpu.make_async_copy(
-                weight_ref.at[:, pl.ds(at, early)],
-                out_ref.at[:, pl.ds(sub * early, early)],
-                sems.at[sub],
-            )
-        )
-    for copy in copies:
-        copy.start()
-    for copy in copies:
-        copy.wait()
-
-
 def pack_kernel(early, attended_ref, weight_ref, out_ref):
     rows, width = attended_ref.shape
     for i in range(width // early):
@@ -198,19 +181,22 @@
                 shift(out_weight, "sub", subs, i) for i in range(1, subs)
             ]
 
-        early = LANES if heads == 2 and columns % LANES == 0 and columns > 4 * LANES else 0
+        early = EARLY if heads == 2 and columns % LANES == 0 and columns > 4 * LANES else 0
         if early:
             with jax.named_scope("early_weight"):
-                early_weight = call(
-                    functools.partial(early_weight_kernel, subs, columns, early),
-                    jax.ShapeDtypeStruct((width, subs * early), jnp.bfloat16),
-                    [ANYWHERE] * 2,
-                    IN_VMEM,
-                    "early_weight",
-                    moved=4 * width * subs * early,
-                    scratch_shapes=[pltpu.SemaphoreType.DMA((subs,))],
-                    vmem=60 * 1024 * 1024,
-                )(out_weight, residual)
+                chip = (1 - lax.axis_index("head")) * subs
+                slices = [
+                    lax.dynamic_slice(out_weight, (0, (chip + i) * columns), (width, early))
+                    for i in range(subs)
+                ]
+                low = jnp.bfloat16(-jnp.inf)
+                early_weight = functools.reduce(
+                    jnp.maximum,
+                    [
+                        lax.pad(piece, low, ((0, 0, 0), (i * early, (subs - 1 - i) * early, 0)))
+                        for i, piece in enumerate(slices)
+                    ],
+                )
                 early_weight = shift(early_weight, "head", heads, 1)
 
         def weight_and_start(i, step, skip=0):

time: 32.4 us -> 24.4 us (0.75); the launches traced: 31.7 us -> 24.1 us
  Pallas kernels: 7.58 us -> 2.39 us
  waiting for transfers between devices: 9.56 us -> 5.52 us
  local copies, waits for them, and re-layouts: 2.68 us -> 3.66 us
  starting transfers between devices: 10.8 us -> 11.5 us
    ppermute x9, waiting for transfers between devices: 9.56 us -> 5.52 us  [shift(): lax.ppermute(array, axis, [(i, (i + step) % size) for i in range(size)])]
    pallas_call x1, Pallas kernels: 2.08 us -> 0.32 us  [per_device(): call(functools.partial(sent_term_kernel, start), sent, [IN_VMEM] * len(pa...]
    pallas_call x1, Pallas kernels: 2.09 us -> 0.37 us  [per_device(): call(functools.partial(base_kernel, start), term, [IN_VMEM] * (2 + len(pa...]
    pallas_call x1 -> x0, Pallas kernels: 1.71 us -> none  [per_device(): call(functools.partial(early_weight_kernel, subs, columns, early), jax.Sh...]
    dynamic_slice x0 -> x1, local copies, waits for them, and re-layouts: none -> 0.99 us  [per_device(): lax.dynamic_slice(out_weight, (0, (chip + i) * columns), (width, early))]
    ppermute x9, starting transfers between devices: 10.8 us -> 11.5 us  [shift(): lax.ppermute(array, axis, [(i, (i + step) % size) for i in range(size)])]
    unnamed x14 -> x12, local copies, waits for them, and re-layouts: 2.67 us -> 2.67 us
  transfers between devices with their start and end apart: 9 -> 9, of which waited for: 3 -> 4; matrix products, arithmetic and copies ran while one was open for 3% -> 8% of each run, Pallas kernels for 22% -> 7%
where the time goes in v9:
time: 24.4 us; the launch traced here: 24.1 us
  starting transfers between devices  11.5 us (47%)
  waiting for transfers between devices  5.52 us (23%)
  local copies, waits for them, and re-layouts  3.66 us (15%)
  Pallas kernels  2.39 us (10%)
  other arithmetic  0.97 us (4%)
    ppermute x9, starting transfers between devices, shift(): lax.ppermute(array, axis, [(i, (i + step) % size) for i in range(size)])  11.5 us
    ppermute x9, waiting for transfers between devices, shift(): lax.ppermute(array, axis, [(i, (i + step) % size) for i in range(size)])  5.52 us
    unnamed x12, local copies, waits for them, and re-layouts  2.67 us
    dynamic_slice x1, local copies, waits for them, and re-layouts, per_device(): lax.dynamic_slice(out_weight, (0, (chip + i) * columns), (width, early))  0.99 us
    convert_element_type x1, other arithmetic, per_device(): residual = jnp.maximum(lax.pad(key_change, low, ((0, 0, 0), (0, width, 0)...  0.95 us
    pallas_call x1, Pallas kernels, per_device(): call(functools.partial(final_kernel, early), jax.ShapeDtypeStruct((rows,...  0.75 us
    pallas_call x1, Pallas kernels, per_device(): call(functools.partial(attention_kernel, 1.0 / math.sqrt(HD)), jax.ShapeD...  0.53 us
  transfers between devices with their start and end apart: 9, of which 4 were waited for; matrix products, arithmetic and copies ran while one was open for 8% of the time, Pallas kernels for 7%

profile of v9, /device:TPU:0, one launch (start us, length us, event | category | flops | bytes accessed | tf_op | source)
XLA Modules:
  0.0 24.1 jit_solution(18418218818426584847)
XLA Ops:
  0.0 0.5 %collective-permute-start.4 = (bf16[256,5120]{1,0:T(8,128)(2,1)}, bf16[256,5120]{1,0:T(8,128)(2,1)S(1)}, u32[]{:S(2)}, u32[]{:S(2)}) collective-permute-start(bf16[256,5120]{1,0:T(8,128)(2,1)} %refs_1_.3), channel_id=1, source_target_pairs={{0,1},{1,0},{2,3},{3,2},{4,5},{5,4},{6,7},{7,6},{8,9},{9,8},{10,11... | collective-permute-start | bytes 7864328 | tf_op jit(solution)/shard_map/weight_swap/ppermute | solution.py:44
  0.5 1.0 %maximum_convert_fusion.refs_0_ = bf16[96,512]{1,0:T(8,128)(2,1)S(1)} fusion(f32[96,256]{1,0:T(8,128)} %param.12, f32[96,256]{1,0:T(8,128)} %param.11), kind=kLoop, calls=%fused_computation.1 | loop fusion | flops 196608 | bytes 294912 | tf_op jit(solution)/shard_map/residual_gather/convert_element_type | solution.py:174
  1.4 2.6 %collective-permute-start.2 = (bf16[96,512]{1,0:T(8,128)(2,1)S(1)}, bf16[96,512]{1,0:T(8,128)(2,1)S(1)}, u32[]{:S(2)}, u32[]{:S(2)}) collective-permute-start(bf16[96,512]{1,0:T(8,128)(2,1)S(1)} %maximum_convert_fusion.refs_0_), channel_id=1, source_target_pairs={{0,4},{4,8},{8,12},{12,0},{1,5},{5,9},{9,13},{13,1},{2,6},{6,10},{... | collective-permute-start | bytes 294920 | tf_op jit(solution)/shard_map/residual_gather/ppermute | solution.py:44
  4.0 2.6 %collective-permute-start.1 = (bf16[96,512]{1,0:T(8,128)(2,1)S(1)}, bf16[96,512]{1,0:T(8,128)(2,1)S(1)}, u32[]{:S(2)}, u32[]{:S(2)}) collective-permute-start(bf16[96,512]{1,0:T(8,128)(2,1)S(1)} %maximum_convert_fusion.refs_0_), channel_id=1, source_target_pairs={{0,8},{4,12},{8,0},{12,4},{1,9},{5,13},{9,1},{13,5},{2,10},{6,14},... | collective-permute-start | bytes 294920 | tf_op jit(solution)/shard_map/residual_gather/ppermute | solution.py:44
  6.6 1.3 %collective-permute-start = (bf16[96,512]{1,0:T(8,128)(2,1)S(1)}, bf16[96,512]{1,0:T(8,128)(2,1)S(1)}, u32[]{:S(2)}, u32[]{:S(2)}) collective-permute-start(bf16[96,512]{1,0:T(8,128)(2,1)S(1)} %maximum_convert_fusion.refs_0_), channel_id=1, source_target_pairs={{0,12},{4,0},{8,4},{12,8},{1,13},{5,1},{9,5},{13,9},{2,14},{6,2},{... | collective-permute-start | bytes 294920 | tf_op jit(solution)/shard_map/residual_gather/ppermute | solution.py:44
  8.0 1.0 %constant_dynamic-slice_fusion.1 = (bf16[256,256]{1,0:T(8,128)(2,1)S(1)}, bf16[256,256]{1,0:T(8,128)(2,1)S(1)}) fusion(bf16[256,5120]{1,0:T(8,128)(2,1)} %refs_1_.3, s32[]{:T(128)S(6)} %select_n.6, s32[]{:T(128)S(6)} %select_n.7), kind=kLoop, calls=%fused_computation.3 | loop fusion | bytes 524296 | tf_op jit(solution)/shard_map/early_weight/dynamic_slice | solution.py:189
  9.0 1.6 %collective-permute-start.6 = (bf16[256,512]{1,0:T(8,128)(2,1)S(1)}, bf16[256,512]{1,0:T(8,128)(2,1)S(1)}, u32[]{:S(2)}, u32[]{:S(2)}) collective-permute-start(bf16[256,512]{1,0:T(8,128)(2,1)S(1)} %pad_maximum_fusion), channel_id=1, source_target_pairs={{0,2},{2,0},{1,3},{3,1},{4,6},{6,4},{5,7},{7,5},{8,10},{10,8},{9,1... | collective-permute-start | bytes 786440 | tf_op jit(solution)/shard_map/early_weight/ppermute | solution.py:44
  10.6 0.0 copy-start.2
  10.6 0.9 %copy-done.2 = bf16[384,256]{1,0:T(8,128)(2,1)S(1)} copy-done((bf16[384,256]{1,0:T(8,128)(2,1)S(1)}, bf16[384,256]{1,0:T(8,128)(2,1)}, u32[]{:S(2)}) %copy-start.2) | copy-done | bytes 196632
  11.5 0.0 copy-start.3
  11.5 0.9 %copy-done.3 = bf16[384,256]{1,0:T(8,128)(2,1)S(1)} copy-done((bf16[384,256]{1,0:T(8,128)(2,1)S(1)}, bf16[384,256]{1,0:T(8,128)(2,1)}, u32[]{:S(2)}) %copy-start.3) | copy-done | bytes 196632
  12.4 0.0 copy-start.4
  12.4 0.8 %copy-done.4 = bf16[96,256]{1,0:T(8,128)(2,1)S(1)} copy-done((bf16[96,256]{1,0:T(8,128)(2,1)S(1)}, bf16[96,256]{1,0:T(8,128)(2,1)}, u32[]{:S(2)}) %copy-start.4) | copy-done | bytes 49176
  13.2 0.2 stage.1
  13.4 0.0 collective-permute-done.2.refs_3_
  13.4 0.4 %collective-permute-done.1.refs_2_ = bf16[96,512]{1,0:T(8,128)(2,1)S(1)} collective-permute-done((bf16[96,512]{1,0:T(8,128)(2,1)S(1)}, bf16[96,512]{1,0:T(8,128)(2,1)S(1)}, u32[]{:S(2)}, u32[]{:S(2)}) %collective-permute-start.1) | collective-permute-done | bytes 98336 | tf_op jit(solution)/shard_map/residual_gather/ppermute | solution.py:44
  13.8 0.0 collective-permute-done.refs_1_
  13.8 0.0 copy-start
  13.8 0.5 %attention.1.refs_0_ = bf16[96,256]{1,0:T(8,128)(2,1)S(1)} custom-call(bf16[96,256]{1,0:T(8,128)(2,1)S(1)} %copy-done.4, f32[2,96,384]{2,1,0:T(8,128)S(1)} %get-tuple-element.7.products_ref, bf16[384,256]{1,0:T(8,128)(2,1)S(1)} %get-tuple-element.8.values_ref, bf16[96,512]{1,0:T(8,128)(2,1)S(1)} %maximum_convert_fusion.refs_0_, ...), custom_call_target="tpu_custom_call" | custom-call | flops 2000000000 | tf_op jit(solution)/shard_map/attention/attention/pallas_call | solution.py:232
  14.3 0.0 copy-start.5
  14.4 0.0 copy-start.1
  14.4 0.1 collective-permute-start.3
  14.5 1.6 %collective-permute-start.5 = (bf16[96,256]{1,0:T(8,128)(2,1)S(1)}, bf16[96,256]{1,0:T(8,128)(2,1)S(1)}, u32[]{:S(2)}, u32[]{:S(2)}) collective-permute-start(bf16[96,256]{1,0:T(8,128)(2,1)S(1)} %attention.1.refs_0_), channel_id=1, source_target_pairs={{0,2},{2,0},{1,3},{3,1},{4,6},{6,4},{5,7},{7,5},{8,10},{10,8},{9,1... | collective-permute-start | bytes 147464 | tf_op jit(solution)/shard_map/attended_swap/ppermute | solution.py:44
  16.0 0.0 collective-permute-done.3.refs_2_
  16.0 0.0 collective-permute-done.4.refs_3_
  16.0 0.0 copy-done
  16.0 0.3 %sent_term.1 = bf16[96,1024]{1,0:T(8,128)(2,1)S(1)} custom-call(bf16[96,256]{1,0:T(8,128)(2,1)S(1)} %attention.1.refs_0_, bf16[256,5120]{1,0:T(8,128)(2,1)S(1)} %copy-done, bf16[96,256]{1,0:T(8,128)(2,1)S(1)} %collective-permute-done.3.refs_2_, bf16[256,5120]{1,0:T(8,128)(2,1)S(1)} %collective-permute-done.4.refs_3_), custom_call_target="tpu_custom_call" | custom-call | flops 125829120 | tf_op jit(solution)/shard_map/projection/sent_term/pallas_call | solution.py:255
  16.3 1.2 %collective-permute-start.8 = (bf16[96,1024]{1,0:T(8,128)(2,1)S(1)}, bf16[96,1024]{1,0:T(8,128)(2,1)S(1)}, u32[]{:S(2)}, u32[]{:S(2)}) collective-permute-start(bf16[96,1024]{1,0:T(8,128)(2,1)S(1)} %sent_term.1), channel_id=1, source_target_pairs={{0,2},{2,0},{1,3},{3,1},{4,6},{6,4},{5,7},{7,5},{8,10},{10,8},{9,1... | collective-permute-start | bytes 589832 | tf_op jit(solution)/shard_map/projection/ppermute | solution.py:44
  17.5 1.1 %collective-permute-done.5.attended_ref = bf16[96,256]{1,0:T(8,128)(2,1)S(1)} collective-permute-done((bf16[96,256]{1,0:T(8,128)(2,1)S(1)}, bf16[96,256]{1,0:T(8,128)(2,1)S(1)}, u32[]{:S(2)}, u32[]{:S(2)}) %collective-permute-start.5) | collective-permute-done | bytes 49184 | tf_op jit(solution)/shard_map/attended_swap/ppermute | solution.py:44
  18.6 0.0 collective-permute-done.6.weight_ref
  18.6 0.1 collective-permute-start.7
  18.7 0.0 copy-done.5
  18.7 0.0 copy-done.1
  18.7 0.4 %base.1.base_ref = f32[96,1280]{1,0:T(8,128)S(1)} custom-call(bf16[96,1280]{1,0:T(8,128)(2,1)S(1)} %copy-done.1, f32[1,1280]{1,0:T(1,128)S(1)} %reshape.3.gate_ref, bf16[96,256]{1,0:T(8,128)(2,1)S(1)} %attention.1.refs_0_, bf16[256,5120]{1,0:T(8,128)(2,1)S(1)} %copy-done, bf16[96,256]{1,0:T(8,128)(2,1)S(1)} %collective-permute-done.3.refs_2_, ...), custom_call_target="tpu_custom_call" | custom-call | flops 125829120 | tf_op jit(solution)/shard_map/projection/base/pallas_call | solution.py:266
  19.1 1.0 %collective-permute-done.7.packed_ref = bf16[352,256]{1,0:T(8,128)(2,1)S(1)} collective-permute-done((bf16[352,256]{1,0:T(8,128)(2,1)S(1)}, bf16[352,256]{1,0:T(8,128)(2,1)S(1)}, u32[]{:S(2)}, u32[]{:S(2)}) %collective-permute-start.7) | collective-permute-done | bytes 180256 | tf_op jit(solution)/shard_map/projection/ppermute | solution.py:44
  20.1 0.2 early.1.base_ref
  20.3 3.1 %collective-permute-done.8.refs_0_ = bf16[96,1024]{1,0:T(8,128)(2,1)S(1)} collective-permute-done((bf16[96,1024]{1,0:T(8,128)(2,1)S(1)}, bf16[96,1024]{1,0:T(8,128)(2,1)S(1)}, u32[]{:S(2)}, u32[]{:S(2)}) %collective-permute-start.8) | collective-permute-done | bytes 196640 | tf_op jit(solution)/shard_map/projection/ppermute | solution.py:44
  23.4 0.7 %final.1 = bf16[96,1280]{1,0:T(8,128)(2,1)} custom-call(f32[96,1280]{1,0:T(8,128)S(1)} %early.1.base_ref, f32[1,1280]{1,0:T(1,128)S(1)} %reshape.3.gate_ref, bf16[96,1024]{1,0:T(8,128)(2,1)S(1)} %collective-permute-done.8.refs_0_), custom_call_target="tpu_custom_call" | custom-call | bytes 983040 | tf_op jit(solution)/shard_map/projection/final/pallas_call | solution.py:291
  (3 shorter events, 0.0 us)
Async XLA Ops:
  0.0 16.0 %collective-permute-start.4 = (bf16[256,5120]{1,0:T(8,128)(2,1)}, bf16[256,5120]{1,0:T(8,128)(2,1)S(1)}, u32[]{:S(2)}, u32[]{:S(2)}) collective-permute-start(bf16[256,5120]{1,0:T(8,128)(2,1)} %refs_1_.3), channel_id=1, source_target_pairs={{0,1},{1,0},{2,3},{3,2},{4,5},{5,4},{6,7},{7,6},{8,9},{9,8},{10,11... | collective-permute-start | bytes 7864328 | tf_op jit(solution)/shard_map/weight_swap/ppermute | solution.py:44
  1.4 12.0 %collective-permute-start.2 = (bf16[96,512]{1,0:T(8,128)(2,1)S(1)}, bf16[96,512]{1,0:T(8,128)(2,1)S(1)}, u32[]{:S(2)}, u32[]{:S(2)}) collective-permute-start(bf16[96,512]{1,0:T(8,128)(2,1)S(1)} %maximum_convert_fusion.refs_0_), channel_id=1, source_target_pairs={{0,4},{4,8},{8,12},{12,0},{1,5},{5,9},{9,13},{13,1},{2,6},{6,10},{... | collective-permute-start | bytes 294920 | tf_op jit(solution)/shard_map/residual_gather/ppermute | solution.py:44
  4.0 9.8 %collective-permute-start.1 = (bf16[96,512]{1,0:T(8,128)(2,1)S(1)}, bf16[96,512]{1,0:T(8,128)(2,1)S(1)}, u32[]{:S(2)}, u32[]{:S(2)}) collective-permute-start(bf16[96,512]{1,0:T(8,128)(2,1)S(1)} %maximum_convert_fusion.refs_0_), channel_id=1, source_target_pairs={{0,8},{4,12},{8,0},{12,4},{1,9},{5,13},{9,1},{13,5},{2,10},{6,14},... | collective-permute-start | bytes 294920 | tf_op jit(solution)/shard_map/residual_gather/ppermute | solution.py:44
  6.6 7.2 %collective-permute-start = (bf16[96,512]{1,0:T(8,128)(2,1)S(1)}, bf16[96,512]{1,0:T(8,128)(2,1)S(1)}, u32[]{:S(2)}, u32[]{:S(2)}) collective-permute-start(bf16[96,512]{1,0:T(8,128)(2,1)S(1)} %maximum_convert_fusion.refs_0_), channel_id=1, source_target_pairs={{0,12},{4,0},{8,4},{12,8},{1,13},{5,1},{9,5},{13,9},{2,14},{6,2},{... | collective-permute-start | bytes 294920 | tf_op jit(solution)/shard_map/residual_gather/ppermute | solution.py:44
  9.0 9.6 %collective-permute-start.6 = (bf16[256,512]{1,0:T(8,128)(2,1)S(1)}, bf16[256,512]{1,0:T(8,128)(2,1)S(1)}, u32[]{:S(2)}, u32[]{:S(2)}) collective-permute-start(bf16[256,512]{1,0:T(8,128)(2,1)S(1)} %pad_maximum_fusion), channel_id=1, source_target_pairs={{0,2},{2,0},{1,3},{3,1},{4,6},{6,4},{5,7},{7,5},{8,10},{10,8},{9,1... | collective-permute-start | bytes 786440 | tf_op jit(solution)/shard_map/early_weight/ppermute | solution.py:44
  10.6 0.9 %copy-start.2 = (bf16[384,256]{1,0:T(8,128)(2,1)S(1)}, bf16[384,256]{1,0:T(8,128)(2,1)}, u32[]{:S(2)}) copy-start(bf16[384,256]{1,0:T(8,128)(2,1)} %held_k_ref.1) | copy-start | bytes 589828
  11.5 0.9 %copy-start.3 = (bf16[384,256]{1,0:T(8,128)(2,1)S(1)}, bf16[384,256]{1,0:T(8,128)(2,1)}, u32[]{:S(2)}) copy-start(bf16[384,256]{1,0:T(8,128)(2,1)} %held_v_ref.1) | copy-start | bytes 589828
  12.4 0.8 %copy-start.4 = (bf16[96,256]{1,0:T(8,128)(2,1)S(1)}, bf16[96,256]{1,0:T(8,128)(2,1)}, u32[]{:S(2)}) copy-start(bf16[96,256]{1,0:T(8,128)(2,1)} %q_ref.3) | copy-start | bytes 147460
  13.8 2.2 %copy-start = (bf16[256,5120]{1,0:T(8,128)(2,1)S(1)}, bf16[256,5120]{1,0:T(8,128)(2,1)}, u32[]{:S(2)}) copy-start(bf16[256,5120]{1,0:T(8,128)(2,1)} %refs_1_.3) | copy-start | bytes 7864324
  14.3 4.4 %copy-start.5 = (f32[1280]{0:T(1024)S(1)}, f32[1280]{0:T(1024)}, u32[]{:S(2)}) copy-start(f32[1280]{0:T(1024)} %param.15) | copy-start | bytes 15364
  14.4 4.4 %copy-start.1 = (bf16[96,1280]{1,0:T(8,128)(2,1)S(1)}, bf16[96,1280]{1,0:T(8,128)(2,1)}, u32[]{:S(2)}) copy-start(bf16[96,1280]{1,0:T(8,128)(2,1)} %hidden_ref.1) | copy-start | bytes 737284
  14.4 1.6 %collective-permute-start.3 = (bf16[96,256]{1,0:T(8,128)(2,1)S(1)}, bf16[96,256]{1,0:T(8,128)(2,1)S(1)}, u32[]{:S(2)}, u32[]{:S(2)}) collective-permute-start(bf16[96,256]{1,0:T(8,128)(2,1)S(1)} %attention.1.refs_0_), channel_id=1, source_target_pairs={{0,1},{1,0},{2,3},{3,2},{4,5},{5,4},{6,7},{7,6},{8,9},{9,8},{10,11... | collective-permute-start | bytes 147464 | tf_op jit(solution)/shard_map/attended_swap/ppermute | solution.py:44
  14.5 4.2 %collective-permute-start.5 = (bf16[96,256]{1,0:T(8,128)(2,1)S(1)}, bf16[96,256]{1,0:T(8,128)(2,1)S(1)}, u32[]{:S(2)}, u32[]{:S(2)}) collective-permute-start(bf16[96,256]{1,0:T(8,128)(2,1)S(1)} %attention.1.refs_0_), channel_id=1, source_target_pairs={{0,2},{2,0},{1,3},{3,1},{4,6},{6,4},{5,7},{7,5},{8,10},{10,8},{9,1... | collective-permute-start | bytes 147464 | tf_op jit(solution)/shard_map/attended_swap/ppermute | solution.py:44
  16.3 7.0 %collective-permute-start.8 = (bf16[96,1024]{1,0:T(8,128)(2,1)S(1)}, bf16[96,1024]{1,0:T(8,128)(2,1)S(1)}, u32[]{:S(2)}, u32[]{:S(2)}) collective-permute-start(bf16[96,1024]{1,0:T(8,128)(2,1)S(1)} %sent_term.1), channel_id=1, source_target_pairs={{0,2},{2,0},{1,3},{3,1},{4,6},{6,4},{5,7},{7,5},{8,10},{10,8},{9,1... | collective-permute-start | bytes 589832 | tf_op jit(solution)/shard_map/projection/ppermute | solution.py:44
  18.6 1.5 %collective-permute-start.7 = (bf16[352,256]{1,0:T(8,128)(2,1)S(1)}, bf16[352,256]{1,0:T(8,128)(2,1)S(1)}, u32[]{:S(2)}, u32[]{:S(2)}) collective-permute-start(bf16[352,256]{1,0:T(8,128)(2,1)S(1)} %pack.1), channel_id=1, source_target_pairs={{0,1},{1,0},{2,3},{3,2},{4,5},{5,4},{6,7},{7,6},{8,9},{9,8},{10,11... | collective-permute-start | bytes 540680 | tf_op jit(solution)/shard_map/projection/ppermute | solution.py:44

commit v10 on v9

--- a/solution.py
+++ b/solution.py
@@ -45,7 +45,7 @@
 
 
 def gather_steps(patches):
-    return list(range(patches - 1, 0, -1))
+    return list(range(1, patches))
 
 
 def gather_sources(patches, place):
@@ -172,14 +172,6 @@
                 lax.pad(key_change, low, ((0, 0, 0), (0, width, 0))),
                 lax.pad(value_change, low, ((0, 0, 0), (width, 0, 0))),
             ).astype(jnp.bfloat16)
-            blocks = [residual] + [
-                shift(residual, "patch", patches, step) for step in gather_steps(patches)
-            ]
-
-        with jax.named_scope("weight_swap"):
-            weights = [out_weight] + [
-                shift(out_weight, "sub", subs, i) for i in range(1, subs)
-            ]
 
         early = EARLY if heads == 2 and columns % LANES == 0 and columns > 4 * LANES else 0
         if early:
@@ -197,6 +189,23 @@
                         for i, piece in enumerate(slices)
                     ],
                 )
+
+        with jax.named_scope("residual_gather"):
+            last = residual
+            if early:
+                last, early_weight = lax.optimization_barrier((residual, early_weight))
+            blocks = [residual] + [
+                shift(last if step == patches - 1 else residual, "patch", patches, step)
+                for step in gather_steps(patches)
+            ]
+
+        with jax.named_scope("weight_swap"):
+            weights = [out_weight] + [
+                shift(out_weight, "sub", subs, i) for i in range(1, subs)
+            ]
+
+        if early:
+            with jax.named_scope("early_weight"):
                 early_weight = shift(early_weight, "head", heads, 1)
 
         def weight_and_start(i, step, skip=0):

time: 24.4 us -> 24.9 us (1.020)
  waiting for transfers between devices: 5.52 us -> 6.09 us
    ppermute x9, waiting for transfers between devices: 5.52 us -> 6.09 us  [shift(): lax.ppermute(array, axis, [(i, (i + step) % size) for i in range(size)])]
where the time goes in v10:
time: 24.9 us; the launch traced here: 24.7 us
  starting transfers between devices  11.5 us (46%)
  waiting for transfers between devices  6.09 us (24%)
  local copies, waits for them, and re-layouts  3.66 us (15%)
  Pallas kernels  2.38 us (10%)
  other arithmetic  0.97 us (4%)
    ppermute x9, starting transfers between devices, shift(): lax.ppermute(array, axis, [(i, (i + step) % size) for i in range(size)])  11.5 us
    ppermute x9, waiting for transfers between devices, shift(): lax.ppermute(array, axis, [(i, (i + step) % size) for i in range(size)])  6.09 us
    unnamed x12, local copies, waits for them, and re-layouts  2.67 us
    dynamic_slice x1, local copies, waits for them, and re-layouts, per_device(): lax.dynamic_slice(out_weight, (0, (chip + i) * columns), (width, early))  0.99 us
    convert_element_type x1, other arithmetic, per_device(): residual = jnp.maximum(lax.pad(key_change, low, ((0, 0, 0), (0, width, 0)...  0.95 us
    pallas_call x1, Pallas kernels, per_device(): call(functools.partial(final_kernel, early), jax.ShapeDtypeStruct((rows,...  0.75 us
    pallas_call x1, Pallas kernels, per_device(): call(functools.partial(attention_kernel, 1.0 / math.sqrt(HD)), jax.ShapeD...  0.53 us
  transfers between devices with their start and end apart: 9, of which 4 were waited for; matrix products, arithmetic and copies ran while one was open for 8% of the time, Pallas kernels for 7%

profile of v10, /device:TPU:0, one launch (start us, length us, event | category | flops | bytes accessed | tf_op | source)
XLA Modules:
  0.0 24.7 jit_solution(1250865969403876589)
XLA Ops:
  0.0 0.5 %collective-permute-start.4 = (bf16[256,5120]{1,0:T(8,128)(2,1)}, bf16[256,5120]{1,0:T(8,128)(2,1)S(1)}, u32[]{:S(2)}, u32[]{:S(2)}) collective-permute-start(bf16[256,5120]{1,0:T(8,128)(2,1)} %refs_1_.3), channel_id=1, source_target_pairs={{0,1},{1,0},{2,3},{3,2},{4,5},{5,4},{6,7},{7,6},{8,9},{9,8},{10,11... | collective-permute-start | bytes 7864328 | tf_op jit(solution)/shard_map/weight_swap/ppermute | solution.py:44
  0.5 1.0 %maximum_convert_fusion.refs_0_ = bf16[96,512]{1,0:T(8,128)(2,1)S(1)} fusion(f32[96,256]{1,0:T(8,128)} %param.12, f32[96,256]{1,0:T(8,128)} %param.11), kind=kLoop, calls=%fused_computation.1 | loop fusion | flops 196608 | bytes 294912 | tf_op jit(solution)/shard_map/residual_gather/convert_element_type | solution.py:174
  1.4 2.6 %collective-permute-start = (bf16[96,512]{1,0:T(8,128)(2,1)S(1)}, bf16[96,512]{1,0:T(8,128)(2,1)S(1)}, u32[]{:S(2)}, u32[]{:S(2)}) collective-permute-start(bf16[96,512]{1,0:T(8,128)(2,1)S(1)} %maximum_convert_fusion.refs_0_), channel_id=1, source_target_pairs={{0,4},{4,8},{8,12},{12,0},{1,5},{5,9},{9,13},{13,1},{2,6},{6,10},{... | collective-permute-start | bytes 294920 | tf_op jit(solution)/shard_map/residual_gather/ppermute | solution.py:44
  4.0 2.6 %collective-permute-start.1 = (bf16[96,512]{1,0:T(8,128)(2,1)S(1)}, bf16[96,512]{1,0:T(8,128)(2,1)S(1)}, u32[]{:S(2)}, u32[]{:S(2)}) collective-permute-start(bf16[96,512]{1,0:T(8,128)(2,1)S(1)} %maximum_convert_fusion.refs_0_), channel_id=1, source_target_pairs={{0,8},{4,12},{8,0},{12,4},{1,9},{5,13},{9,1},{13,5},{2,10},{6,14},... | collective-permute-start | bytes 294920 | tf_op jit(solution)/shard_map/residual_gather/ppermute | solution.py:44
  6.6 1.0 %constant_dynamic-slice_fusion.1 = (bf16[256,256]{1,0:T(8,128)(2,1)S(1)}, bf16[256,256]{1,0:T(8,128)(2,1)S(1)}) fusion(bf16[256,5120]{1,0:T(8,128)(2,1)} %refs_1_.3, s32[]{:T(128)S(6)} %select_n.6, s32[]{:T(128)S(6)} %select_n.7), kind=kLoop, calls=%fused_computation.3 | loop fusion | bytes 524296 | tf_op jit(solution)/shard_map/early_weight/dynamic_slice | solution.py:181
  7.6 1.4 %collective-permute-start.2 = (bf16[96,512]{1,0:T(8,128)(2,1)S(1)}, bf16[96,512]{1,0:T(8,128)(2,1)S(1)}, u32[]{:S(2)}, u32[]{:S(2)}) collective-permute-start(bf16[96,512]{1,0:T(8,128)(2,1)S(1)} %maximum_convert_fusion.refs_0_), channel_id=1, source_target_pairs={{0,12},{4,0},{8,4},{12,8},{1,13},{5,1},{9,5},{13,9},{2,14},{6,2},{... | collective-permute-start | bytes 294920 | tf_op jit(solution)/shard_map/residual_gather/ppermute | solution.py:44
  9.0 1.5 %collective-permute-start.6 = (bf16[256,512]{1,0:T(8,128)(2,1)S(1)}, bf16[256,512]{1,0:T(8,128)(2,1)S(1)}, u32[]{:S(2)}, u32[]{:S(2)}) collective-permute-start(bf16[256,512]{1,0:T(8,128)(2,1)S(1)} %pad_maximum_fusion), channel_id=1, source_target_pairs={{0,2},{2,0},{1,3},{3,1},{4,6},{6,4},{5,7},{7,5},{8,10},{10,8},{9,1... | collective-permute-start | bytes 786440 | tf_op jit(solution)/shard_map/early_weight/ppermute | solution.py:44
  10.5 0.0 copy-start.2
  10.5 0.9 %copy-done.2 = bf16[384,256]{1,0:T(8,128)(2,1)S(1)} copy-done((bf16[384,256]{1,0:T(8,128)(2,1)S(1)}, bf16[384,256]{1,0:T(8,128)(2,1)}, u32[]{:S(2)}) %copy-start.2) | copy-done | bytes 196632
  11.5 0.0 copy-start.3
  11.5 0.9 %copy-done.3 = bf16[384,256]{1,0:T(8,128)(2,1)S(1)} copy-done((bf16[384,256]{1,0:T(8,128)(2,1)S(1)}, bf16[384,256]{1,0:T(8,128)(2,1)}, u32[]{:S(2)}) %copy-start.3) | copy-done | bytes 196632
  12.4 0.0 copy-start.4
  12.4 0.8 %copy-done.4 = bf16[96,256]{1,0:T(8,128)(2,1)S(1)} copy-done((bf16[96,256]{1,0:T(8,128)(2,1)S(1)}, bf16[96,256]{1,0:T(8,128)(2,1)}, u32[]{:S(2)}) %copy-start.4) | copy-done | bytes 49176
  13.2 0.2 stage.1
  13.4 0.9 %collective-permute-done.2.refs_3_ = bf16[96,512]{1,0:T(8,128)(2,1)S(1)} collective-permute-done((bf16[96,512]{1,0:T(8,128)(2,1)S(1)}, bf16[96,512]{1,0:T(8,128)(2,1)S(1)}, u32[]{:S(2)}, u32[]{:S(2)}) %collective-permute-start.2) | collective-permute-done | bytes 98336 | tf_op jit(solution)/shard_map/residual_gather/ppermute | solution.py:44
  14.4 0.0 collective-permute-done.refs_1_
  14.4 0.0 collective-permute-done.1.refs_2_
  14.4 0.0 copy-start
  14.4 0.5 %attention.1.refs_0_ = bf16[96,256]{1,0:T(8,128)(2,1)S(1)} custom-call(bf16[96,256]{1,0:T(8,128)(2,1)S(1)} %copy-done.4, f32[2,96,384]{2,1,0:T(8,128)S(1)} %get-tuple-element.9.products_ref, bf16[384,256]{1,0:T(8,128)(2,1)S(1)} %get-tuple-element.10.values_ref, bf16[96,512]{1,0:T(8,128)(2,1)S(1)} %maximum_convert_fusion.refs_0_, ...), custom_call_target="tpu_custom_call" | custom-call | flops 2000000000 | tf_op jit(solution)/shard_map/attention/attention/pallas_call | solution.py:241
  14.9 0.0 copy-start.5
  14.9 0.0 copy-start.1
  14.9 0.1 collective-permute-start.3
  15.0 1.6 %collective-permute-start.5 = (bf16[96,256]{1,0:T(8,128)(2,1)S(1)}, bf16[96,256]{1,0:T(8,128)(2,1)S(1)}, u32[]{:S(2)}, u32[]{:S(2)}) collective-permute-start(bf16[96,256]{1,0:T(8,128)(2,1)S(1)} %attention.1.refs_0_), channel_id=1, source_target_pairs={{0,2},{2,0},{1,3},{3,1},{4,6},{6,4},{5,7},{7,5},{8,10},{10,8},{9,1... | collective-permute-start | bytes 147464 | tf_op jit(solution)/shard_map/attended_swap/ppermute | solution.py:44
  16.6 0.0 collective-permute-done.3.refs_2_
  16.6 0.0 collective-permute-done.4.refs_3_
  16.6 0.0 copy-done
  16.6 0.3 %sent_term.1 = bf16[96,1024]{1,0:T(8,128)(2,1)S(1)} custom-call(bf16[96,256]{1,0:T(8,128)(2,1)S(1)} %attention.1.refs_0_, bf16[256,5120]{1,0:T(8,128)(2,1)S(1)} %copy-done, bf16[96,256]{1,0:T(8,128)(2,1)S(1)} %collective-permute-done.3.refs_2_, bf16[256,5120]{1,0:T(8,128)(2,1)S(1)} %collective-permute-done.4.refs_3_), custom_call_target="tpu_custom_call" | custom-call | flops 125829120 | tf_op jit(solution)/shard_map/projection/sent_term/pallas_call | solution.py:264
  16.9 1.2 %collective-permute-start.8 = (bf16[96,1024]{1,0:T(8,128)(2,1)S(1)}, bf16[96,1024]{1,0:T(8,128)(2,1)S(1)}, u32[]{:S(2)}, u32[]{:S(2)}) collective-permute-start(bf16[96,1024]{1,0:T(8,128)(2,1)S(1)} %sent_term.1), channel_id=1, source_target_pairs={{0,2},{2,0},{1,3},{3,1},{4,6},{6,4},{5,7},{7,5},{8,10},{10,8},{9,1... | collective-permute-start | bytes 589832 | tf_op jit(solution)/shard_map/projection/ppermute | solution.py:44
  18.1 1.1 %collective-permute-done.5.attended_ref = bf16[96,256]{1,0:T(8,128)(2,1)S(1)} collective-permute-done((bf16[96,256]{1,0:T(8,128)(2,1)S(1)}, bf16[96,256]{1,0:T(8,128)(2,1)S(1)}, u32[]{:S(2)}, u32[]{:S(2)}) %collective-permute-start.5) | collective-permute-done | bytes 49184 | tf_op jit(solution)/shard_map/attended_swap/ppermute | solution.py:44
  19.2 0.0 collective-permute-done.6.weight_ref
  19.2 0.1 collective-permute-start.7
  19.3 0.0 copy-done.5
  19.3 0.0 copy-done.1
  19.3 0.4 %base.1.base_ref = f32[96,1280]{1,0:T(8,128)S(1)} custom-call(bf16[96,1280]{1,0:T(8,128)(2,1)S(1)} %copy-done.1, f32[1,1280]{1,0:T(1,128)S(1)} %reshape.3.gate_ref, bf16[96,256]{1,0:T(8,128)(2,1)S(1)} %attention.1.refs_0_, bf16[256,5120]{1,0:T(8,128)(2,1)S(1)} %copy-done, bf16[96,256]{1,0:T(8,128)(2,1)S(1)} %collective-permute-done.3.refs_2_, ...), custom_call_target="tpu_custom_call" | custom-call | flops 125829120 | tf_op jit(solution)/shard_map/projection/base/pallas_call | solution.py:275
  19.7 1.0 %collective-permute-done.7.packed_ref = bf16[352,256]{1,0:T(8,128)(2,1)S(1)} collective-permute-done((bf16[352,256]{1,0:T(8,128)(2,1)S(1)}, bf16[352,256]{1,0:T(8,128)(2,1)S(1)}, u32[]{:S(2)}, u32[]{:S(2)}) %collective-permute-start.7) | collective-permute-done | bytes 180256 | tf_op jit(solution)/shard_map/projection/ppermute | solution.py:44
  20.7 0.2 early.1.base_ref
  20.9 3.1 %collective-permute-done.8.refs_0_ = bf16[96,1024]{1,0:T(8,128)(2,1)S(1)} collective-permute-done((bf16[96,1024]{1,0:T(8,128)(2,1)S(1)}, bf16[96,1024]{1,0:T(8,128)(2,1)S(1)}, u32[]{:S(2)}, u32[]{:S(2)}) %collective-permute-start.8) | collective-permute-done | bytes 196640 | tf_op jit(solution)/shard_map/projection/ppermute | solution.py:44
  23.9 0.7 %final.1 = bf16[96,1280]{1,0:T(8,128)(2,1)} custom-call(f32[96,1280]{1,0:T(8,128)S(1)} %early.1.base_ref, f32[1,1280]{1,0:T(1,128)S(1)} %reshape.3.gate_ref, bf16[96,1024]{1,0:T(8,128)(2,1)S(1)} %collective-permute-done.8.refs_0_), custom_call_target="tpu_custom_call" | custom-call | bytes 983040 | tf_op jit(solution)/shard_map/projection/final/pallas_call | solution.py:300
  (3 shorter events, 0.0 us)
Async XLA Ops:
  0.0 16.6 %collective-permute-start.4 = (bf16[256,5120]{1,0:T(8,128)(2,1)}, bf16[256,5120]{1,0:T(8,128)(2,1)S(1)}, u32[]{:S(2)}, u32[]{:S(2)}) collective-permute-start(bf16[256,5120]{1,0:T(8,128)(2,1)} %refs_1_.3), channel_id=1, source_target_pairs={{0,1},{1,0},{2,3},{3,2},{4,5},{5,4},{6,7},{7,6},{8,9},{9,8},{10,11... | collective-permute-start | bytes 7864328 | tf_op jit(solution)/shard_map/weight_swap/ppermute | solution.py:44
  1.4 12.9 %collective-permute-start = (bf16[96,512]{1,0:T(8,128)(2,1)S(1)}, bf16[96,512]{1,0:T(8,128)(2,1)S(1)}, u32[]{:S(2)}, u32[]{:S(2)}) collective-permute-start(bf16[96,512]{1,0:T(8,128)(2,1)S(1)} %maximum_convert_fusion.refs_0_), channel_id=1, source_target_pairs={{0,4},{4,8},{8,12},{12,0},{1,5},{5,9},{9,13},{13,1},{2,6},{6,10},{... | collective-permute-start | bytes 294920 | tf_op jit(solution)/shard_map/residual_gather/ppermute | solution.py:44
  4.0 10.3 %collective-permute-start.1 = (bf16[96,512]{1,0:T(8,128)(2,1)S(1)}, bf16[96,512]{1,0:T(8,128)(2,1)S(1)}, u32[]{:S(2)}, u32[]{:S(2)}) collective-permute-start(bf16[96,512]{1,0:T(8,128)(2,1)S(1)} %maximum_convert_fusion.refs_0_), channel_id=1, source_target_pairs={{0,8},{4,12},{8,0},{12,4},{1,9},{5,13},{9,1},{13,5},{2,10},{6,14},... | collective-permute-start | bytes 294920 | tf_op jit(solution)/shard_map/residual_gather/ppermute | solution.py:44
  7.6 6.7 %collective-permute-start.2 = (bf16[96,512]{1,0:T(8,128)(2,1)S(1)}, bf16[96,512]{1,0:T(8,128)(2,1)S(1)}, u32[]{:S(2)}, u32[]{:S(2)}) collective-permute-start(bf16[96,512]{1,0:T(8,128)(2,1)S(1)} %maximum_convert_fusion.refs_0_), channel_id=1, source_target_pairs={{0,12},{4,0},{8,4},{12,8},{1,13},{5,1},{9,5},{13,9},{2,14},{6,2},{... | collective-permute-start | bytes 294920 | tf_op jit(solution)/shard_map/residual_gather/ppermute | solution.py:44
  9.0 10.1 %collective-permute-start.6 = (bf16[256,512]{1,0:T(8,128)(2,1)S(1)}, bf16[256,512]{1,0:T(8,128)(2,1)S(1)}, u32[]{:S(2)}, u32[]{:S(2)}) collective-permute-start(bf16[256,512]{1,0:T(8,128)(2,1)S(1)} %pad_maximum_fusion), channel_id=1, source_target_pairs={{0,2},{2,0},{1,3},{3,1},{4,6},{6,4},{5,7},{7,5},{8,10},{10,8},{9,1... | collective-permute-start | bytes 786440 | tf_op jit(solution)/shard_map/early_weight/ppermute | solution.py:44
  10.5 0.9 %copy-start.2 = (bf16[384,256]{1,0:T(8,128)(2,1)S(1)}, bf16[384,256]{1,0:T(8,128)(2,1)}, u32[]{:S(2)}) copy-start(bf16[384,256]{1,0:T(8,128)(2,1)} %held_k_ref.1) | copy-start | bytes 589828
  11.5 0.9 %copy-start.3 = (bf16[384,256]{1,0:T(8,128)(2,1)S(1)}, bf16[384,256]{1,0:T(8,128)(2,1)}, u32[]{:S(2)}) copy-start(bf16[384,256]{1,0:T(8,128)(2,1)} %held_v_ref.1) | copy-start | bytes 589828
  12.4 0.8 %copy-start.4 = (bf16[96,256]{1,0:T(8,128)(2,1)S(1)}, bf16[96,256]{1,0:T(8,128)(2,1)}, u32[]{:S(2)}) copy-start(bf16[96,256]{1,0:T(8,128)(2,1)} %q_ref.3) | copy-start | bytes 147460
  14.4 2.2 %copy-start = (bf16[256,5120]{1,0:T(8,128)(2,1)S(1)}, bf16[256,5120]{1,0:T(8,128)(2,1)}, u32[]{:S(2)}) copy-start(bf16[256,5120]{1,0:T(8,128)(2,1)} %refs_1_.3) | copy-start | bytes 7864324
  14.9 4.4 %copy-start.5 = (f32[1280]{0:T(1024)S(1)}, f32[1280]{0:T(1024)}, u32[]{:S(2)}) copy-start(f32[1280]{0:T(1024)} %param.15) | copy-start | bytes 15364
  14.9 4.4 %copy-start.1 = (bf16[96,1280]{1,0:T(8,128)(2,1)S(1)}, bf16[96,1280]{1,0:T(8,128)(2,1)}, u32[]{:S(2)}) copy-start(bf16[96,1280]{1,0:T(8,128)(2,1)} %hidden_ref.1) | copy-start | bytes 737284
  14.9 1.6 %collective-permute-start.3 = (bf16[96,256]{1,0:T(8,128)(2,1)S(1)}, bf16[96,256]{1,0:T(8,128)(2,1)S(1)}, u32[]{:S(2)}, u32[]{:S(2)}) collective-permute-start(bf16[96,256]{1,0:T(8,128)(2,1)S(1)} %attention.1.refs_0_), channel_id=1, source_target_pairs={{0,1},{1,0},{2,3},{3,2},{4,5},{5,4},{6,7},{7,6},{8,9},{9,8},{10,11... | collective-permute-start | bytes 147464 | tf_op jit(solution)/shard_map/attended_swap/ppermute | solution.py:44
  15.0 4.2 %collective-permute-start.5 = (bf16[96,256]{1,0:T(8,128)(2,1)S(1)}, bf16[96,256]{1,0:T(8,128)(2,1)S(1)}, u32[]{:S(2)}, u32[]{:S(2)}) collective-permute-start(bf16[96,256]{1,0:T(8,128)(2,1)S(1)} %attention.1.refs_0_), channel_id=1, source_target_pairs={{0,2},{2,0},{1,3},{3,1},{4,6},{6,4},{5,7},{7,5},{8,10},{10,8},{9,1... | collective-permute-start | bytes 147464 | tf_op jit(solution)/shard_map/attended_swap/ppermute | solution.py:44
  16.9 7.0 %collective-permute-start.8 = (bf16[96,1024]{1,0:T(8,128)(2,1)S(1)}, bf16[96,1024]{1,0:T(8,128)(2,1)S(1)}, u32[]{:S(2)}, u32[]{:S(2)}) collective-permute-start(bf16[96,1024]{1,0:T(8,128)(2,1)S(1)} %sent_term.1), channel_id=1, source_target_pairs={{0,2},{2,0},{1,3},{3,1},{4,6},{6,4},{5,7},{7,5},{8,10},{10,8},{9,1... | collective-permute-start | bytes 589832 | tf_op jit(solution)/shard_map/projection/ppermute | solution.py:44
  19.2 1.5 %collective-permute-start.7 = (bf16[352,256]{1,0:T(8,128)(2,1)S(1)}, bf16[352,256]{1,0:T(8,128)(2,1)S(1)}, u32[]{:S(2)}, u32[]{:S(2)}) collective-permute-start(bf16[352,256]{1,0:T(8,128)(2,1)S(1)} %pack.1), channel_id=1, source_target_pairs={{0,1},{1,0},{2,3},{3,2},{4,5},{5,4},{6,7},{7,6},{8,9},{9,8},{10,11... | collective-permute-start | bytes 540680 | tf_op jit(solution)/shard_map/projection/ppermute | solution.py:44

commit v11 on v9

--- a/solution.py
+++ b/solution.py
@@ -50,6 +50,35 @@
 
 def gather_sources(patches, place):
     return [place] + [lax.rem(place + patches - step, patches) for step in gather_steps(patches)]
+
+
+def prepare_kernel(subs, columns, early, *refs):
+    changes, weights = refs[:2], refs[2:3] if early else ()
+    residual_ref, early_refs = refs[2 + len(weights)], refs[3 + len(weights) : -3]
+    buffers, sems = refs[-3:-1], refs[-1]
+    width = buffers[0].shape[1]
+    copies = [
+        pltpu.make_async_copy(change, buffer, sems.at[i])
+        for i, (change, buffer) in enumerate(zip(changes, buffers))
+    ]
+    if early:
+        chip = (1 - lax.axis_index("head")) * subs
+        for sub in range(subs):
+            at = pl.multiple_of((chip + sub) * columns, LANES)
+            copies.append(
+                pltpu.make_async_copy(
+                    weights[0].at[:, pl.ds(at, early)],
+                    early_refs[0].at[:, pl.ds(sub * early, early)],
+                    sems.at[2 + sub],
+                )
+            )
+    for copy in copies:
+        copy.start()
+    for i, buffer in enumerate(buffers):
+        copies[i].wait()
+        residual_ref[:, i * width : (i + 1) * width] = buffer[...].astype(jnp.bfloat16)
+    for copy in copies[2:]:
+        copy.wait()
 
 
 def stage_kernel(patches, q_ref, held_k_ref, held_v_ref, products_ref, values_ref):
@@ -166,12 +195,24 @@
         rows, width = queries.shape
         columns = hidden_in.shape[1]
 
+        early = EARLY if heads == 2 and columns % LANES == 0 and columns > 4 * LANES else 0
         with jax.named_scope("residual_gather"):
-            low = jnp.float32(-jnp.inf)
-            residual = jnp.maximum(
-                lax.pad(key_change, low, ((0, 0, 0), (0, width, 0))),
-                lax.pad(value_change, low, ((0, 0, 0), (width, 0, 0))),
-            ).astype(jnp.bfloat16)
+            operands = [key_change, value_change] + ([out_weight] if early else [])
+            shapes = [jax.ShapeDtypeStruct((rows, 2 * width), jnp.bfloat16)]
+            if early:
+                shapes.append(jax.ShapeDtypeStruct((width, subs * early), jnp.bfloat16))
+            residual, *early_weights = call(
+                functools.partial(prepare_kernel, subs, columns, early),
+                shapes,
+                [ANYWHERE] * len(operands),
+                [IN_VMEM] * len(shapes),
+                "prepare",
+                scratch_shapes=[
+                    pltpu.VMEM((rows, width), jnp.float32),
+                    pltpu.VMEM((rows, width), jnp.float32),
+                    pltpu.SemaphoreType.DMA((2 + subs,)),
+                ],
+            )(*[pltpu.with_memory_space_constraint(x, pltpu.HBM) for x in operands])
             blocks = [residual] + [
                 shift(residual, "patch", patches, step) for step in gather_steps(patches)
             ]
@@ -181,23 +222,9 @@
                 shift(out_weight, "sub", subs, i) for i in range(1, subs)
             ]
 
-        early = EARLY if heads == 2 and columns % LANES == 0 and columns > 4 * LANES else 0
         if early:
             with jax.named_scope("early_weight"):
-                chip = (1 - lax.axis_index("head")) * subs
-                slices = [
-                    lax.dynamic_slice(out_weight, (0, (chip + i) * columns), (width, early))
-                    for i in range(subs)
-                ]
-                low = jnp.bfloat16(-jnp.inf)
-                early_weight = functools.reduce(
-                    jnp.maximum,
-                    [
-                        lax.pad(piece, low, ((0, 0, 0), (i * early, (subs - 1 - i) * early, 0)))
-                        for i, piece in enumerate(slices)
-                    ],
-                )
-                early_weight = shift(early_weight, "head", heads, 1)
+                early_weight = shift(early_weights[0], "head", heads, 1)
 
         def weight_and_start(i, step, skip=0):
             def start():

time: 24.4 us -> 24.5 us (level)
  local copies, waits for them, and re-layouts: 3.66 us -> 0.03 us
  waiting for transfers between devices: 5.52 us -> 9.12 us
  Pallas kernels: 2.39 us -> 3.49 us
  other arithmetic: 0.97 us -> 0 us
    ppermute x9, waiting for transfers between devices: 5.52 us -> 9.12 us  [shift(): lax.ppermute(array, axis, [(i, (i + step) % size) for i in range(size)])]
    unnamed x12, local copies, waits for them, and re-layouts: 2.67 us -> 0.03 us
    pallas_call x0 -> x1, Pallas kernels: none -> 1.1 us  [per_device(): call(functools.partial(prepare_kernel, subs, columns, early), shapes, [AN...]
    dynamic_slice x1 -> x0, local copies, waits for them, and re-layouts: 0.99 us -> none  [per_device(): lax.dynamic_slice(out_weight, (0, (chip + i) * columns), (width, early))]
    convert_element_type x1 -> x0, other arithmetic: 0.95 us -> none  [per_device(): residual = jnp.maximum(lax.pad(key_change, low, ((0, 0, 0), (0, width, 0)...]
  transfers between devices with their start and end apart: 9 -> 9, of which waited for: 4 -> 5; matrix products, arithmetic and copies ran while one was open for 8% -> 0% of each run, Pallas kernels for 7% -> 11%
where the time goes in v11:
time: 24.5 us; the launch traced here: 24.4 us
  starting transfers between devices  11.6 us (47%)
  waiting for transfers between devices  9.12 us (37%)
  Pallas kernels  3.49 us (14%)
    ppermute x9, starting transfers between devices, shift(): lax.ppermute(array, axis, [(i, (i + step) % size) for i in range(size)])  11.6 us
    ppermute x9, waiting for transfers between devices, shift(): lax.ppermute(array, axis, [(i, (i + step) % size) for i in range(size)])  9.12 us
    pallas_call x1, Pallas kernels, per_device(): call(functools.partial(prepare_kernel, subs, columns, early), shapes, [AN...  1.1 us
    pallas_call x1, Pallas kernels, per_device(): call(functools.partial(final_kernel, early), jax.ShapeDtypeStruct((rows,...  0.75 us
    pallas_call x1, Pallas kernels, per_device(): call(functools.partial(attention_kernel, 1.0 / math.sqrt(HD)), jax.ShapeD...  0.53 us
  transfers between devices with their start and end apart: 9, of which 5 were waited for; matrix products, arithmetic and copies ran while one was open for 0% of the time, Pallas kernels for 11%

profile of v11, /device:TPU:0, one launch (start us, length us, event | category | flops | bytes accessed | tf_op | source)
XLA Modules:
  0.0 24.4 jit_solution(786109530977017507)
XLA Ops:
  0.0 0.0 copy-start.4
  0.0 0.0 copy-start.3
  0.0 0.0 copy-start.2
  0.0 0.5 %collective-permute-start.4 = (bf16[256,5120]{1,0:T(8,128)(2,1)}, bf16[256,5120]{1,0:T(8,128)(2,1)S(1)}, u32[]{:S(2)}, u32[]{:S(2)}) collective-permute-start(bf16[256,5120]{1,0:T(8,128)(2,1)} %refs_1_.5), channel_id=1, source_target_pairs={{0,1},{1,0},{2,3},{3,2},{4,5},{5,4},{6,7},{7,6},{8,9},{9,8},{10,11... | collective-permute-start | bytes 7864328 | tf_op jit(solution)/shard_map/weight_swap/ppermute | solution.py:44
  0.5 1.1 %prepare.1 = (bf16[96,512]{1,0:T(8,128)(2,1)S(1)}, bf16[256,512]{1,0:T(8,128)(2,1)S(1)}) custom-call(f32[96,256]{1,0:T(8,128)} %refs_0_.1, f32[96,256]{1,0:T(8,128)} %refs_1_.3, bf16[256,5120]{1,0:T(8,128)(2,1)} %refs_1_.5), custom_call_target="tpu_custom_call" | custom-call | tf_op jit(solution)/shard_map/residual_gather/prepare/pallas_call | solution.py:204
  1.6 2.8 %collective-permute-start.2 = (bf16[96,512]{1,0:T(8,128)(2,1)S(1)}, bf16[96,512]{1,0:T(8,128)(2,1)S(1)}, u32[]{:S(2)}, u32[]{:S(2)}) collective-permute-start(bf16[96,512]{1,0:T(8,128)(2,1)S(1)} %get-tuple-element.11.refs_0_), channel_id=1, source_target_pairs={{0,4},{4,8},{8,12},{12,0},{1,5},{5,9},{9,13},{13,1},{2,6},{6,10},{... | collective-permute-start | bytes 294920 | tf_op jit(solution)/shard_map/residual_gather/ppermute | solution.py:44
  4.4 2.6 %collective-permute-start.1 = (bf16[96,512]{1,0:T(8,128)(2,1)S(1)}, bf16[96,512]{1,0:T(8,128)(2,1)S(1)}, u32[]{:S(2)}, u32[]{:S(2)}) collective-permute-start(bf16[96,512]{1,0:T(8,128)(2,1)S(1)} %get-tuple-element.11.refs_0_), channel_id=1, source_target_pairs={{0,8},{4,12},{8,0},{12,4},{1,9},{5,13},{9,1},{13,5},{2,10},{6,14},... | collective-permute-start | bytes 294920 | tf_op jit(solution)/shard_map/residual_gather/ppermute | solution.py:44
  7.0 1.3 %collective-permute-start = (bf16[96,512]{1,0:T(8,128)(2,1)S(1)}, bf16[96,512]{1,0:T(8,128)(2,1)S(1)}, u32[]{:S(2)}, u32[]{:S(2)}) collective-permute-start(bf16[96,512]{1,0:T(8,128)(2,1)S(1)} %get-tuple-element.11.refs_0_), channel_id=1, source_target_pairs={{0,12},{4,0},{8,4},{12,8},{1,13},{5,1},{9,5},{13,9},{2,14},{6,2},{... | collective-permute-start | bytes 294920 | tf_op jit(solution)/shard_map/residual_gather/ppermute | solution.py:44
  8.3 1.5 %collective-permute-start.6 = (bf16[256,512]{1,0:T(8,128)(2,1)S(1)}, bf16[256,512]{1,0:T(8,128)(2,1)S(1)}, u32[]{:S(2)}, u32[]{:S(2)}) collective-permute-start(bf16[256,512]{1,0:T(8,128)(2,1)S(1)} %get-tuple-element.12), channel_id=1, source_target_pairs={{0,2},{2,0},{1,3},{3,1},{4,6},{6,4},{5,7},{7,5},{8,10},{10,8},{9,1... | collective-permute-start | bytes 786440 | tf_op jit(solution)/shard_map/early_weight/ppermute | solution.py:44
  9.8 0.0 copy-done.4
  9.8 0.0 copy-done.3
  9.8 0.0 copy-done.2
  9.8 0.2 stage.1
  10.1 0.1 collective-permute-done.2.refs_3_
  10.2 3.9 %collective-permute-done.1.refs_2_ = bf16[96,512]{1,0:T(8,128)(2,1)S(1)} collective-permute-done((bf16[96,512]{1,0:T(8,128)(2,1)S(1)}, bf16[96,512]{1,0:T(8,128)(2,1)S(1)}, u32[]{:S(2)}, u32[]{:S(2)}) %collective-permute-start.1) | collective-permute-done | bytes 98336 | tf_op jit(solution)/shard_map/residual_gather/ppermute | solution.py:44
  14.0 0.0 collective-permute-done.refs_1_
  14.1 0.0 copy-start
  14.1 0.5 %attention.1.refs_0_ = bf16[96,256]{1,0:T(8,128)(2,1)S(1)} custom-call(bf16[96,256]{1,0:T(8,128)(2,1)S(1)} %copy-done.4, f32[2,96,384]{2,1,0:T(8,128)S(1)} %get-tuple-element.9.products_ref, bf16[384,256]{1,0:T(8,128)(2,1)S(1)} %get-tuple-element.10.values_ref, bf16[96,512]{1,0:T(8,128)(2,1)S(1)} %get-tuple-element.11.refs_0_, ...), custom_call_target="tpu_custom_call" | custom-call | flops 2000000000 | tf_op jit(solution)/shard_map/attention/attention/pallas_call | solution.py:259
  14.6 0.0 copy-start.5
  14.6 0.0 copy-start.1
  14.6 0.1 collective-permute-start.3
  14.7 1.6 %collective-permute-start.5 = (bf16[96,256]{1,0:T(8,128)(2,1)S(1)}, bf16[96,256]{1,0:T(8,128)(2,1)S(1)}, u32[]{:S(2)}, u32[]{:S(2)}) collective-permute-start(bf16[96,256]{1,0:T(8,128)(2,1)S(1)} %attention.1.refs_0_), channel_id=1, source_target_pairs={{0,2},{2,0},{1,3},{3,1},{4,6},{6,4},{5,7},{7,5},{8,10},{10,8},{9,1... | collective-permute-start | bytes 147464 | tf_op jit(solution)/shard_map/attended_swap/ppermute | solution.py:44
  16.2 0.0 collective-permute-done.3.refs_2_
  16.3 0.0 collective-permute-done.4.refs_3_
  16.3 0.0 copy-done
  16.3 0.3 %sent_term.1 = bf16[96,1024]{1,0:T(8,128)(2,1)S(1)} custom-call(bf16[96,256]{1,0:T(8,128)(2,1)S(1)} %attention.1.refs_0_, bf16[256,5120]{1,0:T(8,128)(2,1)S(1)} %copy-done, bf16[96,256]{1,0:T(8,128)(2,1)S(1)} %collective-permute-done.3.refs_2_, bf16[256,5120]{1,0:T(8,128)(2,1)S(1)} %collective-permute-done.4.refs_3_), custom_call_target="tpu_custom_call" | custom-call | flops 125829120 | tf_op jit(solution)/shard_map/projection/sent_term/pallas_call | solution.py:282
  16.6 1.2 %collective-permute-start.8 = (bf16[96,1024]{1,0:T(8,128)(2,1)S(1)}, bf16[96,1024]{1,0:T(8,128)(2,1)S(1)}, u32[]{:S(2)}, u32[]{:S(2)}) collective-permute-start(bf16[96,1024]{1,0:T(8,128)(2,1)S(1)} %sent_term.1), channel_id=1, source_target_pairs={{0,2},{2,0},{1,3},{3,1},{4,6},{6,4},{5,7},{7,5},{8,10},{10,8},{9,1... | collective-permute-start | bytes 589832 | tf_op jit(solution)/shard_map/projection/ppermute | solution.py:44
  17.8 1.1 %collective-permute-done.5.attended_ref = bf16[96,256]{1,0:T(8,128)(2,1)S(1)} collective-permute-done((bf16[96,256]{1,0:T(8,128)(2,1)S(1)}, bf16[96,256]{1,0:T(8,128)(2,1)S(1)}, u32[]{:S(2)}, u32[]{:S(2)}) %collective-permute-start.5) | collective-permute-done | bytes 49184 | tf_op jit(solution)/shard_map/attended_swap/ppermute | solution.py:44
  18.8 0.0 collective-permute-done.6.weight_ref
  18.9 0.1 collective-permute-start.7
  18.9 0.0 copy-done.5
  19.0 0.0 copy-done.1
  19.0 0.4 %base.1.base_ref = f32[96,1280]{1,0:T(8,128)S(1)} custom-call(bf16[96,1280]{1,0:T(8,128)(2,1)S(1)} %copy-done.1, f32[1,1280]{1,0:T(1,128)S(1)} %reshape.3.gate_ref, bf16[96,256]{1,0:T(8,128)(2,1)S(1)} %attention.1.refs_0_, bf16[256,5120]{1,0:T(8,128)(2,1)S(1)} %copy-done, bf16[96,256]{1,0:T(8,128)(2,1)S(1)} %collective-permute-done.3.refs_2_, ...), custom_call_target="tpu_custom_call" | custom-call | flops 125829120 | tf_op jit(solution)/shard_map/projection/base/pallas_call | solution.py:293
  19.4 1.0 %collective-permute-done.7.packed_ref = bf16[352,256]{1,0:T(8,128)(2,1)S(1)} collective-permute-done((bf16[352,256]{1,0:T(8,128)(2,1)S(1)}, bf16[352,256]{1,0:T(8,128)(2,1)S(1)}, u32[]{:S(2)}, u32[]{:S(2)}) %collective-permute-start.7) | collective-permute-done | bytes 180256 | tf_op jit(solution)/shard_map/projection/ppermute | solution.py:44
  20.4 0.2 early.1.base_ref
  20.6 3.1 %collective-permute-done.8.refs_0_ = bf16[96,1024]{1,0:T(8,128)(2,1)S(1)} collective-permute-done((bf16[96,1024]{1,0:T(8,128)(2,1)S(1)}, bf16[96,1024]{1,0:T(8,128)(2,1)S(1)}, u32[]{:S(2)}, u32[]{:S(2)}) %collective-permute-start.8) | collective-permute-done | bytes 196640 | tf_op jit(solution)/shard_map/projection/ppermute | solution.py:44
  23.6 0.7 %final.1 = bf16[96,1280]{1,0:T(8,128)(2,1)} custom-call(f32[96,1280]{1,0:T(8,128)S(1)} %early.1.base_ref, f32[1,1280]{1,0:T(1,128)S(1)} %reshape.3.gate_ref, bf16[96,1024]{1,0:T(8,128)(2,1)S(1)} %collective-permute-done.8.refs_0_), custom_call_target="tpu_custom_call" | custom-call | bytes 983040 | tf_op jit(solution)/shard_map/projection/final/pallas_call | solution.py:318
  (2 shorter events, 0.0 us)
Async XLA Ops:
  0.0 9.8 %copy-start.4 = (bf16[96,256]{1,0:T(8,128)(2,1)S(1)}, bf16[96,256]{1,0:T(8,128)(2,1)}, u32[]{:S(2)}) copy-start(bf16[96,256]{1,0:T(8,128)(2,1)} %q_ref.3) | copy-start | bytes 147460
  0.0 9.8 %copy-start.3 = (bf16[384,256]{1,0:T(8,128)(2,1)S(1)}, bf16[384,256]{1,0:T(8,128)(2,1)}, u32[]{:S(2)}) copy-start(bf16[384,256]{1,0:T(8,128)(2,1)} %held_v_ref.1) | copy-start | bytes 589828
  0.0 9.8 %copy-start.2 = (bf16[384,256]{1,0:T(8,128)(2,1)S(1)}, bf16[384,256]{1,0:T(8,128)(2,1)}, u32[]{:S(2)}) copy-start(bf16[384,256]{1,0:T(8,128)(2,1)} %held_k_ref.1) | copy-start | bytes 589828
  0.0 16.2 %collective-permute-start.4 = (bf16[256,5120]{1,0:T(8,128)(2,1)}, bf16[256,5120]{1,0:T(8,128)(2,1)S(1)}, u32[]{:S(2)}, u32[]{:S(2)}) collective-permute-start(bf16[256,5120]{1,0:T(8,128)(2,1)} %refs_1_.5), channel_id=1, source_target_pairs={{0,1},{1,0},{2,3},{3,2},{4,5},{5,4},{6,7},{7,6},{8,9},{9,8},{10,11... | collective-permute-start | bytes 7864328 | tf_op jit(solution)/shard_map/weight_swap/ppermute | solution.py:44
  1.6 8.5 %collective-permute-start.2 = (bf16[96,512]{1,0:T(8,128)(2,1)S(1)}, bf16[96,512]{1,0:T(8,128)(2,1)S(1)}, u32[]{:S(2)}, u32[]{:S(2)}) collective-permute-start(bf16[96,512]{1,0:T(8,128)(2,1)S(1)} %get-tuple-element.11.refs_0_), channel_id=1, source_target_pairs={{0,4},{4,8},{8,12},{12,0},{1,5},{5,9},{9,13},{13,1},{2,6},{6,10},{... | collective-permute-start | bytes 294920 | tf_op jit(solution)/shard_map/residual_gather/ppermute | solution.py:44
  4.4 9.6 %collective-permute-start.1 = (bf16[96,512]{1,0:T(8,128)(2,1)S(1)}, bf16[96,512]{1,0:T(8,128)(2,1)S(1)}, u32[]{:S(2)}, u32[]{:S(2)}) collective-permute-start(bf16[96,512]{1,0:T(8,128)(2,1)S(1)} %get-tuple-element.11.refs_0_), channel_id=1, source_target_pairs={{0,8},{4,12},{8,0},{12,4},{1,9},{5,13},{9,1},{13,5},{2,10},{6,14},... | collective-permute-start | bytes 294920 | tf_op jit(solution)/shard_map/residual_gather/ppermute | solution.py:44
  7.0 7.1 %collective-permute-start = (bf16[96,512]{1,0:T(8,128)(2,1)S(1)}, bf16[96,512]{1,0:T(8,128)(2,1)S(1)}, u32[]{:S(2)}, u32[]{:S(2)}) collective-permute-start(bf16[96,512]{1,0:T(8,128)(2,1)S(1)} %get-tuple-element.11.refs_0_), channel_id=1, source_target_pairs={{0,12},{4,0},{8,4},{12,8},{1,13},{5,1},{9,5},{13,9},{2,14},{6,2},{... | collective-permute-start | bytes 294920 | tf_op jit(solution)/shard_map/residual_gather/ppermute | solution.py:44
  8.3 10.5 %collective-permute-start.6 = (bf16[256,512]{1,0:T(8,128)(2,1)S(1)}, bf16[256,512]{1,0:T(8,128)(2,1)S(1)}, u32[]{:S(2)}, u32[]{:S(2)}) collective-permute-start(bf16[256,512]{1,0:T(8,128)(2,1)S(1)} %get-tuple-element.12), channel_id=1, source_target_pairs={{0,2},{2,0},{1,3},{3,1},{4,6},{6,4},{5,7},{7,5},{8,10},{10,8},{9,1... | collective-permute-start | bytes 786440 | tf_op jit(solution)/shard_map/early_weight/ppermute | solution.py:44
  14.1 2.2 %copy-start = (bf16[256,5120]{1,0:T(8,128)(2,1)S(1)}, bf16[256,5120]{1,0:T(8,128)(2,1)}, u32[]{:S(2)}) copy-start(bf16[256,5120]{1,0:T(8,128)(2,1)} %refs_1_.5) | copy-start | bytes 7864324
  14.6 4.4 %copy-start.5 = (f32[1280]{0:T(1024)S(1)}, f32[1280]{0:T(1024)}, u32[]{:S(2)}) copy-start(f32[1280]{0:T(1024)} %param.15) | copy-start | bytes 15364
  14.6 4.4 %copy-start.1 = (bf16[96,1280]{1,0:T(8,128)(2,1)S(1)}, bf16[96,1280]{1,0:T(8,128)(2,1)}, u32[]{:S(2)}) copy-start(bf16[96,1280]{1,0:T(8,128)(2,1)} %hidden_ref.1) | copy-start | bytes 737284
  14.6 1.6 %collective-permute-start.3 = (bf16[96,256]{1,0:T(8,128)(2,1)S(1)}, bf16[96,256]{1,0:T(8,128)(2,1)S(1)}, u32[]{:S(2)}, u32[]{:S(2)}) collective-permute-start(bf16[96,256]{1,0:T(8,128)(2,1)S(1)} %attention.1.refs_0_), channel_id=1, source_target_pairs={{0,1},{1,0},{2,3},{3,2},{4,5},{5,4},{6,7},{7,6},{8,9},{9,8},{10,11... | collective-permute-start | bytes 147464 | tf_op jit(solution)/shard_map/attended_swap/ppermute | solution.py:44
  14.7 4.2 %collective-permute-start.5 = (bf16[96,256]{1,0:T(8,128)(2,1)S(1)}, bf16[96,256]{1,0:T(8,128)(2,1)S(1)}, u32[]{:S(2)}, u32[]{:S(2)}) collective-permute-start(bf16[96,256]{1,0:T(8,128)(2,1)S(1)} %attention.1.refs_0_), channel_id=1, source_target_pairs={{0,2},{2,0},{1,3},{3,1},{4,6},{6,4},{5,7},{7,5},{8,10},{10,8},{9,1... | collective-permute-start | bytes 147464 | tf_op jit(solution)/shard_map/attended_swap/ppermute | solution.py:44
  16.6 7.0 %collective-permute-start.8 = (bf16[96,1024]{1,0:T(8,128)(2,1)S(1)}, bf16[96,1024]{1,0:T(8,128)(2,1)S(1)}, u32[]{:S(2)}, u32[]{:S(2)}) collective-permute-start(bf16[96,1024]{1,0:T(8,128)(2,1)S(1)} %sent_term.1), channel_id=1, source_target_pairs={{0,2},{2,0},{1,3},{3,1},{4,6},{6,4},{5,7},{7,5},{8,10},{10,8},{9,1... | collective-permute-start | bytes 589832 | tf_op jit(solution)/shard_map/projection/ppermute | solution.py:44
  18.9 1.5 %collective-permute-start.7 = (bf16[352,256]{1,0:T(8,128)(2,1)S(1)}, bf16[352,256]{1,0:T(8,128)(2,1)S(1)}, u32[]{:S(2)}, u32[]{:S(2)}) collective-permute-start(bf16[352,256]{1,0:T(8,128)(2,1)S(1)} %pack.1), channel_id=1, source_target_pairs={{0,1},{1,0},{2,3},{3,2},{4,5},{5,4},{6,7},{7,6},{8,9},{9,8},{10,11... | collective-permute-start | bytes 540680 | tf_op jit(solution)/shard_map/projection/ppermute | solution.py:44

commit v12 on v8

--- a/solution.py
+++ b/solution.py
@@ -10,7 +10,9 @@
 
 HD = 128
 LANES = 128
+ROW_TILE = 16
 VMEM_LIMIT = 12 * 1024 * 1024
+EARLY = 256
 
 IN_VMEM = pl.BlockSpec(memory_space=pltpu.VMEM)
 ANYWHERE = pl.BlockSpec(memory_space=pl.ANY)
@@ -39,6 +41,10 @@
     )
 
 
+def in_hbm(array):
+    return pltpu.with_memory_space_constraint(array, pltpu.HBM)
+
+
 def shift(array, axis, size, step):
     return lax.ppermute(array, axis, [(i, (i + step) % size) for i in range(size)])
 
@@ -49,6 +55,38 @@
 
 def gather_sources(patches, place):
     return [place] + [lax.rem(place + patches - step, patches) for step in gather_steps(patches)]
+
+
+def prepare_kernel(*refs):
+    changes, out_ref, buffers, sems = refs[:2], refs[2], refs[3:5], refs[5]
+    width = buffers[0].shape[1]
+    copies = [
+        pltpu.make_async_copy(change, buffer, sems.at[i])
+        for i, (change, buffer) in enumerate(zip(changes, buffers))
+    ]
+    for copy in copies:
+        copy.start()
+    for i, (copy, buffer) in enumerate(zip(copies, buffers)):
+        copy.wait()
+        out_ref[:, i * width : (i + 1) * width] = buffer[...].astype(jnp.bfloat16)
+
+
+def early_weight_kernel(subs, columns, early, weight_ref, out_ref, sems):
+    chip = (1 - lax.axis_index("head")) * subs
+    copies = []
+    for sub in range(subs):
+        at = pl.multiple_of((chip + sub) * columns, LANES)
+        copies.append(
+            pltpu.make_async_copy(
+                weight_ref.at[:, pl.ds(at, early)],
+                out_ref.at[:, pl.ds(sub * early, early)],
+                sems.at[sub],
+            )
+        )
+    for copy in copies:
+        copy.start()
+    for copy in copies:
+        copy.wait()
 
 
 def stage_kernel(patches, q_ref, held_k_ref, held_v_ref, products_ref, values_ref):
@@ -119,30 +157,21 @@
     out_ref[...] = hidden_ref[...].astype(jnp.float32) + gate_ref[...] * total
 
 
-def final_kernel(early, base_ref, gate_ref, *refs):
-    arrived_refs, out_ref = refs[:-1], refs[-1]
-    total = 0.0
-    for ref in arrived_refs:
-        total = total + ref[...].astype(jnp.float32)
-    if early:
-        out_ref[:, :early] = base_ref[:, :early].astype(jnp.bfloat16)
-    out_ref[:, early:] = (base_ref[:, early:] + gate_ref[:, early:] * total).astype(jnp.bfloat16)
-
-
-def early_weight_kernel(subs, columns, early, weight_ref, after_ref, out_ref, sems):
-    chip = (1 - lax.axis_index("head")) * subs
+def final_kernel(early, blocks, base_ref, gate_ref, *refs):
+    arrived_refs, (out_ref, result, sems) = refs[:-3], refs[-3:]
+    rows = base_ref.shape[0] // blocks
     copies = []
-    for sub in range(subs):
-        at = pl.multiple_of((chip + sub) * columns, LANES)
-        copies.append(
-            pltpu.make_async_copy(
-                weight_ref.at[:, pl.ds(at, early)],
-                out_ref.at[:, pl.ds(sub * early, early)],
-                sems.at[sub],
-            )
-        )
-    for copy in copies:
-        copy.start()
+    for n in range(blocks):
+        at = slice(n * rows, (n + 1) * rows)
+        total = 0.0
+        for ref in arrived_refs:
+            total = total + ref[at, :].astype(jnp.float32)
+        if early:
+            result[at, :early] = base_ref[at, :early].astype(jnp.bfloat16)
+        total = base_ref[at, early:] + gate_ref[:, early:] * total
+        result[at, early:] = total.astype(jnp.bfloat16)
+        copies.append(pltpu.make_async_copy(result.at[at, :], out_ref.at[at, :], sems.at[n]))
+        copies[n].start()
     for copy in copies:
         copy.wait()
 
@@ -183,12 +212,20 @@
         rows, width = queries.shape
         columns = hidden_in.shape[1]
 
+        early = EARLY if heads == 2 and columns % LANES == 0 and columns > 4 * LANES else 0
         with jax.named_scope("residual_gather"):
-            low = jnp.float32(-jnp.inf)
-            residual = jnp.maximum(
-                lax.pad(key_change, low, ((0, 0, 0), (0, width, 0))),
-                lax.pad(value_change, low, ((0, 0, 0), (width, 0, 0))),
-            ).astype(jnp.bfloat16)
+            residual = call(
+                prepare_kernel,
+                jax.ShapeDtypeStruct((rows, 2 * width), jnp.bfloat16),
+                [ANYWHERE] * 2,
+                IN_VMEM,
+                "prepare",
+                scratch_shapes=[
+                    pltpu.VMEM((rows, width), jnp.float32),
+                    pltpu.VMEM((rows, width), jnp.float32),
+                    pltpu.SemaphoreType.DMA((2,)),
+                ],
+            )(in_hbm(key_change), in_hbm(value_change))
             blocks = [residual] + [
                 shift(residual, "patch", patches, step) for step in gather_steps(patches)
             ]
@@ -198,19 +235,17 @@
                 shift(out_weight, "sub", subs, i) for i in range(1, subs)
             ]
 
-        early = LANES if heads == 2 and columns % LANES == 0 and columns > 4 * LANES else 0
         if early:
             with jax.named_scope("early_weight"):
                 early_weight = call(
                     functools.partial(early_weight_kernel, subs, columns, early),
                     jax.ShapeDtypeStruct((width, subs * early), jnp.bfloat16),
-                    [ANYWHERE] * 2,
+                    [ANYWHERE],
                     IN_VMEM,
                     "early_weight",
                     moved=4 * width * subs * early,
                     scratch_shapes=[pltpu.SemaphoreType.DMA((subs,))],
-                    vmem=60 * 1024 * 1024,
-                )(out_weight, residual)
+                )(in_hbm(out_weight))
                 early_weight = shift(early_weight, "head", heads, 1)
 
         def weight_and_start(i, step, skip=0):
@@ -302,13 +337,18 @@
                     "early",
                     product_flops // 2,
                 )(base, gate_row, other_attended, early_weight, packed)
+            row_blocks = 3 if rows % (3 * ROW_TILE) == 0 else 1
             return call(
-                functools.partial(final_kernel, early),
+                functools.partial(final_kernel, early, row_blocks),
                 jax.ShapeDtypeStruct((rows, columns), jnp.bfloat16),
                 [IN_VMEM] * (2 + len(arrived)),
-                IN_VMEM,
+                ANYWHERE,
                 "final",
                 moved=rows * columns * 8,
+                scratch_shapes=[
+                    pltpu.VMEM((rows, columns), jnp.bfloat16),
+                    pltpu.SemaphoreType.DMA((row_blocks,)),
+                ],
             )(base, gate_row, *arrived)
 
     in_specs = (

time: 32.4 us -> 24.4 us (0.75); the launches traced: 31.7 us -> 24.2 us
  Pallas kernels: 7.58 us -> 4.34 us
  local copies, waits for them, and re-layouts: 2.68 us -> 0.03 us
  waiting for transfers between devices: 9.56 us -> 8.06 us
  other arithmetic: 0.95 us -> 0 us
  starting transfers between devices: 10.8 us -> 11.7 us
    unnamed x14 -> x12, local copies, waits for them, and re-layouts: 2.67 us -> 0.03 us
    pallas_call x1, Pallas kernels: 2.08 us -> 0.32 us  [per_device(): call(functools.partial(sent_term_kernel, start), sent, [IN_VMEM] * len(pa...]
    pallas_call x1, Pallas kernels: 2.09 us -> 0.37 us  [per_device(): call(functools.partial(base_kernel, start), term, [IN_VMEM] * (2 + len(pa...]
    ppermute x9, waiting for transfers between devices: 9.56 us -> 8.06 us  [shift(): lax.ppermute(array, axis, [(i, (i + step) % size) for i in range(size)])]
    convert_element_type x1 -> x0, other arithmetic: 0.95 us -> none  [per_device(): residual = jnp.maximum(lax.pad(key_change, low, ((0, 0, 0), (0, width, 0)...]
    pallas_call x1 -> x2, Pallas kernels: 0.77 us -> 1.7 us  [the longest x1 0.96 us: per_device(): call(prepare_kernel, jax.ShapeDtypeStruct((rows, 2 * width), jnp.bfloat16...]
    ppermute x9, starting transfers between devices: 10.8 us -> 11.7 us  [shift(): lax.ppermute(array, axis, [(i, (i + step) % size) for i in range(size)])]
    pallas_call x1, Pallas kernels: 1.71 us -> 0.99 us  [per_device(): call(functools.partial(early_weight_kernel, subs, columns, early), jax.Sh...]
  transfers between devices with their start and end apart: 9 -> 9, of which waited for: 3 -> 4; matrix products, arithmetic and copies ran while one was open for 3% -> 0% of each run, Pallas kernels for 22% -> 15%
where the time goes in v12:
time: 24.4 us; the launch traced here: 24.2 us
  starting transfers between devices  11.7 us (48%)
  waiting for transfers between devices  8.06 us (33%)
  Pallas kernels  4.34 us (18%)
    ppermute x9, starting transfers between devices, shift(): lax.ppermute(array, axis, [(i, (i + step) % size) for i in range(size)])  11.7 us
    ppermute x9, waiting for transfers between devices, shift(): lax.ppermute(array, axis, [(i, (i + step) % size) for i in range(size)])  8.06 us
    pallas_call x1, Pallas kernels, per_device(): call(functools.partial(early_weight_kernel, subs, columns, early), jax.Sh...  0.99 us
    pallas_call x1, Pallas kernels, per_device(): call(prepare_kernel, jax.ShapeDtypeStruct((rows, 2 * width), jnp.bfloat16...  0.96 us
    pallas_call x1, Pallas kernels, per_device(): call(functools.partial(final_kernel, early, row_blocks), jax.ShapeDtypeSt...  0.74 us
    pallas_call x1, Pallas kernels, per_device(): call(functools.partial(attention_kernel, 1.0 / math.sqrt(HD)), jax.ShapeD...  0.53 us
  transfers between devices with their start and end apart: 9, of which 4 were waited for; matrix products, arithmetic and copies ran while one was open for 0% of the time, Pallas kernels for 15%

profile of v12, /device:TPU:0, one launch (start us, length us, event | category | flops | bytes accessed | tf_op | source)
XLA Modules:
  0.0 24.2 jit_solution(7917674457057809546)
XLA Ops:
  0.0 0.0 copy-start.4
  0.0 0.0 copy-start.3
  0.0 0.0 copy-start.2
  0.0 0.5 %collective-permute-start.4 = (bf16[256,5120]{1,0:T(8,128)(2,1)}, bf16[256,5120]{1,0:T(8,128)(2,1)S(1)}, u32[]{:S(2)}, u32[]{:S(2)}) collective-permute-start(bf16[256,5120]{1,0:T(8,128)(2,1)} %refs_1_.5), channel_id=1, source_target_pairs={{0,1},{1,0},{2,3},{3,2},{4,5},{5,4},{6,7},{7,6},{8,9},{9,8},{10,11... | collective-permute-start | bytes 7864328 | tf_op jit(solution)/shard_map/weight_swap/ppermute | solution.py:49
  0.5 1.0 %prepare.1.refs_0_ = bf16[96,512]{1,0:T(8,128)(2,1)S(1)} custom-call(f32[96,256]{1,0:T(8,128)} %refs_0_.1, f32[96,256]{1,0:T(8,128)} %refs_1_.3), custom_call_target="tpu_custom_call" | custom-call | tf_op jit(solution)/shard_map/residual_gather/prepare/pallas_call | solution.py:217
  1.5 2.8 %collective-permute-start.2 = (bf16[96,512]{1,0:T(8,128)(2,1)S(1)}, bf16[96,512]{1,0:T(8,128)(2,1)S(1)}, u32[]{:S(2)}, u32[]{:S(2)}) collective-permute-start(bf16[96,512]{1,0:T(8,128)(2,1)S(1)} %prepare.1.refs_0_), channel_id=1, source_target_pairs={{0,4},{4,8},{8,12},{12,0},{1,5},{5,9},{9,13},{13,1},{2,6},{6,10},{... | collective-permute-start | bytes 294920 | tf_op jit(solution)/shard_map/residual_gather/ppermute | solution.py:49
  4.3 2.6 %collective-permute-start.1 = (bf16[96,512]{1,0:T(8,128)(2,1)S(1)}, bf16[96,512]{1,0:T(8,128)(2,1)S(1)}, u32[]{:S(2)}, u32[]{:S(2)}) collective-permute-start(bf16[96,512]{1,0:T(8,128)(2,1)S(1)} %prepare.1.refs_0_), channel_id=1, source_target_pairs={{0,8},{4,12},{8,0},{12,4},{1,9},{5,13},{9,1},{13,5},{2,10},{6,14},... | collective-permute-start | bytes 294920 | tf_op jit(solution)/shard_map/residual_gather/ppermute | solution.py:49
  6.9 1.3 %collective-permute-start = (bf16[96,512]{1,0:T(8,128)(2,1)S(1)}, bf16[96,512]{1,0:T(8,128)(2,1)S(1)}, u32[]{:S(2)}, u32[]{:S(2)}) collective-permute-start(bf16[96,512]{1,0:T(8,128)(2,1)S(1)} %prepare.1.refs_0_), channel_id=1, source_target_pairs={{0,12},{4,0},{8,4},{12,8},{1,13},{5,1},{9,5},{13,9},{2,14},{6,2},{... | collective-permute-start | bytes 294920 | tf_op jit(solution)/shard_map/residual_gather/ppermute | solution.py:49
  8.2 1.0 %early_weight.1 = bf16[256,512]{1,0:T(8,128)(2,1)S(1)} custom-call(bf16[256,5120]{1,0:T(8,128)(2,1)} %refs_1_.5), custom_call_target="tpu_custom_call" | custom-call | bytes 524288 | tf_op jit(solution)/shard_map/early_weight/early_weight/pallas_call | solution.py:240
  9.2 1.6 %collective-permute-start.6 = (bf16[256,512]{1,0:T(8,128)(2,1)S(1)}, bf16[256,512]{1,0:T(8,128)(2,1)S(1)}, u32[]{:S(2)}, u32[]{:S(2)}) collective-permute-start(bf16[256,512]{1,0:T(8,128)(2,1)S(1)} %early_weight.1), channel_id=1, source_target_pairs={{0,2},{2,0},{1,3},{3,1},{4,6},{6,4},{5,7},{7,5},{8,10},{10,8},{9,1... | collective-permute-start | bytes 786440 | tf_op jit(solution)/shard_map/early_weight/ppermute | solution.py:49
  10.8 0.0 copy-done.4
  10.8 0.0 copy-done.3
  10.8 0.0 copy-done.2
  10.8 0.2 stage.1
  11.0 0.0 collective-permute-done.2.refs_3_
  11.0 2.9 %collective-permute-done.1.refs_2_ = bf16[96,512]{1,0:T(8,128)(2,1)S(1)} collective-permute-done((bf16[96,512]{1,0:T(8,128)(2,1)S(1)}, bf16[96,512]{1,0:T(8,128)(2,1)S(1)}, u32[]{:S(2)}, u32[]{:S(2)}) %collective-permute-start.1) | collective-permute-done | bytes 98336 | tf_op jit(solution)/shard_map/residual_gather/ppermute | solution.py:49
  13.9 0.0 collective-permute-done.refs_1_
  13.9 0.0 copy-start
  13.9 0.5 %attention.1.refs_0_ = bf16[96,256]{1,0:T(8,128)(2,1)S(1)} custom-call(bf16[96,256]{1,0:T(8,128)(2,1)S(1)} %copy-done.4, f32[2,96,384]{2,1,0:T(8,128)S(1)} %get-tuple-element.7.products_ref, bf16[384,256]{1,0:T(8,128)(2,1)S(1)} %get-tuple-element.8.values_ref, bf16[96,512]{1,0:T(8,128)(2,1)S(1)} %prepare.1.refs_0_, ...), custom_call_target="tpu_custom_call" | custom-call | flops 2000000000 | tf_op jit(solution)/shard_map/attention/attention/pallas_call | solution.py:281
  14.5 0.0 copy-start.5
  14.5 0.0 copy-start.1
  14.5 0.1 collective-permute-start.3
  14.6 1.6 %collective-permute-start.5 = (bf16[96,256]{1,0:T(8,128)(2,1)S(1)}, bf16[96,256]{1,0:T(8,128)(2,1)S(1)}, u32[]{:S(2)}, u32[]{:S(2)}) collective-permute-start(bf16[96,256]{1,0:T(8,128)(2,1)S(1)} %attention.1.refs_0_), channel_id=1, source_target_pairs={{0,2},{2,0},{1,3},{3,1},{4,6},{6,4},{5,7},{7,5},{8,10},{10,8},{9,1... | collective-permute-start | bytes 147464 | tf_op jit(solution)/shard_map/attended_swap/ppermute | solution.py:49
  16.1 0.0 collective-permute-done.3.refs_2_
  16.1 0.0 collective-permute-done.4.refs_3_
  16.1 0.0 copy-done
  16.1 0.3 %sent_term.1 = bf16[96,1024]{1,0:T(8,128)(2,1)S(1)} custom-call(bf16[96,256]{1,0:T(8,128)(2,1)S(1)} %attention.1.refs_0_, bf16[256,5120]{1,0:T(8,128)(2,1)S(1)} %copy-done, bf16[96,256]{1,0:T(8,128)(2,1)S(1)} %collective-permute-done.3.refs_2_, bf16[256,5120]{1,0:T(8,128)(2,1)S(1)} %collective-permute-done.4.refs_3_), custom_call_target="tpu_custom_call" | custom-call | flops 125829120 | tf_op jit(solution)/shard_map/projection/sent_term/pallas_call | solution.py:304
  16.5 1.2 %collective-permute-start.8 = (bf16[96,1024]{1,0:T(8,128)(2,1)S(1)}, bf16[96,1024]{1,0:T(8,128)(2,1)S(1)}, u32[]{:S(2)}, u32[]{:S(2)}) collective-permute-start(bf16[96,1024]{1,0:T(8,128)(2,1)S(1)} %sent_term.1), channel_id=1, source_target_pairs={{0,2},{2,0},{1,3},{3,1},{4,6},{6,4},{5,7},{7,5},{8,10},{10,8},{9,1... | collective-permute-start | bytes 589832 | tf_op jit(solution)/shard_map/projection/ppermute | solution.py:49
  17.6 1.1 %collective-permute-done.5.attended_ref = bf16[96,256]{1,0:T(8,128)(2,1)S(1)} collective-permute-done((bf16[96,256]{1,0:T(8,128)(2,1)S(1)}, bf16[96,256]{1,0:T(8,128)(2,1)S(1)}, u32[]{:S(2)}, u32[]{:S(2)}) %collective-permute-start.5) | collective-permute-done | bytes 49184 | tf_op jit(solution)/shard_map/attended_swap/ppermute | solution.py:49
  18.7 0.0 collective-permute-done.6.weight_ref
  18.7 0.1 collective-permute-start.7
  18.8 0.0 copy-done.5
  18.8 0.0 copy-done.1
  18.8 0.4 %base.1.base_ref = f32[96,1280]{1,0:T(8,128)S(1)} custom-call(bf16[96,1280]{1,0:T(8,128)(2,1)S(1)} %copy-done.1, f32[1,1280]{1,0:T(1,128)S(1)} %reshape.3.gate_ref, bf16[96,256]{1,0:T(8,128)(2,1)S(1)} %attention.1.refs_0_, bf16[256,5120]{1,0:T(8,128)(2,1)S(1)} %copy-done, bf16[96,256]{1,0:T(8,128)(2,1)S(1)} %collective-permute-done.3.refs_2_, ...), custom_call_target="tpu_custom_call" | custom-call | flops 125829120 | tf_op jit(solution)/shard_map/projection/base/pallas_call | solution.py:315
  19.2 1.0 %collective-permute-done.7.packed_ref = bf16[352,256]{1,0:T(8,128)(2,1)S(1)} collective-permute-done((bf16[352,256]{1,0:T(8,128)(2,1)S(1)}, bf16[352,256]{1,0:T(8,128)(2,1)S(1)}, u32[]{:S(2)}, u32[]{:S(2)}) %collective-permute-start.7) | collective-permute-done | bytes 180256 | tf_op jit(solution)/shard_map/projection/ppermute | solution.py:49
  20.2 0.2 early.1.base_ref
  20.4 3.1 %collective-permute-done.8.refs_0_ = bf16[96,1024]{1,0:T(8,128)(2,1)S(1)} collective-permute-done((bf16[96,1024]{1,0:T(8,128)(2,1)S(1)}, bf16[96,1024]{1,0:T(8,128)(2,1)S(1)}, u32[]{:S(2)}, u32[]{:S(2)}) %collective-permute-start.8) | collective-permute-done | bytes 196640 | tf_op jit(solution)/shard_map/projection/ppermute | solution.py:49
  23.5 0.7 %final.1 = bf16[96,1280]{1,0:T(8,128)(2,1)} custom-call(f32[96,1280]{1,0:T(8,128)S(1)} %early.1.base_ref, f32[1,1280]{1,0:T(1,128)S(1)} %reshape.3.gate_ref, bf16[96,1024]{1,0:T(8,128)(2,1)S(1)} %collective-permute-done.8.refs_0_), custom_call_target="tpu_custom_call" | custom-call | bytes 983040 | tf_op jit(solution)/shard_map/projection/final/pallas_call | solution.py:341
  (2 shorter events, 0.0 us)
Async XLA Ops:
  0.0 10.8 %copy-start.4 = (bf16[96,256]{1,0:T(8,128)(2,1)S(1)}, bf16[96,256]{1,0:T(8,128)(2,1)}, u32[]{:S(2)}) copy-start(bf16[96,256]{1,0:T(8,128)(2,1)} %q_ref.3) | copy-start | bytes 147460
  0.0 10.8 %copy-start.3 = (bf16[384,256]{1,0:T(8,128)(2,1)S(1)}, bf16[384,256]{1,0:T(8,128)(2,1)}, u32[]{:S(2)}) copy-start(bf16[384,256]{1,0:T(8,128)(2,1)} %held_v_ref.1) | copy-start | bytes 589828
  0.0 10.8 %copy-start.2 = (bf16[384,256]{1,0:T(8,128)(2,1)S(1)}, bf16[384,256]{1,0:T(8,128)(2,1)}, u32[]{:S(2)}) copy-start(bf16[384,256]{1,0:T(8,128)(2,1)} %held_k_ref.1) | copy-start | bytes 589828
  0.0 16.1 %collective-permute-start.4 = (bf16[256,5120]{1,0:T(8,128)(2,1)}, bf16[256,5120]{1,0:T(8,128)(2,1)S(1)}, u32[]{:S(2)}, u32[]{:S(2)}) collective-permute-start(bf16[256,5120]{1,0:T(8,128)(2,1)} %refs_1_.5), channel_id=1, source_target_pairs={{0,1},{1,0},{2,3},{3,2},{4,5},{5,4},{6,7},{7,6},{8,9},{9,8},{10,11... | collective-permute-start | bytes 7864328 | tf_op jit(solution)/shard_map/weight_swap/ppermute | solution.py:49
  1.5 9.5 %collective-permute-start.2 = (bf16[96,512]{1,0:T(8,128)(2,1)S(1)}, bf16[96,512]{1,0:T(8,128)(2,1)S(1)}, u32[]{:S(2)}, u32[]{:S(2)}) collective-permute-start(bf16[96,512]{1,0:T(8,128)(2,1)S(1)} %prepare.1.refs_0_), channel_id=1, source_target_pairs={{0,4},{4,8},{8,12},{12,0},{1,5},{5,9},{9,13},{13,1},{2,6},{6,10},{... | collective-permute-start | bytes 294920 | tf_op jit(solution)/shard_map/residual_gather/ppermute | solution.py:49
  4.3 9.6 %collective-permute-start.1 = (bf16[96,512]{1,0:T(8,128)(2,1)S(1)}, bf16[96,512]{1,0:T(8,128)(2,1)S(1)}, u32[]{:S(2)}, u32[]{:S(2)}) collective-permute-start(bf16[96,512]{1,0:T(8,128)(2,1)S(1)} %prepare.1.refs_0_), channel_id=1, source_target_pairs={{0,8},{4,12},{8,0},{12,4},{1,9},{5,13},{9,1},{13,5},{2,10},{6,14},... | collective-permute-start | bytes 294920 | tf_op jit(solution)/shard_map/residual_gather/ppermute | solution.py:49
  6.9 7.1 %collective-permute-start = (bf16[96,512]{1,0:T(8,128)(2,1)S(1)}, bf16[96,512]{1,0:T(8,128)(2,1)S(1)}, u32[]{:S(2)}, u32[]{:S(2)}) collective-permute-start(bf16[96,512]{1,0:T(8,128)(2,1)S(1)} %prepare.1.refs_0_), channel_id=1, source_target_pairs={{0,12},{4,0},{8,4},{12,8},{1,13},{5,1},{9,5},{13,9},{2,14},{6,2},{... | collective-permute-start | bytes 294920 | tf_op jit(solution)/shard_map/residual_gather/ppermute | solution.py:49
  9.2 9.5 %collective-permute-start.6 = (bf16[256,512]{1,0:T(8,128)(2,1)S(1)}, bf16[256,512]{1,0:T(8,128)(2,1)S(1)}, u32[]{:S(2)}, u32[]{:S(2)}) collective-permute-start(bf16[256,512]{1,0:T(8,128)(2,1)S(1)} %early_weight.1), channel_id=1, source_target_pairs={{0,2},{2,0},{1,3},{3,1},{4,6},{6,4},{5,7},{7,5},{8,10},{10,8},{9,1... | collective-permute-start | bytes 786440 | tf_op jit(solution)/shard_map/early_weight/ppermute | solution.py:49
  13.9 2.2 %copy-start = (bf16[256,5120]{1,0:T(8,128)(2,1)S(1)}, bf16[256,5120]{1,0:T(8,128)(2,1)}, u32[]{:S(2)}) copy-start(bf16[256,5120]{1,0:T(8,128)(2,1)} %refs_1_.5) | copy-start | bytes 7864324
  14.5 4.4 %copy-start.5 = (f32[1280]{0:T(1024)S(1)}, f32[1280]{0:T(1024)}, u32[]{:S(2)}) copy-start(f32[1280]{0:T(1024)} %param.15) | copy-start | bytes 15364
  14.5 4.4 %copy-start.1 = (bf16[96,1280]{1,0:T(8,128)(2,1)S(1)}, bf16[96,1280]{1,0:T(8,128)(2,1)}, u32[]{:S(2)}) copy-start(bf16[96,1280]{1,0:T(8,128)(2,1)} %hidden_ref.1) | copy-start | bytes 737284
  14.5 1.6 %collective-permute-start.3 = (bf16[96,256]{1,0:T(8,128)(2,1)S(1)}, bf16[96,256]{1,0:T(8,128)(2,1)S(1)}, u32[]{:S(2)}, u32[]{:S(2)}) collective-permute-start(bf16[96,256]{1,0:T(8,128)(2,1)S(1)} %attention.1.refs_0_), channel_id=1, source_target_pairs={{0,1},{1,0},{2,3},{3,2},{4,5},{5,4},{6,7},{7,6},{8,9},{9,8},{10,11... | collective-permute-start | bytes 147464 | tf_op jit(solution)/shard_map/attended_swap/ppermute | solution.py:49
  14.6 4.2 %collective-permute-start.5 = (bf16[96,256]{1,0:T(8,128)(2,1)S(1)}, bf16[96,256]{1,0:T(8,128)(2,1)S(1)}, u32[]{:S(2)}, u32[]{:S(2)}) collective-permute-start(bf16[96,256]{1,0:T(8,128)(2,1)S(1)} %attention.1.refs_0_), channel_id=1, source_target_pairs={{0,2},{2,0},{1,3},{3,1},{4,6},{6,4},{5,7},{7,5},{8,10},{10,8},{9,1... | collective-permute-start | bytes 147464 | tf_op jit(solution)/shard_map/attended_swap/ppermute | solution.py:49
  16.5 7.0 %collective-permute-start.8 = (bf16[96,1024]{1,0:T(8,128)(2,1)S(1)}, bf16[96,1024]{1,0:T(8,128)(2,1)S(1)}, u32[]{:S(2)}, u32[]{:S(2)}) collective-permute-start(bf16[96,1024]{1,0:T(8,128)(2,1)S(1)} %sent_term.1), channel_id=1, source_target_pairs={{0,2},{2,0},{1,3},{3,1},{4,6},{6,4},{5,7},{7,5},{8,10},{10,8},{9,1... | collective-permute-start | bytes 589832 | tf_op jit(solution)/shard_map/projection/ppermute | solution.py:49
  18.7 1.5 %collective-permute-start.7 = (bf16[352,256]{1,0:T(8,128)(2,1)S(1)}, bf16[352,256]{1,0:T(8,128)(2,1)S(1)}, u32[]{:S(2)}, u32[]{:S(2)}) collective-permute-start(bf16[352,256]{1,0:T(8,128)(2,1)S(1)} %pack.1), channel_id=1, source_target_pairs={{0,1},{1,0},{2,3},{3,2},{4,5},{5,4},{6,7},{7,6},{8,9},{9,8},{10,11... | collective-permute-start | bytes 540680 | tf_op jit(solution)/shard_map/projection/ppermute | solution.py:49

commit v13 on v12

--- a/solution.py
+++ b/solution.py
@@ -55,20 +55,6 @@
 
 def gather_sources(patches, place):
     return [place] + [lax.rem(place + patches - step, patches) for step in gather_steps(patches)]
-
-
-def prepare_kernel(*refs):
-    changes, out_ref, buffers, sems = refs[:2], refs[2], refs[3:5], refs[5]
-    width = buffers[0].shape[1]
-    copies = [
-        pltpu.make_async_copy(change, buffer, sems.at[i])
-        for i, (change, buffer) in enumerate(zip(changes, buffers))
-    ]
-    for copy in copies:
-        copy.start()
-    for i, (copy, buffer) in enumerate(zip(copies, buffers)):
-        copy.wait()
-        out_ref[:, i * width : (i + 1) * width] = buffer[...].astype(jnp.bfloat16)
 
 
 def early_weight_kernel(subs, columns, early, weight_ref, out_ref, sems):
@@ -157,25 +143,6 @@
     out_ref[...] = hidden_ref[...].astype(jnp.float32) + gate_ref[...] * total
 
 
-def final_kernel(early, blocks, base_ref, gate_ref, *refs):
-    arrived_refs, (out_ref, result, sems) = refs[:-3], refs[-3:]
-    rows = base_ref.shape[0] // blocks
-    copies = []
-    for n in range(blocks):
-        at = slice(n * rows, (n + 1) * rows)
-        total = 0.0
-        for ref in arrived_refs:
-            total = total + ref[at, :].astype(jnp.float32)
-        if early:
-            result[at, :early] = base_ref[at, :early].astype(jnp.bfloat16)
-        total = base_ref[at, early:] + gate_ref[:, early:] * total
-        result[at, early:] = total.astype(jnp.bfloat16)
-        copies.append(pltpu.make_async_copy(result.at[at, :], out_ref.at[at, :], sems.at[n]))
-        copies[n].start()
-    for copy in copies:
-        copy.wait()
-
-
 def pack_kernel(early, attended_ref, weight_ref, out_ref):
     rows, width = attended_ref.shape
     for i in range(width // early):
@@ -214,18 +181,11 @@
 
         early = EARLY if heads == 2 and columns % LANES == 0 and columns > 4 * LANES else 0
         with jax.named_scope("residual_gather"):
-            residual = call(
-                prepare_kernel,
-                jax.ShapeDtypeStruct((rows, 2 * width), jnp.bfloat16),
-                [ANYWHERE] * 2,
-                IN_VMEM,
-                "prepare",
-                scratch_shapes=[
-                    pltpu.VMEM((rows, width), jnp.float32),
-                    pltpu.VMEM((rows, width), jnp.float32),
-                    pltpu.SemaphoreType.DMA((2,)),
-                ],
-            )(in_hbm(key_change), in_hbm(value_change))
+            low = jnp.float32(-jnp.inf)
+            residual = jnp.maximum(
+                lax.pad(key_change, low, ((0, 0, 0), (0, width, 0))),
+                lax.pad(value_change, low, ((0, 0, 0), (width, 0, 0))),
+            ).astype(jnp.bfloat16)
             blocks = [residual] + [
                 shift(residual, "patch", patches, step) for step in gather_steps(patches)
             ]
@@ -337,19 +297,9 @@
                     "early",
                     product_flops // 2,
                 )(base, gate_row, other_attended, early_weight, packed)
-            row_blocks = 3 if rows % (3 * ROW_TILE) == 0 else 1
-            return call(
-                functools.partial(final_kernel, early, row_blocks),
-                jax.ShapeDtypeStruct((rows, columns), jnp.bfloat16),
-                [IN_VMEM] * (2 + len(arrived)),
-                ANYWHERE,
-                "final",
-                moved=rows * columns * 8,
-                scratch_shapes=[
-                    pltpu.VMEM((rows, columns), jnp.bfloat16),
-                    pltpu.SemaphoreType.DMA((row_blocks,)),
-                ],
-            )(base, gate_row, *arrived)
+            total = functools.reduce(jnp.add, [x.astype(jnp.float32) for x in arrived])
+            total = lax.pad(total, jnp.float32(0), ((0, 0, 0), (early, 0, 0)))
+            return (base + gate_row * total).astype(jnp.bfloat16)
 
     in_specs = (
         P(("groups", "patch"), ("head", "sub")),

time: 24.4 us -> 24.4 us (level)
  Pallas kernels: 4.34 us -> 2.63 us
  other arithmetic: 0 us -> 1.7 us
    convert_element_type x0 -> x2, other arithmetic: none -> 1.7 us  [the longest x1 0.95 us: per_device(): residual = jnp.maximum(lax.pad(key_change, low, ((0, 0, 0), (0, width, 0)...]
    pallas_call x2 -> x0, Pallas kernels: 1.7 us -> none  [the longest x1 0.96 us: per_device(): call(prepare_kernel, jax.ShapeDtypeStruct((rows, 2 * width), jnp.bfloat16...]
  transfers between devices with their start and end apart: 9 -> 9, of which waited for: 4 -> 4; matrix products, arithmetic and copies ran while one was open for 0% -> 4% of each run, Pallas kernels for 15% -> 11%
where the time goes in v13:
time: 24.4 us; the launch traced here: 24.2 us
  starting transfers between devices  11.7 us (48%)
  waiting for transfers between devices  8.06 us (33%)
  Pallas kernels  2.63 us (11%)
  other arithmetic  1.7 us (7%)
    ppermute x9, starting transfers between devices, shift(): lax.ppermute(array, axis, [(i, (i + step) % size) for i in range(size)])  11.7 us
    ppermute x9, waiting for transfers between devices, shift(): lax.ppermute(array, axis, [(i, (i + step) % size) for i in range(size)])  8.06 us
    pallas_call x1, Pallas kernels, per_device(): call(functools.partial(early_weight_kernel, subs, columns, early), jax.Sh...  0.99 us
    convert_element_type x1, other arithmetic, per_device(): residual = jnp.maximum(lax.pad(key_change, low, ((0, 0, 0), (0, width, 0)...  0.95 us
    convert_element_type x1, other arithmetic, per_device(): return (base + gate_row * total).astype(jnp.bfloat16)  0.75 us
    pallas_call x1, Pallas kernels, per_device(): call(functools.partial(attention_kernel, 1.0 / math.sqrt(HD)), jax.ShapeD...  0.53 us
  transfers between devices with their start and end apart: 9, of which 4 were waited for; matrix products, arithmetic and copies ran while one was open for 4% of the time, Pallas kernels for 11%

profile of v13, /device:TPU:0, one launch (start us, length us, event | category | flops | bytes accessed | tf_op | source)
XLA Modules:
  0.0 24.2 jit_solution(4483871727718901374)
XLA Ops:
  0.0 0.0 copy-start.4
  0.0 0.0 copy-start.3
  0.0 0.0 copy-start.2
  0.0 0.5 %collective-permute-start.4 = (bf16[256,5120]{1,0:T(8,128)(2,1)}, bf16[256,5120]{1,0:T(8,128)(2,1)S(1)}, u32[]{:S(2)}, u32[]{:S(2)}) collective-permute-start(bf16[256,5120]{1,0:T(8,128)(2,1)} %refs_1_.3), channel_id=1, source_target_pairs={{0,1},{1,0},{2,3},{3,2},{4,5},{5,4},{6,7},{7,6},{8,9},{9,8},{10,11... | collective-permute-start | bytes 7864328 | tf_op jit(solution)/shard_map/weight_swap/ppermute | solution.py:49
  0.5 1.0 %maximum_convert_fusion.refs_0_ = bf16[96,512]{1,0:T(8,128)(2,1)S(1)} fusion(f32[96,256]{1,0:T(8,128)} %param.12, f32[96,256]{1,0:T(8,128)} %param.11), kind=kLoop, calls=%fused_computation.1 | loop fusion | flops 196608 | bytes 294912 | tf_op jit(solution)/shard_map/residual_gather/convert_element_type | solution.py:188
  1.5 2.8 %collective-permute-start.2 = (bf16[96,512]{1,0:T(8,128)(2,1)S(1)}, bf16[96,512]{1,0:T(8,128)(2,1)S(1)}, u32[]{:S(2)}, u32[]{:S(2)}) collective-permute-start(bf16[96,512]{1,0:T(8,128)(2,1)S(1)} %maximum_convert_fusion.refs_0_), channel_id=1, source_target_pairs={{0,4},{4,8},{8,12},{12,0},{1,5},{5,9},{9,13},{13,1},{2,6},{6,10},{... | collective-permute-start | bytes 294920 | tf_op jit(solution)/shard_map/residual_gather/ppermute | solution.py:49
  4.3 2.6 %collective-permute-start.1 = (bf16[96,512]{1,0:T(8,128)(2,1)S(1)}, bf16[96,512]{1,0:T(8,128)(2,1)S(1)}, u32[]{:S(2)}, u32[]{:S(2)}) collective-permute-start(bf16[96,512]{1,0:T(8,128)(2,1)S(1)} %maximum_convert_fusion.refs_0_), channel_id=1, source_target_pairs={{0,8},{4,12},{8,0},{12,4},{1,9},{5,13},{9,1},{13,5},{2,10},{6,14},... | collective-permute-start | bytes 294920 | tf_op jit(solution)/shard_map/residual_gather/ppermute | solution.py:49
  6.8 1.3 %collective-permute-start = (bf16[96,512]{1,0:T(8,128)(2,1)S(1)}, bf16[96,512]{1,0:T(8,128)(2,1)S(1)}, u32[]{:S(2)}, u32[]{:S(2)}) collective-permute-start(bf16[96,512]{1,0:T(8,128)(2,1)S(1)} %maximum_convert_fusion.refs_0_), channel_id=1, source_target_pairs={{0,12},{4,0},{8,4},{12,8},{1,13},{5,1},{9,5},{13,9},{2,14},{6,2},{... | collective-permute-start | bytes 294920 | tf_op jit(solution)/shard_map/residual_gather/ppermute | solution.py:49
  8.2 1.0 %early_weight.1 = bf16[256,512]{1,0:T(8,128)(2,1)S(1)} custom-call(bf16[256,5120]{1,0:T(8,128)(2,1)} %refs_1_.3), custom_call_target="tpu_custom_call" | custom-call | bytes 524288 | tf_op jit(solution)/shard_map/early_weight/early_weight/pallas_call | solution.py:200
  9.2 1.6 %collective-permute-start.6 = (bf16[256,512]{1,0:T(8,128)(2,1)S(1)}, bf16[256,512]{1,0:T(8,128)(2,1)S(1)}, u32[]{:S(2)}, u32[]{:S(2)}) collective-permute-start(bf16[256,512]{1,0:T(8,128)(2,1)S(1)} %early_weight.1), channel_id=1, source_target_pairs={{0,2},{2,0},{1,3},{3,1},{4,6},{6,4},{5,7},{7,5},{8,10},{10,8},{9,1... | collective-permute-start | bytes 786440 | tf_op jit(solution)/shard_map/early_weight/ppermute | solution.py:49
  10.7 0.0 copy-done.4
  10.7 0.0 copy-done.3
  10.8 0.0 copy-done.2
  10.8 0.2 stage.1
  11.0 0.0 collective-permute-done.2.refs_3_
  11.0 2.9 %collective-permute-done.1.refs_2_ = bf16[96,512]{1,0:T(8,128)(2,1)S(1)} collective-permute-done((bf16[96,512]{1,0:T(8,128)(2,1)S(1)}, bf16[96,512]{1,0:T(8,128)(2,1)S(1)}, u32[]{:S(2)}, u32[]{:S(2)}) %collective-permute-start.1) | collective-permute-done | bytes 98336 | tf_op jit(solution)/shard_map/residual_gather/ppermute | solution.py:49
  13.9 0.0 collective-permute-done.refs_1_
  13.9 0.0 copy-start
  13.9 0.5 %attention.1.refs_0_ = bf16[96,256]{1,0:T(8,128)(2,1)S(1)} custom-call(bf16[96,256]{1,0:T(8,128)(2,1)S(1)} %copy-done.4, f32[2,96,384]{2,1,0:T(8,128)S(1)} %get-tuple-element.7.products_ref, bf16[384,256]{1,0:T(8,128)(2,1)S(1)} %get-tuple-element.8.values_ref, bf16[96,512]{1,0:T(8,128)(2,1)S(1)} %maximum_convert_fusion.refs_0_, ...), custom_call_target="tpu_custom_call" | custom-call | flops 2000000000 | tf_op jit(solution)/shard_map/attention/attention/pallas_call | solution.py:241
  14.4 0.0 copy-start.5
  14.5 0.0 copy-start.1
  14.5 0.1 collective-permute-start.3
  14.5 1.6 %collective-permute-start.5 = (bf16[96,256]{1,0:T(8,128)(2,1)S(1)}, bf16[96,256]{1,0:T(8,128)(2,1)S(1)}, u32[]{:S(2)}, u32[]{:S(2)}) collective-permute-start(bf16[96,256]{1,0:T(8,128)(2,1)S(1)} %attention.1.refs_0_), channel_id=1, source_target_pairs={{0,2},{2,0},{1,3},{3,1},{4,6},{6,4},{5,7},{7,5},{8,10},{10,8},{9,1... | collective-permute-start | bytes 147464 | tf_op jit(solution)/shard_map/attended_swap/ppermute | solution.py:49
  16.1 0.0 collective-permute-done.3.refs_2_
  16.1 0.0 collective-permute-done.4.refs_3_
  16.1 0.0 copy-done
  16.1 0.3 %sent_term.1 = bf16[96,1024]{1,0:T(8,128)(2,1)S(1)} custom-call(bf16[96,256]{1,0:T(8,128)(2,1)S(1)} %attention.1.refs_0_, bf16[256,5120]{1,0:T(8,128)(2,1)S(1)} %copy-done, bf16[96,256]{1,0:T(8,128)(2,1)S(1)} %collective-permute-done.3.refs_2_, bf16[256,5120]{1,0:T(8,128)(2,1)S(1)} %collective-permute-done.4.refs_3_), custom_call_target="tpu_custom_call" | custom-call | flops 125829120 | tf_op jit(solution)/shard_map/projection/sent_term/pallas_call | solution.py:264
  16.4 1.2 %collective-permute-start.8 = (bf16[96,1024]{1,0:T(8,128)(2,1)S(1)}, bf16[96,1024]{1,0:T(8,128)(2,1)S(1)}, u32[]{:S(2)}, u32[]{:S(2)}) collective-permute-start(bf16[96,1024]{1,0:T(8,128)(2,1)S(1)} %sent_term.1), channel_id=1, source_target_pairs={{0,2},{2,0},{1,3},{3,1},{4,6},{6,4},{5,7},{7,5},{8,10},{10,8},{9,1... | collective-permute-start | bytes 589832 | tf_op jit(solution)/shard_map/projection/ppermute | solution.py:49
  17.6 1.1 %collective-permute-done.5.attended_ref = bf16[96,256]{1,0:T(8,128)(2,1)S(1)} collective-permute-done((bf16[96,256]{1,0:T(8,128)(2,1)S(1)}, bf16[96,256]{1,0:T(8,128)(2,1)S(1)}, u32[]{:S(2)}, u32[]{:S(2)}) %collective-permute-start.5) | collective-permute-done | bytes 49184 | tf_op jit(solution)/shard_map/attended_swap/ppermute | solution.py:49
  18.7 0.0 collective-permute-done.6.weight_ref
  18.7 0.1 collective-permute-start.7
  18.8 0.0 copy-done.5
  18.8 0.0 copy-done.1
  18.8 0.4 %base.1.base_ref = f32[96,1280]{1,0:T(8,128)S(1)} custom-call(bf16[96,1280]{1,0:T(8,128)(2,1)S(1)} %copy-done.1, f32[1,1280]{1,0:T(1,128)S(1)} %reshape.4.gate_ref, bf16[96,256]{1,0:T(8,128)(2,1)S(1)} %attention.1.refs_0_, bf16[256,5120]{1,0:T(8,128)(2,1)S(1)} %copy-done, bf16[96,256]{1,0:T(8,128)(2,1)S(1)} %collective-permute-done.3.refs_2_, ...), custom_call_target="tpu_custom_call" | custom-call | flops 125829120 | tf_op jit(solution)/shard_map/projection/base/pallas_call | solution.py:275
  19.2 1.0 %collective-permute-done.7.packed_ref = bf16[352,256]{1,0:T(8,128)(2,1)S(1)} collective-permute-done((bf16[352,256]{1,0:T(8,128)(2,1)S(1)}, bf16[352,256]{1,0:T(8,128)(2,1)S(1)}, u32[]{:S(2)}, u32[]{:S(2)}) %collective-permute-start.7) | collective-permute-done | bytes 180256 | tf_op jit(solution)/shard_map/projection/ppermute | solution.py:49
  20.2 0.2 early.1
  20.4 3.1 %collective-permute-done.8 = bf16[96,1024]{1,0:T(8,128)(2,1)S(1)} collective-permute-done((bf16[96,1024]{1,0:T(8,128)(2,1)S(1)}, bf16[96,1024]{1,0:T(8,128)(2,1)S(1)}, u32[]{:S(2)}, u32[]{:S(2)}) %collective-permute-start.8) | collective-permute-done | bytes 196640 | tf_op jit(solution)/shard_map/projection/ppermute | solution.py:49
  23.5 0.8 %add_convert_fusion = bf16[96,1280]{1,0:T(8,128)(2,1)} fusion(f32[96,1280]{1,0:T(8,128)S(1)} %early.1, bf16[96,1024]{1,0:T(8,128)(2,1)S(1)} %collective-permute-done.8, f32[1280]{0:T(1024)S(1)} %copy-done.5), kind=kLoop, calls=%fused_computation | loop fusion | flops 491520 | bytes 939008 | tf_op jit(solution)/shard_map/projection/convert_element_type | solution.py:302
  (2 shorter events, 0.0 us)
Async XLA Ops:
  0.0 10.7 %copy-start.4 = (bf16[96,256]{1,0:T(8,128)(2,1)S(1)}, bf16[96,256]{1,0:T(8,128)(2,1)}, u32[]{:S(2)}) copy-start(bf16[96,256]{1,0:T(8,128)(2,1)} %q_ref.3) | copy-start | bytes 147460
  0.0 10.7 %copy-start.3 = (bf16[384,256]{1,0:T(8,128)(2,1)S(1)}, bf16[384,256]{1,0:T(8,128)(2,1)}, u32[]{:S(2)}) copy-start(bf16[384,256]{1,0:T(8,128)(2,1)} %held_v_ref.1) | copy-start | bytes 589828
  0.0 10.7 %copy-start.2 = (bf16[384,256]{1,0:T(8,128)(2,1)S(1)}, bf16[384,256]{1,0:T(8,128)(2,1)}, u32[]{:S(2)}) copy-start(bf16[384,256]{1,0:T(8,128)(2,1)} %held_k_ref.1) | copy-start | bytes 589828
  0.0 16.1 %collective-permute-start.4 = (bf16[256,5120]{1,0:T(8,128)(2,1)}, bf16[256,5120]{1,0:T(8,128)(2,1)S(1)}, u32[]{:S(2)}, u32[]{:S(2)}) collective-permute-start(bf16[256,5120]{1,0:T(8,128)(2,1)} %refs_1_.3), channel_id=1, source_target_pairs={{0,1},{1,0},{2,3},{3,2},{4,5},{5,4},{6,7},{7,6},{8,9},{9,8},{10,11... | collective-permute-start | bytes 7864328 | tf_op jit(solution)/shard_map/weight_swap/ppermute | solution.py:49
  1.5 9.5 %collective-permute-start.2 = (bf16[96,512]{1,0:T(8,128)(2,1)S(1)}, bf16[96,512]{1,0:T(8,128)(2,1)S(1)}, u32[]{:S(2)}, u32[]{:S(2)}) collective-permute-start(bf16[96,512]{1,0:T(8,128)(2,1)S(1)} %maximum_convert_fusion.refs_0_), channel_id=1, source_target_pairs={{0,4},{4,8},{8,12},{12,0},{1,5},{5,9},{9,13},{13,1},{2,6},{6,10},{... | collective-permute-start | bytes 294920 | tf_op jit(solution)/shard_map/residual_gather/ppermute | solution.py:49
  4.3 9.6 %collective-permute-start.1 = (bf16[96,512]{1,0:T(8,128)(2,1)S(1)}, bf16[96,512]{1,0:T(8,128)(2,1)S(1)}, u32[]{:S(2)}, u32[]{:S(2)}) collective-permute-start(bf16[96,512]{1,0:T(8,128)(2,1)S(1)} %maximum_convert_fusion.refs_0_), channel_id=1, source_target_pairs={{0,8},{4,12},{8,0},{12,4},{1,9},{5,13},{9,1},{13,5},{2,10},{6,14},... | collective-permute-start | bytes 294920 | tf_op jit(solution)/shard_map/residual_gather/ppermute | solution.py:49
  6.8 7.1 %collective-permute-start = (bf16[96,512]{1,0:T(8,128)(2,1)S(1)}, bf16[96,512]{1,0:T(8,128)(2,1)S(1)}, u32[]{:S(2)}, u32[]{:S(2)}) collective-permute-start(bf16[96,512]{1,0:T(8,128)(2,1)S(1)} %maximum_convert_fusion.refs_0_), channel_id=1, source_target_pairs={{0,12},{4,0},{8,4},{12,8},{1,13},{5,1},{9,5},{13,9},{2,14},{6,2},{... | collective-permute-start | bytes 294920 | tf_op jit(solution)/shard_map/residual_gather/ppermute | solution.py:49
  9.2 9.5 %collective-permute-start.6 = (bf16[256,512]{1,0:T(8,128)(2,1)S(1)}, bf16[256,512]{1,0:T(8,128)(2,1)S(1)}, u32[]{:S(2)}, u32[]{:S(2)}) collective-permute-start(bf16[256,512]{1,0:T(8,128)(2,1)S(1)} %early_weight.1), channel_id=1, source_target_pairs={{0,2},{2,0},{1,3},{3,1},{4,6},{6,4},{5,7},{7,5},{8,10},{10,8},{9,1... | collective-permute-start | bytes 786440 | tf_op jit(solution)/shard_map/early_weight/ppermute | solution.py:49
  13.9 2.2 %copy-start = (bf16[256,5120]{1,0:T(8,128)(2,1)S(1)}, bf16[256,5120]{1,0:T(8,128)(2,1)}, u32[]{:S(2)}) copy-start(bf16[256,5120]{1,0:T(8,128)(2,1)} %refs_1_.3) | copy-start | bytes 7864324
  14.4 4.4 %copy-start.5 = (f32[1280]{0:T(1024)S(1)}, f32[1280]{0:T(1024)}, u32[]{:S(2)}) copy-start(f32[1280]{0:T(1024)} %param.15) | copy-start | bytes 15364
  14.5 4.4 %copy-start.1 = (bf16[96,1280]{1,0:T(8,128)(2,1)S(1)}, bf16[96,1280]{1,0:T(8,128)(2,1)}, u32[]{:S(2)}) copy-start(bf16[96,1280]{1,0:T(8,128)(2,1)} %hidden_ref.1) | copy-start | bytes 737284
  14.5 1.6 %collective-permute-start.3 = (bf16[96,256]{1,0:T(8,128)(2,1)S(1)}, bf16[96,256]{1,0:T(8,128)(2,1)S(1)}, u32[]{:S(2)}, u32[]{:S(2)}) collective-permute-start(bf16[96,256]{1,0:T(8,128)(2,1)S(1)} %attention.1.refs_0_), channel_id=1, source_target_pairs={{0,1},{1,0},{2,3},{3,2},{4,5},{5,4},{6,7},{7,6},{8,9},{9,8},{10,11... | collective-permute-start | bytes 147464 | tf_op jit(solution)/shard_map/attended_swap/ppermute | solution.py:49
  14.5 4.2 %collective-permute-start.5 = (bf16[96,256]{1,0:T(8,128)(2,1)S(1)}, bf16[96,256]{1,0:T(8,128)(2,1)S(1)}, u32[]{:S(2)}, u32[]{:S(2)}) collective-permute-start(bf16[96,256]{1,0:T(8,128)(2,1)S(1)} %attention.1.refs_0_), channel_id=1, source_target_pairs={{0,2},{2,0},{1,3},{3,1},{4,6},{6,4},{5,7},{7,5},{8,10},{10,8},{9,1... | collective-permute-start | bytes 147464 | tf_op jit(solution)/shard_map/attended_swap/ppermute | solution.py:49
  16.4 7.0 %collective-permute-start.8 = (bf16[96,1024]{1,0:T(8,128)(2,1)S(1)}, bf16[96,1024]{1,0:T(8,128)(2,1)S(1)}, u32[]{:S(2)}, u32[]{:S(2)}) collective-permute-start(bf16[96,1024]{1,0:T(8,128)(2,1)S(1)} %sent_term.1), channel_id=1, source_target_pairs={{0,2},{2,0},{1,3},{3,1},{4,6},{6,4},{5,7},{7,5},{8,10},{10,8},{9,1... | collective-permute-start | bytes 589832 | tf_op jit(solution)/shard_map/projection/ppermute | solution.py:49
  18.7 1.5 %collective-permute-start.7 = (bf16[352,256]{1,0:T(8,128)(2,1)S(1)}, bf16[352,256]{1,0:T(8,128)(2,1)S(1)}, u32[]{:S(2)}, u32[]{:S(2)}) collective-permute-start(bf16[352,256]{1,0:T(8,128)(2,1)S(1)} %pack.1), channel_id=1, source_target_pairs={{0,1},{1,0},{2,3},{3,2},{4,5},{5,4},{6,7},{7,6},{8,9},{9,8},{10,11... | collective-permute-start | bytes 540680 | tf_op jit(solution)/shard_map/projection/ppermute | solution.py:49

commit v14 on v12

--- a/solution.py
+++ b/solution.py
@@ -57,20 +57,6 @@
     return [place] + [lax.rem(place + patches - step, patches) for step in gather_steps(patches)]
 
 
-def prepare_kernel(*refs):
-    changes, out_ref, buffers, sems = refs[:2], refs[2], refs[3:5], refs[5]
-    width = buffers[0].shape[1]
-    copies = [
-        pltpu.make_async_copy(change, buffer, sems.at[i])
-        for i, (change, buffer) in enumerate(zip(changes, buffers))
-    ]
-    for copy in copies:
-        copy.start()
-    for i, (copy, buffer) in enumerate(zip(copies, buffers)):
-        copy.wait()
-        out_ref[:, i * width : (i + 1) * width] = buffer[...].astype(jnp.bfloat16)
-
-
 def early_weight_kernel(subs, columns, early, weight_ref, out_ref, sems):
     chip = (1 - lax.axis_index("head")) * subs
     copies = []
@@ -89,16 +75,29 @@
         copy.wait()
 
 
-def stage_kernel(patches, q_ref, held_k_ref, held_v_ref, products_ref, values_ref):
+def stage_kernel(
+    patches, q_hbm, held_k_hbm, held_v_hbm, q_ref, products_ref, values_ref, keys_ref, sems
+):
     rows, width = q_ref.shape
     sources = gather_sources(patches, lax.axis_index("patch"))
-    starts = [pl.multiple_of(source * rows, rows) for source in sources]
-    for i, at in enumerate(starts):
-        values_ref[i * rows : (i + 1) * rows, :] = held_v_ref[pl.ds(at, rows), :]
+    copies = [pltpu.make_async_copy(q_hbm, q_ref, sems.at[0])]
+    for i, source in enumerate(sources):
+        at = pl.multiple_of(source * rows, rows)
+        for n, (held, ref) in enumerate(((held_k_hbm, keys_ref), (held_v_hbm, values_ref))):
+            copies.append(
+                pltpu.make_async_copy(
+                    held.at[pl.ds(at, rows), :],
+                    ref.at[i * rows : (i + 1) * rows, :],
+                    sems.at[1 + 2 * i + n],
+                )
+            )
+    for copy in copies:
+        copy.start()
+    for copy in copies:
+        copy.wait()
     for head in range(width // HD):
         cols = slice(head * HD, (head + 1) * HD)
-        keys = jnp.concatenate([held_k_ref[pl.ds(at, rows), cols] for at in starts], axis=0)
-        products_ref[head] = dot_transposed(q_ref[:, cols], keys)
+        products_ref[head] = dot_transposed(q_ref[:, cols], keys_ref[:, cols])
 
 
 def dot_transposed(a, b):
@@ -214,26 +213,18 @@
 
         early = EARLY if heads == 2 and columns % LANES == 0 and columns > 4 * LANES else 0
         with jax.named_scope("residual_gather"):
-            residual = call(
-                prepare_kernel,
-                jax.ShapeDtypeStruct((rows, 2 * width), jnp.bfloat16),
-                [ANYWHERE] * 2,
-                IN_VMEM,
-                "prepare",
-                scratch_shapes=[
-                    pltpu.VMEM((rows, width), jnp.float32),
-                    pltpu.VMEM((rows, width), jnp.float32),
-                    pltpu.SemaphoreType.DMA((2,)),
-                ],
-            )(in_hbm(key_change), in_hbm(value_change))
+            low = jnp.float32(-jnp.inf)
+            residual = jnp.maximum(
+                lax.pad(key_change, low, ((0, 0, 0), (0, width, 0))),
+                lax.pad(value_change, low, ((0, 0, 0), (width, 0, 0))),
+            ).astype(jnp.bfloat16)
             blocks = [residual] + [
                 shift(residual, "patch", patches, step) for step in gather_steps(patches)
             ]
 
         with jax.named_scope("weight_swap"):
-            weights = [out_weight] + [
-                shift(out_weight, "sub", subs, i) for i in range(1, subs)
-            ]
+            swapped, _ = lax.optimization_barrier((out_weight, residual))
+            weights = [out_weight] + [shift(swapped, "sub", subs, i) for i in range(1, subs)]
 
         if early:
             with jax.named_scope("early_weight"):
@@ -267,17 +258,22 @@
 
         tokens = rows * patches
         with jax.named_scope("attention"):
-            products, values = call(
+            staged_queries, products, values = call(
                 functools.partial(stage_kernel, patches),
                 [
+                    jax.ShapeDtypeStruct((rows, width), jnp.bfloat16),
                     jax.ShapeDtypeStruct((width // HD, rows, tokens), jnp.float32),
                     jax.ShapeDtypeStruct((tokens, width), jnp.bfloat16),
                 ],
+                [ANYWHERE] * 3,
                 [IN_VMEM] * 3,
-                [IN_VMEM] * 2,
                 "stage",
                 flops=2_000_000_000,
-            )(queries, held_keys, held_values)
+                scratch_shapes=[
+                    pltpu.VMEM((tokens, width), jnp.bfloat16),
+                    pltpu.SemaphoreType.DMA((1 + 2 * patches,)),
+                ],
+            )(in_hbm(queries), in_hbm(held_keys), in_hbm(held_values))
             attended = call(
                 functools.partial(attention_kernel, 1.0 / math.sqrt(HD)),
                 jax.ShapeDtypeStruct((rows, width), jnp.bfloat16),
@@ -285,7 +281,7 @@
                 IN_VMEM,
                 "attention",
                 flops=2_000_000_000,
-            )(queries, products, values, *blocks)
+            )(staged_queries, products, values, *blocks)
 
         with jax.named_scope("attended_swap"):
             attended_parts = [attended] + [

time: 24.4 us -> 24.4 us (level)
  waiting for transfers between devices: 8.06 us -> 7.07 us
  other arithmetic: 0 us -> 0.95 us
    ppermute x9, waiting for transfers between devices: 8.06 us -> 7.07 us  [shift(): lax.ppermute(array, axis, [(i, (i + step) % size) for i in range(size)])]
    convert_element_type x0 -> x1, other arithmetic: none -> 0.95 us  [per_device(): residual = jnp.maximum(lax.pad(key_change, low, ((0, 0, 0), (0, width, 0)...]
    pallas_call x2 -> x1, Pallas kernels: 1.19 us -> 1.29 us  [per_device(): call(functools.partial(stage_kernel, patches), [jax.ShapeDtypeStruct((row...]
where the time goes in v14:
time: 24.4 us; the launch traced here: 24.1 us
  starting transfers between devices  11.5 us (47%)
  waiting for transfers between devices  7.07 us (29%)
  Pallas kernels  4.43 us (18%)
  other arithmetic  0.95 us (4%)
    ppermute x9, starting transfers between devices, shift(): lax.ppermute(array, axis, [(i, (i + step) % size) for i in range(size)])  11.5 us
    ppermute x9, waiting for transfers between devices, shift(): lax.ppermute(array, axis, [(i, (i + step) % size) for i in range(size)])  7.07 us
    pallas_call x1, Pallas kernels, per_device(): call(functools.partial(stage_kernel, patches), [jax.ShapeDtypeStruct((row...  1.29 us
    pallas_call x1, Pallas kernels, per_device(): call(functools.partial(early_weight_kernel, subs, columns, early), jax.Sh...  0.99 us
    convert_element_type x1, other arithmetic, per_device(): residual = jnp.maximum(lax.pad(key_change, low, ((0, 0, 0), (0, width, 0)...  0.95 us
    pallas_call x1, Pallas kernels, per_device(): call(functools.partial(final_kernel, early, row_blocks), jax.ShapeDtypeSt...  0.74 us
    pallas_call x1, Pallas kernels, per_device(): call(functools.partial(attention_kernel, 1.0 / math.sqrt(HD)), jax.ShapeD...  0.53 us
  transfers between devices with their start and end apart: 9, of which 4 were waited for; matrix products, arithmetic and copies ran while one was open for 0% of the time, Pallas kernels for 15%

profile of v14, /device:TPU:0, one launch (start us, length us, event | category | flops | bytes accessed | tf_op | source)
XLA Modules:
  0.0 24.1 jit_solution(11551063465270062819)
XLA Ops:
  0.0 1.0 %maximum_convert_fusion.refs_0_ = bf16[96,512]{1,0:T(8,128)(2,1)S(1)} fusion(f32[96,256]{1,0:T(8,128)} %param.12, f32[96,256]{1,0:T(8,128)} %param.11), kind=kLoop, calls=%fused_computation | loop fusion | flops 196608 | bytes 294912 | tf_op jit(solution)/shard_map/residual_gather/convert_element_type | solution.py:220
  1.0 0.5 %collective-permute-start.4 = (bf16[256,5120]{1,0:T(8,128)(2,1)}, bf16[256,5120]{1,0:T(8,128)(2,1)S(1)}, u32[]{:S(2)}, u32[]{:S(2)}) collective-permute-start(bf16[256,5120]{1,0:T(8,128)(2,1)} %refs_1_.3), channel_id=1, source_target_pairs={{0,1},{1,0},{2,3},{3,2},{4,5},{5,4},{6,7},{7,6},{8,9},{9,8},{10,11... | collective-permute-start | bytes 7864328 | tf_op jit(solution)/shard_map/weight_swap/ppermute | solution.py:49
  1.5 2.6 %collective-permute-start.2 = (bf16[96,512]{1,0:T(8,128)(2,1)S(1)}, bf16[96,512]{1,0:T(8,128)(2,1)S(1)}, u32[]{:S(2)}, u32[]{:S(2)}) collective-permute-start(bf16[96,512]{1,0:T(8,128)(2,1)S(1)} %maximum_convert_fusion.refs_0_), channel_id=1, source_target_pairs={{0,4},{4,8},{8,12},{12,0},{1,5},{5,9},{9,13},{13,1},{2,6},{6,10},{... | collective-permute-start | bytes 294920 | tf_op jit(solution)/shard_map/residual_gather/ppermute | solution.py:49
  4.1 2.6 %collective-permute-start.1 = (bf16[96,512]{1,0:T(8,128)(2,1)S(1)}, bf16[96,512]{1,0:T(8,128)(2,1)S(1)}, u32[]{:S(2)}, u32[]{:S(2)}) collective-permute-start(bf16[96,512]{1,0:T(8,128)(2,1)S(1)} %maximum_convert_fusion.refs_0_), channel_id=1, source_target_pairs={{0,8},{4,12},{8,0},{12,4},{1,9},{5,13},{9,1},{13,5},{2,10},{6,14},... | collective-permute-start | bytes 294920 | tf_op jit(solution)/shard_map/residual_gather/ppermute | solution.py:49
  6.7 1.3 %collective-permute-start = (bf16[96,512]{1,0:T(8,128)(2,1)S(1)}, bf16[96,512]{1,0:T(8,128)(2,1)S(1)}, u32[]{:S(2)}, u32[]{:S(2)}) collective-permute-start(bf16[96,512]{1,0:T(8,128)(2,1)S(1)} %maximum_convert_fusion.refs_0_), channel_id=1, source_target_pairs={{0,12},{4,0},{8,4},{12,8},{1,13},{5,1},{9,5},{13,9},{2,14},{6,2},{... | collective-permute-start | bytes 294920 | tf_op jit(solution)/shard_map/residual_gather/ppermute | solution.py:49
  8.1 1.0 %early_weight.1 = bf16[256,512]{1,0:T(8,128)(2,1)S(1)} custom-call(bf16[256,5120]{1,0:T(8,128)(2,1)} %refs_1_.3), custom_call_target="tpu_custom_call" | custom-call | bytes 524288 | tf_op jit(solution)/shard_map/early_weight/early_weight/pallas_call | solution.py:231
  9.0 1.6 %collective-permute-start.6 = (bf16[256,512]{1,0:T(8,128)(2,1)S(1)}, bf16[256,512]{1,0:T(8,128)(2,1)S(1)}, u32[]{:S(2)}, u32[]{:S(2)}) collective-permute-start(bf16[256,512]{1,0:T(8,128)(2,1)S(1)} %early_weight.1), channel_id=1, source_target_pairs={{0,2},{2,0},{1,3},{3,1},{4,6},{6,4},{5,7},{7,5},{8,10},{10,8},{9,1... | collective-permute-start | bytes 786440 | tf_op jit(solution)/shard_map/early_weight/ppermute | solution.py:49
  10.6 1.3 %stage.1 = (bf16[96,256]{1,0:T(8,128)(2,1)S(1)}, f32[2,96,384]{2,1,0:T(8,128)S(1)}, bf16[384,256]{1,0:T(8,128)(2,1)S(1)}) custom-call(bf16[96,256]{1,0:T(8,128)(2,1)} %q_hbm.1, bf16[384,256]{1,0:T(8,128)(2,1)} %held_k_hbm.1, bf16[384,256]{1,0:T(8,128)(2,1)} %held_v_hbm.1), custom_call_target="tpu_custom_call" | custom-call | flops 2000000000 | tf_op jit(solution)/shard_map/attention/stage/pallas_call | solution.py:261
  11.9 0.0 collective-permute-done.2.refs_3_
  11.9 1.9 %collective-permute-done.1.refs_2_ = bf16[96,512]{1,0:T(8,128)(2,1)S(1)} collective-permute-done((bf16[96,512]{1,0:T(8,128)(2,1)S(1)}, bf16[96,512]{1,0:T(8,128)(2,1)S(1)}, u32[]{:S(2)}, u32[]{:S(2)}) %collective-permute-start.1) | collective-permute-done | bytes 98336 | tf_op jit(solution)/shard_map/residual_gather/ppermute | solution.py:49
  13.8 0.0 collective-permute-done.refs_1_
  13.8 0.0 copy-start
  13.8 0.5 %attention.1.refs_0_ = bf16[96,256]{1,0:T(8,128)(2,1)S(1)} custom-call(bf16[96,256]{1,0:T(8,128)(2,1)S(1)} %get-tuple-element.9.q_ref, f32[2,96,384]{2,1,0:T(8,128)S(1)} %get-tuple-element.10.products_ref, bf16[384,256]{1,0:T(8,128)(2,1)S(1)} %get-tuple-element.11.values_ref, bf16[96,512]{1,0:T(8,128)(2,1)S(1)} %maximum_convert_fusion.refs_0_, ...), custom_call_target="tpu_custom_call" | custom-call | flops 2000000000 | tf_op jit(solution)/shard_map/attention/attention/pallas_call | solution.py:277
  14.4 0.0 copy-start.2
  14.4 0.0 copy-start.1
  14.4 0.1 collective-permute-start.3
  14.5 1.6 %collective-permute-start.5 = (bf16[96,256]{1,0:T(8,128)(2,1)S(1)}, bf16[96,256]{1,0:T(8,128)(2,1)S(1)}, u32[]{:S(2)}, u32[]{:S(2)}) collective-permute-start(bf16[96,256]{1,0:T(8,128)(2,1)S(1)} %attention.1.refs_0_), channel_id=1, source_target_pairs={{0,2},{2,0},{1,3},{3,1},{4,6},{6,4},{5,7},{7,5},{8,10},{10,8},{9,1... | collective-permute-start | bytes 147464 | tf_op jit(solution)/shard_map/attended_swap/ppermute | solution.py:49
  16.0 0.0 collective-permute-done.3.refs_2_
  16.0 0.0 collective-permute-done.4.refs_3_
  16.0 0.0 copy-done
  16.0 0.3 %sent_term.1 = bf16[96,1024]{1,0:T(8,128)(2,1)S(1)} custom-call(bf16[96,256]{1,0:T(8,128)(2,1)S(1)} %attention.1.refs_0_, bf16[256,5120]{1,0:T(8,128)(2,1)S(1)} %copy-done, bf16[96,256]{1,0:T(8,128)(2,1)S(1)} %collective-permute-done.3.refs_2_, bf16[256,5120]{1,0:T(8,128)(2,1)S(1)} %collective-permute-done.4.refs_3_), custom_call_target="tpu_custom_call" | custom-call | flops 125829120 | tf_op jit(solution)/shard_map/projection/sent_term/pallas_call | solution.py:300
  16.4 1.2 %collective-permute-start.8 = (bf16[96,1024]{1,0:T(8,128)(2,1)S(1)}, bf16[96,1024]{1,0:T(8,128)(2,1)S(1)}, u32[]{:S(2)}, u32[]{:S(2)}) collective-permute-start(bf16[96,1024]{1,0:T(8,128)(2,1)S(1)} %sent_term.1), channel_id=1, source_target_pairs={{0,2},{2,0},{1,3},{3,1},{4,6},{6,4},{5,7},{7,5},{8,10},{10,8},{9,1... | collective-permute-start | bytes 589832 | tf_op jit(solution)/shard_map/projection/ppermute | solution.py:49
  17.6 1.1 %collective-permute-done.5.attended_ref = bf16[96,256]{1,0:T(8,128)(2,1)S(1)} collective-permute-done((bf16[96,256]{1,0:T(8,128)(2,1)S(1)}, bf16[96,256]{1,0:T(8,128)(2,1)S(1)}, u32[]{:S(2)}, u32[]{:S(2)}) %collective-permute-start.5) | collective-permute-done | bytes 49184 | tf_op jit(solution)/shard_map/attended_swap/ppermute | solution.py:49
  18.6 0.0 collective-permute-done.6.weight_ref
  18.6 0.1 collective-permute-start.7
  18.7 0.0 copy-done.2
  18.7 0.0 copy-done.1
  18.8 0.4 %base.1.base_ref = f32[96,1280]{1,0:T(8,128)S(1)} custom-call(bf16[96,1280]{1,0:T(8,128)(2,1)S(1)} %copy-done.1, f32[1,1280]{1,0:T(1,128)S(1)} %reshape.3.gate_ref, bf16[96,256]{1,0:T(8,128)(2,1)S(1)} %attention.1.refs_0_, bf16[256,5120]{1,0:T(8,128)(2,1)S(1)} %copy-done, bf16[96,256]{1,0:T(8,128)(2,1)S(1)} %collective-permute-done.3.refs_2_, ...), custom_call_target="tpu_custom_call" | custom-call | flops 125829120 | tf_op jit(solution)/shard_map/projection/base/pallas_call | solution.py:311
  19.1 1.0 %collective-permute-done.7.packed_ref = bf16[352,256]{1,0:T(8,128)(2,1)S(1)} collective-permute-done((bf16[352,256]{1,0:T(8,128)(2,1)S(1)}, bf16[352,256]{1,0:T(8,128)(2,1)S(1)}, u32[]{:S(2)}, u32[]{:S(2)}) %collective-permute-start.7) | collective-permute-done | bytes 180256 | tf_op jit(solution)/shard_map/projection/ppermute | solution.py:49
  20.1 0.2 early.1.base_ref
  20.3 3.1 %collective-permute-done.8.refs_0_ = bf16[96,1024]{1,0:T(8,128)(2,1)S(1)} collective-permute-done((bf16[96,1024]{1,0:T(8,128)(2,1)S(1)}, bf16[96,1024]{1,0:T(8,128)(2,1)S(1)}, u32[]{:S(2)}, u32[]{:S(2)}) %collective-permute-start.8) | collective-permute-done | bytes 196640 | tf_op jit(solution)/shard_map/projection/ppermute | solution.py:49
  23.4 0.7 %final.1 = bf16[96,1280]{1,0:T(8,128)(2,1)} custom-call(f32[96,1280]{1,0:T(8,128)S(1)} %early.1.base_ref, f32[1,1280]{1,0:T(1,128)S(1)} %reshape.3.gate_ref, bf16[96,1024]{1,0:T(8,128)(2,1)S(1)} %collective-permute-done.8.refs_0_), custom_call_target="tpu_custom_call" | custom-call | bytes 983040 | tf_op jit(solution)/shard_map/projection/final/pallas_call | solution.py:337
  (2 shorter events, 0.0 us)
Async XLA Ops:
  1.0 15.1 %collective-permute-start.4 = (bf16[256,5120]{1,0:T(8,128)(2,1)}, bf16[256,5120]{1,0:T(8,128)(2,1)S(1)}, u32[]{:S(2)}, u32[]{:S(2)}) collective-permute-start(bf16[256,5120]{1,0:T(8,128)(2,1)} %refs_1_.3), channel_id=1, source_target_pairs={{0,1},{1,0},{2,3},{3,2},{4,5},{5,4},{6,7},{7,6},{8,9},{9,8},{10,11... | collective-permute-start | bytes 7864328 | tf_op jit(solution)/shard_map/weight_swap/ppermute | solution.py:49
  1.5 10.4 %collective-permute-start.2 = (bf16[96,512]{1,0:T(8,128)(2,1)S(1)}, bf16[96,512]{1,0:T(8,128)(2,1)S(1)}, u32[]{:S(2)}, u32[]{:S(2)}) collective-permute-start(bf16[96,512]{1,0:T(8,128)(2,1)S(1)} %maximum_convert_fusion.refs_0_), channel_id=1, source_target_pairs={{0,4},{4,8},{8,12},{12,0},{1,5},{5,9},{9,13},{13,1},{2,6},{6,10},{... | collective-permute-start | bytes 294920 | tf_op jit(solution)/shard_map/residual_gather/ppermute | solution.py:49
  4.1 9.7 %collective-permute-start.1 = (bf16[96,512]{1,0:T(8,128)(2,1)S(1)}, bf16[96,512]{1,0:T(8,128)(2,1)S(1)}, u32[]{:S(2)}, u32[]{:S(2)}) collective-permute-start(bf16[96,512]{1,0:T(8,128)(2,1)S(1)} %maximum_convert_fusion.refs_0_), channel_id=1, source_target_pairs={{0,8},{4,12},{8,0},{12,4},{1,9},{5,13},{9,1},{13,5},{2,10},{6,14},... | collective-permute-start | bytes 294920 | tf_op jit(solution)/shard_map/residual_gather/ppermute | solution.py:49
  6.7 7.1 %collective-permute-start = (bf16[96,512]{1,0:T(8,128)(2,1)S(1)}, bf16[96,512]{1,0:T(8,128)(2,1)S(1)}, u32[]{:S(2)}, u32[]{:S(2)}) collective-permute-start(bf16[96,512]{1,0:T(8,128)(2,1)S(1)} %maximum_convert_fusion.refs_0_), channel_id=1, source_target_pairs={{0,12},{4,0},{8,4},{12,8},{1,13},{5,1},{9,5},{13,9},{2,14},{6,2},{... | collective-permute-start | bytes 294920 | tf_op jit(solution)/shard_map/residual_gather/ppermute | solution.py:49
  9.0 9.6 %collective-permute-start.6 = (bf16[256,512]{1,0:T(8,128)(2,1)S(1)}, bf16[256,512]{1,0:T(8,128)(2,1)S(1)}, u32[]{:S(2)}, u32[]{:S(2)}) collective-permute-start(bf16[256,512]{1,0:T(8,128)(2,1)S(1)} %early_weight.1), channel_id=1, source_target_pairs={{0,2},{2,0},{1,3},{3,1},{4,6},{6,4},{5,7},{7,5},{8,10},{10,8},{9,1... | collective-permute-start | bytes 786440 | tf_op jit(solution)/shard_map/early_weight/ppermute | solution.py:49
  13.8 2.2 %copy-start = (bf16[256,5120]{1,0:T(8,128)(2,1)S(1)}, bf16[256,5120]{1,0:T(8,128)(2,1)}, u32[]{:S(2)}) copy-start(bf16[256,5120]{1,0:T(8,128)(2,1)} %refs_1_.3) | copy-start | bytes 7864324
  14.4 4.4 %copy-start.2 = (f32[1280]{0:T(1024)S(1)}, f32[1280]{0:T(1024)}, u32[]{:S(2)}) copy-start(f32[1280]{0:T(1024)} %param.15) | copy-start | bytes 15364
  14.4 4.4 %copy-start.1 = (bf16[96,1280]{1,0:T(8,128)(2,1)S(1)}, bf16[96,1280]{1,0:T(8,128)(2,1)}, u32[]{:S(2)}) copy-start(bf16[96,1280]{1,0:T(8,128)(2,1)} %hidden_ref.1) | copy-start | bytes 737284
  14.4 1.6 %collective-permute-start.3 = (bf16[96,256]{1,0:T(8,128)(2,1)S(1)}, bf16[96,256]{1,0:T(8,128)(2,1)S(1)}, u32[]{:S(2)}, u32[]{:S(2)}) collective-permute-start(bf16[96,256]{1,0:T(8,128)(2,1)S(1)} %attention.1.refs_0_), channel_id=1, source_target_pairs={{0,1},{1,0},{2,3},{3,2},{4,5},{5,4},{6,7},{7,6},{8,9},{9,8},{10,11... | collective-permute-start | bytes 147464 | tf_op jit(solution)/shard_map/attended_swap/ppermute | solution.py:49
  14.5 4.2 %collective-permute-start.5 = (bf16[96,256]{1,0:T(8,128)(2,1)S(1)}, bf16[96,256]{1,0:T(8,128)(2,1)S(1)}, u32[]{:S(2)}, u32[]{:S(2)}) collective-permute-start(bf16[96,256]{1,0:T(8,128)(2,1)S(1)} %attention.1.refs_0_), channel_id=1, source_target_pairs={{0,2},{2,0},{1,3},{3,1},{4,6},{6,4},{5,7},{7,5},{8,10},{10,8},{9,1... | collective-permute-start | bytes 147464 | tf_op jit(solution)/shard_map/attended_swap/ppermute | solution.py:49
  16.4 7.0 %collective-permute-start.8 = (bf16[96,1024]{1,0:T(8,128)(2,1)S(1)}, bf16[96,1024]{1,0:T(8,128)(2,1)S(1)}, u32[]{:S(2)}, u32[]{:S(2)}) collective-permute-start(bf16[96,1024]{1,0:T(8,128)(2,1)S(1)} %sent_term.1), channel_id=1, source_target_pairs={{0,2},{2,0},{1,3},{3,1},{4,6},{6,4},{5,7},{7,5},{8,10},{10,8},{9,1... | collective-permute-start | bytes 589832 | tf_op jit(solution)/shard_map/projection/ppermute | solution.py:49
  18.6 1.5 %collective-permute-start.7 = (bf16[352,256]{1,0:T(8,128)(2,1)S(1)}, bf16[352,256]{1,0:T(8,128)(2,1)S(1)}, u32[]{:S(2)}, u32[]{:S(2)}) collective-permute-start(bf16[352,256]{1,0:T(8,128)(2,1)S(1)} %pack.1), channel_id=1, source_target_pairs={{0,1},{1,0},{2,3},{3,2},{4,5},{5,4},{6,7},{7,6},{8,9},{9,8},{10,11... | collective-permute-start | bytes 540680 | tf_op jit(solution)/shard_map/projection/ppermute | solution.py:49

commit v15 on v14

--- a/solution.py
+++ b/solution.py
@@ -50,7 +50,7 @@
 
 
 def gather_steps(patches):
-    return list(range(patches - 1, 0, -1))
+    return [3, 1, 2] if patches == 4 else list(range(patches - 1, 0, -1))
 
 
 def gather_sources(patches, place):

time: 24.4 us -> 24.9 us (1.020)
  starting transfers between devices: 11.5 us -> 12.5 us
  waiting for transfers between devices: 7.07 us -> 6.67 us
    ppermute x9, starting transfers between devices: 11.5 us -> 12.5 us  [shift(): lax.ppermute(array, axis, [(i, (i + step) % size) for i in range(size)])]
    ppermute x9, waiting for transfers between devices: 7.07 us -> 6.67 us  [shift(): lax.ppermute(array, axis, [(i, (i + step) % size) for i in range(size)])]
  transfers between devices with their start and end apart: 9 -> 9, of which waited for: 4 -> 5; matrix products, arithmetic and copies ran while one was open for 0% -> 0% of each run, Pallas kernels for 15% -> 15%
where the time goes in v15:
time: 24.9 us; the launch traced here: 24.7 us
  starting transfers between devices  12.5 us (50%)
  waiting for transfers between devices  6.67 us (27%)
  Pallas kernels  4.43 us (18%)
  other arithmetic  0.95 us (4%)
    ppermute x9, starting transfers between devices, shift(): lax.ppermute(array, axis, [(i, (i + step) % size) for i in range(size)])  12.5 us
    ppermute x9, waiting for transfers between devices, shift(): lax.ppermute(array, axis, [(i, (i + step) % size) for i in range(size)])  6.67 us
    pallas_call x1, Pallas kernels, per_device(): call(functools.partial(stage_kernel, patches), [jax.ShapeDtypeStruct((row...  1.28 us
    pallas_call x1, Pallas kernels, per_device(): call(functools.partial(early_weight_kernel, subs, columns, early), jax.Sh...  0.99 us
    convert_element_type x1, other arithmetic, per_device(): residual = jnp.maximum(lax.pad(key_change, low, ((0, 0, 0), (0, width, 0)...  0.95 us
    pallas_call x1, Pallas kernels, per_device(): call(functools.partial(final_kernel, early, row_blocks), jax.ShapeDtypeSt...  0.74 us
    pallas_call x1, Pallas kernels, per_device(): call(functools.partial(attention_kernel, 1.0 / math.sqrt(HD)), jax.ShapeD...  0.53 us
  transfers between devices with their start and end apart: 9, of which 5 were waited for; matrix products, arithmetic and copies ran while one was open for 0% of the time, Pallas kernels for 15%

profile of v15, /device:TPU:0, one launch (start us, length us, event | category | flops | bytes accessed | tf_op | source)
XLA Modules:
  0.0 24.7 jit_solution(3148510052885612566)
XLA Ops:
  0.0 1.0 %maximum_convert_fusion.refs_0_ = bf16[96,512]{1,0:T(8,128)(2,1)S(1)} fusion(f32[96,256]{1,0:T(8,128)} %param.12, f32[96,256]{1,0:T(8,128)} %param.11), kind=kLoop, calls=%fused_computation | loop fusion | flops 196608 | bytes 294912 | tf_op jit(solution)/shard_map/residual_gather/convert_element_type | solution.py:220
  1.0 0.5 %collective-permute-start.4 = (bf16[256,5120]{1,0:T(8,128)(2,1)}, bf16[256,5120]{1,0:T(8,128)(2,1)S(1)}, u32[]{:S(2)}, u32[]{:S(2)}) collective-permute-start(bf16[256,5120]{1,0:T(8,128)(2,1)} %refs_1_.3), channel_id=1, source_target_pairs={{0,1},{1,0},{2,3},{3,2},{4,5},{5,4},{6,7},{7,6},{8,9},{9,8},{10,11... | collective-permute-start | bytes 7864328 | tf_op jit(solution)/shard_map/weight_swap/ppermute | solution.py:49
  1.5 3.7 %collective-permute-start.2 = (bf16[96,512]{1,0:T(8,128)(2,1)S(1)}, bf16[96,512]{1,0:T(8,128)(2,1)S(1)}, u32[]{:S(2)}, u32[]{:S(2)}) collective-permute-start(bf16[96,512]{1,0:T(8,128)(2,1)S(1)} %maximum_convert_fusion.refs_0_), channel_id=1, source_target_pairs={{0,8},{4,12},{8,0},{12,4},{1,9},{5,13},{9,1},{13,5},{2,10},{6,14},... | collective-permute-start | bytes 294920 | tf_op jit(solution)/shard_map/residual_gather/ppermute | solution.py:49
  5.1 1.6 %collective-permute-start.1 = (bf16[96,512]{1,0:T(8,128)(2,1)S(1)}, bf16[96,512]{1,0:T(8,128)(2,1)S(1)}, u32[]{:S(2)}, u32[]{:S(2)}) collective-permute-start(bf16[96,512]{1,0:T(8,128)(2,1)S(1)} %maximum_convert_fusion.refs_0_), channel_id=1, source_target_pairs={{0,4},{4,8},{8,12},{12,0},{1,5},{5,9},{9,13},{13,1},{2,6},{6,10},{... | collective-permute-start | bytes 294920 | tf_op jit(solution)/shard_map/residual_gather/ppermute | solution.py:49
  6.7 2.2 %collective-permute-start = (bf16[96,512]{1,0:T(8,128)(2,1)S(1)}, bf16[96,512]{1,0:T(8,128)(2,1)S(1)}, u32[]{:S(2)}, u32[]{:S(2)}) collective-permute-start(bf16[96,512]{1,0:T(8,128)(2,1)S(1)} %maximum_convert_fusion.refs_0_), channel_id=1, source_target_pairs={{0,12},{4,0},{8,4},{12,8},{1,13},{5,1},{9,5},{13,9},{2,14},{6,2},{... | collective-permute-start | bytes 294920 | tf_op jit(solution)/shard_map/residual_gather/ppermute | solution.py:49
  9.0 1.0 %early_weight.1 = bf16[256,512]{1,0:T(8,128)(2,1)S(1)} custom-call(bf16[256,5120]{1,0:T(8,128)(2,1)} %refs_1_.3), custom_call_target="tpu_custom_call" | custom-call | bytes 524288 | tf_op jit(solution)/shard_map/early_weight/early_weight/pallas_call | solution.py:231
  10.0 1.6 %collective-permute-start.6 = (bf16[256,512]{1,0:T(8,128)(2,1)S(1)}, bf16[256,512]{1,0:T(8,128)(2,1)S(1)}, u32[]{:S(2)}, u32[]{:S(2)}) collective-permute-start(bf16[256,512]{1,0:T(8,128)(2,1)S(1)} %early_weight.1), channel_id=1, source_target_pairs={{0,2},{2,0},{1,3},{3,1},{4,6},{6,4},{5,7},{7,5},{8,10},{10,8},{9,1... | collective-permute-start | bytes 786440 | tf_op jit(solution)/shard_map/early_weight/ppermute | solution.py:49
  11.5 1.3 %stage.1 = (bf16[96,256]{1,0:T(8,128)(2,1)S(1)}, f32[2,96,384]{2,1,0:T(8,128)S(1)}, bf16[384,256]{1,0:T(8,128)(2,1)S(1)}) custom-call(bf16[96,256]{1,0:T(8,128)(2,1)} %q_hbm.1, bf16[384,256]{1,0:T(8,128)(2,1)} %held_k_hbm.1, bf16[384,256]{1,0:T(8,128)(2,1)} %held_v_hbm.1), custom_call_target="tpu_custom_call" | custom-call | flops 2000000000 | tf_op jit(solution)/shard_map/attention/stage/pallas_call | solution.py:261
  12.8 0.2 collective-permute-done.2.refs_3_
  13.1 0.0 collective-permute-done.1.refs_2_
  13.1 1.3 %collective-permute-done.refs_1_ = bf16[96,512]{1,0:T(8,128)(2,1)S(1)} collective-permute-done((bf16[96,512]{1,0:T(8,128)(2,1)S(1)}, bf16[96,512]{1,0:T(8,128)(2,1)S(1)}, u32[]{:S(2)}, u32[]{:S(2)}) %collective-permute-start) | collective-permute-done | bytes 98336 | tf_op jit(solution)/shard_map/residual_gather/ppermute | solution.py:49
  14.3 0.0 copy-start
  14.3 0.5 %attention.1.refs_0_ = bf16[96,256]{1,0:T(8,128)(2,1)S(1)} custom-call(bf16[96,256]{1,0:T(8,128)(2,1)S(1)} %get-tuple-element.9.q_ref, f32[2,96,384]{2,1,0:T(8,128)S(1)} %get-tuple-element.10.products_ref, bf16[384,256]{1,0:T(8,128)(2,1)S(1)} %get-tuple-element.11.values_ref, bf16[96,512]{1,0:T(8,128)(2,1)S(1)} %maximum_convert_fusion.refs_0_, ...), custom_call_target="tpu_custom_call" | custom-call | flops 2000000000 | tf_op jit(solution)/shard_map/attention/attention/pallas_call | solution.py:277
  14.9 0.0 copy-start.2
  14.9 0.0 copy-start.1
  14.9 0.1 collective-permute-start.3
  15.0 1.6 %collective-permute-start.5 = (bf16[96,256]{1,0:T(8,128)(2,1)S(1)}, bf16[96,256]{1,0:T(8,128)(2,1)S(1)}, u32[]{:S(2)}, u32[]{:S(2)}) collective-permute-start(bf16[96,256]{1,0:T(8,128)(2,1)S(1)} %attention.1.refs_0_), channel_id=1, source_target_pairs={{0,2},{2,0},{1,3},{3,1},{4,6},{6,4},{5,7},{7,5},{8,10},{10,8},{9,1... | collective-permute-start | bytes 147464 | tf_op jit(solution)/shard_map/attended_swap/ppermute | solution.py:49
  16.6 0.0 collective-permute-done.3.refs_2_
  16.6 0.0 collective-permute-done.4.refs_3_
  16.6 0.0 copy-done
  16.6 0.3 %sent_term.1 = bf16[96,1024]{1,0:T(8,128)(2,1)S(1)} custom-call(bf16[96,256]{1,0:T(8,128)(2,1)S(1)} %attention.1.refs_0_, bf16[256,5120]{1,0:T(8,128)(2,1)S(1)} %copy-done, bf16[96,256]{1,0:T(8,128)(2,1)S(1)} %collective-permute-done.3.refs_2_, bf16[256,5120]{1,0:T(8,128)(2,1)S(1)} %collective-permute-done.4.refs_3_), custom_call_target="tpu_custom_call" | custom-call | flops 125829120 | tf_op jit(solution)/shard_map/projection/sent_term/pallas_call | solution.py:300
  16.9 1.2 %collective-permute-start.8 = (bf16[96,1024]{1,0:T(8,128)(2,1)S(1)}, bf16[96,1024]{1,0:T(8,128)(2,1)S(1)}, u32[]{:S(2)}, u32[]{:S(2)}) collective-permute-start(bf16[96,1024]{1,0:T(8,128)(2,1)S(1)} %sent_term.1), channel_id=1, source_target_pairs={{0,2},{2,0},{1,3},{3,1},{4,6},{6,4},{5,7},{7,5},{8,10},{10,8},{9,1... | collective-permute-start | bytes 589832 | tf_op jit(solution)/shard_map/projection/ppermute | solution.py:49
  18.1 1.0 %collective-permute-done.5.attended_ref = bf16[96,256]{1,0:T(8,128)(2,1)S(1)} collective-permute-done((bf16[96,256]{1,0:T(8,128)(2,1)S(1)}, bf16[96,256]{1,0:T(8,128)(2,1)S(1)}, u32[]{:S(2)}, u32[]{:S(2)}) %collective-permute-start.5) | collective-permute-done | bytes 49184 | tf_op jit(solution)/shard_map/attended_swap/ppermute | solution.py:49
  19.1 0.0 collective-permute-done.6.weight_ref
  19.2 0.1 collective-permute-start.7
  19.2 0.0 copy-done.2
  19.3 0.0 copy-done.1
  19.3 0.4 %base.1.base_ref = f32[96,1280]{1,0:T(8,128)S(1)} custom-call(bf16[96,1280]{1,0:T(8,128)(2,1)S(1)} %copy-done.1, f32[1,1280]{1,0:T(1,128)S(1)} %reshape.3.gate_ref, bf16[96,256]{1,0:T(8,128)(2,1)S(1)} %attention.1.refs_0_, bf16[256,5120]{1,0:T(8,128)(2,1)S(1)} %copy-done, bf16[96,256]{1,0:T(8,128)(2,1)S(1)} %collective-permute-done.3.refs_2_, ...), custom_call_target="tpu_custom_call" | custom-call | flops 125829120 | tf_op jit(solution)/shard_map/projection/base/pallas_call | solution.py:311
  19.6 1.0 %collective-permute-done.7.packed_ref = bf16[352,256]{1,0:T(8,128)(2,1)S(1)} collective-permute-done((bf16[352,256]{1,0:T(8,128)(2,1)S(1)}, bf16[352,256]{1,0:T(8,128)(2,1)S(1)}, u32[]{:S(2)}, u32[]{:S(2)}) %collective-permute-start.7) | collective-permute-done | bytes 180256 | tf_op jit(solution)/shard_map/projection/ppermute | solution.py:49
  20.6 0.2 early.1.base_ref
  20.8 3.1 %collective-permute-done.8.refs_0_ = bf16[96,1024]{1,0:T(8,128)(2,1)S(1)} collective-permute-done((bf16[96,1024]{1,0:T(8,128)(2,1)S(1)}, bf16[96,1024]{1,0:T(8,128)(2,1)S(1)}, u32[]{:S(2)}, u32[]{:S(2)}) %collective-permute-start.8) | collective-permute-done | bytes 196640 | tf_op jit(solution)/shard_map/projection/ppermute | solution.py:49
  24.0 0.7 %final.1 = bf16[96,1280]{1,0:T(8,128)(2,1)} custom-call(f32[96,1280]{1,0:T(8,128)S(1)} %early.1.base_ref, f32[1,1280]{1,0:T(1,128)S(1)} %reshape.3.gate_ref, bf16[96,1024]{1,0:T(8,128)(2,1)S(1)} %collective-permute-done.8.refs_0_), custom_call_target="tpu_custom_call" | custom-call | bytes 983040 | tf_op jit(solution)/shard_map/projection/final/pallas_call | solution.py:337
  (2 shorter events, 0.0 us)
Async XLA Ops:
  1.0 15.6 %collective-permute-start.4 = (bf16[256,5120]{1,0:T(8,128)(2,1)}, bf16[256,5120]{1,0:T(8,128)(2,1)S(1)}, u32[]{:S(2)}, u32[]{:S(2)}) collective-permute-start(bf16[256,5120]{1,0:T(8,128)(2,1)} %refs_1_.3), channel_id=1, source_target_pairs={{0,1},{1,0},{2,3},{3,2},{4,5},{5,4},{6,7},{7,6},{8,9},{9,8},{10,11... | collective-permute-start | bytes 7864328 | tf_op jit(solution)/shard_map/weight_swap/ppermute | solution.py:49
  1.5 11.6 %collective-permute-start.2 = (bf16[96,512]{1,0:T(8,128)(2,1)S(1)}, bf16[96,512]{1,0:T(8,128)(2,1)S(1)}, u32[]{:S(2)}, u32[]{:S(2)}) collective-permute-start(bf16[96,512]{1,0:T(8,128)(2,1)S(1)} %maximum_convert_fusion.refs_0_), channel_id=1, source_target_pairs={{0,8},{4,12},{8,0},{12,4},{1,9},{5,13},{9,1},{13,5},{2,10},{6,14},... | collective-permute-start | bytes 294920 | tf_op jit(solution)/shard_map/residual_gather/ppermute | solution.py:49
  5.1 7.9 %collective-permute-start.1 = (bf16[96,512]{1,0:T(8,128)(2,1)S(1)}, bf16[96,512]{1,0:T(8,128)(2,1)S(1)}, u32[]{:S(2)}, u32[]{:S(2)}) collective-permute-start(bf16[96,512]{1,0:T(8,128)(2,1)S(1)} %maximum_convert_fusion.refs_0_), channel_id=1, source_target_pairs={{0,4},{4,8},{8,12},{12,0},{1,5},{5,9},{9,13},{13,1},{2,6},{6,10},{... | collective-permute-start | bytes 294920 | tf_op jit(solution)/shard_map/residual_gather/ppermute | solution.py:49
  6.7 7.6 %collective-permute-start = (bf16[96,512]{1,0:T(8,128)(2,1)S(1)}, bf16[96,512]{1,0:T(8,128)(2,1)S(1)}, u32[]{:S(2)}, u32[]{:S(2)}) collective-permute-start(bf16[96,512]{1,0:T(8,128)(2,1)S(1)} %maximum_convert_fusion.refs_0_), channel_id=1, source_target_pairs={{0,12},{4,0},{8,4},{12,8},{1,13},{5,1},{9,5},{13,9},{2,14},{6,2},{... | collective-permute-start | bytes 294920 | tf_op jit(solution)/shard_map/residual_gather/ppermute | solution.py:49
  10.0 9.2 %collective-permute-start.6 = (bf16[256,512]{1,0:T(8,128)(2,1)S(1)}, bf16[256,512]{1,0:T(8,128)(2,1)S(1)}, u32[]{:S(2)}, u32[]{:S(2)}) collective-permute-start(bf16[256,512]{1,0:T(8,128)(2,1)S(1)} %early_weight.1), channel_id=1, source_target_pairs={{0,2},{2,0},{1,3},{3,1},{4,6},{6,4},{5,7},{7,5},{8,10},{10,8},{9,1... | collective-permute-start | bytes 786440 | tf_op jit(solution)/shard_map/early_weight/ppermute | solution.py:49
  14.3 2.3 %copy-start = (bf16[256,5120]{1,0:T(8,128)(2,1)S(1)}, bf16[256,5120]{1,0:T(8,128)(2,1)}, u32[]{:S(2)}) copy-start(bf16[256,5120]{1,0:T(8,128)(2,1)} %refs_1_.3) | copy-start | bytes 7864324
  14.9 4.4 %copy-start.2 = (f32[1280]{0:T(1024)S(1)}, f32[1280]{0:T(1024)}, u32[]{:S(2)}) copy-start(f32[1280]{0:T(1024)} %param.15) | copy-start | bytes 15364
  14.9 4.4 %copy-start.1 = (bf16[96,1280]{1,0:T(8,128)(2,1)S(1)}, bf16[96,1280]{1,0:T(8,128)(2,1)}, u32[]{:S(2)}) copy-start(bf16[96,1280]{1,0:T(8,128)(2,1)} %hidden_ref.1) | copy-start | bytes 737284
  14.9 1.7 %collective-permute-start.3 = (bf16[96,256]{1,0:T(8,128)(2,1)S(1)}, bf16[96,256]{1,0:T(8,128)(2,1)S(1)}, u32[]{:S(2)}, u32[]{:S(2)}) collective-permute-start(bf16[96,256]{1,0:T(8,128)(2,1)S(1)} %attention.1.refs_0_), channel_id=1, source_target_pairs={{0,1},{1,0},{2,3},{3,2},{4,5},{5,4},{6,7},{7,6},{8,9},{9,8},{10,11... | collective-permute-start | bytes 147464 | tf_op jit(solution)/shard_map/attended_swap/ppermute | solution.py:49
  15.0 4.2 %collective-permute-start.5 = (bf16[96,256]{1,0:T(8,128)(2,1)S(1)}, bf16[96,256]{1,0:T(8,128)(2,1)S(1)}, u32[]{:S(2)}, u32[]{:S(2)}) collective-permute-start(bf16[96,256]{1,0:T(8,128)(2,1)S(1)} %attention.1.refs_0_), channel_id=1, source_target_pairs={{0,2},{2,0},{1,3},{3,1},{4,6},{6,4},{5,7},{7,5},{8,10},{10,8},{9,1... | collective-permute-start | bytes 147464 | tf_op jit(solution)/shard_map/attended_swap/ppermute | solution.py:49
  16.9 7.0 %collective-permute-start.8 = (bf16[96,1024]{1,0:T(8,128)(2,1)S(1)}, bf16[96,1024]{1,0:T(8,128)(2,1)S(1)}, u32[]{:S(2)}, u32[]{:S(2)}) collective-permute-start(bf16[96,1024]{1,0:T(8,128)(2,1)S(1)} %sent_term.1), channel_id=1, source_target_pairs={{0,2},{2,0},{1,3},{3,1},{4,6},{6,4},{5,7},{7,5},{8,10},{10,8},{9,1... | collective-permute-start | bytes 589832 | tf_op jit(solution)/shard_map/projection/ppermute | solution.py:49
  19.2 1.5 %collective-permute-start.7 = (bf16[352,256]{1,0:T(8,128)(2,1)S(1)}, bf16[352,256]{1,0:T(8,128)(2,1)S(1)}, u32[]{:S(2)}, u32[]{:S(2)}) collective-permute-start(bf16[352,256]{1,0:T(8,128)(2,1)S(1)} %pack.1), channel_id=1, source_target_pairs={{0,1},{1,0},{2,3},{3,2},{4,5},{5,4},{6,7},{7,6},{8,9},{9,8},{10,11... | collective-permute-start | bytes 540680 | tf_op jit(solution)/shard_map/projection/ppermute | solution.py:49

commit v16 on v0

v16 whole, which is shorter than its diff:
```python
import functools
import math

import jax
import jax.numpy as jnp
from jax import lax
from jax.experimental import pallas as pl
from jax.experimental.pallas import tpu as pltpu
from jax.sharding import PartitionSpec as P

HD = 128
LANES = 128
ROW_TILE = 16
VMEM_LIMIT = 12 * 1024 * 1024

IN_VMEM = pl.BlockSpec(memory_space=pltpu.VMEM)
ANYWHERE = pl.BlockSpec(memory_space=pl.ANY)


def call(kernel, out_shape, in_specs, out_specs, name, flops=0, moved=0, scratch_shapes=()):
    return pl.pallas_call(
        kernel,
        out_shape=out_shape,
        in_specs=in_specs,
        out_specs=out_specs,
        scratch_shapes=scratch_shapes,
        name=name,
        cost_estimate=pl.CostEstimate(flops=flops, bytes_accessed=moved, transcendentals=0),
        compiler_params=pltpu.CompilerParams(vmem_limit_bytes=VMEM_LIMIT),
    )


def in_hbm(array):
    return pltpu.with_memory_space_constraint(array, pltpu.HBM)


def shift(array, axis, size, step):
    return lax.ppermute(array, axis, [(i, (i + step) % size) for i in range(size)])


def to_neighbour(array, patches):
    return lax.ppermute(array, "patch", [(i, i ^ 1) for i in range(patches)])


def to_neighbours_other_core(array, patches, subs):
    pairs = [
        (place * subs + sub, (place ^ 1) * subs + (subs - 1 - sub))
        for place in range(patches)
        for sub in range(subs)
    ]
    return lax.ppermute(array, ("patch", "sub"), pairs)


def start_all(copies):
    for copy in copies:
        copy.start()
    return copies


def prepare_kernel(
    keys_hbm, values_hbm, queries_hbm, same_ref, flip_ref, q_same_ref, q_flip_ref, buffers, sems
):
    parity = lax.rem(lax.axis_index("patch"), 2)
    head_cols = [
        pl.ds(pl.multiple_of(head * HD, LANES), HD) for head in (1 - parity, parity)
    ]
    copies = start_all(
        [
            pltpu.make_async_copy(source.at[:, cols], buffers.at[2 * i + n], sems.at[2 * i + n])
            for i, cols in enumerate(head_cols)
            for n, source in enumerate((keys_hbm, values_hbm))
        ]
        + [
            pltpu.make_async_copy(queries_hbm.at[:, cols], ref, sems.at[4 + i])
            for i, (cols, ref) in enumerate(zip(head_cols, (q_flip_ref, q_same_ref)))
        ]
    )
    for i, ref in enumerate((flip_ref, same_ref)):
        for n in range(2):
            copies[2 * i + n].wait()
            ref[:, n * HD : (n + 1) * HD] = buffers[2 * i + n].astype(jnp.bfloat16)
    for copy in copies[4:]:
        copy.wait()


def stage_kernel(steps, patches, held_k_hbm, held_v_hbm, keys_ref, values_ref, sems):
    rows = keys_ref.shape[0] // patches
    place = lax.axis_index("patch")
    cols = pl.ds(pl.multiple_of(lax.rem(place, 2) * HD, LANES), HD)
    copies = []
    for i, step in enumerate(steps):
        at = pl.ds(pl.multiple_of(lax.rem(place + patches - step, patches) * rows, rows), rows)
        for n, (held, ref) in enumerate(((held_k_hbm, keys_ref), (held_v_hbm, values_ref))):
            copies.append(
                pltpu.make_async_copy(
                    held.at[at, cols], ref.at[i * rows : (i + 1) * rows, :], sems.at[2 * i + n]
                )
            )
    for copy in start_all(copies):
        copy.wait()


def attention_kernel(scale, q_own_ref, q_other_ref, keys_ref, values_ref, *refs):
    block_refs, out_refs = refs[:-2], refs[-2:]
    rows = q_own_ref.shape[0]
    blocks = jnp.concatenate([ref[...] for ref in block_refs], axis=0)
    q = jnp.concatenate([q_own_ref[...], q_other_ref[...]], axis=0)
    products = lax.dot_general(
        jnp.concatenate([q, q], axis=1),
        jnp.concatenate([keys_ref[...], blocks[:, :HD]], axis=1),
        (((1,), (1,)), ((), ())),
        preferred_element_type=jnp.float32,
    )
    scores = products * scale
    weights = jnp.exp(scores - jnp.max(scores, axis=1, keepdims=True))
    totals = jnp.sum(weights, axis=1, keepdims=True)
    high = weights.astype(jnp.bfloat16)
    low = (weights - high.astype(jnp.float32)).astype(jnp.bfloat16)
    sums = jnp.dot(
        jnp.concatenate([high, low], axis=0),
        jnp.concatenate([values_ref[...], blocks[:, HD:]], axis=1),
        preferred_element_type=jnp.float32,
    )
    sums = sums[: 2 * rows] + sums[2 * rows :]
    sums = sums[:, :HD] + sums[:, HD:]
    attended = (sums / totals).astype(jnp.bfloat16)
    for n, ref in enumerate(out_refs):
        ref[...] = attended[n * rows : (n + 1) * rows, :]


def block_products(start, columns, refs):
    even = lax.rem(lax.axis_index("patch"), 2) == 0
    total = 0.0
    for same_ref, flip_ref, weight_ref in zip(refs[::3], refs[1::3], refs[2::3]):
        same, flip = same_ref[...], flip_ref[...]
        attended = jnp.concatenate(
            [jnp.where(even, same, flip), jnp.where(even, flip, same)], axis=1
        )
        if start is None:
            weight = weight_ref[...]
        else:
            weight = weight_ref[:, pl.ds(pl.multiple_of(start, LANES), columns)]
        total = total + jnp.dot(attended, weight, preferred_element_type=jnp.float32)
    return total


def sent_kernel(start, *refs):
    out_ref = refs[-1]
    out_ref[...] = block_products(start(), out_ref.shape[1], refs[:-1]).astype(jnp.bfloat16)


def base_kernel(start, hidden_ref, gate_ref, *refs):
    out_ref = refs[-1]
    total = block_products(start(), out_ref.shape[1], refs[:-1])
    out_ref[...] = hidden_ref[...].astype(jnp.float32) + gate_ref[...] * total


def final_kernel(base_ref, gate_ref, *refs):
    arrived_refs, out_ref = refs[:-1], refs[-1]
    total = 0.0
    for ref in arrived_refs:
        total = total + ref[...].astype(jnp.float32)
    out_ref[...] = (base_ref[...] + gate_ref[...] * total).astype(jnp.bfloat16)


def solution(mesh):
    patches, heads, subs = mesh.shape["patch"], mesh.shape["head"], mesh.shape["sub"]

    def per_device(
        queries, held_keys, held_values, key_change, value_change, out_weight, hidden_in, gate
    ):
        rows, width = queries.shape
        columns = hidden_in.shape[1]
        tokens = rows * patches
        assert width == 2 * HD and patches % 2 == 0 and subs == 2

        def rows_of(count, kind=jnp.bfloat16):
            return jax.ShapeDtypeStruct((rows, count), kind)

        with jax.named_scope("residual_exchange"):
            same, flip, q_same, q_flip = call(
                prepare_kernel,
                [rows_of(2 * HD), rows_of(2 * HD), rows_of(HD), rows_of(HD)],
                [ANYWHERE] * 3,
                [IN_VMEM] * 4,
                "prepare",
                scratch_shapes=[
                    pltpu.VMEM((4, rows, HD), jnp.float32),
                    pltpu.SemaphoreType.DMA((6,)),
                ],
            )(in_hbm(key_change), in_hbm(value_change), in_hbm(queries))
            steps = [0] + list(range(patches - 1, 0, -1))
            blocks = [same] + [
                shift(same if step % 2 == 0 else flip, "patch", patches, step)
                for step in steps[1:]
            ]
            q_other = to_neighbour(q_flip, patches)

        with jax.named_scope("weight_swap"):
            swapped, _ = lax.optimization_barrier((out_weight, same))
            weights = [out_weight, shift(swapped, "sub", subs, 1)]

        with jax.named_scope("attention"):
            keys, values = call(
                functools.partial(stage_kernel, steps, patches),
                [jax.ShapeDtypeStruct((tokens, HD), jnp.bfloat16)] * 2,
                [ANYWHERE] * 2,
                [IN_VMEM] * 2,
                "stage",
                flops=2_000_000_000,
                scratch_shapes=[pltpu.SemaphoreType.DMA((2 * patches,))],
            )(in_hbm(held_keys), in_hbm(held_values))
            own_same, other_same = call(
                functools.partial(attention_kernel, 1.0 / math.sqrt(HD)),
                [rows_of(HD)] * 2,
                [IN_VMEM] * (4 + patches),
                [IN_VMEM] * 2,
                "attention",
                flops=2_000_000_000,
            )(q_same, q_other, keys, values, *blocks)

        with jax.named_scope("attended_exchange"):
            attended = [
                (own_same, to_neighbour(other_same, patches)),
                (
                    shift(own_same, "sub", subs, 1),
                    to_neighbours_other_core(other_same, patches, subs),
                ),
            ]

        def operands_and_start(step):
            def start():
                to = lax.rem(lax.axis_index("head") + step, heads) * subs + lax.axis_index("sub")
                return to * columns

            def block(weight):
                if columns % LANES == 0:
                    return weight
                return lax.dynamic_slice(weight, (0, start()), (width, columns))

            operands = [
                x for pair, weight in zip(attended, weights) for x in (*pair, block(weight))
            ]
            return operands, start if columns % LANES == 0 else lambda: None

        product_flops = 4 * rows * width * columns
        with jax.named_scope("projection"):
            arrived = []
            for step in range(1, heads):
                operands, start = operands_and_start(step)
                term = call(
                    functools.partial(sent_kernel, start),
                    rows_of(columns),
                    [IN_VMEM] * len(operands),
                    IN_VMEM,
                    "sent_term",
                    product_flops,
                )(*operands)
                arrived.append(shift(term, "head", heads, step))
            gate_row = gate.reshape(1, columns)
            operands, start = operands_and_start(0)
            base = call(
                functools.partial(base_kernel, start),
                rows_of(columns, jnp.float32),
                [IN_VMEM] * (2 + len(operands)),
                IN_VMEM,
                "base",
                product_flops,
            )(hidden_in, gate_row, *operands)
            return call(
                final_kernel,
                rows_of(columns),
                [IN_VMEM] * (2 + len(arrived)),
                IN_VMEM,
                "final",
                moved=rows * columns * 8,
            )(base, gate_row, *arrived)

    in_specs = (
        P(("groups", "patch"), ("head", "sub")),
        P("groups", ("head", "sub")),
        P("groups", ("head", "sub")),
        P(("groups", "patch"), ("head", "sub")),
        P(("groups", "patch"), ("head", "sub")),
        P(("head", "sub"), None),
        P(("groups", "patch"), ("head", "sub")),
        P(("groups", "head", "sub")),
    )
    out_specs = P(("groups", "patch"), ("head", "sub"))
    return jax.shard_map(
        per_device, mesh=mesh, in_specs=in_specs, out_specs=out_specs, check_vma=False
    )
```

time: 71.2 us -> 25.8 us (0.36)
  waiting for transfers between devices: 32.5 us -> 10.4 us
  blocking collectives: 16.2 us -> 0 us
  between operations: 13.4 us -> 0.06 us
  starting transfers between devices: 0.01 us -> 11.2 us
  other arithmetic: 5.07 us -> 0 us
  Pallas kernels: 0 us -> 3.91 us
  matrix products: 3.63 us -> 0 us
    reduce_scatter x1 -> x0, waiting for transfers between devices: 32.5 us -> none  [per_device(): lax.psum_scatter(terms, ('head', 'sub'), scatter_dimension=1, tiled=True)]
    all_gather x1 -> x0, blocking collectives: 16.2 us -> none  [per_device(): gathered = lax.all_gather(residual, 'patch', axis=0, tiled=True)]
    ppermute x0 -> x9, starting transfers between devices: none -> 11.2 us  [the longest x6 8.26 us: shift(): lax.ppermute(array, axis, [(i, (i + step) % size) for i in range(size)])]
    ppermute x0 -> x9, waiting for transfers between devices: none -> 10.4 us  [the longest x6 6.77 us: shift(): lax.ppermute(array, axis, [(i, (i + step) % size) for i in range(size)])]
    pallas_call x0 -> x6, Pallas kernels: none -> 3.91 us  [the longest x1 0.93 us: per_device(): call(functools.partial(stage_kernel, steps, patches), [jax.ShapeDtypeStru...]
    convert_element_type x3 -> x0, other arithmetic: 3.73 us -> none  [the longest x1 1.78 us: per_device(): (hidden_in.astype(jnp.float32) + gate[None, :] * projected).astype(jnp.bf...]
    dot_general x3 -> x0, matrix products: 3.63 us -> none  [the longest x1 1.84 us: per_device(): terms = jnp.dot(rounded, out_weight, preferred_element_type=jnp.float32)]
    unnamed x1 -> x0, other arithmetic: 1.12 us -> none
  transfers between devices with their start and end apart: 1 -> 9, of which waited for: 1 -> 5; matrix products, arithmetic and copies ran while one was open for 0% -> 0% of each run, Pallas kernels for 0% -> 7%
where the time goes in v16:
time: 25.8 us; the launch traced here: 25.6 us
  starting transfers between devices  11.2 us (43%)
  waiting for transfers between devices  10.4 us (40%)
  Pallas kernels  3.91 us (15%)
    ppermute x6, starting transfers between devices, shift(): lax.ppermute(array, axis, [(i, (i + step) % size) for i in range(size)])  8.26 us
    ppermute x6, waiting for transfers between devices, shift(): lax.ppermute(array, axis, [(i, (i + step) % size) for i in range(size)])  6.77 us
    ppermute x2, starting transfers between devices, to_neighbour(): return lax.ppermute(array, 'patch', [(i, i ^ 1) for i in range(patches)])  2.91 us
    ppermute x2, waiting for transfers between devices, to_neighbour(): return lax.ppermute(array, 'patch', [(i, i ^ 1) for i in range(patches)])  2.06 us
    ppermute x1, waiting for transfers between devices, to_neighbours_other_core(): return lax.ppermute(array, ('patch', 'sub'), pairs)  1.55 us
    pallas_call x1, Pallas kernels, per_device(): call(functools.partial(stage_kernel, steps, patches), [jax.ShapeDtypeStru...  0.93 us
    pallas_call x1, Pallas kernels, per_device(): call(prepare_kernel, [rows_of(2 * HD), rows_of(2 * HD), rows_of(HD), rows...  0.93 us
    pallas_call x1, Pallas kernels, per_device(): call(final_kernel, rows_of(columns), [IN_VMEM] * (2 + len(arrived)), IN_V...  0.75 us
  transfers between devices with their start and end apart: 9, of which 5 were waited for; matrix products, arithmetic and copies ran while one was open for 0% of the time, Pallas kernels for 7%

profile of v16, /device:TPU:0, one launch (start us, length us, event | category | flops | bytes accessed | tf_op | source)
XLA Modules:
  0.0 25.6 jit_solution(17741397347017969494)
XLA Ops:
  0.0 0.9 %prepare.1 = (bf16[96,256]{1,0:T(8,128)(2,1)S(1)}, bf16[96,256]{1,0:T(8,128)(2,1)S(1)}, bf16[96,128]{1,0:T(8,128)(2,1)S(1)}, bf16[96,128]{1,0:T(8,128)(2,1)S(1)}) custom-call(f32[96,256]{1,0:T(8,128)} %keys_hbm.1, f32[96,256]{1,0:T(8,128)} %values_hbm.1, bf16[96,256]{1,0:T(8,128)(2,1)} %queries_hbm.1), custom_call_target="tpu_custom_call" | custom-call | tf_op jit(solution)/shard_map/residual_exchange/prepare/pallas_call | solution.py:181
  0.9 0.5 %collective-permute-start.7 = (bf16[256,5120]{1,0:T(8,128)(2,1)}, bf16[256,5120]{1,0:T(8,128)(2,1)S(1)}, u32[]{:S(2)}, u32[]{:S(2)}) collective-permute-start(bf16[256,5120]{1,0:T(8,128)(2,1)} %refs_2_.3), channel_id=1, source_target_pairs={{0,1},{1,0},{2,3},{3,2},{4,5},{5,4},{6,7},{7,6},{8,9},{9,8},{10,11... | collective-permute-start | bytes 7864328 | tf_op jit(solution)/shard_map/weight_swap/ppermute | solution.py:38
  1.5 2.6 %collective-permute-start.3 = (bf16[96,256]{1,0:T(8,128)(2,1)S(1)}, bf16[96,256]{1,0:T(8,128)(2,1)S(1)}, u32[]{:S(2)}, u32[]{:S(2)}) collective-permute-start(bf16[96,256]{1,0:T(8,128)(2,1)S(1)} %get-tuple-element.19), channel_id=1, source_target_pairs={{0,4},{4,8},{8,12},{12,0},{1,5},{5,9},{9,13},{13,1},{2,6},{6,10},{... | collective-permute-start | bytes 147464 | tf_op jit(solution)/shard_map/residual_exchange/ppermute | solution.py:38
  4.1 2.1 %collective-permute-start.1 = (bf16[96,256]{1,0:T(8,128)(2,1)S(1)}, bf16[96,256]{1,0:T(8,128)(2,1)S(1)}, u32[]{:S(2)}, u32[]{:S(2)}) collective-permute-start(bf16[96,256]{1,0:T(8,128)(2,1)S(1)} %get-tuple-element.19), channel_id=1, source_target_pairs={{0,12},{4,0},{8,4},{12,8},{1,13},{5,1},{9,5},{13,9},{2,14},{6,2},{... | collective-permute-start | bytes 147464 | tf_op jit(solution)/shard_map/residual_exchange/ppermute | solution.py:38
  6.2 0.9 %collective-permute-start.2 = (bf16[96,256]{1,0:T(8,128)(2,1)S(1)}, bf16[96,256]{1,0:T(8,128)(2,1)S(1)}, u32[]{:S(2)}, u32[]{:S(2)}) collective-permute-start(bf16[96,256]{1,0:T(8,128)(2,1)S(1)} %get-tuple-element.18.refs_0_), channel_id=1, source_target_pairs={{0,8},{4,12},{8,0},{12,4},{1,9},{5,13},{9,1},{13,5},{2,10},{6,14},... | collective-permute-start | bytes 147464 | tf_op jit(solution)/shard_map/residual_exchange/ppermute | solution.py:38
  7.1 1.6 %collective-permute-start = (bf16[96,128]{1,0:T(8,128)(2,1)S(1)}, bf16[96,128]{1,0:T(8,128)(2,1)S(1)}, u32[]{:S(2)}, u32[]{:S(2)}) collective-permute-start(bf16[96,128]{1,0:T(8,128)(2,1)S(1)} %get-tuple-element.15), channel_id=1, source_target_pairs={{0,4},{4,0},{8,12},{12,8},{1,5},{5,1},{9,13},{13,9},{2,6},{6,2},{1... | collective-permute-start | bytes 73736 | tf_op jit(solution)/shard_map/residual_exchange/ppermute | solution.py:42
  8.7 0.9 %stage.1 = (bf16[384,128]{1,0:T(8,128)(2,1)S(1)}, bf16[384,128]{1,0:T(8,128)(2,1)S(1)}) custom-call(bf16[384,256]{1,0:T(8,128)(2,1)} %held_k_hbm.1, bf16[384,256]{1,0:T(8,128)(2,1)} %held_v_hbm.1), custom_call_target="tpu_custom_call" | custom-call | flops 2000000000 | tf_op jit(solution)/shard_map/attention/stage/pallas_call | solution.py:204
  9.6 1.3 %collective-permute-done.q_other_ref = bf16[96,128]{1,0:T(8,128)(2,1)S(1)} collective-permute-done((bf16[96,128]{1,0:T(8,128)(2,1)S(1)}, bf16[96,128]{1,0:T(8,128)(2,1)S(1)}, u32[]{:S(2)}, u32[]{:S(2)}) %collective-permute-start) | collective-permute-done | bytes 24608 | tf_op jit(solution)/shard_map/residual_exchange/ppermute | solution.py:42
  11.0 0.0 collective-permute-done.3.refs_3_
  11.0 0.0 collective-permute-done.1.refs_1_
  11.0 0.7 %collective-permute-done.2.refs_2_ = bf16[96,256]{1,0:T(8,128)(2,1)S(1)} collective-permute-done((bf16[96,256]{1,0:T(8,128)(2,1)S(1)}, bf16[96,256]{1,0:T(8,128)(2,1)S(1)}, u32[]{:S(2)}, u32[]{:S(2)}) %collective-permute-start.2) | collective-permute-done | bytes 49184 | tf_op jit(solution)/shard_map/residual_exchange/ppermute | solution.py:38
  11.6 0.0 copy-start
  11.6 0.6 %attention.1 = (bf16[96,128]{1,0:T(8,128)(2,1)S(1)}, bf16[96,128]{1,0:T(8,128)(2,1)S(1)}) custom-call(bf16[96,128]{1,0:T(8,128)(2,1)S(1)} %get-tuple-element.14.q_own_ref, bf16[96,128]{1,0:T(8,128)(2,1)S(1)} %collective-permute-done.q_other_ref, bf16[384,128]{1,0:T(8,128)(2,1)S(1)} %get-tuple-element.16.keys_ref, ...), custom_call_target="tpu_custom_call" | custom-call | flops 2000000000 | tf_op jit(solution)/shard_map/attention/attention/pallas_call | solution.py:213
  12.2 0.1 collective-permute-start.6
  12.3 1.3 %collective-permute-start.4 = (bf16[96,128]{1,0:T(8,128)(2,1)S(1)}, bf16[96,128]{1,0:T(8,128)(2,1)S(1)}, u32[]{:S(2)}, u32[]{:S(2)}) collective-permute-start(bf16[96,128]{1,0:T(8,128)(2,1)S(1)} %get-tuple-element.21), channel_id=1, source_target_pairs={{0,4},{4,0},{8,12},{12,8},{1,5},{5,1},{9,13},{13,9},{2,6},{6,2},{1... | collective-permute-start | bytes 73736 | tf_op jit(solution)/shard_map/attended_exchange/ppermute | solution.py:42
  13.6 0.0 copy-start.2
  13.6 0.0 copy-start.1
  13.6 0.5 %collective-permute-start.5 = (bf16[96,128]{1,0:T(8,128)(2,1)S(1)}, bf16[96,128]{1,0:T(8,128)(2,1)S(1)}, u32[]{:S(2)}, u32[]{:S(2)}) collective-permute-start(bf16[96,128]{1,0:T(8,128)(2,1)S(1)} %get-tuple-element.20.refs_0_), channel_id=1, source_target_pairs={{0,1},{1,0},{2,3},{3,2},{4,5},{5,4},{6,7},{7,6},{8,9},{9,8},{10,11... | collective-permute-start | bytes 73736 | tf_op jit(solution)/shard_map/attended_exchange/ppermute | solution.py:38
  14.1 1.5 %collective-permute-done.6.refs_4_ = bf16[96,128]{1,0:T(8,128)(2,1)S(1)} collective-permute-done((bf16[96,128]{1,0:T(8,128)(2,1)S(1)}, bf16[96,128]{1,0:T(8,128)(2,1)S(1)}, u32[]{:S(2)}, u32[]{:S(2)}) %collective-permute-start.6) | collective-permute-done | bytes 24608 | tf_op jit(solution)/shard_map/attended_exchange/ppermute | solution.py:51
  15.7 0.7 %collective-permute-done.4.refs_1_ = bf16[96,128]{1,0:T(8,128)(2,1)S(1)} collective-permute-done((bf16[96,128]{1,0:T(8,128)(2,1)S(1)}, bf16[96,128]{1,0:T(8,128)(2,1)S(1)}, u32[]{:S(2)}, u32[]{:S(2)}) %collective-permute-start.4) | collective-permute-done | bytes 24608 | tf_op jit(solution)/shard_map/attended_exchange/ppermute | solution.py:42
  16.4 0.0 collective-permute-done.5.refs_3_
  16.4 0.0 collective-permute-done.7.refs_5_
  16.4 0.0 copy-done
  16.4 0.4 %sent_term.1 = bf16[96,1280]{1,0:T(8,128)(2,1)S(1)} custom-call(bf16[96,128]{1,0:T(8,128)(2,1)S(1)} %get-tuple-element.20.refs_0_, bf16[96,128]{1,0:T(8,128)(2,1)S(1)} %collective-permute-done.4.refs_1_, bf16[256,5120]{1,0:T(8,128)(2,1)S(1)} %copy-done, bf16[96,128]{1,0:T(8,128)(2,1)S(1)} %collective-permute-done.5.refs_3_, ...), custom_call_target="tpu_custom_call" | custom-call | flops 125829120 | tf_op jit(solution)/shard_map/projection/sent_term/pallas_call | solution.py:251
  16.8 1.6 %collective-permute-start.8 = (bf16[96,1280]{1,0:T(8,128)(2,1)S(1)}, bf16[96,1280]{1,0:T(8,128)(2,1)S(1)}, u32[]{:S(2)}, u32[]{:S(2)}) collective-permute-start(bf16[96,1280]{1,0:T(8,128)(2,1)S(1)} %sent_term.1), channel_id=1, source_target_pairs={{0,2},{2,0},{1,3},{3,1},{4,6},{6,4},{5,7},{7,5},{8,10},{10,8},{9,1... | collective-permute-start | bytes 737288 | tf_op jit(solution)/shard_map/projection/ppermute | solution.py:38
  18.4 0.0 copy-done.2
  18.4 0.0 copy-done.1
  18.4 0.4 %base.1.base_ref = f32[96,1280]{1,0:T(8,128)S(1)} custom-call(bf16[96,1280]{1,0:T(8,128)(2,1)S(1)} %copy-done.1, f32[1,1280]{1,0:T(1,128)S(1)} %reshape.3.gate_ref, bf16[96,128]{1,0:T(8,128)(2,1)S(1)} %get-tuple-element.20.refs_0_, bf16[96,128]{1,0:T(8,128)(2,1)S(1)} %collective-permute-done.4.refs_1_, bf16[256,5120]{1,0:T(8,128)(2,1)S(1)} %copy-done, ...), custom_call_target="tpu_custom_call" | custom-call | flops 125829120 | tf_op jit(solution)/shard_map/projection/base/pallas_call | solution.py:262
  18.8 6.1 %collective-permute-done.8.refs_0_ = bf16[96,1280]{1,0:T(8,128)(2,1)S(1)} collective-permute-done((bf16[96,1280]{1,0:T(8,128)(2,1)S(1)}, bf16[96,1280]{1,0:T(8,128)(2,1)S(1)}, u32[]{:S(2)}, u32[]{:S(2)}) %collective-permute-start.8) | collective-permute-done | bytes 245792 | tf_op jit(solution)/shard_map/projection/ppermute | solution.py:38
  24.9 0.8 %final.1 = bf16[96,1280]{1,0:T(8,128)(2,1)} custom-call(f32[96,1280]{1,0:T(8,128)S(1)} %base.1.base_ref, f32[1,1280]{1,0:T(1,128)S(1)} %reshape.3.gate_ref, bf16[96,1280]{1,0:T(8,128)(2,1)S(1)} %collective-permute-done.8.refs_0_), custom_call_target="tpu_custom_call" | custom-call | bytes 983040 | tf_op jit(solution)/shard_map/projection/final/pallas_call | solution.py:270
  (1 shorter events, 0.0 us)
Async XLA Ops:
  0.9 15.5 %collective-permute-start.7 = (bf16[256,5120]{1,0:T(8,128)(2,1)}, bf16[256,5120]{1,0:T(8,128)(2,1)S(1)}, u32[]{:S(2)}, u32[]{:S(2)}) collective-permute-start(bf16[256,5120]{1,0:T(8,128)(2,1)} %refs_2_.3), channel_id=1, source_target_pairs={{0,1},{1,0},{2,3},{3,2},{4,5},{5,4},{6,7},{7,6},{8,9},{9,8},{10,11... | collective-permute-start | bytes 7864328 | tf_op jit(solution)/shard_map/weight_swap/ppermute | solution.py:38
  1.5 9.5 %collective-permute-start.3 = (bf16[96,256]{1,0:T(8,128)(2,1)S(1)}, bf16[96,256]{1,0:T(8,128)(2,1)S(1)}, u32[]{:S(2)}, u32[]{:S(2)}) collective-permute-start(bf16[96,256]{1,0:T(8,128)(2,1)S(1)} %get-tuple-element.19), channel_id=1, source_target_pairs={{0,4},{4,8},{8,12},{12,0},{1,5},{5,9},{9,13},{13,1},{2,6},{6,10},{... | collective-permute-start | bytes 147464 | tf_op jit(solution)/shard_map/residual_exchange/ppermute | solution.py:38
  4.1 6.9 %collective-permute-start.1 = (bf16[96,256]{1,0:T(8,128)(2,1)S(1)}, bf16[96,256]{1,0:T(8,128)(2,1)S(1)}, u32[]{:S(2)}, u32[]{:S(2)}) collective-permute-start(bf16[96,256]{1,0:T(8,128)(2,1)S(1)} %get-tuple-element.19), channel_id=1, source_target_pairs={{0,12},{4,0},{8,4},{12,8},{1,13},{5,1},{9,5},{13,9},{2,14},{6,2},{... | collective-permute-start | bytes 147464 | tf_op jit(solution)/shard_map/residual_exchange/ppermute | solution.py:38
  6.2 5.4 %collective-permute-start.2 = (bf16[96,256]{1,0:T(8,128)(2,1)S(1)}, bf16[96,256]{1,0:T(8,128)(2,1)S(1)}, u32[]{:S(2)}, u32[]{:S(2)}) collective-permute-start(bf16[96,256]{1,0:T(8,128)(2,1)S(1)} %get-tuple-element.18.refs_0_), channel_id=1, source_target_pairs={{0,8},{4,12},{8,0},{12,4},{1,9},{5,13},{9,1},{13,5},{2,10},{6,14},... | collective-permute-start | bytes 147464 | tf_op jit(solution)/shard_map/residual_exchange/ppermute | solution.py:38
  7.1 3.8 %collective-permute-start = (bf16[96,128]{1,0:T(8,128)(2,1)S(1)}, bf16[96,128]{1,0:T(8,128)(2,1)S(1)}, u32[]{:S(2)}, u32[]{:S(2)}) collective-permute-start(bf16[96,128]{1,0:T(8,128)(2,1)S(1)} %get-tuple-element.15), channel_id=1, source_target_pairs={{0,4},{4,0},{8,12},{12,8},{1,5},{5,1},{9,13},{13,9},{2,6},{6,2},{1... | collective-permute-start | bytes 73736 | tf_op jit(solution)/shard_map/residual_exchange/ppermute | solution.py:42
  11.6 4.8 %copy-start = (bf16[256,5120]{1,0:T(8,128)(2,1)S(1)}, bf16[256,5120]{1,0:T(8,128)(2,1)}, u32[]{:S(2)}) copy-start(bf16[256,5120]{1,0:T(8,128)(2,1)} %refs_2_.3) | copy-start | bytes 7864324
  12.2 3.5 %collective-permute-start.6 = (bf16[96,128]{1,0:T(8,128)(2,1)S(1)}, bf16[96,128]{1,0:T(8,128)(2,1)S(1)}, u32[]{:S(2)}, u32[]{:S(2)}) collective-permute-start(bf16[96,128]{1,0:T(8,128)(2,1)S(1)} %get-tuple-element.21), channel_id=1, source_target_pairs={{0,5},{1,4},{4,1},{5,0},{8,13},{9,12},{12,9},{13,8},{2,7},{3,6},{6... | collective-permute-start | bytes 73736 | tf_op jit(solution)/shard_map/attended_exchange/ppermute | solution.py:51
  12.3 4.2 %collective-permute-start.4 = (bf16[96,128]{1,0:T(8,128)(2,1)S(1)}, bf16[96,128]{1,0:T(8,128)(2,1)S(1)}, u32[]{:S(2)}, u32[]{:S(2)}) collective-permute-start(bf16[96,128]{1,0:T(8,128)(2,1)S(1)} %get-tuple-element.21), channel_id=1, source_target_pairs={{0,4},{4,0},{8,12},{12,8},{1,5},{5,1},{9,13},{13,9},{2,6},{6,2},{1... | collective-permute-start | bytes 73736 | tf_op jit(solution)/shard_map/attended_exchange/ppermute | solution.py:42
  13.6 4.8 %copy-start.2 = (f32[1280]{0:T(1024)S(1)}, f32[1280]{0:T(1024)}, u32[]{:S(2)}) copy-start(f32[1280]{0:T(1024)} %param.15) | copy-start | bytes 15364
  13.6 4.8 %copy-start.1 = (bf16[96,1280]{1,0:T(8,128)(2,1)S(1)}, bf16[96,1280]{1,0:T(8,128)(2,1)}, u32[]{:S(2)}) copy-start(bf16[96,1280]{1,0:T(8,128)(2,1)} %hidden_ref.1) | copy-start | bytes 737284
  13.6 2.8 %collective-permute-start.5 = (bf16[96,128]{1,0:T(8,128)(2,1)S(1)}, bf16[96,128]{1,0:T(8,128)(2,1)S(1)}, u32[]{:S(2)}, u32[]{:S(2)}) collective-permute-start(bf16[96,128]{1,0:T(8,128)(2,1)S(1)} %get-tuple-element.20.refs_0_), channel_id=1, source_target_pairs={{0,1},{1,0},{2,3},{3,2},{4,5},{5,4},{6,7},{7,6},{8,9},{9,8},{10,11... | collective-permute-start | bytes 73736 | tf_op jit(solution)/shard_map/attended_exchange/ppermute | solution.py:38
  16.8 8.0 %collective-permute-start.8 = (bf16[96,1280]{1,0:T(8,128)(2,1)S(1)}, bf16[96,1280]{1,0:T(8,128)(2,1)S(1)}, u32[]{:S(2)}, u32[]{:S(2)}) collective-permute-start(bf16[96,1280]{1,0:T(8,128)(2,1)S(1)} %sent_term.1), channel_id=1, source_target_pairs={{0,2},{2,0},{1,3},{3,1},{4,6},{6,4},{5,7},{7,5},{8,10},{10,8},{9,1... | collective-permute-start | bytes 737288 | tf_op jit(solution)/shard_map/projection/ppermute | solution.py:38

commit v17 on v15

--- a/solution.py
+++ b/solution.py
@@ -49,12 +49,47 @@
     return lax.ppermute(array, axis, [(i, (i + step) % size) for i in range(size)])
 
 
-def gather_steps(patches):
-    return [3, 1, 2] if patches == 4 else list(range(patches - 1, 0, -1))
+FIRST = ((0, 2), (2, 3), (3, 1), (1, 0))
+SECOND = ((0, 1), (1, 3), (3, 2), (2, 0))
+MIDDLE = ((1, 2), (2, 1), (0, 0), (3, 3))
+PASSED = ((0, 1), (1, 0), (2, 3), (3, 2))
+
+
+def gather(own, patches):
+    if patches != 4:
+        return [own] + [shift(own, "patch", patches, step) for step in range(patches - 1, 0, -1)]
+    first = lax.ppermute(own, "patch", FIRST)
+    second = lax.ppermute(own, "patch", SECOND)
+    middle = lax.ppermute(own, "patch", MIDDLE)
+    passed = lax.ppermute(first, "patch", PASSED)
+    return [own, middle, second, first, passed]
+
+
+def gathered(refs):
+    blocks = [ref[...] for ref in refs]
+    if len(blocks) != 5:
+        return blocks
+    place = lax.axis_index("patch")
+    inner = jnp.logical_and(place > 0, place < 3)
+    own, middle, second, first, passed = blocks
+    return [own, first, second, jnp.where(inner, middle, passed)]
+
+
+def by_place(place, entries):
+    value = jnp.int32(entries[0])
+    for i, entry in enumerate(entries[1:], 1):
+        value = jnp.where(place == i, jnp.int32(entry), value)
+    return value
 
 
 def gather_sources(patches, place):
-    return [place] + [lax.rem(place + patches - step, patches) for step in gather_steps(patches)]
+    if patches != 4:
+        return [place] + [
+            lax.rem(place + patches - step, patches) for step in range(patches - 1, 0, -1)
+        ]
+    return [place] + [
+        by_place(place, entries) for entries in ((1, 3, 0, 2), (2, 0, 3, 1), (3, 2, 1, 0))
+    ]
 
 
 def early_weight_kernel(subs, columns, early, weight_ref, out_ref, sems):
@@ -109,7 +144,7 @@
 def attention_kernel(scale, q_ref, products_ref, values_ref, *refs):
     block_refs, out_ref = refs[:-1], refs[-1]
     rows, width = q_ref.shape
-    blocks = jnp.concatenate([ref[...] for ref in block_refs], axis=0)
+    blocks = jnp.concatenate(gathered(block_refs), axis=0)
     for head in range(width // HD):
         cols = slice(head * HD, (head + 1) * HD)
         value_cols = slice(width + head * HD, width + (head + 1) * HD)
@@ -218,9 +253,7 @@
                 lax.pad(key_change, low, ((0, 0, 0), (0, width, 0))),
                 lax.pad(value_change, low, ((0, 0, 0), (width, 0, 0))),
             ).astype(jnp.bfloat16)
-            blocks = [residual] + [
-                shift(residual, "patch", patches, step) for step in gather_steps(patches)
-            ]
+            blocks = gather(residual, patches)
 
         with jax.named_scope("weight_swap"):
             swapped, _ = lax.optimization_barrier((out_weight, residual))

time: 24.9 us -> 25.9 us (1.040)
  waiting for transfers between devices: 6.67 us -> 7.29 us
  starting transfers between devices: 12.5 us -> 12.8 us
    ppermute x0 -> x4, starting transfers between devices: none -> 9.04 us  [the longest x1 4.73 us: gather(): passed = lax.ppermute(first, 'patch', PASSED)]
    ppermute x9 -> x6, starting transfers between devices: 12.5 us -> 3.77 us  [shift(): lax.ppermute(array, axis, [(i, (i + step) % size) for i in range(size)])]
    ppermute x0 -> x4, waiting for transfers between devices: none -> 1.29 us  [the longest x1 1.28 us: gather(): passed = lax.ppermute(first, 'patch', PASSED)]
    ppermute x9 -> x6, waiting for transfers between devices: 6.67 us -> 6 us  [shift(): lax.ppermute(array, axis, [(i, (i + step) % size) for i in range(size)])]
  transfers between devices with their start and end apart: 9 -> 10, of which waited for: 5 -> 5; matrix products, arithmetic and copies ran while one was open for 0% -> 0% of each run, Pallas kernels for 15% -> 14%
where the time goes in v17:
time: 25.9 us; the launch traced here: 25.6 us
  starting transfers between devices  12.8 us (49%)
  waiting for transfers between devices  7.29 us (28%)
  Pallas kernels  4.43 us (17%)
  other arithmetic  0.95 us (4%)
    ppermute x6, waiting for transfers between devices, shift(): lax.ppermute(array, axis, [(i, (i + step) % size) for i in range(size)])  6 us
    ppermute x1, starting transfers between devices, gather(): passed = lax.ppermute(first, 'patch', PASSED)  4.73 us
    ppermute x6, starting transfers between devices, shift(): lax.ppermute(array, axis, [(i, (i + step) % size) for i in range(size)])  3.77 us
    ppermute x1, starting transfers between devices, gather(): first = lax.ppermute(own, 'patch', FIRST)  3.65 us
    pallas_call x1, Pallas kernels, per_device(): call(functools.partial(stage_kernel, patches), [jax.ShapeDtypeStruct((row...  1.29 us
    ppermute x1, waiting for transfers between devices, gather(): passed = lax.ppermute(first, 'patch', PASSED)  1.28 us
    pallas_call x1, Pallas kernels, per_device(): call(functools.partial(early_weight_kernel, subs, columns, early), jax.Sh...  1 us
    convert_element_type x1, other arithmetic, per_device(): residual = jnp.maximum(lax.pad(key_change, low, ((0, 0, 0), (0, width, 0)...  0.95 us
  transfers between devices with their start and end apart: 10, of which 5 were waited for; matrix products, arithmetic and copies ran while one was open for 0% of the time, Pallas kernels for 14%

profile of v17, /device:TPU:0, one launch (start us, length us, event | category | flops | bytes accessed | tf_op | source)
XLA Modules:
  0.0 25.6 jit_solution(10668671388745933580)
XLA Ops:
  0.0 1.0 %maximum_convert_fusion.refs_0_ = bf16[96,512]{1,0:T(8,128)(2,1)S(1)} fusion(f32[96,256]{1,0:T(8,128)} %param.12, f32[96,256]{1,0:T(8,128)} %param.11), kind=kLoop, calls=%fused_computation | loop fusion | flops 196608 | bytes 294912 | tf_op jit(solution)/shard_map/residual_gather/convert_element_type | solution.py:255
  1.0 0.5 %collective-permute-start.5 = (bf16[256,5120]{1,0:T(8,128)(2,1)}, bf16[256,5120]{1,0:T(8,128)(2,1)S(1)}, u32[]{:S(2)}, u32[]{:S(2)}) collective-permute-start(bf16[256,5120]{1,0:T(8,128)(2,1)} %refs_1_.3), channel_id=1, source_target_pairs={{0,1},{1,0},{2,3},{3,2},{4,5},{5,4},{6,7},{7,6},{8,9},{9,8},{10,11... | collective-permute-start | bytes 7864328 | tf_op jit(solution)/shard_map/weight_swap/ppermute | solution.py:49
  1.5 3.7 %collective-permute-start.2 = (bf16[96,512]{1,0:T(8,128)(2,1)S(1)}, bf16[96,512]{1,0:T(8,128)(2,1)S(1)}, u32[]{:S(2)}, u32[]{:S(2)}) collective-permute-start(bf16[96,512]{1,0:T(8,128)(2,1)S(1)} %maximum_convert_fusion.refs_0_), channel_id=1, source_target_pairs={{0,8},{8,12},{12,4},{4,0},{1,9},{9,13},{13,5},{5,1},{2,10},{10,14}... | collective-permute-start | bytes 294920 | tf_op jit(solution)/shard_map/residual_gather/ppermute | solution.py:61
  5.1 0.0 collective-permute-start.1
  5.1 0.7 %collective-permute-start = (bf16[96,512]{1,0:T(8,128)(2,1)S(1)}, bf16[96,512]{1,0:T(8,128)(2,1)S(1)}, u32[]{:S(2)}, u32[]{:S(2)}) collective-permute-start(bf16[96,512]{1,0:T(8,128)(2,1)S(1)} %maximum_convert_fusion.refs_0_), channel_id=1, source_target_pairs={{4,8},{8,4},{0,0},{12,12},{5,9},{9,5},{1,1},{13,13},{6,10},{10,6},... | collective-permute-start | bytes 294920 | tf_op jit(solution)/shard_map/residual_gather/ppermute | solution.py:63
  5.8 1.0 %early_weight.1 = bf16[256,512]{1,0:T(8,128)(2,1)S(1)} custom-call(bf16[256,5120]{1,0:T(8,128)(2,1)} %refs_1_.3), custom_call_target="tpu_custom_call" | custom-call | bytes 524288 | tf_op jit(solution)/shard_map/early_weight/early_weight/pallas_call | solution.py:264
  6.8 1.6 %collective-permute-start.7 = (bf16[256,512]{1,0:T(8,128)(2,1)S(1)}, bf16[256,512]{1,0:T(8,128)(2,1)S(1)}, u32[]{:S(2)}, u32[]{:S(2)}) collective-permute-start(bf16[256,512]{1,0:T(8,128)(2,1)S(1)} %early_weight.1), channel_id=1, source_target_pairs={{0,2},{2,0},{1,3},{3,1},{4,6},{6,4},{5,7},{7,5},{8,10},{10,8},{9,1... | collective-permute-start | bytes 786440 | tf_op jit(solution)/shard_map/early_weight/ppermute | solution.py:49
  8.4 0.0 collective-permute-done.2.refs_3_
  8.4 4.7 %collective-permute-start.3 = (bf16[96,512]{1,0:T(8,128)(2,1)S(1)}, bf16[96,512]{1,0:T(8,128)(2,1)S(1)}, u32[]{:S(2)}, u32[]{:S(2)}) collective-permute-start(bf16[96,512]{1,0:T(8,128)(2,1)S(1)} %collective-permute-done.2.refs_3_), channel_id=1, source_target_pairs={{0,4},{4,0},{8,12},{12,8},{1,5},{5,1},{9,13},{13,9},{2,6},{6,2},{1... | collective-permute-start | bytes 294920 | tf_op jit(solution)/shard_map/residual_gather/ppermute | solution.py:64
  13.1 1.3 %stage.1 = (bf16[96,256]{1,0:T(8,128)(2,1)S(1)}, f32[2,96,384]{2,1,0:T(8,128)S(1)}, bf16[384,256]{1,0:T(8,128)(2,1)S(1)}) custom-call(bf16[96,256]{1,0:T(8,128)(2,1)} %q_hbm.1, bf16[384,256]{1,0:T(8,128)(2,1)} %held_k_hbm.1, bf16[384,256]{1,0:T(8,128)(2,1)} %held_v_hbm.1), custom_call_target="tpu_custom_call" | custom-call | flops 2000000000 | tf_op jit(solution)/shard_map/attention/stage/pallas_call | solution.py:294
  14.4 0.0 collective-permute-done.1.refs_2_
  14.4 0.0 collective-permute-done.refs_1_
  14.4 1.3 %collective-permute-done.3.refs_4_ = bf16[96,512]{1,0:T(8,128)(2,1)S(1)} collective-permute-done((bf16[96,512]{1,0:T(8,128)(2,1)S(1)}, bf16[96,512]{1,0:T(8,128)(2,1)S(1)}, u32[]{:S(2)}, u32[]{:S(2)}) %collective-permute-start.3) | collective-permute-done | bytes 98336 | tf_op jit(solution)/shard_map/residual_gather/ppermute | solution.py:64
  15.7 0.0 copy-start
  15.7 0.5 %attention.1.refs_0_ = bf16[96,256]{1,0:T(8,128)(2,1)S(1)} custom-call(bf16[96,256]{1,0:T(8,128)(2,1)S(1)} %get-tuple-element.9.q_ref, f32[2,96,384]{2,1,0:T(8,128)S(1)} %get-tuple-element.10.products_ref, bf16[384,256]{1,0:T(8,128)(2,1)S(1)} %get-tuple-element.11.values_ref, bf16[96,512]{1,0:T(8,128)(2,1)S(1)} %maximum_convert_fusion.refs_0_, ...), custom_call_target="tpu_custom_call" | custom-call | flops 2000000000 | tf_op jit(solution)/shard_map/attention/attention/pallas_call | solution.py:310
  16.2 0.0 copy-start.2
  16.2 0.0 copy-start.1
  16.2 0.1 collective-permute-start.4
  16.3 0.6 %collective-permute-start.6 = (bf16[96,256]{1,0:T(8,128)(2,1)S(1)}, bf16[96,256]{1,0:T(8,128)(2,1)S(1)}, u32[]{:S(2)}, u32[]{:S(2)}) collective-permute-start(bf16[96,256]{1,0:T(8,128)(2,1)S(1)} %attention.1.refs_0_), channel_id=1, source_target_pairs={{0,2},{2,0},{1,3},{3,1},{4,6},{6,4},{5,7},{7,5},{8,10},{10,8},{9,1... | collective-permute-start | bytes 147464 | tf_op jit(solution)/shard_map/attended_swap/ppermute | solution.py:49
  16.9 0.6 %collective-permute-done.4.refs_2_ = bf16[96,256]{1,0:T(8,128)(2,1)S(1)} collective-permute-done((bf16[96,256]{1,0:T(8,128)(2,1)S(1)}, bf16[96,256]{1,0:T(8,128)(2,1)S(1)}, u32[]{:S(2)}, u32[]{:S(2)}) %collective-permute-start.4) | collective-permute-done | bytes 49184 | tf_op jit(solution)/shard_map/attended_swap/ppermute | solution.py:49
  17.5 0.0 collective-permute-done.5.refs_3_
  17.5 0.0 copy-done
  17.6 0.3 %sent_term.1 = bf16[96,1024]{1,0:T(8,128)(2,1)S(1)} custom-call(bf16[96,256]{1,0:T(8,128)(2,1)S(1)} %attention.1.refs_0_, bf16[256,5120]{1,0:T(8,128)(2,1)S(1)} %copy-done, bf16[96,256]{1,0:T(8,128)(2,1)S(1)} %collective-permute-done.4.refs_2_, bf16[256,5120]{1,0:T(8,128)(2,1)S(1)} %collective-permute-done.5.refs_3_), custom_call_target="tpu_custom_call" | custom-call | flops 125829120 | tf_op jit(solution)/shard_map/projection/sent_term/pallas_call | solution.py:333
  17.9 1.0 %collective-permute-start.9 = (bf16[96,1024]{1,0:T(8,128)(2,1)S(1)}, bf16[96,1024]{1,0:T(8,128)(2,1)S(1)}, u32[]{:S(2)}, u32[]{:S(2)}) collective-permute-start(bf16[96,1024]{1,0:T(8,128)(2,1)S(1)} %sent_term.1), channel_id=1, source_target_pairs={{0,2},{2,0},{1,3},{3,1},{4,6},{6,4},{5,7},{7,5},{8,10},{10,8},{9,1... | collective-permute-start | bytes 589832 | tf_op jit(solution)/shard_map/projection/ppermute | solution.py:49
  18.8 1.7 %collective-permute-done.6.attended_ref = bf16[96,256]{1,0:T(8,128)(2,1)S(1)} collective-permute-done((bf16[96,256]{1,0:T(8,128)(2,1)S(1)}, bf16[96,256]{1,0:T(8,128)(2,1)S(1)}, u32[]{:S(2)}, u32[]{:S(2)}) %collective-permute-start.6) | collective-permute-done | bytes 49184 | tf_op jit(solution)/shard_map/attended_swap/ppermute | solution.py:49
  20.5 0.0 collective-permute-done.7.weight_ref
  20.5 0.1 collective-permute-start.8
  20.6 0.0 copy-done.2
  20.6 0.0 copy-done.1
  20.6 0.4 %base.1.base_ref = f32[96,1280]{1,0:T(8,128)S(1)} custom-call(bf16[96,1280]{1,0:T(8,128)(2,1)S(1)} %copy-done.1, f32[1,1280]{1,0:T(1,128)S(1)} %reshape.3.gate_ref, bf16[96,256]{1,0:T(8,128)(2,1)S(1)} %attention.1.refs_0_, bf16[256,5120]{1,0:T(8,128)(2,1)S(1)} %copy-done, bf16[96,256]{1,0:T(8,128)(2,1)S(1)} %collective-permute-done.4.refs_2_, ...), custom_call_target="tpu_custom_call" | custom-call | flops 125829120 | tf_op jit(solution)/shard_map/projection/base/pallas_call | solution.py:344
  21.0 1.0 %collective-permute-done.8.packed_ref = bf16[352,256]{1,0:T(8,128)(2,1)S(1)} collective-permute-done((bf16[352,256]{1,0:T(8,128)(2,1)S(1)}, bf16[352,256]{1,0:T(8,128)(2,1)S(1)}, u32[]{:S(2)}, u32[]{:S(2)}) %collective-permute-start.8) | collective-permute-done | bytes 180256 | tf_op jit(solution)/shard_map/projection/ppermute | solution.py:49
  22.0 0.2 early.1.base_ref
  22.2 2.7 %collective-permute-done.9.refs_0_ = bf16[96,1024]{1,0:T(8,128)(2,1)S(1)} collective-permute-done((bf16[96,1024]{1,0:T(8,128)(2,1)S(1)}, bf16[96,1024]{1,0:T(8,128)(2,1)S(1)}, u32[]{:S(2)}, u32[]{:S(2)}) %collective-permute-start.9) | collective-permute-done | bytes 196640 | tf_op jit(solution)/shard_map/projection/ppermute | solution.py:49
  24.9 0.7 %final.1 = bf16[96,1280]{1,0:T(8,128)(2,1)} custom-call(f32[96,1280]{1,0:T(8,128)S(1)} %early.1.base_ref, f32[1,1280]{1,0:T(1,128)S(1)} %reshape.3.gate_ref, bf16[96,1024]{1,0:T(8,128)(2,1)S(1)} %collective-permute-done.9.refs_0_), custom_call_target="tpu_custom_call" | custom-call | bytes 983040 | tf_op jit(solution)/shard_map/projection/final/pallas_call | solution.py:370
  (2 shorter events, 0.0 us)
Async XLA Ops:
  1.0 16.6 %collective-permute-start.5 = (bf16[256,5120]{1,0:T(8,128)(2,1)}, bf16[256,5120]{1,0:T(8,128)(2,1)S(1)}, u32[]{:S(2)}, u32[]{:S(2)}) collective-permute-start(bf16[256,5120]{1,0:T(8,128)(2,1)} %refs_1_.3), channel_id=1, source_target_pairs={{0,1},{1,0},{2,3},{3,2},{4,5},{5,4},{6,7},{7,6},{8,9},{9,8},{10,11... | collective-permute-start | bytes 7864328 | tf_op jit(solution)/shard_map/weight_swap/ppermute | solution.py:49
  1.5 6.9 %collective-permute-start.2 = (bf16[96,512]{1,0:T(8,128)(2,1)S(1)}, bf16[96,512]{1,0:T(8,128)(2,1)S(1)}, u32[]{:S(2)}, u32[]{:S(2)}) collective-permute-start(bf16[96,512]{1,0:T(8,128)(2,1)S(1)} %maximum_convert_fusion.refs_0_), channel_id=1, source_target_pairs={{0,8},{8,12},{12,4},{4,0},{1,9},{9,13},{13,5},{5,1},{2,10},{10,14}... | collective-permute-start | bytes 294920 | tf_op jit(solution)/shard_map/residual_gather/ppermute | solution.py:61
  5.1 9.3 %collective-permute-start.1 = (bf16[96,512]{1,0:T(8,128)(2,1)S(1)}, bf16[96,512]{1,0:T(8,128)(2,1)S(1)}, u32[]{:S(2)}, u32[]{:S(2)}) collective-permute-start(bf16[96,512]{1,0:T(8,128)(2,1)S(1)} %maximum_convert_fusion.refs_0_), channel_id=1, source_target_pairs={{0,4},{4,12},{12,8},{8,0},{1,5},{5,13},{13,9},{9,1},{2,6},{6,14},{... | collective-permute-start | bytes 294920 | tf_op jit(solution)/shard_map/residual_gather/ppermute | solution.py:62
  5.1 9.3 %collective-permute-start = (bf16[96,512]{1,0:T(8,128)(2,1)S(1)}, bf16[96,512]{1,0:T(8,128)(2,1)S(1)}, u32[]{:S(2)}, u32[]{:S(2)}) collective-permute-start(bf16[96,512]{1,0:T(8,128)(2,1)S(1)} %maximum_convert_fusion.refs_0_), channel_id=1, source_target_pairs={{4,8},{8,4},{0,0},{12,12},{5,9},{9,5},{1,1},{13,13},{6,10},{10,6},... | collective-permute-start | bytes 294920 | tf_op jit(solution)/shard_map/residual_gather/ppermute | solution.py:63
  6.8 13.7 %collective-permute-start.7 = (bf16[256,512]{1,0:T(8,128)(2,1)S(1)}, bf16[256,512]{1,0:T(8,128)(2,1)S(1)}, u32[]{:S(2)}, u32[]{:S(2)}) collective-permute-start(bf16[256,512]{1,0:T(8,128)(2,1)S(1)} %early_weight.1), channel_id=1, source_target_pairs={{0,2},{2,0},{1,3},{3,1},{4,6},{6,4},{5,7},{7,5},{8,10},{10,8},{9,1... | collective-permute-start | bytes 786440 | tf_op jit(solution)/shard_map/early_weight/ppermute | solution.py:49
  8.4 7.3 %collective-permute-start.3 = (bf16[96,512]{1,0:T(8,128)(2,1)S(1)}, bf16[96,512]{1,0:T(8,128)(2,1)S(1)}, u32[]{:S(2)}, u32[]{:S(2)}) collective-permute-start(bf16[96,512]{1,0:T(8,128)(2,1)S(1)} %collective-permute-done.2.refs_3_), channel_id=1, source_target_pairs={{0,4},{4,0},{8,12},{12,8},{1,5},{5,1},{9,13},{13,9},{2,6},{6,2},{1... | collective-permute-start | bytes 294920 | tf_op jit(solution)/shard_map/residual_gather/ppermute | solution.py:64
  15.7 1.9 %copy-start = (bf16[256,5120]{1,0:T(8,128)(2,1)S(1)}, bf16[256,5120]{1,0:T(8,128)(2,1)}, u32[]{:S(2)}) copy-start(bf16[256,5120]{1,0:T(8,128)(2,1)} %refs_1_.3) | copy-start | bytes 7864324
  16.2 4.4 %copy-start.2 = (f32[1280]{0:T(1024)S(1)}, f32[1280]{0:T(1024)}, u32[]{:S(2)}) copy-start(f32[1280]{0:T(1024)} %param.15) | copy-start | bytes 15364
  16.2 4.4 %copy-start.1 = (bf16[96,1280]{1,0:T(8,128)(2,1)S(1)}, bf16[96,1280]{1,0:T(8,128)(2,1)}, u32[]{:S(2)}) copy-start(bf16[96,1280]{1,0:T(8,128)(2,1)} %hidden_ref.1) | copy-start | bytes 737284
  16.2 1.3 %collective-permute-start.4 = (bf16[96,256]{1,0:T(8,128)(2,1)S(1)}, bf16[96,256]{1,0:T(8,128)(2,1)S(1)}, u32[]{:S(2)}, u32[]{:S(2)}) collective-permute-start(bf16[96,256]{1,0:T(8,128)(2,1)S(1)} %attention.1.refs_0_), channel_id=1, source_target_pairs={{0,1},{1,0},{2,3},{3,2},{4,5},{5,4},{6,7},{7,6},{8,9},{9,8},{10,11... | collective-permute-start | bytes 147464 | tf_op jit(solution)/shard_map/attended_swap/ppermute | solution.py:49
  16.3 4.2 %collective-permute-start.6 = (bf16[96,256]{1,0:T(8,128)(2,1)S(1)}, bf16[96,256]{1,0:T(8,128)(2,1)S(1)}, u32[]{:S(2)}, u32[]{:S(2)}) collective-permute-start(bf16[96,256]{1,0:T(8,128)(2,1)S(1)} %attention.1.refs_0_), channel_id=1, source_target_pairs={{0,2},{2,0},{1,3},{3,1},{4,6},{6,4},{5,7},{7,5},{8,10},{10,8},{9,1... | collective-permute-start | bytes 147464 | tf_op jit(solution)/shard_map/attended_swap/ppermute | solution.py:49
  17.9 7.0 %collective-permute-start.9 = (bf16[96,1024]{1,0:T(8,128)(2,1)S(1)}, bf16[96,1024]{1,0:T(8,128)(2,1)S(1)}, u32[]{:S(2)}, u32[]{:S(2)}) collective-permute-start(bf16[96,1024]{1,0:T(8,128)(2,1)S(1)} %sent_term.1), channel_id=1, source_target_pairs={{0,2},{2,0},{1,3},{3,1},{4,6},{6,4},{5,7},{7,5},{8,10},{10,8},{9,1... | collective-permute-start | bytes 589832 | tf_op jit(solution)/shard_map/projection/ppermute | solution.py:49
  20.5 1.5 %collective-permute-start.8 = (bf16[352,256]{1,0:T(8,128)(2,1)S(1)}, bf16[352,256]{1,0:T(8,128)(2,1)S(1)}, u32[]{:S(2)}, u32[]{:S(2)}) collective-permute-start(bf16[352,256]{1,0:T(8,128)(2,1)S(1)} %pack.1), channel_id=1, source_target_pairs={{0,1},{1,0},{2,3},{3,2},{4,5},{5,4},{6,7},{7,6},{8,9},{9,8},{10,11... | collective-permute-start | bytes 540680 | tf_op jit(solution)/shard_map/projection/ppermute | solution.py:49

commit v18 on v14

--- a/solution.py
+++ b/solution.py
@@ -177,26 +177,20 @@
 
 def pack_kernel(early, attended_ref, weight_ref, out_ref):
     rows, width = attended_ref.shape
-    for i in range(width // early):
-        out_ref[i * rows : (i + 1) * rows, :] = attended_ref[:, i * early : (i + 1) * early]
     other = pl.multiple_of((1 - lax.axis_index("sub")) * early, LANES)
-    out_ref[rows * (width // early) :, :] = weight_ref[:, pl.ds(other, early)]
+    out_ref[:rows, :width] = attended_ref[...]
+    out_ref[rows:, :early] = weight_ref[:, pl.ds(other, early)]
 
 
 def early_kernel(early, base_ref, gate_ref, attended_ref, weight_ref, packed_ref, out_ref):
     rows, width = attended_ref.shape
-    pieces = width // early
     mine = pl.multiple_of(lax.axis_index("sub") * early, LANES)
     total = jnp.dot(
         attended_ref[...],
         weight_ref[:, pl.ds(mine, early)],
         preferred_element_type=jnp.float32,
     ) + jnp.dot(
-        jnp.concatenate(
-            [packed_ref[i * rows : (i + 1) * rows, :] for i in range(pieces)], axis=1
-        ),
-        packed_ref[pieces * rows :, :],
-        preferred_element_type=jnp.float32,
+        packed_ref[:rows, :width], packed_ref[rows:, :early], preferred_element_type=jnp.float32
     )
     out_ref[...] = base_ref[...]
     out_ref[:, :early] = base_ref[:, :early] + gate_ref[:, :early] * total
@@ -212,20 +206,6 @@
         columns = hidden_in.shape[1]
 
         early = EARLY if heads == 2 and columns % LANES == 0 and columns > 4 * LANES else 0
-        with jax.named_scope("residual_gather"):
-            low = jnp.float32(-jnp.inf)
-            residual = jnp.maximum(
-                lax.pad(key_change, low, ((0, 0, 0), (0, width, 0))),
-                lax.pad(value_change, low, ((0, 0, 0), (width, 0, 0))),
-            ).astype(jnp.bfloat16)
-            blocks = [residual] + [
-                shift(residual, "patch", patches, step) for step in gather_steps(patches)
-            ]
-
-        with jax.named_scope("weight_swap"):
-            swapped, _ = lax.optimization_barrier((out_weight, residual))
-            weights = [out_weight] + [shift(swapped, "sub", subs, i) for i in range(1, subs)]
-
         if early:
             with jax.named_scope("early_weight"):
                 early_weight = call(
@@ -237,6 +217,25 @@
                     moved=4 * width * subs * early,
                     scratch_shapes=[pltpu.SemaphoreType.DMA((subs,))],
                 )(in_hbm(out_weight))
+                key_change, value_change, early_weight = lax.optimization_barrier(
+                    (key_change, value_change, early_weight)
+                )
+
+        with jax.named_scope("residual_gather"):
+            low = jnp.float32(-jnp.inf)
+            residual = jnp.maximum(
+                lax.pad(key_change, low, ((0, 0, 0), (0, width, 0))),
+                lax.pad(value_change, low, ((0, 0, 0), (width, 0, 0))),
+            ).astype(jnp.bfloat16)
+            blocks = [residual] + [
+                shift(residual, "patch", patches, step) for step in gather_steps(patches)
+            ]
+
+        with jax.named_scope("weight_swap"):
+            weights = [out_weight] + [shift(out_weight, "sub", subs, i) for i in range(1, subs)]
+
+        if early:
+            with jax.named_scope("early_weight"):
                 early_weight = shift(early_weight, "head", heads, 1)
 
         def weight_and_start(i, step, skip=0):
@@ -319,7 +318,7 @@
             if early:
                 packed = call(
                     functools.partial(pack_kernel, early),
-                    jax.ShapeDtypeStruct((rows * (width // early) + width, early), jnp.bfloat16),
+                    jax.ShapeDtypeStruct((rows + width, max(early, width)), jnp.bfloat16),
                     [IN_VMEM] * 2,
                     IN_VMEM,
                     "pack",

time: 24.4 us -> 24.4 us (level)
  waiting for transfers between devices: 7.07 us -> 8.13 us
  other arithmetic: 0.95 us -> 0.01 us
    ppermute x9, waiting for transfers between devices: 7.07 us -> 8.13 us  [shift(): lax.ppermute(array, axis, [(i, (i + step) % size) for i in range(size)])]
    convert_element_type x1, other arithmetic: 0.95 us -> 0.01 us  [per_device(): residual = jnp.maximum(lax.pad(key_change, low, ((0, 0, 0), (0, width, 0)...]
where the time goes in v18:
time: 24.4 us; the launch traced here: 24.2 us
  starting transfers between devices  11.5 us (47%)
  waiting for transfers between devices  8.13 us (33%)
  Pallas kernels  4.43 us (18%)
    ppermute x9, starting transfers between devices, shift(): lax.ppermute(array, axis, [(i, (i + step) % size) for i in range(size)])  11.5 us
    ppermute x9, waiting for transfers between devices, shift(): lax.ppermute(array, axis, [(i, (i + step) % size) for i in range(size)])  8.13 us
    pallas_call x1, Pallas kernels, per_device(): call(functools.partial(stage_kernel, patches), [jax.ShapeDtypeStruct((row...  1.29 us
    pallas_call x1, Pallas kernels, per_device(): call(functools.partial(early_weight_kernel, subs, columns, early), jax.Sh...  0.99 us
    pallas_call x1, Pallas kernels, per_device(): call(functools.partial(final_kernel, early, row_blocks), jax.ShapeDtypeSt...  0.74 us
    pallas_call x1, Pallas kernels, per_device(): call(functools.partial(attention_kernel, 1.0 / math.sqrt(HD)), jax.ShapeD...  0.53 us
  transfers between devices with their start and end apart: 9, of which 4 were waited for; matrix products, arithmetic and copies ran while one was open for 0% of the time, Pallas kernels for 15%

profile of v18, /device:TPU:0, one launch (start us, length us, event | category | flops | bytes accessed | tf_op | source)
XLA Modules:
  0.0 24.2 jit_solution(3886702877831073967)
XLA Ops:
  0.0 0.0 copy-start.2
  0.0 0.0 copy-start.3
  0.0 0.5 %collective-permute-start.4 = (bf16[256,5120]{1,0:T(8,128)(2,1)}, bf16[256,5120]{1,0:T(8,128)(2,1)S(1)}, u32[]{:S(2)}, u32[]{:S(2)}) collective-permute-start(bf16[256,5120]{1,0:T(8,128)(2,1)} %refs_1_.3), channel_id=1, source_target_pairs={{0,1},{1,0},{2,3},{3,2},{4,5},{5,4},{6,7},{7,6},{8,9},{9,8},{10,11... | collective-permute-start | bytes 7864328 | tf_op jit(solution)/shard_map/weight_swap/ppermute | solution.py:49
  0.5 1.0 %early_weight.1 = bf16[256,512]{1,0:T(8,128)(2,1)S(1)} custom-call(bf16[256,5120]{1,0:T(8,128)(2,1)} %refs_1_.3), custom_call_target="tpu_custom_call" | custom-call | bytes 524288 | tf_op jit(solution)/shard_map/early_weight/early_weight/pallas_call | solution.py:211
  1.5 0.0 copy-done.2
  1.5 0.0 copy-done.3
  1.5 2.7 %collective-permute-start.2 = (bf16[96,512]{1,0:T(8,128)(2,1)S(1)}, bf16[96,512]{1,0:T(8,128)(2,1)S(1)}, u32[]{:S(2)}, u32[]{:S(2)}) collective-permute-start(bf16[96,512]{1,0:T(8,128)(2,1)S(1)} %maximum_convert_fusion.refs_0_), channel_id=1, source_target_pairs={{0,4},{4,8},{8,12},{12,0},{1,5},{5,9},{9,13},{13,1},{2,6},{6,10},{... | collective-permute-start | bytes 294920 | tf_op jit(solution)/shard_map/residual_gather/ppermute | solution.py:49
  4.2 2.6 %collective-permute-start.1 = (bf16[96,512]{1,0:T(8,128)(2,1)S(1)}, bf16[96,512]{1,0:T(8,128)(2,1)S(1)}, u32[]{:S(2)}, u32[]{:S(2)}) collective-permute-start(bf16[96,512]{1,0:T(8,128)(2,1)S(1)} %maximum_convert_fusion.refs_0_), channel_id=1, source_target_pairs={{0,8},{4,12},{8,0},{12,4},{1,9},{5,13},{9,1},{13,5},{2,10},{6,14},... | collective-permute-start | bytes 294920 | tf_op jit(solution)/shard_map/residual_gather/ppermute | solution.py:49
  6.8 1.3 %collective-permute-start = (bf16[96,512]{1,0:T(8,128)(2,1)S(1)}, bf16[96,512]{1,0:T(8,128)(2,1)S(1)}, u32[]{:S(2)}, u32[]{:S(2)}) collective-permute-start(bf16[96,512]{1,0:T(8,128)(2,1)S(1)} %maximum_convert_fusion.refs_0_), channel_id=1, source_target_pairs={{0,12},{4,0},{8,4},{12,8},{1,13},{5,1},{9,5},{13,9},{2,14},{6,2},{... | collective-permute-start | bytes 294920 | tf_op jit(solution)/shard_map/residual_gather/ppermute | solution.py:49
  8.1 1.5 %collective-permute-start.6 = (bf16[256,512]{1,0:T(8,128)(2,1)S(1)}, bf16[256,512]{1,0:T(8,128)(2,1)S(1)}, u32[]{:S(2)}, u32[]{:S(2)}) collective-permute-start(bf16[256,512]{1,0:T(8,128)(2,1)S(1)} %early_weight.1), channel_id=1, source_target_pairs={{0,2},{2,0},{1,3},{3,1},{4,6},{6,4},{5,7},{7,5},{8,10},{10,8},{9,1... | collective-permute-start | bytes 786440 | tf_op jit(solution)/shard_map/early_weight/ppermute | solution.py:49
  9.6 1.3 %stage.1 = (bf16[96,256]{1,0:T(8,128)(2,1)S(1)}, f32[2,96,384]{2,1,0:T(8,128)S(1)}, bf16[384,256]{1,0:T(8,128)(2,1)S(1)}) custom-call(bf16[96,256]{1,0:T(8,128)(2,1)} %q_hbm.1, bf16[384,256]{1,0:T(8,128)(2,1)} %held_k_hbm.1, bf16[384,256]{1,0:T(8,128)(2,1)} %held_v_hbm.1), custom_call_target="tpu_custom_call" | custom-call | flops 2000000000 | tf_op jit(solution)/shard_map/attention/stage/pallas_call | solution.py:260
  10.9 0.0 collective-permute-done.2.refs_3_
  10.9 3.0 %collective-permute-done.1.refs_2_ = bf16[96,512]{1,0:T(8,128)(2,1)S(1)} collective-permute-done((bf16[96,512]{1,0:T(8,128)(2,1)S(1)}, bf16[96,512]{1,0:T(8,128)(2,1)S(1)}, u32[]{:S(2)}, u32[]{:S(2)}) %collective-permute-start.1) | collective-permute-done | bytes 98336 | tf_op jit(solution)/shard_map/residual_gather/ppermute | solution.py:49
  13.9 0.0 collective-permute-done.refs_1_
  13.9 0.0 copy-start
  13.9 0.5 %attention.1.refs_0_ = bf16[96,256]{1,0:T(8,128)(2,1)S(1)} custom-call(bf16[96,256]{1,0:T(8,128)(2,1)S(1)} %get-tuple-element.11.q_ref, f32[2,96,384]{2,1,0:T(8,128)S(1)} %get-tuple-element.12.products_ref, bf16[384,256]{1,0:T(8,128)(2,1)S(1)} %get-tuple-element.13.values_ref, bf16[96,512]{1,0:T(8,128)(2,1)S(1)} %maximum_convert_fusion.refs_0_, ...), custom_call_target="tpu_custom_call" | custom-call | flops 2000000000 | tf_op jit(solution)/shard_map/attention/attention/pallas_call | solution.py:276
  14.4 0.0 copy-start.4
  14.4 0.0 copy-start.1
  14.5 0.1 collective-permute-start.3
  14.5 1.6 %collective-permute-start.5 = (bf16[96,256]{1,0:T(8,128)(2,1)S(1)}, bf16[96,256]{1,0:T(8,128)(2,1)S(1)}, u32[]{:S(2)}, u32[]{:S(2)}) collective-permute-start(bf16[96,256]{1,0:T(8,128)(2,1)S(1)} %attention.1.refs_0_), channel_id=1, source_target_pairs={{0,2},{2,0},{1,3},{3,1},{4,6},{6,4},{5,7},{7,5},{8,10},{10,8},{9,1... | collective-permute-start | bytes 147464 | tf_op jit(solution)/shard_map/attended_swap/ppermute | solution.py:49
  16.1 0.0 collective-permute-done.3.refs_2_
  16.1 0.0 collective-permute-done.4.refs_3_
  16.1 0.0 copy-done
  16.1 0.3 %sent_term.1 = bf16[96,1024]{1,0:T(8,128)(2,1)S(1)} custom-call(bf16[96,256]{1,0:T(8,128)(2,1)S(1)} %attention.1.refs_0_, bf16[256,5120]{1,0:T(8,128)(2,1)S(1)} %copy-done, bf16[96,256]{1,0:T(8,128)(2,1)S(1)} %collective-permute-done.3.refs_2_, bf16[256,5120]{1,0:T(8,128)(2,1)S(1)} %collective-permute-done.4.refs_3_), custom_call_target="tpu_custom_call" | custom-call | flops 125829120 | tf_op jit(solution)/shard_map/projection/sent_term/pallas_call | solution.py:299
  16.4 1.2 %collective-permute-start.8 = (bf16[96,1024]{1,0:T(8,128)(2,1)S(1)}, bf16[96,1024]{1,0:T(8,128)(2,1)S(1)}, u32[]{:S(2)}, u32[]{:S(2)}) collective-permute-start(bf16[96,1024]{1,0:T(8,128)(2,1)S(1)} %sent_term.1), channel_id=1, source_target_pairs={{0,2},{2,0},{1,3},{3,1},{4,6},{6,4},{5,7},{7,5},{8,10},{10,8},{9,1... | collective-permute-start | bytes 589832 | tf_op jit(solution)/shard_map/projection/ppermute | solution.py:49
  17.6 1.1 %collective-permute-done.5.attended_ref = bf16[96,256]{1,0:T(8,128)(2,1)S(1)} collective-permute-done((bf16[96,256]{1,0:T(8,128)(2,1)S(1)}, bf16[96,256]{1,0:T(8,128)(2,1)S(1)}, u32[]{:S(2)}, u32[]{:S(2)}) %collective-permute-start.5) | collective-permute-done | bytes 49184 | tf_op jit(solution)/shard_map/attended_swap/ppermute | solution.py:49
  18.7 0.0 collective-permute-done.6.weight_ref
  18.7 0.1 collective-permute-start.7
  18.8 0.0 copy-done.4
  18.8 0.0 copy-done.1
  18.8 0.4 %base.1.base_ref = f32[96,1280]{1,0:T(8,128)S(1)} custom-call(bf16[96,1280]{1,0:T(8,128)(2,1)S(1)} %copy-done.1, f32[1,1280]{1,0:T(1,128)S(1)} %reshape.3.gate_ref, bf16[96,256]{1,0:T(8,128)(2,1)S(1)} %attention.1.refs_0_, bf16[256,5120]{1,0:T(8,128)(2,1)S(1)} %copy-done, bf16[96,256]{1,0:T(8,128)(2,1)S(1)} %collective-permute-done.3.refs_2_, ...), custom_call_target="tpu_custom_call" | custom-call | flops 125829120 | tf_op jit(solution)/shard_map/projection/base/pallas_call | solution.py:310
  19.2 1.0 %collective-permute-done.7.packed_ref = bf16[352,256]{1,0:T(8,128)(2,1)S(1)} collective-permute-done((bf16[352,256]{1,0:T(8,128)(2,1)S(1)}, bf16[352,256]{1,0:T(8,128)(2,1)S(1)}, u32[]{:S(2)}, u32[]{:S(2)}) %collective-permute-start.7) | collective-permute-done | bytes 180256 | tf_op jit(solution)/shard_map/projection/ppermute | solution.py:49
  20.2 0.2 early.1.base_ref
  20.4 3.1 %collective-permute-done.8.refs_0_ = bf16[96,1024]{1,0:T(8,128)(2,1)S(1)} collective-permute-done((bf16[96,1024]{1,0:T(8,128)(2,1)S(1)}, bf16[96,1024]{1,0:T(8,128)(2,1)S(1)}, u32[]{:S(2)}, u32[]{:S(2)}) %collective-permute-start.8) | collective-permute-done | bytes 196640 | tf_op jit(solution)/shard_map/projection/ppermute | solution.py:49
  23.5 0.7 %final.1 = bf16[96,1280]{1,0:T(8,128)(2,1)} custom-call(f32[96,1280]{1,0:T(8,128)S(1)} %early.1.base_ref, f32[1,1280]{1,0:T(1,128)S(1)} %reshape.3.gate_ref, bf16[96,1024]{1,0:T(8,128)(2,1)S(1)} %collective-permute-done.8.refs_0_), custom_call_target="tpu_custom_call" | custom-call | bytes 983040 | tf_op jit(solution)/shard_map/projection/final/pallas_call | solution.py:336
  (3 shorter events, 0.0 us)
Async XLA Ops:
  0.0 1.5 %copy-start.2 = (f32[96,256]{1,0:T(8,128)S(1)}, f32[96,256]{1,0:T(8,128)}, u32[]{:S(2)}) copy-start(f32[96,256]{1,0:T(8,128)} %param.12) | copy-start | bytes 294916
  0.0 1.5 %copy-start.3 = (f32[96,256]{1,0:T(8,128)S(1)}, f32[96,256]{1,0:T(8,128)}, u32[]{:S(2)}) copy-start(f32[96,256]{1,0:T(8,128)} %param.11) | copy-start | bytes 294916
  0.0 16.1 %collective-permute-start.4 = (bf16[256,5120]{1,0:T(8,128)(2,1)}, bf16[256,5120]{1,0:T(8,128)(2,1)S(1)}, u32[]{:S(2)}, u32[]{:S(2)}) collective-permute-start(bf16[256,5120]{1,0:T(8,128)(2,1)} %refs_1_.3), channel_id=1, source_target_pairs={{0,1},{1,0},{2,3},{3,2},{4,5},{5,4},{6,7},{7,6},{8,9},{9,8},{10,11... | collective-permute-start | bytes 7864328 | tf_op jit(solution)/shard_map/weight_swap/ppermute | solution.py:49
  1.5 9.4 %collective-permute-start.2 = (bf16[96,512]{1,0:T(8,128)(2,1)S(1)}, bf16[96,512]{1,0:T(8,128)(2,1)S(1)}, u32[]{:S(2)}, u32[]{:S(2)}) collective-permute-start(bf16[96,512]{1,0:T(8,128)(2,1)S(1)} %maximum_convert_fusion.refs_0_), channel_id=1, source_target_pairs={{0,4},{4,8},{8,12},{12,0},{1,5},{5,9},{9,13},{13,1},{2,6},{6,10},{... | collective-permute-start | bytes 294920 | tf_op jit(solution)/shard_map/residual_gather/ppermute | solution.py:49
  4.2 9.7 %collective-permute-start.1 = (bf16[96,512]{1,0:T(8,128)(2,1)S(1)}, bf16[96,512]{1,0:T(8,128)(2,1)S(1)}, u32[]{:S(2)}, u32[]{:S(2)}) collective-permute-start(bf16[96,512]{1,0:T(8,128)(2,1)S(1)} %maximum_convert_fusion.refs_0_), channel_id=1, source_target_pairs={{0,8},{4,12},{8,0},{12,4},{1,9},{5,13},{9,1},{13,5},{2,10},{6,14},... | collective-permute-start | bytes 294920 | tf_op jit(solution)/shard_map/residual_gather/ppermute | solution.py:49
  6.8 7.1 %collective-permute-start = (bf16[96,512]{1,0:T(8,128)(2,1)S(1)}, bf16[96,512]{1,0:T(8,128)(2,1)S(1)}, u32[]{:S(2)}, u32[]{:S(2)}) collective-permute-start(bf16[96,512]{1,0:T(8,128)(2,1)S(1)} %maximum_convert_fusion.refs_0_), channel_id=1, source_target_pairs={{0,12},{4,0},{8,4},{12,8},{1,13},{5,1},{9,5},{13,9},{2,14},{6,2},{... | collective-permute-start | bytes 294920 | tf_op jit(solution)/shard_map/residual_gather/ppermute | solution.py:49
  8.1 10.6 %collective-permute-start.6 = (bf16[256,512]{1,0:T(8,128)(2,1)S(1)}, bf16[256,512]{1,0:T(8,128)(2,1)S(1)}, u32[]{:S(2)}, u32[]{:S(2)}) collective-permute-start(bf16[256,512]{1,0:T(8,128)(2,1)S(1)} %early_weight.1), channel_id=1, source_target_pairs={{0,2},{2,0},{1,3},{3,1},{4,6},{6,4},{5,7},{7,5},{8,10},{10,8},{9,1... | collective-permute-start | bytes 786440 | tf_op jit(solution)/shard_map/early_weight/ppermute | solution.py:49
  13.9 2.2 %copy-start = (bf16[256,5120]{1,0:T(8,128)(2,1)S(1)}, bf16[256,5120]{1,0:T(8,128)(2,1)}, u32[]{:S(2)}) copy-start(bf16[256,5120]{1,0:T(8,128)(2,1)} %refs_1_.3) | copy-start | bytes 7864324
  14.4 4.4 %copy-start.4 = (f32[1280]{0:T(1024)S(1)}, f32[1280]{0:T(1024)}, u32[]{:S(2)}) copy-start(f32[1280]{0:T(1024)} %param.15) | copy-start | bytes 15364
  14.4 4.4 %copy-start.1 = (bf16[96,1280]{1,0:T(8,128)(2,1)S(1)}, bf16[96,1280]{1,0:T(8,128)(2,1)}, u32[]{:S(2)}) copy-start(bf16[96,1280]{1,0:T(8,128)(2,1)} %hidden_ref.1) | copy-start | bytes 737284
  14.5 1.6 %collective-permute-start.3 = (bf16[96,256]{1,0:T(8,128)(2,1)S(1)}, bf16[96,256]{1,0:T(8,128)(2,1)S(1)}, u32[]{:S(2)}, u32[]{:S(2)}) collective-permute-start(bf16[96,256]{1,0:T(8,128)(2,1)S(1)} %attention.1.refs_0_), channel_id=1, source_target_pairs={{0,1},{1,0},{2,3},{3,2},{4,5},{5,4},{6,7},{7,6},{8,9},{9,8},{10,11... | collective-permute-start | bytes 147464 | tf_op jit(solution)/shard_map/attended_swap/ppermute | solution.py:49
  14.5 4.2 %collective-permute-start.5 = (bf16[96,256]{1,0:T(8,128)(2,1)S(1)}, bf16[96,256]{1,0:T(8,128)(2,1)S(1)}, u32[]{:S(2)}, u32[]{:S(2)}) collective-permute-start(bf16[96,256]{1,0:T(8,128)(2,1)S(1)} %attention.1.refs_0_), channel_id=1, source_target_pairs={{0,2},{2,0},{1,3},{3,1},{4,6},{6,4},{5,7},{7,5},{8,10},{10,8},{9,1... | collective-permute-start | bytes 147464 | tf_op jit(solution)/shard_map/attended_swap/ppermute | solution.py:49
  16.4 7.0 %collective-permute-start.8 = (bf16[96,1024]{1,0:T(8,128)(2,1)S(1)}, bf16[96,1024]{1,0:T(8,128)(2,1)S(1)}, u32[]{:S(2)}, u32[]{:S(2)}) collective-permute-start(bf16[96,1024]{1,0:T(8,128)(2,1)S(1)} %sent_term.1), channel_id=1, source_target_pairs={{0,2},{2,0},{1,3},{3,1},{4,6},{6,4},{5,7},{7,5},{8,10},{10,8},{9,1... | collective-permute-start | bytes 589832 | tf_op jit(solution)/shard_map/projection/ppermute | solution.py:49
  18.7 1.5 %collective-permute-start.7 = (bf16[352,256]{1,0:T(8,128)(2,1)S(1)}, bf16[352,256]{1,0:T(8,128)(2,1)S(1)}, u32[]{:S(2)}, u32[]{:S(2)}) collective-permute-start(bf16[352,256]{1,0:T(8,128)(2,1)S(1)} %pack.1), channel_id=1, source_target_pairs={{0,1},{1,0},{2,3},{3,2},{4,5},{5,4},{6,7},{7,6},{8,9},{9,8},{10,11... | collective-permute-start | bytes 540680 | tf_op jit(solution)/shard_map/projection/ppermute | solution.py:49

commit v19 on v18

--- a/solution.py
+++ b/solution.py
@@ -49,12 +49,30 @@
     return lax.ppermute(array, axis, [(i, (i + step) % size) for i in range(size)])
 
 
-def gather_steps(patches):
-    return list(range(patches - 1, 0, -1))
+LINE_OF_FOUR = (
+    ((0, 2), (1, 0), (2, 3), (3, 1)),
+    ((0, 3), (1, 2), (2, 1), (3, 0)),
+    ((0, 1), (1, 3), (2, 0), (3, 2)),
+)
+
+
+def gather_permutes(patches):
+    if patches == 4:
+        return LINE_OF_FOUR
+    return [
+        [(i, (i + step) % patches) for i in range(patches)] for step in range(patches - 1, 0, -1)
+    ]
 
 
 def gather_sources(patches, place):
-    return [place] + [lax.rem(place + patches - step, patches) for step in gather_steps(patches)]
+    sources = [place]
+    for pairs in gather_permutes(patches):
+        before = {target: source for source, target in pairs}
+        value = jnp.int32(before[0])
+        for i in range(1, patches):
+            value = jnp.where(place == i, jnp.int32(before[i]), value)
+        sources.append(value)
+    return sources
 
 
 def early_weight_kernel(subs, columns, early, weight_ref, out_ref, sems):
@@ -228,7 +246,7 @@
                 lax.pad(value_change, low, ((0, 0, 0), (width, 0, 0))),
             ).astype(jnp.bfloat16)
             blocks = [residual] + [
-                shift(residual, "patch", patches, step) for step in gather_steps(patches)
+                lax.ppermute(residual, "patch", pairs) for pairs in gather_permutes(patches)
             ]
 
         with jax.named_scope("weight_swap"):

time: 24.4 us -> 24.2 us (level)
  the two profiles are of different devices: /device:TPU:0 before, /device:TPU:20 now
where the time goes in v19:
time: 24.2 us; the launch traced here: 24 us
  waiting for transfers between devices  11.5 us (48%)
  starting transfers between devices  7.81 us (32%)
  Pallas kernels  4.48 us (19%)
    ppermute x3, waiting for transfers between devices, per_device(): lax.ppermute(residual, 'patch', pairs)  6.36 us
    ppermute x6, waiting for transfers between devices, shift(): lax.ppermute(array, axis, [(i, (i + step) % size) for i in range(size)])  5.15 us
    ppermute x6, starting transfers between devices, shift(): lax.ppermute(array, axis, [(i, (i + step) % size) for i in range(size)])  4.38 us
    ppermute x3, starting transfers between devices, per_device(): lax.ppermute(residual, 'patch', pairs)  3.43 us
    pallas_call x1, Pallas kernels, per_device(): call(functools.partial(stage_kernel, patches), [jax.ShapeDtypeStruct((row...  1.28 us
    pallas_call x1, Pallas kernels, per_device(): call(functools.partial(early_weight_kernel, subs, columns, early), jax.Sh...  1.04 us
    pallas_call x1, Pallas kernels, per_device(): call(functools.partial(final_kernel, early, row_blocks), jax.ShapeDtypeSt...  0.74 us
    pallas_call x1, Pallas kernels, per_device(): call(functools.partial(attention_kernel, 1.0 / math.sqrt(HD)), jax.ShapeD...  0.53 us
  transfers between devices with their start and end apart: 9, of which 4 were waited for; matrix products, arithmetic and copies ran while one was open for 0% of the time, Pallas kernels for 16%

profile of v19, /device:TPU:20, one launch (start us, length us, event | category | flops | bytes accessed | tf_op | source)
XLA Modules:
  0.0 24.0 jit_solution(15120020753727372821)
XLA Ops:
  0.0 0.0 copy-start.2
  0.0 0.0 copy-start.3
  0.0 0.0 collective-permute-start.4
  0.0 1.0 %early_weight.1 = bf16[256,512]{1,0:T(8,128)(2,1)S(1)} custom-call(bf16[256,5120]{1,0:T(8,128)(2,1)} %refs_1_.3), custom_call_target="tpu_custom_call" | custom-call | bytes 524288 | tf_op jit(solution)/shard_map/early_weight/early_weight/pallas_call | solution.py:229
  1.1 0.0 copy-done.2
  1.1 0.0 copy-done.3
  1.1 0.4 %collective-permute-start.2 = (bf16[96,512]{1,0:T(8,128)(2,1)S(1)}, bf16[96,512]{1,0:T(8,128)(2,1)S(1)}, u32[]{:S(2)}, u32[]{:S(2)}) collective-permute-start(bf16[96,512]{1,0:T(8,128)(2,1)S(1)} %maximum_convert_fusion.refs_0_), channel_id=1, source_target_pairs={{0,4},{4,12},{8,0},{12,8},{1,5},{5,13},{9,1},{13,9},{2,6},{6,14},{... | collective-permute-start | bytes 294920 | tf_op jit(solution)/shard_map/residual_gather/ppermute | solution.py:249
  1.5 2.7 %collective-permute-start.1 = (bf16[96,512]{1,0:T(8,128)(2,1)S(1)}, bf16[96,512]{1,0:T(8,128)(2,1)S(1)}, u32[]{:S(2)}, u32[]{:S(2)}) collective-permute-start(bf16[96,512]{1,0:T(8,128)(2,1)S(1)} %maximum_convert_fusion.refs_0_), channel_id=1, source_target_pairs={{0,12},{4,8},{8,4},{12,0},{1,13},{5,9},{9,5},{13,1},{2,14},{6,10},... | collective-permute-start | bytes 294920 | tf_op jit(solution)/shard_map/residual_gather/ppermute | solution.py:249
  4.2 0.3 %collective-permute-start = (bf16[96,512]{1,0:T(8,128)(2,1)S(1)}, bf16[96,512]{1,0:T(8,128)(2,1)S(1)}, u32[]{:S(2)}, u32[]{:S(2)}) collective-permute-start(bf16[96,512]{1,0:T(8,128)(2,1)S(1)} %maximum_convert_fusion.refs_0_), channel_id=1, source_target_pairs={{0,8},{4,0},{8,12},{12,4},{1,9},{5,1},{9,13},{13,5},{2,10},{6,2},{... | collective-permute-start | bytes 294920 | tf_op jit(solution)/shard_map/residual_gather/ppermute | solution.py:249
  4.5 1.5 %collective-permute-start.6 = (bf16[256,512]{1,0:T(8,128)(2,1)S(1)}, bf16[256,512]{1,0:T(8,128)(2,1)S(1)}, u32[]{:S(2)}, u32[]{:S(2)}) collective-permute-start(bf16[256,512]{1,0:T(8,128)(2,1)S(1)} %early_weight.1), channel_id=1, source_target_pairs={{0,2},{2,0},{1,3},{3,1},{4,6},{6,4},{5,7},{7,5},{8,10},{10,8},{9,1... | collective-permute-start | bytes 786440 | tf_op jit(solution)/shard_map/early_weight/ppermute | solution.py:49
  6.0 1.3 %stage.1 = (bf16[96,256]{1,0:T(8,128)(2,1)S(1)}, f32[2,96,384]{2,1,0:T(8,128)S(1)}, bf16[384,256]{1,0:T(8,128)(2,1)S(1)}) custom-call(bf16[96,256]{1,0:T(8,128)(2,1)} %q_hbm.1, bf16[384,256]{1,0:T(8,128)(2,1)} %held_k_hbm.1, bf16[384,256]{1,0:T(8,128)(2,1)} %held_v_hbm.1), custom_call_target="tpu_custom_call" | custom-call | flops 2000000000 | tf_op jit(solution)/shard_map/attention/stage/pallas_call | solution.py:278
  7.3 0.0 collective-permute-done.2.refs_3_
  7.3 6.4 %collective-permute-done.1.refs_2_ = bf16[96,512]{1,0:T(8,128)(2,1)S(1)} collective-permute-done((bf16[96,512]{1,0:T(8,128)(2,1)S(1)}, bf16[96,512]{1,0:T(8,128)(2,1)S(1)}, u32[]{:S(2)}, u32[]{:S(2)}) %collective-permute-start.1) | collective-permute-done | bytes 98336 | tf_op jit(solution)/shard_map/residual_gather/ppermute | solution.py:249
  13.7 0.0 collective-permute-done.refs_1_
  13.7 0.0 copy-start
  13.7 0.5 %attention.1.refs_0_ = bf16[96,256]{1,0:T(8,128)(2,1)S(1)} custom-call(bf16[96,256]{1,0:T(8,128)(2,1)S(1)} %get-tuple-element.11.q_ref, f32[2,96,384]{2,1,0:T(8,128)S(1)} %get-tuple-element.12.products_ref, bf16[384,256]{1,0:T(8,128)(2,1)S(1)} %get-tuple-element.13.values_ref, bf16[96,512]{1,0:T(8,128)(2,1)S(1)} %maximum_convert_fusion.refs_0_, ...), custom_call_target="tpu_custom_call" | custom-call | flops 2000000000 | tf_op jit(solution)/shard_map/attention/attention/pallas_call | solution.py:294
  14.2 0.0 copy-start.4
  14.2 0.0 copy-start.1
  14.2 0.1 collective-permute-start.3
  14.3 1.6 %collective-permute-start.5 = (bf16[96,256]{1,0:T(8,128)(2,1)S(1)}, bf16[96,256]{1,0:T(8,128)(2,1)S(1)}, u32[]{:S(2)}, u32[]{:S(2)}) collective-permute-start(bf16[96,256]{1,0:T(8,128)(2,1)S(1)} %attention.1.refs_0_), channel_id=1, source_target_pairs={{0,2},{2,0},{1,3},{3,1},{4,6},{6,4},{5,7},{7,5},{8,10},{10,8},{9,1... | collective-permute-start | bytes 147464 | tf_op jit(solution)/shard_map/attended_swap/ppermute | solution.py:49
  15.9 0.0 collective-permute-done.3.refs_2_
  15.9 0.0 collective-permute-done.4.refs_3_
  15.9 0.0 copy-done
  15.9 0.3 %sent_term.1 = bf16[96,1024]{1,0:T(8,128)(2,1)S(1)} custom-call(bf16[96,256]{1,0:T(8,128)(2,1)S(1)} %attention.1.refs_0_, bf16[256,5120]{1,0:T(8,128)(2,1)S(1)} %copy-done, bf16[96,256]{1,0:T(8,128)(2,1)S(1)} %collective-permute-done.3.refs_2_, bf16[256,5120]{1,0:T(8,128)(2,1)S(1)} %collective-permute-done.4.refs_3_), custom_call_target="tpu_custom_call" | custom-call | flops 125829120 | tf_op jit(solution)/shard_map/projection/sent_term/pallas_call | solution.py:317
  16.2 1.2 %collective-permute-start.8 = (bf16[96,1024]{1,0:T(8,128)(2,1)S(1)}, bf16[96,1024]{1,0:T(8,128)(2,1)S(1)}, u32[]{:S(2)}, u32[]{:S(2)}) collective-permute-start(bf16[96,1024]{1,0:T(8,128)(2,1)S(1)} %sent_term.1), channel_id=1, source_target_pairs={{0,2},{2,0},{1,3},{3,1},{4,6},{6,4},{5,7},{7,5},{8,10},{10,8},{9,1... | collective-permute-start | bytes 589832 | tf_op jit(solution)/shard_map/projection/ppermute | solution.py:49
  17.4 1.1 %collective-permute-done.5.attended_ref = bf16[96,256]{1,0:T(8,128)(2,1)S(1)} collective-permute-done((bf16[96,256]{1,0:T(8,128)(2,1)S(1)}, bf16[96,256]{1,0:T(8,128)(2,1)S(1)}, u32[]{:S(2)}, u32[]{:S(2)}) %collective-permute-start.5) | collective-permute-done | bytes 49184 | tf_op jit(solution)/shard_map/attended_swap/ppermute | solution.py:49
  18.5 0.0 collective-permute-done.6.weight_ref
  18.5 0.1 collective-permute-start.7
  18.6 0.0 copy-done.4
  18.6 0.0 copy-done.1
  18.6 0.4 %base.1.base_ref = f32[96,1280]{1,0:T(8,128)S(1)} custom-call(bf16[96,1280]{1,0:T(8,128)(2,1)S(1)} %copy-done.1, f32[1,1280]{1,0:T(1,128)S(1)} %reshape.3.gate_ref, bf16[96,256]{1,0:T(8,128)(2,1)S(1)} %attention.1.refs_0_, bf16[256,5120]{1,0:T(8,128)(2,1)S(1)} %copy-done, bf16[96,256]{1,0:T(8,128)(2,1)S(1)} %collective-permute-done.3.refs_2_, ...), custom_call_target="tpu_custom_call" | custom-call | flops 125829120 | tf_op jit(solution)/shard_map/projection/base/pallas_call | solution.py:328
  19.0 1.0 %collective-permute-done.7.packed_ref = bf16[352,256]{1,0:T(8,128)(2,1)S(1)} collective-permute-done((bf16[352,256]{1,0:T(8,128)(2,1)S(1)}, bf16[352,256]{1,0:T(8,128)(2,1)S(1)}, u32[]{:S(2)}, u32[]{:S(2)}) %collective-permute-start.7) | collective-permute-done | bytes 180256 | tf_op jit(solution)/shard_map/projection/ppermute | solution.py:49
  20.0 0.2 early.1.base_ref
  20.2 3.1 %collective-permute-done.8.refs_0_ = bf16[96,1024]{1,0:T(8,128)(2,1)S(1)} collective-permute-done((bf16[96,1024]{1,0:T(8,128)(2,1)S(1)}, bf16[96,1024]{1,0:T(8,128)(2,1)S(1)}, u32[]{:S(2)}, u32[]{:S(2)}) %collective-permute-start.8) | collective-permute-done | bytes 196640 | tf_op jit(solution)/shard_map/projection/ppermute | solution.py:49
  23.3 0.7 %final.1 = bf16[96,1280]{1,0:T(8,128)(2,1)} custom-call(f32[96,1280]{1,0:T(8,128)S(1)} %early.1.base_ref, f32[1,1280]{1,0:T(1,128)S(1)} %reshape.3.gate_ref, bf16[96,1024]{1,0:T(8,128)(2,1)S(1)} %collective-permute-done.8.refs_0_), custom_call_target="tpu_custom_call" | custom-call | bytes 983040 | tf_op jit(solution)/shard_map/projection/final/pallas_call | solution.py:354
  (3 shorter events, 0.0 us)
Async XLA Ops:
  0.0 1.1 %copy-start.2 = (f32[96,256]{1,0:T(8,128)S(1)}, f32[96,256]{1,0:T(8,128)}, u32[]{:S(2)}) copy-start(f32[96,256]{1,0:T(8,128)} %param.12) | copy-start | bytes 294916
  0.0 1.1 %copy-start.3 = (f32[96,256]{1,0:T(8,128)S(1)}, f32[96,256]{1,0:T(8,128)}, u32[]{:S(2)}) copy-start(f32[96,256]{1,0:T(8,128)} %param.11) | copy-start | bytes 294916
  0.0 15.9 %collective-permute-start.4 = (bf16[256,5120]{1,0:T(8,128)(2,1)}, bf16[256,5120]{1,0:T(8,128)(2,1)S(1)}, u32[]{:S(2)}, u32[]{:S(2)}) collective-permute-start(bf16[256,5120]{1,0:T(8,128)(2,1)} %refs_1_.3), channel_id=1, source_target_pairs={{0,1},{1,0},{2,3},{3,2},{4,5},{5,4},{6,7},{7,6},{8,9},{9,8},{10,11... | collective-permute-start | bytes 7864328 | tf_op jit(solution)/shard_map/weight_swap/ppermute | solution.py:49
  1.1 6.2 %collective-permute-start.2 = (bf16[96,512]{1,0:T(8,128)(2,1)S(1)}, bf16[96,512]{1,0:T(8,128)(2,1)S(1)}, u32[]{:S(2)}, u32[]{:S(2)}) collective-permute-start(bf16[96,512]{1,0:T(8,128)(2,1)S(1)} %maximum_convert_fusion.refs_0_), channel_id=1, source_target_pairs={{0,4},{4,12},{8,0},{12,8},{1,5},{5,13},{9,1},{13,9},{2,6},{6,14},{... | collective-permute-start | bytes 294920 | tf_op jit(solution)/shard_map/residual_gather/ppermute | solution.py:249
  1.5 12.2 %collective-permute-start.1 = (bf16[96,512]{1,0:T(8,128)(2,1)S(1)}, bf16[96,512]{1,0:T(8,128)(2,1)S(1)}, u32[]{:S(2)}, u32[]{:S(2)}) collective-permute-start(bf16[96,512]{1,0:T(8,128)(2,1)S(1)} %maximum_convert_fusion.refs_0_), channel_id=1, source_target_pairs={{0,12},{4,8},{8,4},{12,0},{1,13},{5,9},{9,5},{13,1},{2,14},{6,10},... | collective-permute-start | bytes 294920 | tf_op jit(solution)/shard_map/residual_gather/ppermute | solution.py:249
  4.2 9.5 %collective-permute-start = (bf16[96,512]{1,0:T(8,128)(2,1)S(1)}, bf16[96,512]{1,0:T(8,128)(2,1)S(1)}, u32[]{:S(2)}, u32[]{:S(2)}) collective-permute-start(bf16[96,512]{1,0:T(8,128)(2,1)S(1)} %maximum_convert_fusion.refs_0_), channel_id=1, source_target_pairs={{0,8},{4,0},{8,12},{12,4},{1,9},{5,1},{9,13},{13,5},{2,10},{6,2},{... | collective-permute-start | bytes 294920 | tf_op jit(solution)/shard_map/residual_gather/ppermute | solution.py:249
  4.5 13.9 %collective-permute-start.6 = (bf16[256,512]{1,0:T(8,128)(2,1)S(1)}, bf16[256,512]{1,0:T(8,128)(2,1)S(1)}, u32[]{:S(2)}, u32[]{:S(2)}) collective-permute-start(bf16[256,512]{1,0:T(8,128)(2,1)S(1)} %early_weight.1), channel_id=1, source_target_pairs={{0,2},{2,0},{1,3},{3,1},{4,6},{6,4},{5,7},{7,5},{8,10},{10,8},{9,1... | collective-permute-start | bytes 786440 | tf_op jit(solution)/shard_map/early_weight/ppermute | solution.py:49
  13.7 2.2 %copy-start = (bf16[256,5120]{1,0:T(8,128)(2,1)S(1)}, bf16[256,5120]{1,0:T(8,128)(2,1)}, u32[]{:S(2)}) copy-start(bf16[256,5120]{1,0:T(8,128)(2,1)} %refs_1_.3) | copy-start | bytes 7864324
  14.2 4.4 %copy-start.4 = (f32[1280]{0:T(1024)S(1)}, f32[1280]{0:T(1024)}, u32[]{:S(2)}) copy-start(f32[1280]{0:T(1024)} %param.15) | copy-start | bytes 15364
  14.2 4.4 %copy-start.1 = (bf16[96,1280]{1,0:T(8,128)(2,1)S(1)}, bf16[96,1280]{1,0:T(8,128)(2,1)}, u32[]{:S(2)}) copy-start(bf16[96,1280]{1,0:T(8,128)(2,1)} %hidden_ref.1) | copy-start | bytes 737284
  14.2 1.6 %collective-permute-start.3 = (bf16[96,256]{1,0:T(8,128)(2,1)S(1)}, bf16[96,256]{1,0:T(8,128)(2,1)S(1)}, u32[]{:S(2)}, u32[]{:S(2)}) collective-permute-start(bf16[96,256]{1,0:T(8,128)(2,1)S(1)} %attention.1.refs_0_), channel_id=1, source_target_pairs={{0,1},{1,0},{2,3},{3,2},{4,5},{5,4},{6,7},{7,6},{8,9},{9,8},{10,11... | collective-permute-start | bytes 147464 | tf_op jit(solution)/shard_map/attended_swap/ppermute | solution.py:49
  14.3 4.2 %collective-permute-start.5 = (bf16[96,256]{1,0:T(8,128)(2,1)S(1)}, bf16[96,256]{1,0:T(8,128)(2,1)S(1)}, u32[]{:S(2)}, u32[]{:S(2)}) collective-permute-start(bf16[96,256]{1,0:T(8,128)(2,1)S(1)} %attention.1.refs_0_), channel_id=1, source_target_pairs={{0,2},{2,0},{1,3},{3,1},{4,6},{6,4},{5,7},{7,5},{8,10},{10,8},{9,1... | collective-permute-start | bytes 147464 | tf_op jit(solution)/shard_map/attended_swap/ppermute | solution.py:49
  16.2 7.0 %collective-permute-start.8 = (bf16[96,1024]{1,0:T(8,128)(2,1)S(1)}, bf16[96,1024]{1,0:T(8,128)(2,1)S(1)}, u32[]{:S(2)}, u32[]{:S(2)}) collective-permute-start(bf16[96,1024]{1,0:T(8,128)(2,1)S(1)} %sent_term.1), channel_id=1, source_target_pairs={{0,2},{2,0},{1,3},{3,1},{4,6},{6,4},{5,7},{7,5},{8,10},{10,8},{9,1... | collective-permute-start | bytes 589832 | tf_op jit(solution)/shard_map/projection/ppermute | solution.py:49
  18.5 1.5 %collective-permute-start.7 = (bf16[352,256]{1,0:T(8,128)(2,1)S(1)}, bf16[352,256]{1,0:T(8,128)(2,1)S(1)}, u32[]{:S(2)}, u32[]{:S(2)}) collective-permute-start(bf16[352,256]{1,0:T(8,128)(2,1)S(1)} %pack.1), channel_id=1, source_target_pairs={{0,1},{1,0},{2,3},{3,2},{4,5},{5,4},{6,7},{7,6},{8,9},{9,8},{10,11... | collective-permute-start | bytes 540680 | tf_op jit(solution)/shard_map/projection/ppermute | solution.py:49

commit v20 on v19

--- a/solution.py
+++ b/solution.py
@@ -50,8 +50,8 @@
 
 
 LINE_OF_FOUR = (
+    ((0, 3), (1, 2), (2, 1), (3, 0)),
     ((0, 2), (1, 0), (2, 3), (3, 1)),
-    ((0, 3), (1, 2), (2, 1), (3, 0)),
     ((0, 1), (1, 3), (2, 0), (3, 2)),
 )
 

time: 24.2 us -> 24.7 us (1.021)
  the two profiles are of different devices: /device:TPU:20 before, /device:TPU:0 now
where the time goes in v20:
time: 24.7 us; the launch traced here: 24.5 us
  starting transfers between devices  12.5 us (51%)
  waiting for transfers between devices  7.4 us (30%)
  Pallas kernels  4.43 us (18%)
    ppermute x3, starting transfers between devices, per_device(): lax.ppermute(residual, 'patch', pairs)  7.64 us
    ppermute x6, waiting for transfers between devices, shift(): lax.ppermute(array, axis, [(i, (i + step) % size) for i in range(size)])  5.15 us
    ppermute x6, starting transfers between devices, shift(): lax.ppermute(array, axis, [(i, (i + step) % size) for i in range(size)])  4.83 us
    ppermute x3, waiting for transfers between devices, per_device(): lax.ppermute(residual, 'patch', pairs)  2.25 us
    pallas_call x1, Pallas kernels, per_device(): call(functools.partial(stage_kernel, patches), [jax.ShapeDtypeStruct((row...  1.28 us
    pallas_call x1, Pallas kernels, per_device(): call(functools.partial(early_weight_kernel, subs, columns, early), jax.Sh...  0.99 us
    pallas_call x1, Pallas kernels, per_device(): call(functools.partial(final_kernel, early, row_blocks), jax.ShapeDtypeSt...  0.74 us
    pallas_call x1, Pallas kernels, per_device(): call(functools.partial(attention_kernel, 1.0 / math.sqrt(HD)), jax.ShapeD...  0.53 us
  transfers between devices with their start and end apart: 9, of which 4 were waited for; matrix products, arithmetic and copies ran while one was open for 0% of the time, Pallas kernels for 15%

profile of v20, /device:TPU:0, one launch (start us, length us, event | category | flops | bytes accessed | tf_op | source)
XLA Modules:
  0.0 24.5 jit_solution(4949176283050750265)
XLA Ops:
  0.0 0.0 copy-start.2
  0.0 0.0 copy-start.3
  0.0 0.5 %collective-permute-start.4 = (bf16[256,5120]{1,0:T(8,128)(2,1)}, bf16[256,5120]{1,0:T(8,128)(2,1)S(1)}, u32[]{:S(2)}, u32[]{:S(2)}) collective-permute-start(bf16[256,5120]{1,0:T(8,128)(2,1)} %refs_1_.3), channel_id=1, source_target_pairs={{0,1},{1,0},{2,3},{3,2},{4,5},{5,4},{6,7},{7,6},{8,9},{9,8},{10,11... | collective-permute-start | bytes 7864328 | tf_op jit(solution)/shard_map/weight_swap/ppermute | solution.py:49
  0.5 1.0 %early_weight.1 = bf16[256,512]{1,0:T(8,128)(2,1)S(1)} custom-call(bf16[256,5120]{1,0:T(8,128)(2,1)} %refs_1_.3), custom_call_target="tpu_custom_call" | custom-call | bytes 524288 | tf_op jit(solution)/shard_map/early_weight/early_weight/pallas_call | solution.py:229
  1.5 0.0 copy-done.2
  1.5 0.0 copy-done.3
  1.5 2.7 %collective-permute-start.2 = (bf16[96,512]{1,0:T(8,128)(2,1)S(1)}, bf16[96,512]{1,0:T(8,128)(2,1)S(1)}, u32[]{:S(2)}, u32[]{:S(2)}) collective-permute-start(bf16[96,512]{1,0:T(8,128)(2,1)S(1)} %maximum_convert_fusion.refs_0_), channel_id=1, source_target_pairs={{0,4},{4,12},{8,0},{12,8},{1,5},{5,13},{9,1},{13,9},{2,6},{6,14},{... | collective-permute-start | bytes 294920 | tf_op jit(solution)/shard_map/residual_gather/ppermute | solution.py:249
  4.2 1.1 %collective-permute-start.1 = (bf16[96,512]{1,0:T(8,128)(2,1)S(1)}, bf16[96,512]{1,0:T(8,128)(2,1)S(1)}, u32[]{:S(2)}, u32[]{:S(2)}) collective-permute-start(bf16[96,512]{1,0:T(8,128)(2,1)S(1)} %maximum_convert_fusion.refs_0_), channel_id=1, source_target_pairs={{0,8},{4,0},{8,12},{12,4},{1,9},{5,1},{9,13},{13,5},{2,10},{6,2},{... | collective-permute-start | bytes 294920 | tf_op jit(solution)/shard_map/residual_gather/ppermute | solution.py:249
  5.3 3.9 %collective-permute-start = (bf16[96,512]{1,0:T(8,128)(2,1)S(1)}, bf16[96,512]{1,0:T(8,128)(2,1)S(1)}, u32[]{:S(2)}, u32[]{:S(2)}) collective-permute-start(bf16[96,512]{1,0:T(8,128)(2,1)S(1)} %maximum_convert_fusion.refs_0_), channel_id=1, source_target_pairs={{0,12},{4,8},{8,4},{12,0},{1,13},{5,9},{9,5},{13,1},{2,14},{6,10},... | collective-permute-start | bytes 294920 | tf_op jit(solution)/shard_map/residual_gather/ppermute | solution.py:249
  9.1 1.5 %collective-permute-start.6 = (bf16[256,512]{1,0:T(8,128)(2,1)S(1)}, bf16[256,512]{1,0:T(8,128)(2,1)S(1)}, u32[]{:S(2)}, u32[]{:S(2)}) collective-permute-start(bf16[256,512]{1,0:T(8,128)(2,1)S(1)} %early_weight.1), channel_id=1, source_target_pairs={{0,2},{2,0},{1,3},{3,1},{4,6},{6,4},{5,7},{7,5},{8,10},{10,8},{9,1... | collective-permute-start | bytes 786440 | tf_op jit(solution)/shard_map/early_weight/ppermute | solution.py:49
  10.6 1.3 %stage.1 = (bf16[96,256]{1,0:T(8,128)(2,1)S(1)}, f32[2,96,384]{2,1,0:T(8,128)S(1)}, bf16[384,256]{1,0:T(8,128)(2,1)S(1)}) custom-call(bf16[96,256]{1,0:T(8,128)(2,1)} %q_hbm.1, bf16[384,256]{1,0:T(8,128)(2,1)} %held_k_hbm.1, bf16[384,256]{1,0:T(8,128)(2,1)} %held_v_hbm.1), custom_call_target="tpu_custom_call" | custom-call | flops 2000000000 | tf_op jit(solution)/shard_map/attention/stage/pallas_call | solution.py:278
  11.9 0.0 collective-permute-done.2.refs_3_
  11.9 0.0 collective-permute-done.1.refs_2_
  11.9 2.2 %collective-permute-done.refs_1_ = bf16[96,512]{1,0:T(8,128)(2,1)S(1)} collective-permute-done((bf16[96,512]{1,0:T(8,128)(2,1)S(1)}, bf16[96,512]{1,0:T(8,128)(2,1)S(1)}, u32[]{:S(2)}, u32[]{:S(2)}) %collective-permute-start) | collective-permute-done | bytes 98336 | tf_op jit(solution)/shard_map/residual_gather/ppermute | solution.py:249
  14.2 0.0 copy-start
  14.2 0.5 %attention.1.refs_0_ = bf16[96,256]{1,0:T(8,128)(2,1)S(1)} custom-call(bf16[96,256]{1,0:T(8,128)(2,1)S(1)} %get-tuple-element.11.q_ref, f32[2,96,384]{2,1,0:T(8,128)S(1)} %get-tuple-element.12.products_ref, bf16[384,256]{1,0:T(8,128)(2,1)S(1)} %get-tuple-element.13.values_ref, bf16[96,512]{1,0:T(8,128)(2,1)S(1)} %maximum_convert_fusion.refs_0_, ...), custom_call_target="tpu_custom_call" | custom-call | flops 2000000000 | tf_op jit(solution)/shard_map/attention/attention/pallas_call | solution.py:294
  14.7 0.0 copy-start.4
  14.7 0.0 copy-start.1
  14.7 0.1 collective-permute-start.3
  14.8 1.6 %collective-permute-start.5 = (bf16[96,256]{1,0:T(8,128)(2,1)S(1)}, bf16[96,256]{1,0:T(8,128)(2,1)S(1)}, u32[]{:S(2)}, u32[]{:S(2)}) collective-permute-start(bf16[96,256]{1,0:T(8,128)(2,1)S(1)} %attention.1.refs_0_), channel_id=1, source_target_pairs={{0,2},{2,0},{1,3},{3,1},{4,6},{6,4},{5,7},{7,5},{8,10},{10,8},{9,1... | collective-permute-start | bytes 147464 | tf_op jit(solution)/shard_map/attended_swap/ppermute | solution.py:49
  16.4 0.0 collective-permute-done.3.refs_2_
  16.4 0.0 collective-permute-done.4.refs_3_
  16.4 0.0 copy-done
  16.4 0.3 %sent_term.1 = bf16[96,1024]{1,0:T(8,128)(2,1)S(1)} custom-call(bf16[96,256]{1,0:T(8,128)(2,1)S(1)} %attention.1.refs_0_, bf16[256,5120]{1,0:T(8,128)(2,1)S(1)} %copy-done, bf16[96,256]{1,0:T(8,128)(2,1)S(1)} %collective-permute-done.3.refs_2_, bf16[256,5120]{1,0:T(8,128)(2,1)S(1)} %collective-permute-done.4.refs_3_), custom_call_target="tpu_custom_call" | custom-call | flops 125829120 | tf_op jit(solution)/shard_map/projection/sent_term/pallas_call | solution.py:317
  16.7 1.2 %collective-permute-start.8 = (bf16[96,1024]{1,0:T(8,128)(2,1)S(1)}, bf16[96,1024]{1,0:T(8,128)(2,1)S(1)}, u32[]{:S(2)}, u32[]{:S(2)}) collective-permute-start(bf16[96,1024]{1,0:T(8,128)(2,1)S(1)} %sent_term.1), channel_id=1, source_target_pairs={{0,2},{2,0},{1,3},{3,1},{4,6},{6,4},{5,7},{7,5},{8,10},{10,8},{9,1... | collective-permute-start | bytes 589832 | tf_op jit(solution)/shard_map/projection/ppermute | solution.py:49
  17.9 1.1 %collective-permute-done.5.attended_ref = bf16[96,256]{1,0:T(8,128)(2,1)S(1)} collective-permute-done((bf16[96,256]{1,0:T(8,128)(2,1)S(1)}, bf16[96,256]{1,0:T(8,128)(2,1)S(1)}, u32[]{:S(2)}, u32[]{:S(2)}) %collective-permute-start.5) | collective-permute-done | bytes 49184 | tf_op jit(solution)/shard_map/attended_swap/ppermute | solution.py:49
  19.0 0.0 collective-permute-done.6.weight_ref
  19.0 0.1 collective-permute-start.7
  19.1 0.0 copy-done.4
  19.1 0.0 copy-done.1
  19.1 0.4 %base.1.base_ref = f32[96,1280]{1,0:T(8,128)S(1)} custom-call(bf16[96,1280]{1,0:T(8,128)(2,1)S(1)} %copy-done.1, f32[1,1280]{1,0:T(1,128)S(1)} %reshape.3.gate_ref, bf16[96,256]{1,0:T(8,128)(2,1)S(1)} %attention.1.refs_0_, bf16[256,5120]{1,0:T(8,128)(2,1)S(1)} %copy-done, bf16[96,256]{1,0:T(8,128)(2,1)S(1)} %collective-permute-done.3.refs_2_, ...), custom_call_target="tpu_custom_call" | custom-call | flops 125829120 | tf_op jit(solution)/shard_map/projection/base/pallas_call | solution.py:328
  19.5 1.0 %collective-permute-done.7.packed_ref = bf16[352,256]{1,0:T(8,128)(2,1)S(1)} collective-permute-done((bf16[352,256]{1,0:T(8,128)(2,1)S(1)}, bf16[352,256]{1,0:T(8,128)(2,1)S(1)}, u32[]{:S(2)}, u32[]{:S(2)}) %collective-permute-start.7) | collective-permute-done | bytes 180256 | tf_op jit(solution)/shard_map/projection/ppermute | solution.py:49
  20.5 0.2 early.1.base_ref
  20.7 3.1 %collective-permute-done.8.refs_0_ = bf16[96,1024]{1,0:T(8,128)(2,1)S(1)} collective-permute-done((bf16[96,1024]{1,0:T(8,128)(2,1)S(1)}, bf16[96,1024]{1,0:T(8,128)(2,1)S(1)}, u32[]{:S(2)}, u32[]{:S(2)}) %collective-permute-start.8) | collective-permute-done | bytes 196640 | tf_op jit(solution)/shard_map/projection/ppermute | solution.py:49
  23.8 0.7 %final.1 = bf16[96,1280]{1,0:T(8,128)(2,1)} custom-call(f32[96,1280]{1,0:T(8,128)S(1)} %early.1.base_ref, f32[1,1280]{1,0:T(1,128)S(1)} %reshape.3.gate_ref, bf16[96,1024]{1,0:T(8,128)(2,1)S(1)} %collective-permute-done.8.refs_0_), custom_call_target="tpu_custom_call" | custom-call | bytes 983040 | tf_op jit(solution)/shard_map/projection/final/pallas_call | solution.py:354
  (3 shorter events, 0.0 us)
Async XLA Ops:
  0.0 1.5 %copy-start.2 = (f32[96,256]{1,0:T(8,128)S(1)}, f32[96,256]{1,0:T(8,128)}, u32[]{:S(2)}) copy-start(f32[96,256]{1,0:T(8,128)} %param.12) | copy-start | bytes 294916
  0.0 1.5 %copy-start.3 = (f32[96,256]{1,0:T(8,128)S(1)}, f32[96,256]{1,0:T(8,128)}, u32[]{:S(2)}) copy-start(f32[96,256]{1,0:T(8,128)} %param.11) | copy-start | bytes 294916
  0.0 16.4 %collective-permute-start.4 = (bf16[256,5120]{1,0:T(8,128)(2,1)}, bf16[256,5120]{1,0:T(8,128)(2,1)S(1)}, u32[]{:S(2)}, u32[]{:S(2)}) collective-permute-start(bf16[256,5120]{1,0:T(8,128)(2,1)} %refs_1_.3), channel_id=1, source_target_pairs={{0,1},{1,0},{2,3},{3,2},{4,5},{5,4},{6,7},{7,6},{8,9},{9,8},{10,11... | collective-permute-start | bytes 7864328 | tf_op jit(solution)/shard_map/weight_swap/ppermute | solution.py:49
  1.5 10.4 %collective-permute-start.2 = (bf16[96,512]{1,0:T(8,128)(2,1)S(1)}, bf16[96,512]{1,0:T(8,128)(2,1)S(1)}, u32[]{:S(2)}, u32[]{:S(2)}) collective-permute-start(bf16[96,512]{1,0:T(8,128)(2,1)S(1)} %maximum_convert_fusion.refs_0_), channel_id=1, source_target_pairs={{0,4},{4,12},{8,0},{12,8},{1,5},{5,13},{9,1},{13,9},{2,6},{6,14},{... | collective-permute-start | bytes 294920 | tf_op jit(solution)/shard_map/residual_gather/ppermute | solution.py:249
  4.2 7.7 %collective-permute-start.1 = (bf16[96,512]{1,0:T(8,128)(2,1)S(1)}, bf16[96,512]{1,0:T(8,128)(2,1)S(1)}, u32[]{:S(2)}, u32[]{:S(2)}) collective-permute-start(bf16[96,512]{1,0:T(8,128)(2,1)S(1)} %maximum_convert_fusion.refs_0_), channel_id=1, source_target_pairs={{0,8},{4,0},{8,12},{12,4},{1,9},{5,1},{9,13},{13,5},{2,10},{6,2},{... | collective-permute-start | bytes 294920 | tf_op jit(solution)/shard_map/residual_gather/ppermute | solution.py:249
  5.3 8.9 %collective-permute-start = (bf16[96,512]{1,0:T(8,128)(2,1)S(1)}, bf16[96,512]{1,0:T(8,128)(2,1)S(1)}, u32[]{:S(2)}, u32[]{:S(2)}) collective-permute-start(bf16[96,512]{1,0:T(8,128)(2,1)S(1)} %maximum_convert_fusion.refs_0_), channel_id=1, source_target_pairs={{0,12},{4,8},{8,4},{12,0},{1,13},{5,9},{9,5},{13,1},{2,14},{6,10},... | collective-permute-start | bytes 294920 | tf_op jit(solution)/shard_map/residual_gather/ppermute | solution.py:249
  9.1 9.9 %collective-permute-start.6 = (bf16[256,512]{1,0:T(8,128)(2,1)S(1)}, bf16[256,512]{1,0:T(8,128)(2,1)S(1)}, u32[]{:S(2)}, u32[]{:S(2)}) collective-permute-start(bf16[256,512]{1,0:T(8,128)(2,1)S(1)} %early_weight.1), channel_id=1, source_target_pairs={{0,2},{2,0},{1,3},{3,1},{4,6},{6,4},{5,7},{7,5},{8,10},{10,8},{9,1... | collective-permute-start | bytes 786440 | tf_op jit(solution)/shard_map/early_weight/ppermute | solution.py:49
  14.2 2.2 %copy-start = (bf16[256,5120]{1,0:T(8,128)(2,1)S(1)}, bf16[256,5120]{1,0:T(8,128)(2,1)}, u32[]{:S(2)}) copy-start(bf16[256,5120]{1,0:T(8,128)(2,1)} %refs_1_.3) | copy-start | bytes 7864324
  14.7 4.4 %copy-start.4 = (f32[1280]{0:T(1024)S(1)}, f32[1280]{0:T(1024)}, u32[]{:S(2)}) copy-start(f32[1280]{0:T(1024)} %param.15) | copy-start | bytes 15364
  14.7 4.4 %copy-start.1 = (bf16[96,1280]{1,0:T(8,128)(2,1)S(1)}, bf16[96,1280]{1,0:T(8,128)(2,1)}, u32[]{:S(2)}) copy-start(bf16[96,1280]{1,0:T(8,128)(2,1)} %hidden_ref.1) | copy-start | bytes 737284
  14.7 1.6 %collective-permute-start.3 = (bf16[96,256]{1,0:T(8,128)(2,1)S(1)}, bf16[96,256]{1,0:T(8,128)(2,1)S(1)}, u32[]{:S(2)}, u32[]{:S(2)}) collective-permute-start(bf16[96,256]{1,0:T(8,128)(2,1)S(1)} %attention.1.refs_0_), channel_id=1, source_target_pairs={{0,1},{1,0},{2,3},{3,2},{4,5},{5,4},{6,7},{7,6},{8,9},{9,8},{10,11... | collective-permute-start | bytes 147464 | tf_op jit(solution)/shard_map/attended_swap/ppermute | solution.py:49
  14.8 4.2 %collective-permute-start.5 = (bf16[96,256]{1,0:T(8,128)(2,1)S(1)}, bf16[96,256]{1,0:T(8,128)(2,1)S(1)}, u32[]{:S(2)}, u32[]{:S(2)}) collective-permute-start(bf16[96,256]{1,0:T(8,128)(2,1)S(1)} %attention.1.refs_0_), channel_id=1, source_target_pairs={{0,2},{2,0},{1,3},{3,1},{4,6},{6,4},{5,7},{7,5},{8,10},{10,8},{9,1... | collective-permute-start | bytes 147464 | tf_op jit(solution)/shard_map/attended_swap/ppermute | solution.py:49
  16.7 7.0 %collective-permute-start.8 = (bf16[96,1024]{1,0:T(8,128)(2,1)S(1)}, bf16[96,1024]{1,0:T(8,128)(2,1)S(1)}, u32[]{:S(2)}, u32[]{:S(2)}) collective-permute-start(bf16[96,1024]{1,0:T(8,128)(2,1)S(1)} %sent_term.1), channel_id=1, source_target_pairs={{0,2},{2,0},{1,3},{3,1},{4,6},{6,4},{5,7},{7,5},{8,10},{10,8},{9,1... | collective-permute-start | bytes 589832 | tf_op jit(solution)/shard_map/projection/ppermute | solution.py:49
  19.0 1.5 %collective-permute-start.7 = (bf16[352,256]{1,0:T(8,128)(2,1)S(1)}, bf16[352,256]{1,0:T(8,128)(2,1)S(1)}, u32[]{:S(2)}, u32[]{:S(2)}) collective-permute-start(bf16[352,256]{1,0:T(8,128)(2,1)S(1)} %pack.1), channel_id=1, source_target_pairs={{0,1},{1,0},{2,3},{3,2},{4,5},{5,4},{6,7},{7,6},{8,9},{9,8},{10,11... | collective-permute-start | bytes 540680 | tf_op jit(solution)/shard_map/projection/ppermute | solution.py:49

commit v21 on v20

--- a/solution.py
+++ b/solution.py
@@ -50,27 +50,42 @@
 
 
 LINE_OF_FOUR = (
-    ((0, 3), (1, 2), (2, 1), (3, 0)),
-    ((0, 2), (1, 0), (2, 3), (3, 1)),
-    ((0, 1), (1, 3), (2, 0), (3, 2)),
+    ((2, 0, 3, 1), (3, 0, 1, 2)),
+    ((3, 2, 1, 0), (2, 3, 0, 1)),
+    ((1, 3, 0, 2), (1, 2, 3, 0)),
 )
 
 
-def gather_permutes(patches):
-    if patches == 4:
+def gather_targets(patches, subs):
+    if patches == 4 and subs == 2:
         return LINE_OF_FOUR
     return [
-        [(i, (i + step) % patches) for i in range(patches)] for step in range(patches - 1, 0, -1)
+        [[(i + step) % patches for i in range(patches)]] * subs
+        for step in range(patches - 1, 0, -1)
     ]
 
 
-def gather_sources(patches, place):
+def gather(own, patches, subs):
+    blocks = [own]
+    for targets in gather_targets(patches, subs):
+        pairs = [
+            (place * subs + sub, targets[sub][place] * subs + sub)
+            for place in range(patches)
+            for sub in range(subs)
+        ]
+        blocks.append(lax.ppermute(own, ("patch", "sub"), pairs))
+    return blocks
+
+
+def gather_sources(patches, subs):
+    place, core = lax.axis_index("patch"), lax.axis_index("sub")
     sources = [place]
-    for pairs in gather_permutes(patches):
-        before = {target: source for source, target in pairs}
-        value = jnp.int32(before[0])
-        for i in range(1, patches):
-            value = jnp.where(place == i, jnp.int32(before[i]), value)
+    for targets in gather_targets(patches, subs):
+        value = jnp.int32(0)
+        for sub in range(subs):
+            for source, target in enumerate(targets[sub]):
+                here = jnp.logical_and(place == target, core == sub)
+                value = jnp.where(here, jnp.int32(source), value)
         sources.append(value)
     return sources
 
@@ -94,10 +109,10 @@
 
 
 def stage_kernel(
-    patches, q_hbm, held_k_hbm, held_v_hbm, q_ref, products_ref, values_ref, keys_ref, sems
+    patches, subs, q_hbm, held_k_hbm, held_v_hbm, q_ref, products_ref, values_ref, keys_ref, sems
 ):
     rows, width = q_ref.shape
-    sources = gather_sources(patches, lax.axis_index("patch"))
+    sources = gather_sources(patches, subs)
     copies = [pltpu.make_async_copy(q_hbm, q_ref, sems.at[0])]
     for i, source in enumerate(sources):
         at = pl.multiple_of(source * rows, rows)
@@ -245,9 +260,7 @@
                 lax.pad(key_change, low, ((0, 0, 0), (0, width, 0))),
                 lax.pad(value_change, low, ((0, 0, 0), (width, 0, 0))),
             ).astype(jnp.bfloat16)
-            blocks = [residual] + [
-                lax.ppermute(residual, "patch", pairs) for pairs in gather_permutes(patches)
-            ]
+            blocks = gather(residual, patches, subs)
 
         with jax.named_scope("weight_swap"):
             weights = [out_weight] + [shift(out_weight, "sub", subs, i) for i in range(1, subs)]
@@ -276,7 +289,7 @@
         tokens = rows * patches
         with jax.named_scope("attention"):
             staged_queries, products, values = call(
-                functools.partial(stage_kernel, patches),
+                functools.partial(stage_kernel, patches, subs),
                 [
                     jax.ShapeDtypeStruct((rows, width), jnp.bfloat16),
                     jax.ShapeDtypeStruct((width // HD, rows, tokens), jnp.float32),

time: 24.7 us -> 24 us (0.972)
  starting transfers between devices: 12.5 us -> 11.9 us
    ppermute x3, starting transfers between devices: 7.64 us -> 6.74 us  [gather(): blocks.append(lax.ppermute(own, ('patch', 'sub'), pairs))]
    ppermute x6, starting transfers between devices: 4.83 us -> 5.13 us  [shift(): lax.ppermute(array, axis, [(i, (i + step) % size) for i in range(size)])]
  transfers between devices with their start and end apart: 9 -> 9, of which waited for: 4 -> 5; matrix products, arithmetic and copies ran while one was open for 0% -> 0% of each run, Pallas kernels for 15% -> 16%
where the time goes in v21:
time: 24 us; the launch traced here: 23.8 us
  starting transfers between devices  11.9 us (50%)
  waiting for transfers between devices  7.3 us (30%)
  Pallas kernels  4.44 us (19%)
    ppermute x3, starting transfers between devices, gather(): blocks.append(lax.ppermute(own, ('patch', 'sub'), pairs))  6.74 us
    ppermute x6, starting transfers between devices, shift(): lax.ppermute(array, axis, [(i, (i + step) % size) for i in range(size)])  5.13 us
    ppermute x6, waiting for transfers between devices, shift(): lax.ppermute(array, axis, [(i, (i + step) % size) for i in range(size)])  5.13 us
    ppermute x3, waiting for transfers between devices, gather(): blocks.append(lax.ppermute(own, ('patch', 'sub'), pairs))  2.17 us
    pallas_call x1, Pallas kernels, per_device(): call(functools.partial(stage_kernel, patches, subs), [jax.ShapeDtypeStruc...  1.28 us
    pallas_call x1, Pallas kernels, per_device(): call(functools.partial(early_weight_kernel, subs, columns, early), jax.Sh...  0.99 us
    pallas_call x1, Pallas kernels, per_device(): call(functools.partial(final_kernel, early, row_blocks), jax.ShapeDtypeSt...  0.74 us
    pallas_call x1, Pallas kernels, per_device(): call(functools.partial(attention_kernel, 1.0 / math.sqrt(HD)), jax.ShapeD...  0.53 us
  transfers between devices with their start and end apart: 9, of which 5 were waited for; matrix products, arithmetic and copies ran while one was open for 0% of the time, Pallas kernels for 16%

profile of v21, /device:TPU:0, one launch (start us, length us, event | category | flops | bytes accessed | tf_op | source)
XLA Modules:
  0.0 23.8 jit_solution(16511302386600415427)
XLA Ops:
  0.0 0.0 copy-start.2
  0.0 0.0 copy-start.3
  0.0 0.5 %collective-permute-start.4 = (bf16[256,5120]{1,0:T(8,128)(2,1)}, bf16[256,5120]{1,0:T(8,128)(2,1)S(1)}, u32[]{:S(2)}, u32[]{:S(2)}) collective-permute-start(bf16[256,5120]{1,0:T(8,128)(2,1)} %refs_1_.3), channel_id=1, source_target_pairs={{0,1},{1,0},{2,3},{3,2},{4,5},{5,4},{6,7},{7,6},{8,9},{9,8},{10,11... | collective-permute-start | bytes 7864328 | tf_op jit(solution)/shard_map/weight_swap/ppermute | solution.py:49
  0.5 1.0 %early_weight.1 = bf16[256,512]{1,0:T(8,128)(2,1)S(1)} custom-call(bf16[256,5120]{1,0:T(8,128)(2,1)} %refs_1_.3), custom_call_target="tpu_custom_call" | custom-call | bytes 524288 | tf_op jit(solution)/shard_map/early_weight/early_weight/pallas_call | solution.py:244
  1.5 0.0 copy-done.2
  1.5 0.0 copy-done.3
  1.5 2.7 %collective-permute-start.2 = (bf16[96,512]{1,0:T(8,128)(2,1)S(1)}, bf16[96,512]{1,0:T(8,128)(2,1)S(1)}, u32[]{:S(2)}, u32[]{:S(2)}) collective-permute-start(bf16[96,512]{1,0:T(8,128)(2,1)S(1)} %maximum_convert_fusion.refs_0_), channel_id=1, source_target_pairs={{0,4},{1,5},{4,12},{5,9},{8,0},{9,13},{12,8},{13,1},{2,6},{3,7},{6... | collective-permute-start | bytes 294920 | tf_op jit(solution)/shard_map/residual_gather/ppermute | solution.py:76
  4.2 2.5 %collective-permute-start.1 = (bf16[96,512]{1,0:T(8,128)(2,1)S(1)}, bf16[96,512]{1,0:T(8,128)(2,1)S(1)}, u32[]{:S(2)}, u32[]{:S(2)}) collective-permute-start(bf16[96,512]{1,0:T(8,128)(2,1)S(1)} %maximum_convert_fusion.refs_0_), channel_id=1, source_target_pairs={{0,12},{1,9},{4,8},{5,13},{8,4},{9,1},{12,0},{13,5},{2,14},{3,11},... | collective-permute-start | bytes 294920 | tf_op jit(solution)/shard_map/residual_gather/ppermute | solution.py:76
  6.7 1.6 %collective-permute-start = (bf16[96,512]{1,0:T(8,128)(2,1)S(1)}, bf16[96,512]{1,0:T(8,128)(2,1)S(1)}, u32[]{:S(2)}, u32[]{:S(2)}) collective-permute-start(bf16[96,512]{1,0:T(8,128)(2,1)S(1)} %maximum_convert_fusion.refs_0_), channel_id=1, source_target_pairs={{0,8},{1,13},{4,0},{5,1},{8,12},{9,5},{12,4},{13,9},{2,10},{3,15},... | collective-permute-start | bytes 294920 | tf_op jit(solution)/shard_map/residual_gather/ppermute | solution.py:76
  8.2 1.5 %collective-permute-start.6 = (bf16[256,512]{1,0:T(8,128)(2,1)S(1)}, bf16[256,512]{1,0:T(8,128)(2,1)S(1)}, u32[]{:S(2)}, u32[]{:S(2)}) collective-permute-start(bf16[256,512]{1,0:T(8,128)(2,1)S(1)} %early_weight.1), channel_id=1, source_target_pairs={{0,2},{2,0},{1,3},{3,1},{4,6},{6,4},{5,7},{7,5},{8,10},{10,8},{9,1... | collective-permute-start | bytes 786440 | tf_op jit(solution)/shard_map/early_weight/ppermute | solution.py:49
  9.7 1.3 %stage.1 = (bf16[96,256]{1,0:T(8,128)(2,1)S(1)}, f32[2,96,384]{2,1,0:T(8,128)S(1)}, bf16[384,256]{1,0:T(8,128)(2,1)S(1)}) custom-call(bf16[96,256]{1,0:T(8,128)(2,1)} %q_hbm.1, bf16[384,256]{1,0:T(8,128)(2,1)} %held_k_hbm.1, bf16[384,256]{1,0:T(8,128)(2,1)} %held_v_hbm.1), custom_call_target="tpu_custom_call" | custom-call | flops 2000000000 | tf_op jit(solution)/shard_map/attention/stage/pallas_call | solution.py:291
  11.0 0.0 collective-permute-done.2.refs_3_
  11.0 1.3 %collective-permute-done.1.refs_2_ = bf16[96,512]{1,0:T(8,128)(2,1)S(1)} collective-permute-done((bf16[96,512]{1,0:T(8,128)(2,1)S(1)}, bf16[96,512]{1,0:T(8,128)(2,1)S(1)}, u32[]{:S(2)}, u32[]{:S(2)}) %collective-permute-start.1) | collective-permute-done | bytes 98336 | tf_op jit(solution)/shard_map/residual_gather/ppermute | solution.py:76
  12.4 0.8 %collective-permute-done.refs_1_ = bf16[96,512]{1,0:T(8,128)(2,1)S(1)} collective-permute-done((bf16[96,512]{1,0:T(8,128)(2,1)S(1)}, bf16[96,512]{1,0:T(8,128)(2,1)S(1)}, u32[]{:S(2)}, u32[]{:S(2)}) %collective-permute-start) | collective-permute-done | bytes 98336 | tf_op jit(solution)/shard_map/residual_gather/ppermute | solution.py:76
  13.2 0.0 copy-start
  13.2 0.5 %attention.1.refs_0_ = bf16[96,256]{1,0:T(8,128)(2,1)S(1)} custom-call(bf16[96,256]{1,0:T(8,128)(2,1)S(1)} %get-tuple-element.11.q_ref, f32[2,96,384]{2,1,0:T(8,128)S(1)} %get-tuple-element.12.products_ref, bf16[384,256]{1,0:T(8,128)(2,1)S(1)} %get-tuple-element.13.values_ref, bf16[96,512]{1,0:T(8,128)(2,1)S(1)} %maximum_convert_fusion.refs_0_, ...), custom_call_target="tpu_custom_call" | custom-call | flops 2000000000 | tf_op jit(solution)/shard_map/attention/attention/pallas_call | solution.py:307
  13.7 0.0 copy-start.4
  13.7 0.0 copy-start.1
  13.8 0.1 collective-permute-start.3
  13.8 2.0 %collective-permute-start.5 = (bf16[96,256]{1,0:T(8,128)(2,1)S(1)}, bf16[96,256]{1,0:T(8,128)(2,1)S(1)}, u32[]{:S(2)}, u32[]{:S(2)}) collective-permute-start(bf16[96,256]{1,0:T(8,128)(2,1)S(1)} %attention.1.refs_0_), channel_id=1, source_target_pairs={{0,2},{2,0},{1,3},{3,1},{4,6},{6,4},{5,7},{7,5},{8,10},{10,8},{9,1... | collective-permute-start | bytes 147464 | tf_op jit(solution)/shard_map/attended_swap/ppermute | solution.py:49
  15.8 0.0 collective-permute-done.3.refs_2_
  15.8 0.0 collective-permute-done.4.refs_3_
  15.8 0.0 copy-done
  15.8 0.3 %sent_term.1 = bf16[96,1024]{1,0:T(8,128)(2,1)S(1)} custom-call(bf16[96,256]{1,0:T(8,128)(2,1)S(1)} %attention.1.refs_0_, bf16[256,5120]{1,0:T(8,128)(2,1)S(1)} %copy-done, bf16[96,256]{1,0:T(8,128)(2,1)S(1)} %collective-permute-done.3.refs_2_, bf16[256,5120]{1,0:T(8,128)(2,1)S(1)} %collective-permute-done.4.refs_3_), custom_call_target="tpu_custom_call" | custom-call | flops 125829120 | tf_op jit(solution)/shard_map/projection/sent_term/pallas_call | solution.py:330
  16.2 1.0 %collective-permute-start.8 = (bf16[96,1024]{1,0:T(8,128)(2,1)S(1)}, bf16[96,1024]{1,0:T(8,128)(2,1)S(1)}, u32[]{:S(2)}, u32[]{:S(2)}) collective-permute-start(bf16[96,1024]{1,0:T(8,128)(2,1)S(1)} %sent_term.1), channel_id=1, source_target_pairs={{0,2},{2,0},{1,3},{3,1},{4,6},{6,4},{5,7},{7,5},{8,10},{10,8},{9,1... | collective-permute-start | bytes 589832 | tf_op jit(solution)/shard_map/projection/ppermute | solution.py:49
  17.2 0.8 %collective-permute-done.5.attended_ref = bf16[96,256]{1,0:T(8,128)(2,1)S(1)} collective-permute-done((bf16[96,256]{1,0:T(8,128)(2,1)S(1)}, bf16[96,256]{1,0:T(8,128)(2,1)S(1)}, u32[]{:S(2)}, u32[]{:S(2)}) %collective-permute-start.5) | collective-permute-done | bytes 49184 | tf_op jit(solution)/shard_map/attended_swap/ppermute | solution.py:49
  18.0 0.0 collective-permute-done.6.weight_ref
  18.0 0.1 collective-permute-start.7
  18.1 0.0 copy-done.4
  18.1 0.0 copy-done.1
  18.2 0.4 %base.1.base_ref = f32[96,1280]{1,0:T(8,128)S(1)} custom-call(bf16[96,1280]{1,0:T(8,128)(2,1)S(1)} %copy-done.1, f32[1,1280]{1,0:T(1,128)S(1)} %reshape.3.gate_ref, bf16[96,256]{1,0:T(8,128)(2,1)S(1)} %attention.1.refs_0_, bf16[256,5120]{1,0:T(8,128)(2,1)S(1)} %copy-done, bf16[96,256]{1,0:T(8,128)(2,1)S(1)} %collective-permute-done.3.refs_2_, ...), custom_call_target="tpu_custom_call" | custom-call | flops 125829120 | tf_op jit(solution)/shard_map/projection/base/pallas_call | solution.py:341
  18.5 1.0 %collective-permute-done.7.packed_ref = bf16[352,256]{1,0:T(8,128)(2,1)S(1)} collective-permute-done((bf16[352,256]{1,0:T(8,128)(2,1)S(1)}, bf16[352,256]{1,0:T(8,128)(2,1)S(1)}, u32[]{:S(2)}, u32[]{:S(2)}) %collective-permute-start.7) | collective-permute-done | bytes 180256 | tf_op jit(solution)/shard_map/projection/ppermute | solution.py:49
  19.5 0.2 early.1.base_ref
  19.7 3.3 %collective-permute-done.8.refs_0_ = bf16[96,1024]{1,0:T(8,128)(2,1)S(1)} collective-permute-done((bf16[96,1024]{1,0:T(8,128)(2,1)S(1)}, bf16[96,1024]{1,0:T(8,128)(2,1)S(1)}, u32[]{:S(2)}, u32[]{:S(2)}) %collective-permute-start.8) | collective-permute-done | bytes 196640 | tf_op jit(solution)/shard_map/projection/ppermute | solution.py:49
  23.1 0.7 %final.1 = bf16[96,1280]{1,0:T(8,128)(2,1)} custom-call(f32[96,1280]{1,0:T(8,128)S(1)} %early.1.base_ref, f32[1,1280]{1,0:T(1,128)S(1)} %reshape.3.gate_ref, bf16[96,1024]{1,0:T(8,128)(2,1)S(1)} %collective-permute-done.8.refs_0_), custom_call_target="tpu_custom_call" | custom-call | bytes 983040 | tf_op jit(solution)/shard_map/projection/final/pallas_call | solution.py:367
  (3 shorter events, 0.0 us)
Async XLA Ops:
  0.0 1.5 %copy-start.2 = (f32[96,256]{1,0:T(8,128)S(1)}, f32[96,256]{1,0:T(8,128)}, u32[]{:S(2)}) copy-start(f32[96,256]{1,0:T(8,128)} %param.12) | copy-start | bytes 294916
  0.0 1.5 %copy-start.3 = (f32[96,256]{1,0:T(8,128)S(1)}, f32[96,256]{1,0:T(8,128)}, u32[]{:S(2)}) copy-start(f32[96,256]{1,0:T(8,128)} %param.11) | copy-start | bytes 294916
  0.0 15.8 %collective-permute-start.4 = (bf16[256,5120]{1,0:T(8,128)(2,1)}, bf16[256,5120]{1,0:T(8,128)(2,1)S(1)}, u32[]{:S(2)}, u32[]{:S(2)}) collective-permute-start(bf16[256,5120]{1,0:T(8,128)(2,1)} %refs_1_.3), channel_id=1, source_target_pairs={{0,1},{1,0},{2,3},{3,2},{4,5},{5,4},{6,7},{7,6},{8,9},{9,8},{10,11... | collective-permute-start | bytes 7864328 | tf_op jit(solution)/shard_map/weight_swap/ppermute | solution.py:49
  1.5 9.5 %collective-permute-start.2 = (bf16[96,512]{1,0:T(8,128)(2,1)S(1)}, bf16[96,512]{1,0:T(8,128)(2,1)S(1)}, u32[]{:S(2)}, u32[]{:S(2)}) collective-permute-start(bf16[96,512]{1,0:T(8,128)(2,1)S(1)} %maximum_convert_fusion.refs_0_), channel_id=1, source_target_pairs={{0,4},{1,5},{4,12},{5,9},{8,0},{9,13},{12,8},{13,1},{2,6},{3,7},{6... | collective-permute-start | bytes 294920 | tf_op jit(solution)/shard_map/residual_gather/ppermute | solution.py:76
  4.2 8.2 %collective-permute-start.1 = (bf16[96,512]{1,0:T(8,128)(2,1)S(1)}, bf16[96,512]{1,0:T(8,128)(2,1)S(1)}, u32[]{:S(2)}, u32[]{:S(2)}) collective-permute-start(bf16[96,512]{1,0:T(8,128)(2,1)S(1)} %maximum_convert_fusion.refs_0_), channel_id=1, source_target_pairs={{0,12},{1,9},{4,8},{5,13},{8,4},{9,1},{12,0},{13,5},{2,14},{3,11},... | collective-permute-start | bytes 294920 | tf_op jit(solution)/shard_map/residual_gather/ppermute | solution.py:76
  6.7 6.5 %collective-permute-start = (bf16[96,512]{1,0:T(8,128)(2,1)S(1)}, bf16[96,512]{1,0:T(8,128)(2,1)S(1)}, u32[]{:S(2)}, u32[]{:S(2)}) collective-permute-start(bf16[96,512]{1,0:T(8,128)(2,1)S(1)} %maximum_convert_fusion.refs_0_), channel_id=1, source_target_pairs={{0,8},{1,13},{4,0},{5,1},{8,12},{9,5},{12,4},{13,9},{2,10},{3,15},... | collective-permute-start | bytes 294920 | tf_op jit(solution)/shard_map/residual_gather/ppermute | solution.py:76
  8.2 9.8 %collective-permute-start.6 = (bf16[256,512]{1,0:T(8,128)(2,1)S(1)}, bf16[256,512]{1,0:T(8,128)(2,1)S(1)}, u32[]{:S(2)}, u32[]{:S(2)}) collective-permute-start(bf16[256,512]{1,0:T(8,128)(2,1)S(1)} %early_weight.1), channel_id=1, source_target_pairs={{0,2},{2,0},{1,3},{3,1},{4,6},{6,4},{5,7},{7,5},{8,10},{10,8},{9,1... | collective-permute-start | bytes 786440 | tf_op jit(solution)/shard_map/early_weight/ppermute | solution.py:49
  13.2 2.6 %copy-start = (bf16[256,5120]{1,0:T(8,128)(2,1)S(1)}, bf16[256,5120]{1,0:T(8,128)(2,1)}, u32[]{:S(2)}) copy-start(bf16[256,5120]{1,0:T(8,128)(2,1)} %refs_1_.3) | copy-start | bytes 7864324
  13.7 4.4 %copy-start.4 = (f32[1280]{0:T(1024)S(1)}, f32[1280]{0:T(1024)}, u32[]{:S(2)}) copy-start(f32[1280]{0:T(1024)} %param.15) | copy-start | bytes 15364
  13.7 4.4 %copy-start.1 = (bf16[96,1280]{1,0:T(8,128)(2,1)S(1)}, bf16[96,1280]{1,0:T(8,128)(2,1)}, u32[]{:S(2)}) copy-start(bf16[96,1280]{1,0:T(8,128)(2,1)} %hidden_ref.1) | copy-start | bytes 737284
  13.8 2.1 %collective-permute-start.3 = (bf16[96,256]{1,0:T(8,128)(2,1)S(1)}, bf16[96,256]{1,0:T(8,128)(2,1)S(1)}, u32[]{:S(2)}, u32[]{:S(2)}) collective-permute-start(bf16[96,256]{1,0:T(8,128)(2,1)S(1)} %attention.1.refs_0_), channel_id=1, source_target_pairs={{0,1},{1,0},{2,3},{3,2},{4,5},{5,4},{6,7},{7,6},{8,9},{9,8},{10,11... | collective-permute-start | bytes 147464 | tf_op jit(solution)/shard_map/attended_swap/ppermute | solution.py:49
  13.8 4.2 %collective-permute-start.5 = (bf16[96,256]{1,0:T(8,128)(2,1)S(1)}, bf16[96,256]{1,0:T(8,128)(2,1)S(1)}, u32[]{:S(2)}, u32[]{:S(2)}) collective-permute-start(bf16[96,256]{1,0:T(8,128)(2,1)S(1)} %attention.1.refs_0_), channel_id=1, source_target_pairs={{0,2},{2,0},{1,3},{3,1},{4,6},{6,4},{5,7},{7,5},{8,10},{10,8},{9,1... | collective-permute-start | bytes 147464 | tf_op jit(solution)/shard_map/attended_swap/ppermute | solution.py:49
  16.2 6.9 %collective-permute-start.8 = (bf16[96,1024]{1,0:T(8,128)(2,1)S(1)}, bf16[96,1024]{1,0:T(8,128)(2,1)S(1)}, u32[]{:S(2)}, u32[]{:S(2)}) collective-permute-start(bf16[96,1024]{1,0:T(8,128)(2,1)S(1)} %sent_term.1), channel_id=1, source_target_pairs={{0,2},{2,0},{1,3},{3,1},{4,6},{6,4},{5,7},{7,5},{8,10},{10,8},{9,1... | collective-permute-start | bytes 589832 | tf_op jit(solution)/shard_map/projection/ppermute | solution.py:49
  18.0 1.5 %collective-permute-start.7 = (bf16[352,256]{1,0:T(8,128)(2,1)S(1)}, bf16[352,256]{1,0:T(8,128)(2,1)S(1)}, u32[]{:S(2)}, u32[]{:S(2)}) collective-permute-start(bf16[352,256]{1,0:T(8,128)(2,1)S(1)} %pack.1), channel_id=1, source_target_pairs={{0,1},{1,0},{2,3},{3,2},{4,5},{5,4},{6,7},{7,6},{8,9},{9,8},{10,11... | collective-permute-start | bytes 540680 | tf_op jit(solution)/shard_map/projection/ppermute | solution.py:49

commit v22 on v21

--- a/solution.py
+++ b/solution.py
@@ -50,9 +50,9 @@
 
 
 LINE_OF_FOUR = (
-    ((2, 0, 3, 1), (3, 0, 1, 2)),
-    ((3, 2, 1, 0), (2, 3, 0, 1)),
-    ((1, 3, 0, 2), (1, 2, 3, 0)),
+    ((3, 0, 1, 2), (2, 0, 3, 1)),
+    ((2, 3, 0, 1), (3, 2, 1, 0)),
+    ((1, 2, 3, 0), (1, 3, 0, 2)),
 )
 
 

time: 24 us -> 25 us (1.042)
  waiting for transfers between devices: 7.3 us -> 8.59 us
  starting transfers between devices: 11.9 us -> 11.6 us
    ppermute x3, waiting for transfers between devices: 2.17 us -> 3.44 us  [gather(): blocks.append(lax.ppermute(own, ('patch', 'sub'), pairs))]
  transfers between devices with their start and end apart: 9 -> 9, of which waited for: 5 -> 4; matrix products, arithmetic and copies ran while one was open for 0% -> 0% of each run, Pallas kernels for 16% -> 15%
where the time goes in v22:
time: 25 us; the launch traced here: 24.8 us
  starting transfers between devices  11.6 us (46%)
  waiting for transfers between devices  8.59 us (34%)
  Pallas kernels  4.43 us (18%)
    ppermute x3, starting transfers between devices, gather(): blocks.append(lax.ppermute(own, ('patch', 'sub'), pairs))  6.62 us
    ppermute x6, waiting for transfers between devices, shift(): lax.ppermute(array, axis, [(i, (i + step) % size) for i in range(size)])  5.15 us
    ppermute x6, starting transfers between devices, shift(): lax.ppermute(array, axis, [(i, (i + step) % size) for i in range(size)])  4.95 us
    ppermute x3, waiting for transfers between devices, gather(): blocks.append(lax.ppermute(own, ('patch', 'sub'), pairs))  3.44 us
    pallas_call x1, Pallas kernels, per_device(): call(functools.partial(stage_kernel, patches, subs), [jax.ShapeDtypeStruc...  1.29 us
    pallas_call x1, Pallas kernels, per_device(): call(functools.partial(early_weight_kernel, subs, columns, early), jax.Sh...  0.99 us
    pallas_call x1, Pallas kernels, per_device(): call(functools.partial(final_kernel, early, row_blocks), jax.ShapeDtypeSt...  0.74 us
    pallas_call x1, Pallas kernels, per_device(): call(functools.partial(attention_kernel, 1.0 / math.sqrt(HD)), jax.ShapeD...  0.53 us
  transfers between devices with their start and end apart: 9, of which 4 were waited for; matrix products, arithmetic and copies ran while one was open for 0% of the time, Pallas kernels for 15%

profile of v22, /device:TPU:0, one launch (start us, length us, event | category | flops | bytes accessed | tf_op | source)
XLA Modules:
  0.0 24.8 jit_solution(16972215000382199645)
XLA Ops:
  0.0 0.0 copy-start.2
  0.0 0.0 copy-start.3
  0.0 0.5 %collective-permute-start.4 = (bf16[256,5120]{1,0:T(8,128)(2,1)}, bf16[256,5120]{1,0:T(8,128)(2,1)S(1)}, u32[]{:S(2)}, u32[]{:S(2)}) collective-permute-start(bf16[256,5120]{1,0:T(8,128)(2,1)} %refs_1_.3), channel_id=1, source_target_pairs={{0,1},{1,0},{2,3},{3,2},{4,5},{5,4},{6,7},{7,6},{8,9},{9,8},{10,11... | collective-permute-start | bytes 7864328 | tf_op jit(solution)/shard_map/weight_swap/ppermute | solution.py:49
  0.5 1.0 %early_weight.1 = bf16[256,512]{1,0:T(8,128)(2,1)S(1)} custom-call(bf16[256,5120]{1,0:T(8,128)(2,1)} %refs_1_.3), custom_call_target="tpu_custom_call" | custom-call | bytes 524288 | tf_op jit(solution)/shard_map/early_weight/early_weight/pallas_call | solution.py:244
  1.5 0.0 copy-done.2
  1.5 0.0 copy-done.3
  1.5 2.7 %collective-permute-start.2 = (bf16[96,512]{1,0:T(8,128)(2,1)S(1)}, bf16[96,512]{1,0:T(8,128)(2,1)S(1)}, u32[]{:S(2)}, u32[]{:S(2)}) collective-permute-start(bf16[96,512]{1,0:T(8,128)(2,1)S(1)} %maximum_convert_fusion.refs_0_), channel_id=1, source_target_pairs={{0,4},{1,5},{4,8},{5,13},{8,12},{9,1},{12,0},{13,9},{2,6},{3,7},{6... | collective-permute-start | bytes 294920 | tf_op jit(solution)/shard_map/residual_gather/ppermute | solution.py:76
  4.2 2.6 %collective-permute-start.1 = (bf16[96,512]{1,0:T(8,128)(2,1)S(1)}, bf16[96,512]{1,0:T(8,128)(2,1)S(1)}, u32[]{:S(2)}, u32[]{:S(2)}) collective-permute-start(bf16[96,512]{1,0:T(8,128)(2,1)S(1)} %maximum_convert_fusion.refs_0_), channel_id=1, source_target_pairs={{0,8},{1,13},{4,12},{5,9},{8,0},{9,5},{12,4},{13,1},{2,10},{3,15},... | collective-permute-start | bytes 294920 | tf_op jit(solution)/shard_map/residual_gather/ppermute | solution.py:76
  6.8 1.3 %collective-permute-start = (bf16[96,512]{1,0:T(8,128)(2,1)S(1)}, bf16[96,512]{1,0:T(8,128)(2,1)S(1)}, u32[]{:S(2)}, u32[]{:S(2)}) collective-permute-start(bf16[96,512]{1,0:T(8,128)(2,1)S(1)} %maximum_convert_fusion.refs_0_), channel_id=1, source_target_pairs={{0,12},{1,9},{4,0},{5,1},{8,4},{9,13},{12,8},{13,5},{2,14},{3,11},... | collective-permute-start | bytes 294920 | tf_op jit(solution)/shard_map/residual_gather/ppermute | solution.py:76
  8.1 1.5 %collective-permute-start.6 = (bf16[256,512]{1,0:T(8,128)(2,1)S(1)}, bf16[256,512]{1,0:T(8,128)(2,1)S(1)}, u32[]{:S(2)}, u32[]{:S(2)}) collective-permute-start(bf16[256,512]{1,0:T(8,128)(2,1)S(1)} %early_weight.1), channel_id=1, source_target_pairs={{0,2},{2,0},{1,3},{3,1},{4,6},{6,4},{5,7},{7,5},{8,10},{10,8},{9,1... | collective-permute-start | bytes 786440 | tf_op jit(solution)/shard_map/early_weight/ppermute | solution.py:49
  9.6 1.3 %stage.1 = (bf16[96,256]{1,0:T(8,128)(2,1)S(1)}, f32[2,96,384]{2,1,0:T(8,128)S(1)}, bf16[384,256]{1,0:T(8,128)(2,1)S(1)}) custom-call(bf16[96,256]{1,0:T(8,128)(2,1)} %q_hbm.1, bf16[384,256]{1,0:T(8,128)(2,1)} %held_k_hbm.1, bf16[384,256]{1,0:T(8,128)(2,1)} %held_v_hbm.1), custom_call_target="tpu_custom_call" | custom-call | flops 2000000000 | tf_op jit(solution)/shard_map/attention/stage/pallas_call | solution.py:291
  10.9 0.0 collective-permute-done.2.refs_3_
  10.9 3.4 %collective-permute-done.1.refs_2_ = bf16[96,512]{1,0:T(8,128)(2,1)S(1)} collective-permute-done((bf16[96,512]{1,0:T(8,128)(2,1)S(1)}, bf16[96,512]{1,0:T(8,128)(2,1)S(1)}, u32[]{:S(2)}, u32[]{:S(2)}) %collective-permute-start.1) | collective-permute-done | bytes 98336 | tf_op jit(solution)/shard_map/residual_gather/ppermute | solution.py:76
  14.4 0.0 collective-permute-done.refs_1_
  14.4 0.0 copy-start
  14.4 0.5 %attention.1.refs_0_ = bf16[96,256]{1,0:T(8,128)(2,1)S(1)} custom-call(bf16[96,256]{1,0:T(8,128)(2,1)S(1)} %get-tuple-element.11.q_ref, f32[2,96,384]{2,1,0:T(8,128)S(1)} %get-tuple-element.12.products_ref, bf16[384,256]{1,0:T(8,128)(2,1)S(1)} %get-tuple-element.13.values_ref, bf16[96,512]{1,0:T(8,128)(2,1)S(1)} %maximum_convert_fusion.refs_0_, ...), custom_call_target="tpu_custom_call" | custom-call | flops 2000000000 | tf_op jit(solution)/shard_map/attention/attention/pallas_call | solution.py:307
  14.9 0.0 copy-start.4
  14.9 0.0 copy-start.1
  14.9 0.1 collective-permute-start.3
  15.0 1.7 %collective-permute-start.5 = (bf16[96,256]{1,0:T(8,128)(2,1)S(1)}, bf16[96,256]{1,0:T(8,128)(2,1)S(1)}, u32[]{:S(2)}, u32[]{:S(2)}) collective-permute-start(bf16[96,256]{1,0:T(8,128)(2,1)S(1)} %attention.1.refs_0_), channel_id=1, source_target_pairs={{0,2},{2,0},{1,3},{3,1},{4,6},{6,4},{5,7},{7,5},{8,10},{10,8},{9,1... | collective-permute-start | bytes 147464 | tf_op jit(solution)/shard_map/attended_swap/ppermute | solution.py:49
  16.7 0.0 collective-permute-done.3.refs_2_
  16.7 0.0 collective-permute-done.4.refs_3_
  16.7 0.0 copy-done
  16.7 0.3 %sent_term.1 = bf16[96,1024]{1,0:T(8,128)(2,1)S(1)} custom-call(bf16[96,256]{1,0:T(8,128)(2,1)S(1)} %attention.1.refs_0_, bf16[256,5120]{1,0:T(8,128)(2,1)S(1)} %copy-done, bf16[96,256]{1,0:T(8,128)(2,1)S(1)} %collective-permute-done.3.refs_2_, bf16[256,5120]{1,0:T(8,128)(2,1)S(1)} %collective-permute-done.4.refs_3_), custom_call_target="tpu_custom_call" | custom-call | flops 125829120 | tf_op jit(solution)/shard_map/projection/sent_term/pallas_call | solution.py:330
  17.0 1.2 %collective-permute-start.8 = (bf16[96,1024]{1,0:T(8,128)(2,1)S(1)}, bf16[96,1024]{1,0:T(8,128)(2,1)S(1)}, u32[]{:S(2)}, u32[]{:S(2)}) collective-permute-start(bf16[96,1024]{1,0:T(8,128)(2,1)S(1)} %sent_term.1), channel_id=1, source_target_pairs={{0,2},{2,0},{1,3},{3,1},{4,6},{6,4},{5,7},{7,5},{8,10},{10,8},{9,1... | collective-permute-start | bytes 589832 | tf_op jit(solution)/shard_map/projection/ppermute | solution.py:49
  18.2 1.0 %collective-permute-done.5.attended_ref = bf16[96,256]{1,0:T(8,128)(2,1)S(1)} collective-permute-done((bf16[96,256]{1,0:T(8,128)(2,1)S(1)}, bf16[96,256]{1,0:T(8,128)(2,1)S(1)}, u32[]{:S(2)}, u32[]{:S(2)}) %collective-permute-start.5) | collective-permute-done | bytes 49184 | tf_op jit(solution)/shard_map/attended_swap/ppermute | solution.py:49
  19.1 0.0 collective-permute-done.6.weight_ref
  19.2 0.1 collective-permute-start.7
  19.2 0.0 copy-done.4
  19.3 0.0 copy-done.1
  19.3 0.4 %base.1.base_ref = f32[96,1280]{1,0:T(8,128)S(1)} custom-call(bf16[96,1280]{1,0:T(8,128)(2,1)S(1)} %copy-done.1, f32[1,1280]{1,0:T(1,128)S(1)} %reshape.3.gate_ref, bf16[96,256]{1,0:T(8,128)(2,1)S(1)} %attention.1.refs_0_, bf16[256,5120]{1,0:T(8,128)(2,1)S(1)} %copy-done, bf16[96,256]{1,0:T(8,128)(2,1)S(1)} %collective-permute-done.3.refs_2_, ...), custom_call_target="tpu_custom_call" | custom-call | flops 125829120 | tf_op jit(solution)/shard_map/projection/base/pallas_call | solution.py:341
  19.7 1.0 %collective-permute-done.7.packed_ref = bf16[352,256]{1,0:T(8,128)(2,1)S(1)} collective-permute-done((bf16[352,256]{1,0:T(8,128)(2,1)S(1)}, bf16[352,256]{1,0:T(8,128)(2,1)S(1)}, u32[]{:S(2)}, u32[]{:S(2)}) %collective-permute-start.7) | collective-permute-done | bytes 180256 | tf_op jit(solution)/shard_map/projection/ppermute | solution.py:49
  20.7 0.2 early.1.base_ref
  20.9 3.2 %collective-permute-done.8.refs_0_ = bf16[96,1024]{1,0:T(8,128)(2,1)S(1)} collective-permute-done((bf16[96,1024]{1,0:T(8,128)(2,1)S(1)}, bf16[96,1024]{1,0:T(8,128)(2,1)S(1)}, u32[]{:S(2)}, u32[]{:S(2)}) %collective-permute-start.8) | collective-permute-done | bytes 196640 | tf_op jit(solution)/shard_map/projection/ppermute | solution.py:49
  24.0 0.7 %final.1 = bf16[96,1280]{1,0:T(8,128)(2,1)} custom-call(f32[96,1280]{1,0:T(8,128)S(1)} %early.1.base_ref, f32[1,1280]{1,0:T(1,128)S(1)} %reshape.3.gate_ref, bf16[96,1024]{1,0:T(8,128)(2,1)S(1)} %collective-permute-done.8.refs_0_), custom_call_target="tpu_custom_call" | custom-call | bytes 983040 | tf_op jit(solution)/shard_map/projection/final/pallas_call | solution.py:367
  (3 shorter events, 0.0 us)
Async XLA Ops:
  0.0 1.5 %copy-start.2 = (f32[96,256]{1,0:T(8,128)S(1)}, f32[96,256]{1,0:T(8,128)}, u32[]{:S(2)}) copy-start(f32[96,256]{1,0:T(8,128)} %param.12) | copy-start | bytes 294916
  0.0 1.5 %copy-start.3 = (f32[96,256]{1,0:T(8,128)S(1)}, f32[96,256]{1,0:T(8,128)}, u32[]{:S(2)}) copy-start(f32[96,256]{1,0:T(8,128)} %param.11) | copy-start | bytes 294916
  0.0 16.7 %collective-permute-start.4 = (bf16[256,5120]{1,0:T(8,128)(2,1)}, bf16[256,5120]{1,0:T(8,128)(2,1)S(1)}, u32[]{:S(2)}, u32[]{:S(2)}) collective-permute-start(bf16[256,5120]{1,0:T(8,128)(2,1)} %refs_1_.3), channel_id=1, source_target_pairs={{0,1},{1,0},{2,3},{3,2},{4,5},{5,4},{6,7},{7,6},{8,9},{9,8},{10,11... | collective-permute-start | bytes 7864328 | tf_op jit(solution)/shard_map/weight_swap/ppermute | solution.py:49
  1.5 9.4 %collective-permute-start.2 = (bf16[96,512]{1,0:T(8,128)(2,1)S(1)}, bf16[96,512]{1,0:T(8,128)(2,1)S(1)}, u32[]{:S(2)}, u32[]{:S(2)}) collective-permute-start(bf16[96,512]{1,0:T(8,128)(2,1)S(1)} %maximum_convert_fusion.refs_0_), channel_id=1, source_target_pairs={{0,4},{1,5},{4,8},{5,13},{8,12},{9,1},{12,0},{13,9},{2,6},{3,7},{6... | collective-permute-start | bytes 294920 | tf_op jit(solution)/shard_map/residual_gather/ppermute | solution.py:76
  4.2 10.2 %collective-permute-start.1 = (bf16[96,512]{1,0:T(8,128)(2,1)S(1)}, bf16[96,512]{1,0:T(8,128)(2,1)S(1)}, u32[]{:S(2)}, u32[]{:S(2)}) collective-permute-start(bf16[96,512]{1,0:T(8,128)(2,1)S(1)} %maximum_convert_fusion.refs_0_), channel_id=1, source_target_pairs={{0,8},{1,13},{4,12},{5,9},{8,0},{9,5},{12,4},{13,1},{2,10},{3,15},... | collective-permute-start | bytes 294920 | tf_op jit(solution)/shard_map/residual_gather/ppermute | solution.py:76
  6.8 7.6 %collective-permute-start = (bf16[96,512]{1,0:T(8,128)(2,1)S(1)}, bf16[96,512]{1,0:T(8,128)(2,1)S(1)}, u32[]{:S(2)}, u32[]{:S(2)}) collective-permute-start(bf16[96,512]{1,0:T(8,128)(2,1)S(1)} %maximum_convert_fusion.refs_0_), channel_id=1, source_target_pairs={{0,12},{1,9},{4,0},{5,1},{8,4},{9,13},{12,8},{13,5},{2,14},{3,11},... | collective-permute-start | bytes 294920 | tf_op jit(solution)/shard_map/residual_gather/ppermute | solution.py:76
  8.1 11.0 %collective-permute-start.6 = (bf16[256,512]{1,0:T(8,128)(2,1)S(1)}, bf16[256,512]{1,0:T(8,128)(2,1)S(1)}, u32[]{:S(2)}, u32[]{:S(2)}) collective-permute-start(bf16[256,512]{1,0:T(8,128)(2,1)S(1)} %early_weight.1), channel_id=1, source_target_pairs={{0,2},{2,0},{1,3},{3,1},{4,6},{6,4},{5,7},{7,5},{8,10},{10,8},{9,1... | collective-permute-start | bytes 786440 | tf_op jit(solution)/shard_map/early_weight/ppermute | solution.py:49
  14.4 2.3 %copy-start = (bf16[256,5120]{1,0:T(8,128)(2,1)S(1)}, bf16[256,5120]{1,0:T(8,128)(2,1)}, u32[]{:S(2)}) copy-start(bf16[256,5120]{1,0:T(8,128)(2,1)} %refs_1_.3) | copy-start | bytes 7864324
  14.9 4.4 %copy-start.4 = (f32[1280]{0:T(1024)S(1)}, f32[1280]{0:T(1024)}, u32[]{:S(2)}) copy-start(f32[1280]{0:T(1024)} %param.15) | copy-start | bytes 15364
  14.9 4.4 %copy-start.1 = (bf16[96,1280]{1,0:T(8,128)(2,1)S(1)}, bf16[96,1280]{1,0:T(8,128)(2,1)}, u32[]{:S(2)}) copy-start(bf16[96,1280]{1,0:T(8,128)(2,1)} %hidden_ref.1) | copy-start | bytes 737284
  14.9 1.7 %collective-permute-start.3 = (bf16[96,256]{1,0:T(8,128)(2,1)S(1)}, bf16[96,256]{1,0:T(8,128)(2,1)S(1)}, u32[]{:S(2)}, u32[]{:S(2)}) collective-permute-start(bf16[96,256]{1,0:T(8,128)(2,1)S(1)} %attention.1.refs_0_), channel_id=1, source_target_pairs={{0,1},{1,0},{2,3},{3,2},{4,5},{5,4},{6,7},{7,6},{8,9},{9,8},{10,11... | collective-permute-start | bytes 147464 | tf_op jit(solution)/shard_map/attended_swap/ppermute | solution.py:49
  15.0 4.2 %collective-permute-start.5 = (bf16[96,256]{1,0:T(8,128)(2,1)S(1)}, bf16[96,256]{1,0:T(8,128)(2,1)S(1)}, u32[]{:S(2)}, u32[]{:S(2)}) collective-permute-start(bf16[96,256]{1,0:T(8,128)(2,1)S(1)} %attention.1.refs_0_), channel_id=1, source_target_pairs={{0,2},{2,0},{1,3},{3,1},{4,6},{6,4},{5,7},{7,5},{8,10},{10,8},{9,1... | collective-permute-start | bytes 147464 | tf_op jit(solution)/shard_map/attended_swap/ppermute | solution.py:49
  17.0 7.0 %collective-permute-start.8 = (bf16[96,1024]{1,0:T(8,128)(2,1)S(1)}, bf16[96,1024]{1,0:T(8,128)(2,1)S(1)}, u32[]{:S(2)}, u32[]{:S(2)}) collective-permute-start(bf16[96,1024]{1,0:T(8,128)(2,1)S(1)} %sent_term.1), channel_id=1, source_target_pairs={{0,2},{2,0},{1,3},{3,1},{4,6},{6,4},{5,7},{7,5},{8,10},{10,8},{9,1... | collective-permute-start | bytes 589832 | tf_op jit(solution)/shard_map/projection/ppermute | solution.py:49
  19.2 1.5 %collective-permute-start.7 = (bf16[352,256]{1,0:T(8,128)(2,1)S(1)}, bf16[352,256]{1,0:T(8,128)(2,1)S(1)}, u32[]{:S(2)}, u32[]{:S(2)}) collective-permute-start(bf16[352,256]{1,0:T(8,128)(2,1)S(1)} %pack.1), channel_id=1, source_target_pairs={{0,1},{1,0},{2,3},{3,2},{4,5},{5,4},{6,7},{7,6},{8,9},{9,8},{10,11... | collective-permute-start | bytes 540680 | tf_op jit(solution)/shard_map/projection/ppermute | solution.py:49

commit v23 on v21

--- a/solution.py
+++ b/solution.py
@@ -143,23 +143,29 @@
     block_refs, out_ref = refs[:-1], refs[-1]
     rows, width = q_ref.shape
     blocks = jnp.concatenate([ref[...] for ref in block_refs], axis=0)
-    for head in range(width // HD):
-        cols = slice(head * HD, (head + 1) * HD)
-        value_cols = slice(width + head * HD, width + (head + 1) * HD)
-        products = products_ref[head] + dot_transposed(q_ref[:, cols], blocks[:, cols])
-        scores = products * scale
-        weights = jnp.exp(scores - jnp.max(scores, axis=1, keepdims=True))
-        totals = jnp.sum(weights, axis=1, keepdims=True)
-        high = weights.astype(jnp.bfloat16)
-        low = (weights - high.astype(jnp.float32)).astype(jnp.bfloat16)
-        sums = jnp.dot(
-            jnp.concatenate([high, low], axis=0),
-            jnp.concatenate([values_ref[:, cols], blocks[:, value_cols]], axis=1),
+    heads = [slice(at, at + HD) for at in range(0, width, HD)]
+    products = [
+        products_ref[n] + dot_transposed(q_ref[:, cols], blocks[:, cols])
+        for n, cols in enumerate(heads)
+    ]
+    highest = [jnp.max(p, axis=1, keepdims=True) for p in products]
+    weights = [jnp.exp((p - h) * scale) for p, h in zip(products, highest)]
+    totals = [jnp.sum(w, axis=1, keepdims=True) for w in weights]
+    high = [w.astype(jnp.bfloat16) for w in weights]
+    low = [(w - h.astype(jnp.float32)).astype(jnp.bfloat16) for w, h in zip(weights, high)]
+    sums = [
+        jnp.dot(
+            jnp.concatenate([high[n], low[n]], axis=0),
+            jnp.concatenate(
+                [values_ref[:, cols], blocks[:, width + cols.start : width + cols.stop]], axis=1
+            ),
             preferred_element_type=jnp.float32,
         )
-        sums = sums[:rows] + sums[rows:]
-        sums = sums[:, :HD] + sums[:, HD:]
-        out_ref[:, cols] = (sums / totals).astype(jnp.bfloat16)
+        for n, cols in enumerate(heads)
+    ]
+    for cols, total, both in zip(heads, totals, sums):
+        both = both[:rows] + both[rows:]
+        out_ref[:, cols] = ((both[:, :HD] + both[:, HD:]) / total).astype(jnp.bfloat16)
 
 
 def block_dot(a_ref, weight_ref, start, columns):

time: 24 us -> 24 us (level)
  transfers between devices with their start and end apart: 9 -> 9, of which waited for: 5 -> 5; matrix products, arithmetic and copies ran while one was open for 0% -> 0% of each run, Pallas kernels for 16% -> 15%
where the time goes in v23:
time: 24 us; the launch traced here: 23.8 us
  starting transfers between devices  11.9 us (50%)
  waiting for transfers between devices  7.3 us (30%)
  Pallas kernels  4.43 us (18%)
    ppermute x3, starting transfers between devices, gather(): blocks.append(lax.ppermute(own, ('patch', 'sub'), pairs))  6.74 us
    ppermute x6, starting transfers between devices, shift(): lax.ppermute(array, axis, [(i, (i + step) % size) for i in range(size)])  5.13 us
    ppermute x6, waiting for transfers between devices, shift(): lax.ppermute(array, axis, [(i, (i + step) % size) for i in range(size)])  5.13 us
    ppermute x3, waiting for transfers between devices, gather(): blocks.append(lax.ppermute(own, ('patch', 'sub'), pairs))  2.17 us
    pallas_call x1, Pallas kernels, per_device(): call(functools.partial(stage_kernel, patches, subs), [jax.ShapeDtypeStruc...  1.28 us
    pallas_call x1, Pallas kernels, per_device(): call(functools.partial(early_weight_kernel, subs, columns, early), jax.Sh...  0.99 us
    pallas_call x1, Pallas kernels, per_device(): call(functools.partial(final_kernel, early, row_blocks), jax.ShapeDtypeSt...  0.74 us
    pallas_call x1, Pallas kernels, per_device(): call(functools.partial(attention_kernel, 1.0 / math.sqrt(HD)), jax.ShapeD...  0.53 us
  transfers between devices with their start and end apart: 9, of which 5 were waited for; matrix products, arithmetic and copies ran while one was open for 0% of the time, Pallas kernels for 15%

profile of v23, /device:TPU:0, one launch (start us, length us, event | category | flops | bytes accessed | tf_op | source)
XLA Modules:
  0.0 23.8 jit_solution(17282208652667154102)
XLA Ops:
  0.0 0.0 copy-start.2
  0.0 0.0 copy-start.3
  0.0 0.5 %collective-permute-start.4 = (bf16[256,5120]{1,0:T(8,128)(2,1)}, bf16[256,5120]{1,0:T(8,128)(2,1)S(1)}, u32[]{:S(2)}, u32[]{:S(2)}) collective-permute-start(bf16[256,5120]{1,0:T(8,128)(2,1)} %refs_1_.3), channel_id=1, source_target_pairs={{0,1},{1,0},{2,3},{3,2},{4,5},{5,4},{6,7},{7,6},{8,9},{9,8},{10,11... | collective-permute-start | bytes 7864328 | tf_op jit(solution)/shard_map/weight_swap/ppermute | solution.py:49
  0.5 1.0 %early_weight.1 = bf16[256,512]{1,0:T(8,128)(2,1)S(1)} custom-call(bf16[256,5120]{1,0:T(8,128)(2,1)} %refs_1_.3), custom_call_target="tpu_custom_call" | custom-call | bytes 524288 | tf_op jit(solution)/shard_map/early_weight/early_weight/pallas_call | solution.py:250
  1.5 0.0 copy-done.2
  1.5 0.0 copy-done.3
  1.5 2.7 %collective-permute-start.2 = (bf16[96,512]{1,0:T(8,128)(2,1)S(1)}, bf16[96,512]{1,0:T(8,128)(2,1)S(1)}, u32[]{:S(2)}, u32[]{:S(2)}) collective-permute-start(bf16[96,512]{1,0:T(8,128)(2,1)S(1)} %maximum_convert_fusion.refs_0_), channel_id=1, source_target_pairs={{0,4},{1,5},{4,12},{5,9},{8,0},{9,13},{12,8},{13,1},{2,6},{3,7},{6... | collective-permute-start | bytes 294920 | tf_op jit(solution)/shard_map/residual_gather/ppermute | solution.py:76
  4.2 2.5 %collective-permute-start.1 = (bf16[96,512]{1,0:T(8,128)(2,1)S(1)}, bf16[96,512]{1,0:T(8,128)(2,1)S(1)}, u32[]{:S(2)}, u32[]{:S(2)}) collective-permute-start(bf16[96,512]{1,0:T(8,128)(2,1)S(1)} %maximum_convert_fusion.refs_0_), channel_id=1, source_target_pairs={{0,12},{1,9},{4,8},{5,13},{8,4},{9,1},{12,0},{13,5},{2,14},{3,11},... | collective-permute-start | bytes 294920 | tf_op jit(solution)/shard_map/residual_gather/ppermute | solution.py:76
  6.7 1.6 %collective-permute-start = (bf16[96,512]{1,0:T(8,128)(2,1)S(1)}, bf16[96,512]{1,0:T(8,128)(2,1)S(1)}, u32[]{:S(2)}, u32[]{:S(2)}) collective-permute-start(bf16[96,512]{1,0:T(8,128)(2,1)S(1)} %maximum_convert_fusion.refs_0_), channel_id=1, source_target_pairs={{0,8},{1,13},{4,0},{5,1},{8,12},{9,5},{12,4},{13,9},{2,10},{3,15},... | collective-permute-start | bytes 294920 | tf_op jit(solution)/shard_map/residual_gather/ppermute | solution.py:76
  8.2 1.5 %collective-permute-start.6 = (bf16[256,512]{1,0:T(8,128)(2,1)S(1)}, bf16[256,512]{1,0:T(8,128)(2,1)S(1)}, u32[]{:S(2)}, u32[]{:S(2)}) collective-permute-start(bf16[256,512]{1,0:T(8,128)(2,1)S(1)} %early_weight.1), channel_id=1, source_target_pairs={{0,2},{2,0},{1,3},{3,1},{4,6},{6,4},{5,7},{7,5},{8,10},{10,8},{9,1... | collective-permute-start | bytes 786440 | tf_op jit(solution)/shard_map/early_weight/ppermute | solution.py:49
  9.7 1.3 %stage.1 = (bf16[96,256]{1,0:T(8,128)(2,1)S(1)}, f32[2,96,384]{2,1,0:T(8,128)S(1)}, bf16[384,256]{1,0:T(8,128)(2,1)S(1)}) custom-call(bf16[96,256]{1,0:T(8,128)(2,1)} %q_hbm.1, bf16[384,256]{1,0:T(8,128)(2,1)} %held_k_hbm.1, bf16[384,256]{1,0:T(8,128)(2,1)} %held_v_hbm.1), custom_call_target="tpu_custom_call" | custom-call | flops 2000000000 | tf_op jit(solution)/shard_map/attention/stage/pallas_call | solution.py:297
  11.0 0.0 collective-permute-done.2.refs_3_
  11.0 1.3 %collective-permute-done.1.refs_2_ = bf16[96,512]{1,0:T(8,128)(2,1)S(1)} collective-permute-done((bf16[96,512]{1,0:T(8,128)(2,1)S(1)}, bf16[96,512]{1,0:T(8,128)(2,1)S(1)}, u32[]{:S(2)}, u32[]{:S(2)}) %collective-permute-start.1) | collective-permute-done | bytes 98336 | tf_op jit(solution)/shard_map/residual_gather/ppermute | solution.py:76
  12.4 0.8 %collective-permute-done.refs_1_ = bf16[96,512]{1,0:T(8,128)(2,1)S(1)} collective-permute-done((bf16[96,512]{1,0:T(8,128)(2,1)S(1)}, bf16[96,512]{1,0:T(8,128)(2,1)S(1)}, u32[]{:S(2)}, u32[]{:S(2)}) %collective-permute-start) | collective-permute-done | bytes 98336 | tf_op jit(solution)/shard_map/residual_gather/ppermute | solution.py:76
  13.2 0.0 copy-start
  13.2 0.5 %attention.1.refs_0_ = bf16[96,256]{1,0:T(8,128)(2,1)S(1)} custom-call(bf16[96,256]{1,0:T(8,128)(2,1)S(1)} %get-tuple-element.11.q_ref, f32[2,96,384]{2,1,0:T(8,128)S(1)} %get-tuple-element.12.products_ref, bf16[384,256]{1,0:T(8,128)(2,1)S(1)} %get-tuple-element.13.values_ref, bf16[96,512]{1,0:T(8,128)(2,1)S(1)} %maximum_convert_fusion.refs_0_, ...), custom_call_target="tpu_custom_call" | custom-call | flops 2000000000 | tf_op jit(solution)/shard_map/attention/attention/pallas_call | solution.py:313
  13.7 0.0 copy-start.4
  13.7 0.0 copy-start.1
  13.8 0.1 collective-permute-start.3
  13.8 2.0 %collective-permute-start.5 = (bf16[96,256]{1,0:T(8,128)(2,1)S(1)}, bf16[96,256]{1,0:T(8,128)(2,1)S(1)}, u32[]{:S(2)}, u32[]{:S(2)}) collective-permute-start(bf16[96,256]{1,0:T(8,128)(2,1)S(1)} %attention.1.refs_0_), channel_id=1, source_target_pairs={{0,2},{2,0},{1,3},{3,1},{4,6},{6,4},{5,7},{7,5},{8,10},{10,8},{9,1... | collective-permute-start | bytes 147464 | tf_op jit(solution)/shard_map/attended_swap/ppermute | solution.py:49
  15.8 0.0 collective-permute-done.3.refs_2_
  15.8 0.0 collective-permute-done.4.refs_3_
  15.8 0.0 copy-done
  15.8 0.3 %sent_term.1 = bf16[96,1024]{1,0:T(8,128)(2,1)S(1)} custom-call(bf16[96,256]{1,0:T(8,128)(2,1)S(1)} %attention.1.refs_0_, bf16[256,5120]{1,0:T(8,128)(2,1)S(1)} %copy-done, bf16[96,256]{1,0:T(8,128)(2,1)S(1)} %collective-permute-done.3.refs_2_, bf16[256,5120]{1,0:T(8,128)(2,1)S(1)} %collective-permute-done.4.refs_3_), custom_call_target="tpu_custom_call" | custom-call | flops 125829120 | tf_op jit(solution)/shard_map/projection/sent_term/pallas_call | solution.py:336
  16.2 1.0 %collective-permute-start.8 = (bf16[96,1024]{1,0:T(8,128)(2,1)S(1)}, bf16[96,1024]{1,0:T(8,128)(2,1)S(1)}, u32[]{:S(2)}, u32[]{:S(2)}) collective-permute-start(bf16[96,1024]{1,0:T(8,128)(2,1)S(1)} %sent_term.1), channel_id=1, source_target_pairs={{0,2},{2,0},{1,3},{3,1},{4,6},{6,4},{5,7},{7,5},{8,10},{10,8},{9,1... | collective-permute-start | bytes 589832 | tf_op jit(solution)/shard_map/projection/ppermute | solution.py:49
  17.2 0.8 %collective-permute-done.5.attended_ref = bf16[96,256]{1,0:T(8,128)(2,1)S(1)} collective-permute-done((bf16[96,256]{1,0:T(8,128)(2,1)S(1)}, bf16[96,256]{1,0:T(8,128)(2,1)S(1)}, u32[]{:S(2)}, u32[]{:S(2)}) %collective-permute-start.5) | collective-permute-done | bytes 49184 | tf_op jit(solution)/shard_map/attended_swap/ppermute | solution.py:49
  18.0 0.0 collective-permute-done.6.weight_ref
  18.0 0.1 collective-permute-start.7
  18.1 0.0 copy-done.4
  18.1 0.0 copy-done.1
  18.2 0.4 %base.1.base_ref = f32[96,1280]{1,0:T(8,128)S(1)} custom-call(bf16[96,1280]{1,0:T(8,128)(2,1)S(1)} %copy-done.1, f32[1,1280]{1,0:T(1,128)S(1)} %reshape.3.gate_ref, bf16[96,256]{1,0:T(8,128)(2,1)S(1)} %attention.1.refs_0_, bf16[256,5120]{1,0:T(8,128)(2,1)S(1)} %copy-done, bf16[96,256]{1,0:T(8,128)(2,1)S(1)} %collective-permute-done.3.refs_2_, ...), custom_call_target="tpu_custom_call" | custom-call | flops 125829120 | tf_op jit(solution)/shard_map/projection/base/pallas_call | solution.py:347
  18.5 1.0 %collective-permute-done.7.packed_ref = bf16[352,256]{1,0:T(8,128)(2,1)S(1)} collective-permute-done((bf16[352,256]{1,0:T(8,128)(2,1)S(1)}, bf16[352,256]{1,0:T(8,128)(2,1)S(1)}, u32[]{:S(2)}, u32[]{:S(2)}) %collective-permute-start.7) | collective-permute-done | bytes 180256 | tf_op jit(solution)/shard_map/projection/ppermute | solution.py:49
  19.5 0.2 early.1.base_ref
  19.7 3.3 %collective-permute-done.8.refs_0_ = bf16[96,1024]{1,0:T(8,128)(2,1)S(1)} collective-permute-done((bf16[96,1024]{1,0:T(8,128)(2,1)S(1)}, bf16[96,1024]{1,0:T(8,128)(2,1)S(1)}, u32[]{:S(2)}, u32[]{:S(2)}) %collective-permute-start.8) | collective-permute-done | bytes 196640 | tf_op jit(solution)/shard_map/projection/ppermute | solution.py:49
  23.1 0.7 %final.1 = bf16[96,1280]{1,0:T(8,128)(2,1)} custom-call(f32[96,1280]{1,0:T(8,128)S(1)} %early.1.base_ref, f32[1,1280]{1,0:T(1,128)S(1)} %reshape.3.gate_ref, bf16[96,1024]{1,0:T(8,128)(2,1)S(1)} %collective-permute-done.8.refs_0_), custom_call_target="tpu_custom_call" | custom-call | bytes 983040 | tf_op jit(solution)/shard_map/projection/final/pallas_call | solution.py:373
  (3 shorter events, 0.0 us)
Async XLA Ops:
  0.0 1.5 %copy-start.2 = (f32[96,256]{1,0:T(8,128)S(1)}, f32[96,256]{1,0:T(8,128)}, u32[]{:S(2)}) copy-start(f32[96,256]{1,0:T(8,128)} %param.12) | copy-start | bytes 294916
  0.0 1.5 %copy-start.3 = (f32[96,256]{1,0:T(8,128)S(1)}, f32[96,256]{1,0:T(8,128)}, u32[]{:S(2)}) copy-start(f32[96,256]{1,0:T(8,128)} %param.11) | copy-start | bytes 294916
  0.0 15.8 %collective-permute-start.4 = (bf16[256,5120]{1,0:T(8,128)(2,1)}, bf16[256,5120]{1,0:T(8,128)(2,1)S(1)}, u32[]{:S(2)}, u32[]{:S(2)}) collective-permute-start(bf16[256,5120]{1,0:T(8,128)(2,1)} %refs_1_.3), channel_id=1, source_target_pairs={{0,1},{1,0},{2,3},{3,2},{4,5},{5,4},{6,7},{7,6},{8,9},{9,8},{10,11... | collective-permute-start | bytes 7864328 | tf_op jit(solution)/shard_map/weight_swap/ppermute | solution.py:49
  1.5 9.5 %collective-permute-start.2 = (bf16[96,512]{1,0:T(8,128)(2,1)S(1)}, bf16[96,512]{1,0:T(8,128)(2,1)S(1)}, u32[]{:S(2)}, u32[]{:S(2)}) collective-permute-start(bf16[96,512]{1,0:T(8,128)(2,1)S(1)} %maximum_convert_fusion.refs_0_), channel_id=1, source_target_pairs={{0,4},{1,5},{4,12},{5,9},{8,0},{9,13},{12,8},{13,1},{2,6},{3,7},{6... | collective-permute-start | bytes 294920 | tf_op jit(solution)/shard_map/residual_gather/ppermute | solution.py:76
  4.2 8.2 %collective-permute-start.1 = (bf16[96,512]{1,0:T(8,128)(2,1)S(1)}, bf16[96,512]{1,0:T(8,128)(2,1)S(1)}, u32[]{:S(2)}, u32[]{:S(2)}) collective-permute-start(bf16[96,512]{1,0:T(8,128)(2,1)S(1)} %maximum_convert_fusion.refs_0_), channel_id=1, source_target_pairs={{0,12},{1,9},{4,8},{5,13},{8,4},{9,1},{12,0},{13,5},{2,14},{3,11},... | collective-permute-start | bytes 294920 | tf_op jit(solution)/shard_map/residual_gather/ppermute | solution.py:76
  6.7 6.5 %collective-permute-start = (bf16[96,512]{1,0:T(8,128)(2,1)S(1)}, bf16[96,512]{1,0:T(8,128)(2,1)S(1)}, u32[]{:S(2)}, u32[]{:S(2)}) collective-permute-start(bf16[96,512]{1,0:T(8,128)(2,1)S(1)} %maximum_convert_fusion.refs_0_), channel_id=1, source_target_pairs={{0,8},{1,13},{4,0},{5,1},{8,12},{9,5},{12,4},{13,9},{2,10},{3,15},... | collective-permute-start | bytes 294920 | tf_op jit(solution)/shard_map/residual_gather/ppermute | solution.py:76
  8.2 9.8 %collective-permute-start.6 = (bf16[256,512]{1,0:T(8,128)(2,1)S(1)}, bf16[256,512]{1,0:T(8,128)(2,1)S(1)}, u32[]{:S(2)}, u32[]{:S(2)}) collective-permute-start(bf16[256,512]{1,0:T(8,128)(2,1)S(1)} %early_weight.1), channel_id=1, source_target_pairs={{0,2},{2,0},{1,3},{3,1},{4,6},{6,4},{5,7},{7,5},{8,10},{10,8},{9,1... | collective-permute-start | bytes 786440 | tf_op jit(solution)/shard_map/early_weight/ppermute | solution.py:49
  13.2 2.6 %copy-start = (bf16[256,5120]{1,0:T(8,128)(2,1)S(1)}, bf16[256,5120]{1,0:T(8,128)(2,1)}, u32[]{:S(2)}) copy-start(bf16[256,5120]{1,0:T(8,128)(2,1)} %refs_1_.3) | copy-start | bytes 7864324
  13.7 4.4 %copy-start.4 = (f32[1280]{0:T(1024)S(1)}, f32[1280]{0:T(1024)}, u32[]{:S(2)}) copy-start(f32[1280]{0:T(1024)} %param.15) | copy-start | bytes 15364
  13.7 4.4 %copy-start.1 = (bf16[96,1280]{1,0:T(8,128)(2,1)S(1)}, bf16[96,1280]{1,0:T(8,128)(2,1)}, u32[]{:S(2)}) copy-start(bf16[96,1280]{1,0:T(8,128)(2,1)} %hidden_ref.1) | copy-start | bytes 737284
  13.8 2.1 %collective-permute-start.3 = (bf16[96,256]{1,0:T(8,128)(2,1)S(1)}, bf16[96,256]{1,0:T(8,128)(2,1)S(1)}, u32[]{:S(2)}, u32[]{:S(2)}) collective-permute-start(bf16[96,256]{1,0:T(8,128)(2,1)S(1)} %attention.1.refs_0_), channel_id=1, source_target_pairs={{0,1},{1,0},{2,3},{3,2},{4,5},{5,4},{6,7},{7,6},{8,9},{9,8},{10,11... | collective-permute-start | bytes 147464 | tf_op jit(solution)/shard_map/attended_swap/ppermute | solution.py:49
  13.8 4.2 %collective-permute-start.5 = (bf16[96,256]{1,0:T(8,128)(2,1)S(1)}, bf16[96,256]{1,0:T(8,128)(2,1)S(1)}, u32[]{:S(2)}, u32[]{:S(2)}) collective-permute-start(bf16[96,256]{1,0:T(8,128)(2,1)S(1)} %attention.1.refs_0_), channel_id=1, source_target_pairs={{0,2},{2,0},{1,3},{3,1},{4,6},{6,4},{5,7},{7,5},{8,10},{10,8},{9,1... | collective-permute-start | bytes 147464 | tf_op jit(solution)/shard_map/attended_swap/ppermute | solution.py:49
  16.2 6.9 %collective-permute-start.8 = (bf16[96,1024]{1,0:T(8,128)(2,1)S(1)}, bf16[96,1024]{1,0:T(8,128)(2,1)S(1)}, u32[]{:S(2)}, u32[]{:S(2)}) collective-permute-start(bf16[96,1024]{1,0:T(8,128)(2,1)S(1)} %sent_term.1), channel_id=1, source_target_pairs={{0,2},{2,0},{1,3},{3,1},{4,6},{6,4},{5,7},{7,5},{8,10},{10,8},{9,1... | collective-permute-start | bytes 589832 | tf_op jit(solution)/shard_map/projection/ppermute | solution.py:49
  18.0 1.5 %collective-permute-start.7 = (bf16[352,256]{1,0:T(8,128)(2,1)S(1)}, bf16[352,256]{1,0:T(8,128)(2,1)S(1)}, u32[]{:S(2)}, u32[]{:S(2)}) collective-permute-start(bf16[352,256]{1,0:T(8,128)(2,1)S(1)} %pack.1), channel_id=1, source_target_pairs={{0,1},{1,0},{2,3},{3,2},{4,5},{5,4},{6,7},{7,6},{8,9},{9,8},{10,11... | collective-permute-start | bytes 540680 | tf_op jit(solution)/shard_map/projection/ppermute | solution.py:49

commit v24 on v23

--- a/solution.py
+++ b/solution.py
@@ -50,9 +50,9 @@
 
 
 LINE_OF_FOUR = (
-    ((2, 0, 3, 1), (3, 0, 1, 2)),
-    ((3, 2, 1, 0), (2, 3, 0, 1)),
-    ((1, 3, 0, 2), (1, 2, 3, 0)),
+    ((2, 0, 3, 1), (1, 2, 3, 0)),
+    ((3, 2, 1, 0), (3, 0, 1, 2)),
+    ((1, 3, 0, 2), (2, 3, 0, 1)),
 )
 
 

time: 24 us -> 24.1 us (level)
  starting transfers between devices: 11.9 us -> 11.6 us
    ppermute x6, starting transfers between devices: 5.13 us -> 4.84 us  [shift(): lax.ppermute(array, axis, [(i, (i + step) % size) for i in range(size)])]
  transfers between devices with their start and end apart: 9 -> 9, of which waited for: 5 -> 5; matrix products, arithmetic and copies ran while one was open for 0% -> 0% of each run, Pallas kernels for 15% -> 16%
where the time goes in v24:
time: 24.1 us; the launch traced here: 23.7 us
  starting transfers between devices  11.6 us (48%)
  waiting for transfers between devices  7.49 us (31%)
  Pallas kernels  4.42 us (18%)
    ppermute x3, starting transfers between devices, gather(): blocks.append(lax.ppermute(own, ('patch', 'sub'), pairs))  6.74 us
    ppermute x6, waiting for transfers between devices, shift(): lax.ppermute(array, axis, [(i, (i + step) % size) for i in range(size)])  5.15 us
    ppermute x6, starting transfers between devices, shift(): lax.ppermute(array, axis, [(i, (i + step) % size) for i in range(size)])  4.84 us
    ppermute x3, waiting for transfers between devices, gather(): blocks.append(lax.ppermute(own, ('patch', 'sub'), pairs))  2.34 us
    pallas_call x1, Pallas kernels, per_device(): call(functools.partial(stage_kernel, patches, subs), [jax.ShapeDtypeStruc...  1.28 us
    pallas_call x1, Pallas kernels, per_device(): call(functools.partial(early_weight_kernel, subs, columns, early), jax.Sh...  0.99 us
    pallas_call x1, Pallas kernels, per_device(): call(functools.partial(final_kernel, early, row_blocks), jax.ShapeDtypeSt...  0.74 us
    pallas_call x1, Pallas kernels, per_device(): call(functools.partial(attention_kernel, 1.0 / math.sqrt(HD)), jax.ShapeD...  0.53 us
  transfers between devices with their start and end apart: 9, of which 5 were waited for; matrix products, arithmetic and copies ran while one was open for 0% of the time, Pallas kernels for 16%

profile of v24, /device:TPU:0, one launch (start us, length us, event | category | flops | bytes accessed | tf_op | source)
XLA Modules:
  0.0 23.7 jit_solution(2720046865941930421)
XLA Ops:
  0.0 0.0 copy-start.2
  0.0 0.0 copy-start.3
  0.0 0.5 %collective-permute-start.4 = (bf16[256,5120]{1,0:T(8,128)(2,1)}, bf16[256,5120]{1,0:T(8,128)(2,1)S(1)}, u32[]{:S(2)}, u32[]{:S(2)}) collective-permute-start(bf16[256,5120]{1,0:T(8,128)(2,1)} %refs_1_.3), channel_id=1, source_target_pairs={{0,1},{1,0},{2,3},{3,2},{4,5},{5,4},{6,7},{7,6},{8,9},{9,8},{10,11... | collective-permute-start | bytes 7864328 | tf_op jit(solution)/shard_map/weight_swap/ppermute | solution.py:49
  0.5 1.0 %early_weight.1 = bf16[256,512]{1,0:T(8,128)(2,1)S(1)} custom-call(bf16[256,5120]{1,0:T(8,128)(2,1)} %refs_1_.3), custom_call_target="tpu_custom_call" | custom-call | bytes 524288 | tf_op jit(solution)/shard_map/early_weight/early_weight/pallas_call | solution.py:250
  1.5 0.0 copy-done.2
  1.5 0.0 copy-done.3
  1.5 2.7 %collective-permute-start.2 = (bf16[96,512]{1,0:T(8,128)(2,1)S(1)}, bf16[96,512]{1,0:T(8,128)(2,1)S(1)}, u32[]{:S(2)}, u32[]{:S(2)}) collective-permute-start(bf16[96,512]{1,0:T(8,128)(2,1)S(1)} %maximum_convert_fusion.refs_0_), channel_id=1, source_target_pairs={{0,4},{1,9},{4,12},{5,13},{8,0},{9,1},{12,8},{13,5},{2,6},{3,11},{... | collective-permute-start | bytes 294920 | tf_op jit(solution)/shard_map/residual_gather/ppermute | solution.py:76
  4.2 2.5 %collective-permute-start.1 = (bf16[96,512]{1,0:T(8,128)(2,1)S(1)}, bf16[96,512]{1,0:T(8,128)(2,1)S(1)}, u32[]{:S(2)}, u32[]{:S(2)}) collective-permute-start(bf16[96,512]{1,0:T(8,128)(2,1)S(1)} %maximum_convert_fusion.refs_0_), channel_id=1, source_target_pairs={{0,12},{1,13},{4,8},{5,1},{8,4},{9,5},{12,0},{13,9},{2,14},{3,15},... | collective-permute-start | bytes 294920 | tf_op jit(solution)/shard_map/residual_gather/ppermute | solution.py:76
  6.7 1.6 %collective-permute-start = (bf16[96,512]{1,0:T(8,128)(2,1)S(1)}, bf16[96,512]{1,0:T(8,128)(2,1)S(1)}, u32[]{:S(2)}, u32[]{:S(2)}) collective-permute-start(bf16[96,512]{1,0:T(8,128)(2,1)S(1)} %maximum_convert_fusion.refs_0_), channel_id=1, source_target_pairs={{0,8},{1,5},{4,0},{5,9},{8,12},{9,13},{12,4},{13,1},{2,10},{3,7},{... | collective-permute-start | bytes 294920 | tf_op jit(solution)/shard_map/residual_gather/ppermute | solution.py:76
  8.2 1.5 %collective-permute-start.6 = (bf16[256,512]{1,0:T(8,128)(2,1)S(1)}, bf16[256,512]{1,0:T(8,128)(2,1)S(1)}, u32[]{:S(2)}, u32[]{:S(2)}) collective-permute-start(bf16[256,512]{1,0:T(8,128)(2,1)S(1)} %early_weight.1), channel_id=1, source_target_pairs={{0,2},{2,0},{1,3},{3,1},{4,6},{6,4},{5,7},{7,5},{8,10},{10,8},{9,1... | collective-permute-start | bytes 786440 | tf_op jit(solution)/shard_map/early_weight/ppermute | solution.py:49
  9.7 1.3 %stage.1 = (bf16[96,256]{1,0:T(8,128)(2,1)S(1)}, f32[2,96,384]{2,1,0:T(8,128)S(1)}, bf16[384,256]{1,0:T(8,128)(2,1)S(1)}) custom-call(bf16[96,256]{1,0:T(8,128)(2,1)} %q_hbm.1, bf16[384,256]{1,0:T(8,128)(2,1)} %held_k_hbm.1, bf16[384,256]{1,0:T(8,128)(2,1)} %held_v_hbm.1), custom_call_target="tpu_custom_call" | custom-call | flops 2000000000 | tf_op jit(solution)/shard_map/attention/stage/pallas_call | solution.py:297
  11.0 0.0 collective-permute-done.2.refs_3_
  11.0 1.5 %collective-permute-done.1.refs_2_ = bf16[96,512]{1,0:T(8,128)(2,1)S(1)} collective-permute-done((bf16[96,512]{1,0:T(8,128)(2,1)S(1)}, bf16[96,512]{1,0:T(8,128)(2,1)S(1)}, u32[]{:S(2)}, u32[]{:S(2)}) %collective-permute-start.1) | collective-permute-done | bytes 98336 | tf_op jit(solution)/shard_map/residual_gather/ppermute | solution.py:76
  12.5 0.9 %collective-permute-done.refs_1_ = bf16[96,512]{1,0:T(8,128)(2,1)S(1)} collective-permute-done((bf16[96,512]{1,0:T(8,128)(2,1)S(1)}, bf16[96,512]{1,0:T(8,128)(2,1)S(1)}, u32[]{:S(2)}, u32[]{:S(2)}) %collective-permute-start) | collective-permute-done | bytes 98336 | tf_op jit(solution)/shard_map/residual_gather/ppermute | solution.py:76
  13.4 0.0 copy-start
  13.4 0.5 %attention.1.refs_0_ = bf16[96,256]{1,0:T(8,128)(2,1)S(1)} custom-call(bf16[96,256]{1,0:T(8,128)(2,1)S(1)} %get-tuple-element.11.q_ref, f32[2,96,384]{2,1,0:T(8,128)S(1)} %get-tuple-element.12.products_ref, bf16[384,256]{1,0:T(8,128)(2,1)S(1)} %get-tuple-element.13.values_ref, bf16[96,512]{1,0:T(8,128)(2,1)S(1)} %maximum_convert_fusion.refs_0_, ...), custom_call_target="tpu_custom_call" | custom-call | flops 2000000000 | tf_op jit(solution)/shard_map/attention/attention/pallas_call | solution.py:313
  13.9 0.0 copy-start.4
  13.9 0.0 copy-start.1
  13.9 0.1 collective-permute-start.3
  14.0 1.6 %collective-permute-start.5 = (bf16[96,256]{1,0:T(8,128)(2,1)S(1)}, bf16[96,256]{1,0:T(8,128)(2,1)S(1)}, u32[]{:S(2)}, u32[]{:S(2)}) collective-permute-start(bf16[96,256]{1,0:T(8,128)(2,1)S(1)} %attention.1.refs_0_), channel_id=1, source_target_pairs={{0,2},{2,0},{1,3},{3,1},{4,6},{6,4},{5,7},{7,5},{8,10},{10,8},{9,1... | collective-permute-start | bytes 147464 | tf_op jit(solution)/shard_map/attended_swap/ppermute | solution.py:49
  15.6 0.0 collective-permute-done.3.refs_2_
  15.6 0.0 collective-permute-done.4.refs_3_
  15.6 0.0 copy-done
  15.6 0.3 %sent_term.1 = bf16[96,1024]{1,0:T(8,128)(2,1)S(1)} custom-call(bf16[96,256]{1,0:T(8,128)(2,1)S(1)} %attention.1.refs_0_, bf16[256,5120]{1,0:T(8,128)(2,1)S(1)} %copy-done, bf16[96,256]{1,0:T(8,128)(2,1)S(1)} %collective-permute-done.3.refs_2_, bf16[256,5120]{1,0:T(8,128)(2,1)S(1)} %collective-permute-done.4.refs_3_), custom_call_target="tpu_custom_call" | custom-call | flops 125829120 | tf_op jit(solution)/shard_map/projection/sent_term/pallas_call | solution.py:336
  15.9 1.2 %collective-permute-start.8 = (bf16[96,1024]{1,0:T(8,128)(2,1)S(1)}, bf16[96,1024]{1,0:T(8,128)(2,1)S(1)}, u32[]{:S(2)}, u32[]{:S(2)}) collective-permute-start(bf16[96,1024]{1,0:T(8,128)(2,1)S(1)} %sent_term.1), channel_id=1, source_target_pairs={{0,2},{2,0},{1,3},{3,1},{4,6},{6,4},{5,7},{7,5},{8,10},{10,8},{9,1... | collective-permute-start | bytes 589832 | tf_op jit(solution)/shard_map/projection/ppermute | solution.py:49
  17.1 1.1 %collective-permute-done.5.attended_ref = bf16[96,256]{1,0:T(8,128)(2,1)S(1)} collective-permute-done((bf16[96,256]{1,0:T(8,128)(2,1)S(1)}, bf16[96,256]{1,0:T(8,128)(2,1)S(1)}, u32[]{:S(2)}, u32[]{:S(2)}) %collective-permute-start.5) | collective-permute-done | bytes 49184 | tf_op jit(solution)/shard_map/attended_swap/ppermute | solution.py:49
  18.2 0.0 collective-permute-done.6.weight_ref
  18.2 0.1 collective-permute-start.7
  18.3 0.0 copy-done.4
  18.3 0.0 copy-done.1
  18.3 0.4 %base.1.base_ref = f32[96,1280]{1,0:T(8,128)S(1)} custom-call(bf16[96,1280]{1,0:T(8,128)(2,1)S(1)} %copy-done.1, f32[1,1280]{1,0:T(1,128)S(1)} %reshape.3.gate_ref, bf16[96,256]{1,0:T(8,128)(2,1)S(1)} %attention.1.refs_0_, bf16[256,5120]{1,0:T(8,128)(2,1)S(1)} %copy-done, bf16[96,256]{1,0:T(8,128)(2,1)S(1)} %collective-permute-done.3.refs_2_, ...), custom_call_target="tpu_custom_call" | custom-call | flops 125829120 | tf_op jit(solution)/shard_map/projection/base/pallas_call | solution.py:347
  18.7 1.0 %collective-permute-done.7.packed_ref = bf16[352,256]{1,0:T(8,128)(2,1)S(1)} collective-permute-done((bf16[352,256]{1,0:T(8,128)(2,1)S(1)}, bf16[352,256]{1,0:T(8,128)(2,1)S(1)}, u32[]{:S(2)}, u32[]{:S(2)}) %collective-permute-start.7) | collective-permute-done | bytes 180256 | tf_op jit(solution)/shard_map/projection/ppermute | solution.py:49
  19.7 0.2 early.1.base_ref
  19.9 3.1 %collective-permute-done.8.refs_0_ = bf16[96,1024]{1,0:T(8,128)(2,1)S(1)} collective-permute-done((bf16[96,1024]{1,0:T(8,128)(2,1)S(1)}, bf16[96,1024]{1,0:T(8,128)(2,1)S(1)}, u32[]{:S(2)}, u32[]{:S(2)}) %collective-permute-start.8) | collective-permute-done | bytes 196640 | tf_op jit(solution)/shard_map/projection/ppermute | solution.py:49
  22.9 0.7 %final.1 = bf16[96,1280]{1,0:T(8,128)(2,1)} custom-call(f32[96,1280]{1,0:T(8,128)S(1)} %early.1.base_ref, f32[1,1280]{1,0:T(1,128)S(1)} %reshape.3.gate_ref, bf16[96,1024]{1,0:T(8,128)(2,1)S(1)} %collective-permute-done.8.refs_0_), custom_call_target="tpu_custom_call" | custom-call | bytes 983040 | tf_op jit(solution)/shard_map/projection/final/pallas_call | solution.py:373
  (3 shorter events, 0.0 us)
Async XLA Ops:
  0.0 1.5 %copy-start.2 = (f32[96,256]{1,0:T(8,128)S(1)}, f32[96,256]{1,0:T(8,128)}, u32[]{:S(2)}) copy-start(f32[96,256]{1,0:T(8,128)} %param.12) | copy-start | bytes 294916
  0.0 1.5 %copy-start.3 = (f32[96,256]{1,0:T(8,128)S(1)}, f32[96,256]{1,0:T(8,128)}, u32[]{:S(2)}) copy-start(f32[96,256]{1,0:T(8,128)} %param.11) | copy-start | bytes 294916
  0.0 15.6 %collective-permute-start.4 = (bf16[256,5120]{1,0:T(8,128)(2,1)}, bf16[256,5120]{1,0:T(8,128)(2,1)S(1)}, u32[]{:S(2)}, u32[]{:S(2)}) collective-permute-start(bf16[256,5120]{1,0:T(8,128)(2,1)} %refs_1_.3), channel_id=1, source_target_pairs={{0,1},{1,0},{2,3},{3,2},{4,5},{5,4},{6,7},{7,6},{8,9},{9,8},{10,11... | collective-permute-start | bytes 7864328 | tf_op jit(solution)/shard_map/weight_swap/ppermute | solution.py:49
  1.5 9.5 %collective-permute-start.2 = (bf16[96,512]{1,0:T(8,128)(2,1)S(1)}, bf16[96,512]{1,0:T(8,128)(2,1)S(1)}, u32[]{:S(2)}, u32[]{:S(2)}) collective-permute-start(bf16[96,512]{1,0:T(8,128)(2,1)S(1)} %maximum_convert_fusion.refs_0_), channel_id=1, source_target_pairs={{0,4},{1,9},{4,12},{5,13},{8,0},{9,1},{12,8},{13,5},{2,6},{3,11},{... | collective-permute-start | bytes 294920 | tf_op jit(solution)/shard_map/residual_gather/ppermute | solution.py:76
  4.2 8.3 %collective-permute-start.1 = (bf16[96,512]{1,0:T(8,128)(2,1)S(1)}, bf16[96,512]{1,0:T(8,128)(2,1)S(1)}, u32[]{:S(2)}, u32[]{:S(2)}) collective-permute-start(bf16[96,512]{1,0:T(8,128)(2,1)S(1)} %maximum_convert_fusion.refs_0_), channel_id=1, source_target_pairs={{0,12},{1,13},{4,8},{5,1},{8,4},{9,5},{12,0},{13,9},{2,14},{3,15},... | collective-permute-start | bytes 294920 | tf_op jit(solution)/shard_map/residual_gather/ppermute | solution.py:76
  6.7 6.7 %collective-permute-start = (bf16[96,512]{1,0:T(8,128)(2,1)S(1)}, bf16[96,512]{1,0:T(8,128)(2,1)S(1)}, u32[]{:S(2)}, u32[]{:S(2)}) collective-permute-start(bf16[96,512]{1,0:T(8,128)(2,1)S(1)} %maximum_convert_fusion.refs_0_), channel_id=1, source_target_pairs={{0,8},{1,5},{4,0},{5,9},{8,12},{9,13},{12,4},{13,1},{2,10},{3,7},{... | collective-permute-start | bytes 294920 | tf_op jit(solution)/shard_map/residual_gather/ppermute | solution.py:76
  8.2 9.9 %collective-permute-start.6 = (bf16[256,512]{1,0:T(8,128)(2,1)S(1)}, bf16[256,512]{1,0:T(8,128)(2,1)S(1)}, u32[]{:S(2)}, u32[]{:S(2)}) collective-permute-start(bf16[256,512]{1,0:T(8,128)(2,1)S(1)} %early_weight.1), channel_id=1, source_target_pairs={{0,2},{2,0},{1,3},{3,1},{4,6},{6,4},{5,7},{7,5},{8,10},{10,8},{9,1... | collective-permute-start | bytes 786440 | tf_op jit(solution)/shard_map/early_weight/ppermute | solution.py:49
  13.4 2.2 %copy-start = (bf16[256,5120]{1,0:T(8,128)(2,1)S(1)}, bf16[256,5120]{1,0:T(8,128)(2,1)}, u32[]{:S(2)}) copy-start(bf16[256,5120]{1,0:T(8,128)(2,1)} %refs_1_.3) | copy-start | bytes 7864324
  13.9 4.4 %copy-start.4 = (f32[1280]{0:T(1024)S(1)}, f32[1280]{0:T(1024)}, u32[]{:S(2)}) copy-start(f32[1280]{0:T(1024)} %param.15) | copy-start | bytes 15364
  13.9 4.4 %copy-start.1 = (bf16[96,1280]{1,0:T(8,128)(2,1)S(1)}, bf16[96,1280]{1,0:T(8,128)(2,1)}, u32[]{:S(2)}) copy-start(bf16[96,1280]{1,0:T(8,128)(2,1)} %hidden_ref.1) | copy-start | bytes 737284
  13.9 1.6 %collective-permute-start.3 = (bf16[96,256]{1,0:T(8,128)(2,1)S(1)}, bf16[96,256]{1,0:T(8,128)(2,1)S(1)}, u32[]{:S(2)}, u32[]{:S(2)}) collective-permute-start(bf16[96,256]{1,0:T(8,128)(2,1)S(1)} %attention.1.refs_0_), channel_id=1, source_target_pairs={{0,1},{1,0},{2,3},{3,2},{4,5},{5,4},{6,7},{7,6},{8,9},{9,8},{10,11... | collective-permute-start | bytes 147464 | tf_op jit(solution)/shard_map/attended_swap/ppermute | solution.py:49
  14.0 4.2 %collective-permute-start.5 = (bf16[96,256]{1,0:T(8,128)(2,1)S(1)}, bf16[96,256]{1,0:T(8,128)(2,1)S(1)}, u32[]{:S(2)}, u32[]{:S(2)}) collective-permute-start(bf16[96,256]{1,0:T(8,128)(2,1)S(1)} %attention.1.refs_0_), channel_id=1, source_target_pairs={{0,2},{2,0},{1,3},{3,1},{4,6},{6,4},{5,7},{7,5},{8,10},{10,8},{9,1... | collective-permute-start | bytes 147464 | tf_op jit(solution)/shard_map/attended_swap/ppermute | solution.py:49
  15.9 7.0 %collective-permute-start.8 = (bf16[96,1024]{1,0:T(8,128)(2,1)S(1)}, bf16[96,1024]{1,0:T(8,128)(2,1)S(1)}, u32[]{:S(2)}, u32[]{:S(2)}) collective-permute-start(bf16[96,1024]{1,0:T(8,128)(2,1)S(1)} %sent_term.1), channel_id=1, source_target_pairs={{0,2},{2,0},{1,3},{3,1},{4,6},{6,4},{5,7},{7,5},{8,10},{10,8},{9,1... | collective-permute-start | bytes 589832 | tf_op jit(solution)/shard_map/projection/ppermute | solution.py:49
  18.2 1.5 %collective-permute-start.7 = (bf16[352,256]{1,0:T(8,128)(2,1)S(1)}, bf16[352,256]{1,0:T(8,128)(2,1)S(1)}, u32[]{:S(2)}, u32[]{:S(2)}) collective-permute-start(bf16[352,256]{1,0:T(8,128)(2,1)S(1)} %pack.1), channel_id=1, source_target_pairs={{0,1},{1,0},{2,3},{3,2},{4,5},{5,4},{6,7},{7,6},{8,9},{9,8},{10,11... | collective-permute-start | bytes 540680 | tf_op jit(solution)/shard_map/projection/ppermute | solution.py:49

commit v25 on v24

--- a/solution.py
+++ b/solution.py
@@ -50,9 +50,9 @@
 
 
 LINE_OF_FOUR = (
-    ((2, 0, 3, 1), (1, 2, 3, 0)),
+    ((2, 0, 3, 1), (2, 3, 0, 1)),
     ((3, 2, 1, 0), (3, 0, 1, 2)),
-    ((1, 3, 0, 2), (2, 3, 0, 1)),
+    ((1, 3, 0, 2), (1, 2, 3, 0)),
 )
 
 

time: 24.1 us -> 25.4 us (1.054)
  starting transfers between devices: 11.6 us -> 14 us
  waiting for transfers between devices: 7.49 us -> 6.64 us
    ppermute x6, starting transfers between devices: 4.84 us -> 7.23 us  [shift(): lax.ppermute(array, axis, [(i, (i + step) % size) for i in range(size)])]
    ppermute x3, waiting for transfers between devices: 2.34 us -> 1.58 us  [gather(): blocks.append(lax.ppermute(own, ('patch', 'sub'), pairs))]
  transfers between devices with their start and end apart: 9 -> 9, of which waited for: 5 -> 5; matrix products, arithmetic and copies ran while one was open for 0% -> 0% of each run, Pallas kernels for 16% -> 15%
where the time goes in v25:
time: 25.4 us; the launch traced here: 25.2 us
  starting transfers between devices  14 us (55%)
  waiting for transfers between devices  6.64 us (26%)
  Pallas kernels  4.43 us (17%)
    ppermute x6, starting transfers between devices, shift(): lax.ppermute(array, axis, [(i, (i + step) % size) for i in range(size)])  7.23 us
    ppermute x3, starting transfers between devices, gather(): blocks.append(lax.ppermute(own, ('patch', 'sub'), pairs))  6.74 us
    ppermute x6, waiting for transfers between devices, shift(): lax.ppermute(array, axis, [(i, (i + step) % size) for i in range(size)])  5.06 us
    ppermute x3, waiting for transfers between devices, gather(): blocks.append(lax.ppermute(own, ('patch', 'sub'), pairs))  1.58 us
    pallas_call x1, Pallas kernels, per_device(): call(functools.partial(stage_kernel, patches, subs), [jax.ShapeDtypeStruc...  1.28 us
    pallas_call x1, Pallas kernels, per_device(): call(functools.partial(early_weight_kernel, subs, columns, early), jax.Sh...  0.99 us
    pallas_call x1, Pallas kernels, per_device(): call(functools.partial(final_kernel, early, row_blocks), jax.ShapeDtypeSt...  0.74 us
    pallas_call x1, Pallas kernels, per_device(): call(functools.partial(attention_kernel, 1.0 / math.sqrt(HD)), jax.ShapeD...  0.53 us
  transfers between devices with their start and end apart: 9, of which 5 were waited for; matrix products, arithmetic and copies ran while one was open for 0% of the time, Pallas kernels for 15%

profile of v25, /device:TPU:0, one launch (start us, length us, event | category | flops | bytes accessed | tf_op | source)
XLA Modules:
  0.0 25.2 jit_solution(16683843447481213937)
XLA Ops:
  0.0 0.0 copy-start.2
  0.0 0.0 copy-start.3
  0.0 0.5 %collective-permute-start.4 = (bf16[256,5120]{1,0:T(8,128)(2,1)}, bf16[256,5120]{1,0:T(8,128)(2,1)S(1)}, u32[]{:S(2)}, u32[]{:S(2)}) collective-permute-start(bf16[256,5120]{1,0:T(8,128)(2,1)} %refs_1_.3), channel_id=1, source_target_pairs={{0,1},{1,0},{2,3},{3,2},{4,5},{5,4},{6,7},{7,6},{8,9},{9,8},{10,11... | collective-permute-start | bytes 7864328 | tf_op jit(solution)/shard_map/weight_swap/ppermute | solution.py:49
  0.5 1.0 %early_weight.1 = bf16[256,512]{1,0:T(8,128)(2,1)S(1)} custom-call(bf16[256,5120]{1,0:T(8,128)(2,1)} %refs_1_.3), custom_call_target="tpu_custom_call" | custom-call | bytes 524288 | tf_op jit(solution)/shard_map/early_weight/early_weight/pallas_call | solution.py:250
  1.5 0.0 copy-done.2
  1.5 0.0 copy-done.3
  1.5 2.7 %collective-permute-start.2 = (bf16[96,512]{1,0:T(8,128)(2,1)S(1)}, bf16[96,512]{1,0:T(8,128)(2,1)S(1)}, u32[]{:S(2)}, u32[]{:S(2)}) collective-permute-start(bf16[96,512]{1,0:T(8,128)(2,1)S(1)} %maximum_convert_fusion.refs_0_), channel_id=1, source_target_pairs={{0,4},{1,5},{4,12},{5,9},{8,0},{9,13},{12,8},{13,1},{2,6},{3,7},{6... | collective-permute-start | bytes 294920 | tf_op jit(solution)/shard_map/residual_gather/ppermute | solution.py:76
  4.2 2.5 %collective-permute-start.1 = (bf16[96,512]{1,0:T(8,128)(2,1)S(1)}, bf16[96,512]{1,0:T(8,128)(2,1)S(1)}, u32[]{:S(2)}, u32[]{:S(2)}) collective-permute-start(bf16[96,512]{1,0:T(8,128)(2,1)S(1)} %maximum_convert_fusion.refs_0_), channel_id=1, source_target_pairs={{0,12},{1,13},{4,8},{5,1},{8,4},{9,5},{12,0},{13,9},{2,14},{3,15},... | collective-permute-start | bytes 294920 | tf_op jit(solution)/shard_map/residual_gather/ppermute | solution.py:76
  6.7 1.6 %collective-permute-start = (bf16[96,512]{1,0:T(8,128)(2,1)S(1)}, bf16[96,512]{1,0:T(8,128)(2,1)S(1)}, u32[]{:S(2)}, u32[]{:S(2)}) collective-permute-start(bf16[96,512]{1,0:T(8,128)(2,1)S(1)} %maximum_convert_fusion.refs_0_), channel_id=1, source_target_pairs={{0,8},{1,9},{4,0},{5,13},{8,12},{9,1},{12,4},{13,5},{2,10},{3,11},... | collective-permute-start | bytes 294920 | tf_op jit(solution)/shard_map/residual_gather/ppermute | solution.py:76
  8.2 1.5 %collective-permute-start.6 = (bf16[256,512]{1,0:T(8,128)(2,1)S(1)}, bf16[256,512]{1,0:T(8,128)(2,1)S(1)}, u32[]{:S(2)}, u32[]{:S(2)}) collective-permute-start(bf16[256,512]{1,0:T(8,128)(2,1)S(1)} %early_weight.1), channel_id=1, source_target_pairs={{0,2},{2,0},{1,3},{3,1},{4,6},{6,4},{5,7},{7,5},{8,10},{10,8},{9,1... | collective-permute-start | bytes 786440 | tf_op jit(solution)/shard_map/early_weight/ppermute | solution.py:49
  9.7 1.3 %stage.1 = (bf16[96,256]{1,0:T(8,128)(2,1)S(1)}, f32[2,96,384]{2,1,0:T(8,128)S(1)}, bf16[384,256]{1,0:T(8,128)(2,1)S(1)}) custom-call(bf16[96,256]{1,0:T(8,128)(2,1)} %q_hbm.1, bf16[384,256]{1,0:T(8,128)(2,1)} %held_k_hbm.1, bf16[384,256]{1,0:T(8,128)(2,1)} %held_v_hbm.1), custom_call_target="tpu_custom_call" | custom-call | flops 2000000000 | tf_op jit(solution)/shard_map/attention/stage/pallas_call | solution.py:297
  11.0 0.0 collective-permute-done.2.refs_3_
  11.0 1.5 %collective-permute-done.1.refs_2_ = bf16[96,512]{1,0:T(8,128)(2,1)S(1)} collective-permute-done((bf16[96,512]{1,0:T(8,128)(2,1)S(1)}, bf16[96,512]{1,0:T(8,128)(2,1)S(1)}, u32[]{:S(2)}, u32[]{:S(2)}) %collective-permute-start.1) | collective-permute-done | bytes 98336 | tf_op jit(solution)/shard_map/residual_gather/ppermute | solution.py:76
  12.5 0.1 collective-permute-done.refs_1_
  12.6 0.0 copy-start
  12.6 0.5 %attention.1.refs_0_ = bf16[96,256]{1,0:T(8,128)(2,1)S(1)} custom-call(bf16[96,256]{1,0:T(8,128)(2,1)S(1)} %get-tuple-element.11.q_ref, f32[2,96,384]{2,1,0:T(8,128)S(1)} %get-tuple-element.12.products_ref, bf16[384,256]{1,0:T(8,128)(2,1)S(1)} %get-tuple-element.13.values_ref, bf16[96,512]{1,0:T(8,128)(2,1)S(1)} %maximum_convert_fusion.refs_0_, ...), custom_call_target="tpu_custom_call" | custom-call | flops 2000000000 | tf_op jit(solution)/shard_map/attention/attention/pallas_call | solution.py:313
  13.1 0.0 copy-start.4
  13.1 0.0 copy-start.1
  13.2 2.5 %collective-permute-start.3 = (bf16[96,256]{1,0:T(8,128)(2,1)S(1)}, bf16[96,256]{1,0:T(8,128)(2,1)S(1)}, u32[]{:S(2)}, u32[]{:S(2)}) collective-permute-start(bf16[96,256]{1,0:T(8,128)(2,1)S(1)} %attention.1.refs_0_), channel_id=1, source_target_pairs={{0,1},{1,0},{2,3},{3,2},{4,5},{5,4},{6,7},{7,6},{8,9},{9,8},{10,11... | collective-permute-start | bytes 147464 | tf_op jit(solution)/shard_map/attended_swap/ppermute | solution.py:49
  15.6 1.8 %collective-permute-start.5 = (bf16[96,256]{1,0:T(8,128)(2,1)S(1)}, bf16[96,256]{1,0:T(8,128)(2,1)S(1)}, u32[]{:S(2)}, u32[]{:S(2)}) collective-permute-start(bf16[96,256]{1,0:T(8,128)(2,1)S(1)} %attention.1.refs_0_), channel_id=1, source_target_pairs={{0,2},{2,0},{1,3},{3,1},{4,6},{6,4},{5,7},{7,5},{8,10},{10,8},{9,1... | collective-permute-start | bytes 147464 | tf_op jit(solution)/shard_map/attended_swap/ppermute | solution.py:49
  17.5 0.0 collective-permute-done.3.refs_2_
  17.5 0.0 collective-permute-done.4.refs_3_
  17.5 0.0 copy-done
  17.5 0.3 %sent_term.1 = bf16[96,1024]{1,0:T(8,128)(2,1)S(1)} custom-call(bf16[96,256]{1,0:T(8,128)(2,1)S(1)} %attention.1.refs_0_, bf16[256,5120]{1,0:T(8,128)(2,1)S(1)} %copy-done, bf16[96,256]{1,0:T(8,128)(2,1)S(1)} %collective-permute-done.3.refs_2_, bf16[256,5120]{1,0:T(8,128)(2,1)S(1)} %collective-permute-done.4.refs_3_), custom_call_target="tpu_custom_call" | custom-call | flops 125829120 | tf_op jit(solution)/shard_map/projection/sent_term/pallas_call | solution.py:336
  17.8 0.9 %collective-permute-start.8 = (bf16[96,1024]{1,0:T(8,128)(2,1)S(1)}, bf16[96,1024]{1,0:T(8,128)(2,1)S(1)}, u32[]{:S(2)}, u32[]{:S(2)}) collective-permute-start(bf16[96,1024]{1,0:T(8,128)(2,1)S(1)} %sent_term.1), channel_id=1, source_target_pairs={{0,2},{2,0},{1,3},{3,1},{4,6},{6,4},{5,7},{7,5},{8,10},{10,8},{9,1... | collective-permute-start | bytes 589832 | tf_op jit(solution)/shard_map/projection/ppermute | solution.py:49
  18.7 1.0 %collective-permute-done.5.attended_ref = bf16[96,256]{1,0:T(8,128)(2,1)S(1)} collective-permute-done((bf16[96,256]{1,0:T(8,128)(2,1)S(1)}, bf16[96,256]{1,0:T(8,128)(2,1)S(1)}, u32[]{:S(2)}, u32[]{:S(2)}) %collective-permute-start.5) | collective-permute-done | bytes 49184 | tf_op jit(solution)/shard_map/attended_swap/ppermute | solution.py:49
  19.7 0.0 collective-permute-done.6.weight_ref
  19.7 0.1 collective-permute-start.7
  19.8 0.0 copy-done.4
  19.8 0.0 copy-done.1
  19.8 0.4 %base.1.base_ref = f32[96,1280]{1,0:T(8,128)S(1)} custom-call(bf16[96,1280]{1,0:T(8,128)(2,1)S(1)} %copy-done.1, f32[1,1280]{1,0:T(1,128)S(1)} %reshape.3.gate_ref, bf16[96,256]{1,0:T(8,128)(2,1)S(1)} %attention.1.refs_0_, bf16[256,5120]{1,0:T(8,128)(2,1)S(1)} %copy-done, bf16[96,256]{1,0:T(8,128)(2,1)S(1)} %collective-permute-done.3.refs_2_, ...), custom_call_target="tpu_custom_call" | custom-call | flops 125829120 | tf_op jit(solution)/shard_map/projection/base/pallas_call | solution.py:347
  20.2 1.0 %collective-permute-done.7.packed_ref = bf16[352,256]{1,0:T(8,128)(2,1)S(1)} collective-permute-done((bf16[352,256]{1,0:T(8,128)(2,1)S(1)}, bf16[352,256]{1,0:T(8,128)(2,1)S(1)}, u32[]{:S(2)}, u32[]{:S(2)}) %collective-permute-start.7) | collective-permute-done | bytes 180256 | tf_op jit(solution)/shard_map/projection/ppermute | solution.py:49
  21.2 0.2 early.1.base_ref
  21.4 3.1 %collective-permute-done.8.refs_0_ = bf16[96,1024]{1,0:T(8,128)(2,1)S(1)} collective-permute-done((bf16[96,1024]{1,0:T(8,128)(2,1)S(1)}, bf16[96,1024]{1,0:T(8,128)(2,1)S(1)}, u32[]{:S(2)}, u32[]{:S(2)}) %collective-permute-start.8) | collective-permute-done | bytes 196640 | tf_op jit(solution)/shard_map/projection/ppermute | solution.py:49
  24.5 0.7 %final.1 = bf16[96,1280]{1,0:T(8,128)(2,1)} custom-call(f32[96,1280]{1,0:T(8,128)S(1)} %early.1.base_ref, f32[1,1280]{1,0:T(1,128)S(1)} %reshape.3.gate_ref, bf16[96,1024]{1,0:T(8,128)(2,1)S(1)} %collective-permute-done.8.refs_0_), custom_call_target="tpu_custom_call" | custom-call | bytes 983040 | tf_op jit(solution)/shard_map/projection/final/pallas_call | solution.py:373
  (3 shorter events, 0.0 us)
Async XLA Ops:
  0.0 1.5 %copy-start.2 = (f32[96,256]{1,0:T(8,128)S(1)}, f32[96,256]{1,0:T(8,128)}, u32[]{:S(2)}) copy-start(f32[96,256]{1,0:T(8,128)} %param.12) | copy-start | bytes 294916
  0.0 1.5 %copy-start.3 = (f32[96,256]{1,0:T(8,128)S(1)}, f32[96,256]{1,0:T(8,128)}, u32[]{:S(2)}) copy-start(f32[96,256]{1,0:T(8,128)} %param.11) | copy-start | bytes 294916
  0.0 17.5 %collective-permute-start.4 = (bf16[256,5120]{1,0:T(8,128)(2,1)}, bf16[256,5120]{1,0:T(8,128)(2,1)S(1)}, u32[]{:S(2)}, u32[]{:S(2)}) collective-permute-start(bf16[256,5120]{1,0:T(8,128)(2,1)} %refs_1_.3), channel_id=1, source_target_pairs={{0,1},{1,0},{2,3},{3,2},{4,5},{5,4},{6,7},{7,6},{8,9},{9,8},{10,11... | collective-permute-start | bytes 7864328 | tf_op jit(solution)/shard_map/weight_swap/ppermute | solution.py:49
  1.5 9.5 %collective-permute-start.2 = (bf16[96,512]{1,0:T(8,128)(2,1)S(1)}, bf16[96,512]{1,0:T(8,128)(2,1)S(1)}, u32[]{:S(2)}, u32[]{:S(2)}) collective-permute-start(bf16[96,512]{1,0:T(8,128)(2,1)S(1)} %maximum_convert_fusion.refs_0_), channel_id=1, source_target_pairs={{0,4},{1,5},{4,12},{5,9},{8,0},{9,13},{12,8},{13,1},{2,6},{3,7},{6... | collective-permute-start | bytes 294920 | tf_op jit(solution)/shard_map/residual_gather/ppermute | solution.py:76
  4.2 8.3 %collective-permute-start.1 = (bf16[96,512]{1,0:T(8,128)(2,1)S(1)}, bf16[96,512]{1,0:T(8,128)(2,1)S(1)}, u32[]{:S(2)}, u32[]{:S(2)}) collective-permute-start(bf16[96,512]{1,0:T(8,128)(2,1)S(1)} %maximum_convert_fusion.refs_0_), channel_id=1, source_target_pairs={{0,12},{1,13},{4,8},{5,1},{8,4},{9,5},{12,0},{13,9},{2,14},{3,15},... | collective-permute-start | bytes 294920 | tf_op jit(solution)/shard_map/residual_gather/ppermute | solution.py:76
  6.7 5.9 %collective-permute-start = (bf16[96,512]{1,0:T(8,128)(2,1)S(1)}, bf16[96,512]{1,0:T(8,128)(2,1)S(1)}, u32[]{:S(2)}, u32[]{:S(2)}) collective-permute-start(bf16[96,512]{1,0:T(8,128)(2,1)S(1)} %maximum_convert_fusion.refs_0_), channel_id=1, source_target_pairs={{0,8},{1,9},{4,0},{5,13},{8,12},{9,1},{12,4},{13,5},{2,10},{3,11},... | collective-permute-start | bytes 294920 | tf_op jit(solution)/shard_map/residual_gather/ppermute | solution.py:76
  8.2 11.5 %collective-permute-start.6 = (bf16[256,512]{1,0:T(8,128)(2,1)S(1)}, bf16[256,512]{1,0:T(8,128)(2,1)S(1)}, u32[]{:S(2)}, u32[]{:S(2)}) collective-permute-start(bf16[256,512]{1,0:T(8,128)(2,1)S(1)} %early_weight.1), channel_id=1, source_target_pairs={{0,2},{2,0},{1,3},{3,1},{4,6},{6,4},{5,7},{7,5},{8,10},{10,8},{9,1... | collective-permute-start | bytes 786440 | tf_op jit(solution)/shard_map/early_weight/ppermute | solution.py:49
  12.6 4.9 %copy-start = (bf16[256,5120]{1,0:T(8,128)(2,1)S(1)}, bf16[256,5120]{1,0:T(8,128)(2,1)}, u32[]{:S(2)}) copy-start(bf16[256,5120]{1,0:T(8,128)(2,1)} %refs_1_.3) | copy-start | bytes 7864324
  13.1 6.7 %copy-start.4 = (f32[1280]{0:T(1024)S(1)}, f32[1280]{0:T(1024)}, u32[]{:S(2)}) copy-start(f32[1280]{0:T(1024)} %param.15) | copy-start | bytes 15364
  13.1 6.7 %copy-start.1 = (bf16[96,1280]{1,0:T(8,128)(2,1)S(1)}, bf16[96,1280]{1,0:T(8,128)(2,1)}, u32[]{:S(2)}) copy-start(bf16[96,1280]{1,0:T(8,128)(2,1)} %hidden_ref.1) | copy-start | bytes 737284
  13.2 4.3 %collective-permute-start.3 = (bf16[96,256]{1,0:T(8,128)(2,1)S(1)}, bf16[96,256]{1,0:T(8,128)(2,1)S(1)}, u32[]{:S(2)}, u32[]{:S(2)}) collective-permute-start(bf16[96,256]{1,0:T(8,128)(2,1)S(1)} %attention.1.refs_0_), channel_id=1, source_target_pairs={{0,1},{1,0},{2,3},{3,2},{4,5},{5,4},{6,7},{7,6},{8,9},{9,8},{10,11... | collective-permute-start | bytes 147464 | tf_op jit(solution)/shard_map/attended_swap/ppermute | solution.py:49
  15.6 4.1 %collective-permute-start.5 = (bf16[96,256]{1,0:T(8,128)(2,1)S(1)}, bf16[96,256]{1,0:T(8,128)(2,1)S(1)}, u32[]{:S(2)}, u32[]{:S(2)}) collective-permute-start(bf16[96,256]{1,0:T(8,128)(2,1)S(1)} %attention.1.refs_0_), channel_id=1, source_target_pairs={{0,2},{2,0},{1,3},{3,1},{4,6},{6,4},{5,7},{7,5},{8,10},{10,8},{9,1... | collective-permute-start | bytes 147464 | tf_op jit(solution)/shard_map/attended_swap/ppermute | solution.py:49
  17.8 6.7 %collective-permute-start.8 = (bf16[96,1024]{1,0:T(8,128)(2,1)S(1)}, bf16[96,1024]{1,0:T(8,128)(2,1)S(1)}, u32[]{:S(2)}, u32[]{:S(2)}) collective-permute-start(bf16[96,1024]{1,0:T(8,128)(2,1)S(1)} %sent_term.1), channel_id=1, source_target_pairs={{0,2},{2,0},{1,3},{3,1},{4,6},{6,4},{5,7},{7,5},{8,10},{10,8},{9,1... | collective-permute-start | bytes 589832 | tf_op jit(solution)/shard_map/projection/ppermute | solution.py:49
  19.7 1.5 %collective-permute-start.7 = (bf16[352,256]{1,0:T(8,128)(2,1)S(1)}, bf16[352,256]{1,0:T(8,128)(2,1)S(1)}, u32[]{:S(2)}, u32[]{:S(2)}) collective-permute-start(bf16[352,256]{1,0:T(8,128)(2,1)S(1)} %pack.1), channel_id=1, source_target_pairs={{0,1},{1,0},{2,3},{3,2},{4,5},{5,4},{6,7},{7,6},{8,9},{9,8},{10,11... | collective-permute-start | bytes 540680 | tf_op jit(solution)/shard_map/projection/ppermute | solution.py:49

commit v26 on v25

--- a/solution.py
+++ b/solution.py
@@ -50,9 +50,9 @@
 
 
 LINE_OF_FOUR = (
-    ((2, 0, 3, 1), (2, 3, 0, 1)),
-    ((3, 2, 1, 0), (3, 0, 1, 2)),
-    ((1, 3, 0, 2), (1, 2, 3, 0)),
+    ((2, 0, 3, 1), (2, 3, 1, 0)),
+    ((3, 2, 1, 0), (1, 0, 3, 2)),
+    ((1, 3, 0, 2), (3, 2, 0, 1)),
 )
 
 

time: 25.4 us -> 24.4 us (0.961)
  starting transfers between devices: 14 us -> 11.6 us
  waiting for transfers between devices: 6.64 us -> 7.93 us
    ppermute x6, starting transfers between devices: 7.23 us -> 4.89 us  [shift(): lax.ppermute(array, axis, [(i, (i + step) % size) for i in range(size)])]
    ppermute x3, waiting for transfers between devices: 1.58 us -> 2.79 us  [gather(): blocks.append(lax.ppermute(own, ('patch', 'sub'), pairs))]
where the time goes in v26:
time: 24.4 us; the launch traced here: 24.2 us
  starting transfers between devices  11.6 us (48%)
  waiting for transfers between devices  7.93 us (32%)
  Pallas kernels  4.43 us (18%)
    ppermute x3, starting transfers between devices, gather(): blocks.append(lax.ppermute(own, ('patch', 'sub'), pairs))  6.74 us
    ppermute x6, waiting for transfers between devices, shift(): lax.ppermute(array, axis, [(i, (i + step) % size) for i in range(size)])  5.14 us
    ppermute x6, starting transfers between devices, shift(): lax.ppermute(array, axis, [(i, (i + step) % size) for i in range(size)])  4.89 us
    ppermute x3, waiting for transfers between devices, gather(): blocks.append(lax.ppermute(own, ('patch', 'sub'), pairs))  2.79 us
    pallas_call x1, Pallas kernels, per_device(): call(functools.partial(stage_kernel, patches, subs), [jax.ShapeDtypeStruc...  1.28 us
    pallas_call x1, Pallas kernels, per_device(): call(functools.partial(early_weight_kernel, subs, columns, early), jax.Sh...  0.99 us
    pallas_call x1, Pallas kernels, per_device(): call(functools.partial(final_kernel, early, row_blocks), jax.ShapeDtypeSt...  0.74 us
    pallas_call x1, Pallas kernels, per_device(): call(functools.partial(attention_kernel, 1.0 / math.sqrt(HD)), jax.ShapeD...  0.53 us
  transfers between devices with their start and end apart: 9, of which 5 were waited for; matrix products, arithmetic and copies ran while one was open for 0% of the time, Pallas kernels for 15%

profile of v26, /device:TPU:0, one launch (start us, length us, event | category | flops | bytes accessed | tf_op | source)
XLA Modules:
  0.0 24.2 jit_solution(12402985766806412132)
XLA Ops:
  0.0 0.0 copy-start.2
  0.0 0.0 copy-start.3
  0.0 0.5 %collective-permute-start.4 = (bf16[256,5120]{1,0:T(8,128)(2,1)}, bf16[256,5120]{1,0:T(8,128)(2,1)S(1)}, u32[]{:S(2)}, u32[]{:S(2)}) collective-permute-start(bf16[256,5120]{1,0:T(8,128)(2,1)} %refs_1_.3), channel_id=1, source_target_pairs={{0,1},{1,0},{2,3},{3,2},{4,5},{5,4},{6,7},{7,6},{8,9},{9,8},{10,11... | collective-permute-start | bytes 7864328 | tf_op jit(solution)/shard_map/weight_swap/ppermute | solution.py:49
  0.5 1.0 %early_weight.1 = bf16[256,512]{1,0:T(8,128)(2,1)S(1)} custom-call(bf16[256,5120]{1,0:T(8,128)(2,1)} %refs_1_.3), custom_call_target="tpu_custom_call" | custom-call | bytes 524288 | tf_op jit(solution)/shard_map/early_weight/early_weight/pallas_call | solution.py:250
  1.5 0.0 copy-done.2
  1.5 0.0 copy-done.3
  1.5 2.7 %collective-permute-start.2 = (bf16[96,512]{1,0:T(8,128)(2,1)S(1)}, bf16[96,512]{1,0:T(8,128)(2,1)S(1)}, u32[]{:S(2)}, u32[]{:S(2)}) collective-permute-start(bf16[96,512]{1,0:T(8,128)(2,1)S(1)} %maximum_convert_fusion.refs_0_), channel_id=1, source_target_pairs={{0,4},{1,13},{4,12},{5,9},{8,0},{9,1},{12,8},{13,5},{2,6},{3,15},{... | collective-permute-start | bytes 294920 | tf_op jit(solution)/shard_map/residual_gather/ppermute | solution.py:76
  4.2 2.5 %collective-permute-start.1 = (bf16[96,512]{1,0:T(8,128)(2,1)S(1)}, bf16[96,512]{1,0:T(8,128)(2,1)S(1)}, u32[]{:S(2)}, u32[]{:S(2)}) collective-permute-start(bf16[96,512]{1,0:T(8,128)(2,1)S(1)} %maximum_convert_fusion.refs_0_), channel_id=1, source_target_pairs={{0,12},{1,5},{4,8},{5,1},{8,4},{9,13},{12,0},{13,9},{2,14},{3,7},{... | collective-permute-start | bytes 294920 | tf_op jit(solution)/shard_map/residual_gather/ppermute | solution.py:76
  6.7 1.6 %collective-permute-start = (bf16[96,512]{1,0:T(8,128)(2,1)S(1)}, bf16[96,512]{1,0:T(8,128)(2,1)S(1)}, u32[]{:S(2)}, u32[]{:S(2)}) collective-permute-start(bf16[96,512]{1,0:T(8,128)(2,1)S(1)} %maximum_convert_fusion.refs_0_), channel_id=1, source_target_pairs={{0,8},{1,9},{4,0},{5,13},{8,12},{9,5},{12,4},{13,1},{2,10},{3,11},... | collective-permute-start | bytes 294920 | tf_op jit(solution)/shard_map/residual_gather/ppermute | solution.py:76
  8.2 1.5 %collective-permute-start.6 = (bf16[256,512]{1,0:T(8,128)(2,1)S(1)}, bf16[256,512]{1,0:T(8,128)(2,1)S(1)}, u32[]{:S(2)}, u32[]{:S(2)}) collective-permute-start(bf16[256,512]{1,0:T(8,128)(2,1)S(1)} %early_weight.1), channel_id=1, source_target_pairs={{0,2},{2,0},{1,3},{3,1},{4,6},{6,4},{5,7},{7,5},{8,10},{10,8},{9,1... | collective-permute-start | bytes 786440 | tf_op jit(solution)/shard_map/early_weight/ppermute | solution.py:49
  9.7 1.3 %stage.1 = (bf16[96,256]{1,0:T(8,128)(2,1)S(1)}, f32[2,96,384]{2,1,0:T(8,128)S(1)}, bf16[384,256]{1,0:T(8,128)(2,1)S(1)}) custom-call(bf16[96,256]{1,0:T(8,128)(2,1)} %q_hbm.1, bf16[384,256]{1,0:T(8,128)(2,1)} %held_k_hbm.1, bf16[384,256]{1,0:T(8,128)(2,1)} %held_v_hbm.1), custom_call_target="tpu_custom_call" | custom-call | flops 2000000000 | tf_op jit(solution)/shard_map/attention/stage/pallas_call | solution.py:297
  11.0 0.0 collective-permute-done.2.refs_3_
  11.0 1.5 %collective-permute-done.1.refs_2_ = bf16[96,512]{1,0:T(8,128)(2,1)S(1)} collective-permute-done((bf16[96,512]{1,0:T(8,128)(2,1)S(1)}, bf16[96,512]{1,0:T(8,128)(2,1)S(1)}, u32[]{:S(2)}, u32[]{:S(2)}) %collective-permute-start.1) | collective-permute-done | bytes 98336 | tf_op jit(solution)/shard_map/residual_gather/ppermute | solution.py:76
  12.5 1.3 %collective-permute-done.refs_1_ = bf16[96,512]{1,0:T(8,128)(2,1)S(1)} collective-permute-done((bf16[96,512]{1,0:T(8,128)(2,1)S(1)}, bf16[96,512]{1,0:T(8,128)(2,1)S(1)}, u32[]{:S(2)}, u32[]{:S(2)}) %collective-permute-start) | collective-permute-done | bytes 98336 | tf_op jit(solution)/shard_map/residual_gather/ppermute | solution.py:76
  13.8 0.0 copy-start
  13.8 0.5 %attention.1.refs_0_ = bf16[96,256]{1,0:T(8,128)(2,1)S(1)} custom-call(bf16[96,256]{1,0:T(8,128)(2,1)S(1)} %get-tuple-element.11.q_ref, f32[2,96,384]{2,1,0:T(8,128)S(1)} %get-tuple-element.12.products_ref, bf16[384,256]{1,0:T(8,128)(2,1)S(1)} %get-tuple-element.13.values_ref, bf16[96,512]{1,0:T(8,128)(2,1)S(1)} %maximum_convert_fusion.refs_0_, ...), custom_call_target="tpu_custom_call" | custom-call | flops 2000000000 | tf_op jit(solution)/shard_map/attention/attention/pallas_call | solution.py:313
  14.3 0.0 copy-start.4
  14.4 0.0 copy-start.1
  14.4 0.1 collective-permute-start.3
  14.5 1.6 %collective-permute-start.5 = (bf16[96,256]{1,0:T(8,128)(2,1)S(1)}, bf16[96,256]{1,0:T(8,128)(2,1)S(1)}, u32[]{:S(2)}, u32[]{:S(2)}) collective-permute-start(bf16[96,256]{1,0:T(8,128)(2,1)S(1)} %attention.1.refs_0_), channel_id=1, source_target_pairs={{0,2},{2,0},{1,3},{3,1},{4,6},{6,4},{5,7},{7,5},{8,10},{10,8},{9,1... | collective-permute-start | bytes 147464 | tf_op jit(solution)/shard_map/attended_swap/ppermute | solution.py:49
  16.1 0.0 collective-permute-done.3.refs_2_
  16.1 0.0 collective-permute-done.4.refs_3_
  16.1 0.0 copy-done
  16.1 0.3 %sent_term.1 = bf16[96,1024]{1,0:T(8,128)(2,1)S(1)} custom-call(bf16[96,256]{1,0:T(8,128)(2,1)S(1)} %attention.1.refs_0_, bf16[256,5120]{1,0:T(8,128)(2,1)S(1)} %copy-done, bf16[96,256]{1,0:T(8,128)(2,1)S(1)} %collective-permute-done.3.refs_2_, bf16[256,5120]{1,0:T(8,128)(2,1)S(1)} %collective-permute-done.4.refs_3_), custom_call_target="tpu_custom_call" | custom-call | flops 125829120 | tf_op jit(solution)/shard_map/projection/sent_term/pallas_call | solution.py:336
  16.4 1.2 %collective-permute-start.8 = (bf16[96,1024]{1,0:T(8,128)(2,1)S(1)}, bf16[96,1024]{1,0:T(8,128)(2,1)S(1)}, u32[]{:S(2)}, u32[]{:S(2)}) collective-permute-start(bf16[96,1024]{1,0:T(8,128)(2,1)S(1)} %sent_term.1), channel_id=1, source_target_pairs={{0,2},{2,0},{1,3},{3,1},{4,6},{6,4},{5,7},{7,5},{8,10},{10,8},{9,1... | collective-permute-start | bytes 589832 | tf_op jit(solution)/shard_map/projection/ppermute | solution.py:49
  17.6 1.0 %collective-permute-done.5.attended_ref = bf16[96,256]{1,0:T(8,128)(2,1)S(1)} collective-permute-done((bf16[96,256]{1,0:T(8,128)(2,1)S(1)}, bf16[96,256]{1,0:T(8,128)(2,1)S(1)}, u32[]{:S(2)}, u32[]{:S(2)}) %collective-permute-start.5) | collective-permute-done | bytes 49184 | tf_op jit(solution)/shard_map/attended_swap/ppermute | solution.py:49
  18.6 0.0 collective-permute-done.6.weight_ref
  18.6 0.1 collective-permute-start.7
  18.7 0.0 copy-done.4
  18.7 0.0 copy-done.1
  18.7 0.4 %base.1.base_ref = f32[96,1280]{1,0:T(8,128)S(1)} custom-call(bf16[96,1280]{1,0:T(8,128)(2,1)S(1)} %copy-done.1, f32[1,1280]{1,0:T(1,128)S(1)} %reshape.3.gate_ref, bf16[96,256]{1,0:T(8,128)(2,1)S(1)} %attention.1.refs_0_, bf16[256,5120]{1,0:T(8,128)(2,1)S(1)} %copy-done, bf16[96,256]{1,0:T(8,128)(2,1)S(1)} %collective-permute-done.3.refs_2_, ...), custom_call_target="tpu_custom_call" | custom-call | flops 125829120 | tf_op jit(solution)/shard_map/projection/base/pallas_call | solution.py:347
  19.1 1.0 %collective-permute-done.7.packed_ref = bf16[352,256]{1,0:T(8,128)(2,1)S(1)} collective-permute-done((bf16[352,256]{1,0:T(8,128)(2,1)S(1)}, bf16[352,256]{1,0:T(8,128)(2,1)S(1)}, u32[]{:S(2)}, u32[]{:S(2)}) %collective-permute-start.7) | collective-permute-done | bytes 180256 | tf_op jit(solution)/shard_map/projection/ppermute | solution.py:49
  20.1 0.2 early.1.base_ref
  20.3 3.1 %collective-permute-done.8.refs_0_ = bf16[96,1024]{1,0:T(8,128)(2,1)S(1)} collective-permute-done((bf16[96,1024]{1,0:T(8,128)(2,1)S(1)}, bf16[96,1024]{1,0:T(8,128)(2,1)S(1)}, u32[]{:S(2)}, u32[]{:S(2)}) %collective-permute-start.8) | collective-permute-done | bytes 196640 | tf_op jit(solution)/shard_map/projection/ppermute | solution.py:49
  23.4 0.7 %final.1 = bf16[96,1280]{1,0:T(8,128)(2,1)} custom-call(f32[96,1280]{1,0:T(8,128)S(1)} %early.1.base_ref, f32[1,1280]{1,0:T(1,128)S(1)} %reshape.3.gate_ref, bf16[96,1024]{1,0:T(8,128)(2,1)S(1)} %collective-permute-done.8.refs_0_), custom_call_target="tpu_custom_call" | custom-call | bytes 983040 | tf_op jit(solution)/shard_map/projection/final/pallas_call | solution.py:373
  (3 shorter events, 0.0 us)
Async XLA Ops:
  0.0 1.5 %copy-start.2 = (f32[96,256]{1,0:T(8,128)S(1)}, f32[96,256]{1,0:T(8,128)}, u32[]{:S(2)}) copy-start(f32[96,256]{1,0:T(8,128)} %param.12) | copy-start | bytes 294916
  0.0 1.5 %copy-start.3 = (f32[96,256]{1,0:T(8,128)S(1)}, f32[96,256]{1,0:T(8,128)}, u32[]{:S(2)}) copy-start(f32[96,256]{1,0:T(8,128)} %param.11) | copy-start | bytes 294916
  0.0 16.1 %collective-permute-start.4 = (bf16[256,5120]{1,0:T(8,128)(2,1)}, bf16[256,5120]{1,0:T(8,128)(2,1)S(1)}, u32[]{:S(2)}, u32[]{:S(2)}) collective-permute-start(bf16[256,5120]{1,0:T(8,128)(2,1)} %refs_1_.3), channel_id=1, source_target_pairs={{0,1},{1,0},{2,3},{3,2},{4,5},{5,4},{6,7},{7,6},{8,9},{9,8},{10,11... | collective-permute-start | bytes 7864328 | tf_op jit(solution)/shard_map/weight_swap/ppermute | solution.py:49
  1.5 9.5 %collective-permute-start.2 = (bf16[96,512]{1,0:T(8,128)(2,1)S(1)}, bf16[96,512]{1,0:T(8,128)(2,1)S(1)}, u32[]{:S(2)}, u32[]{:S(2)}) collective-permute-start(bf16[96,512]{1,0:T(8,128)(2,1)S(1)} %maximum_convert_fusion.refs_0_), channel_id=1, source_target_pairs={{0,4},{1,13},{4,12},{5,9},{8,0},{9,1},{12,8},{13,5},{2,6},{3,15},{... | collective-permute-start | bytes 294920 | tf_op jit(solution)/shard_map/residual_gather/ppermute | solution.py:76
  4.2 8.3 %collective-permute-start.1 = (bf16[96,512]{1,0:T(8,128)(2,1)S(1)}, bf16[96,512]{1,0:T(8,128)(2,1)S(1)}, u32[]{:S(2)}, u32[]{:S(2)}) collective-permute-start(bf16[96,512]{1,0:T(8,128)(2,1)S(1)} %maximum_convert_fusion.refs_0_), channel_id=1, source_target_pairs={{0,12},{1,5},{4,8},{5,1},{8,4},{9,13},{12,0},{13,9},{2,14},{3,7},{... | collective-permute-start | bytes 294920 | tf_op jit(solution)/shard_map/residual_gather/ppermute | solution.py:76
  6.7 7.2 %collective-permute-start = (bf16[96,512]{1,0:T(8,128)(2,1)S(1)}, bf16[96,512]{1,0:T(8,128)(2,1)S(1)}, u32[]{:S(2)}, u32[]{:S(2)}) collective-permute-start(bf16[96,512]{1,0:T(8,128)(2,1)S(1)} %maximum_convert_fusion.refs_0_), channel_id=1, source_target_pairs={{0,8},{1,9},{4,0},{5,13},{8,12},{9,5},{12,4},{13,1},{2,10},{3,11},... | collective-permute-start | bytes 294920 | tf_op jit(solution)/shard_map/residual_gather/ppermute | solution.py:76
  8.2 10.4 %collective-permute-start.6 = (bf16[256,512]{1,0:T(8,128)(2,1)S(1)}, bf16[256,512]{1,0:T(8,128)(2,1)S(1)}, u32[]{:S(2)}, u32[]{:S(2)}) collective-permute-start(bf16[256,512]{1,0:T(8,128)(2,1)S(1)} %early_weight.1), channel_id=1, source_target_pairs={{0,2},{2,0},{1,3},{3,1},{4,6},{6,4},{5,7},{7,5},{8,10},{10,8},{9,1... | collective-permute-start | bytes 786440 | tf_op jit(solution)/shard_map/early_weight/ppermute | solution.py:49
  13.8 2.3 %copy-start = (bf16[256,5120]{1,0:T(8,128)(2,1)S(1)}, bf16[256,5120]{1,0:T(8,128)(2,1)}, u32[]{:S(2)}) copy-start(bf16[256,5120]{1,0:T(8,128)(2,1)} %refs_1_.3) | copy-start | bytes 7864324
  14.3 4.4 %copy-start.4 = (f32[1280]{0:T(1024)S(1)}, f32[1280]{0:T(1024)}, u32[]{:S(2)}) copy-start(f32[1280]{0:T(1024)} %param.15) | copy-start | bytes 15364
  14.4 4.4 %copy-start.1 = (bf16[96,1280]{1,0:T(8,128)(2,1)S(1)}, bf16[96,1280]{1,0:T(8,128)(2,1)}, u32[]{:S(2)}) copy-start(bf16[96,1280]{1,0:T(8,128)(2,1)} %hidden_ref.1) | copy-start | bytes 737284
  14.4 1.7 %collective-permute-start.3 = (bf16[96,256]{1,0:T(8,128)(2,1)S(1)}, bf16[96,256]{1,0:T(8,128)(2,1)S(1)}, u32[]{:S(2)}, u32[]{:S(2)}) collective-permute-start(bf16[96,256]{1,0:T(8,128)(2,1)S(1)} %attention.1.refs_0_), channel_id=1, source_target_pairs={{0,1},{1,0},{2,3},{3,2},{4,5},{5,4},{6,7},{7,6},{8,9},{9,8},{10,11... | collective-permute-start | bytes 147464 | tf_op jit(solution)/shard_map/attended_swap/ppermute | solution.py:49
  14.5 4.2 %collective-permute-start.5 = (bf16[96,256]{1,0:T(8,128)(2,1)S(1)}, bf16[96,256]{1,0:T(8,128)(2,1)S(1)}, u32[]{:S(2)}, u32[]{:S(2)}) collective-permute-start(bf16[96,256]{1,0:T(8,128)(2,1)S(1)} %attention.1.refs_0_), channel_id=1, source_target_pairs={{0,2},{2,0},{1,3},{3,1},{4,6},{6,4},{5,7},{7,5},{8,10},{10,8},{9,1... | collective-permute-start | bytes 147464 | tf_op jit(solution)/shard_map/attended_swap/ppermute | solution.py:49
  16.4 7.0 %collective-permute-start.8 = (bf16[96,1024]{1,0:T(8,128)(2,1)S(1)}, bf16[96,1024]{1,0:T(8,128)(2,1)S(1)}, u32[]{:S(2)}, u32[]{:S(2)}) collective-permute-start(bf16[96,1024]{1,0:T(8,128)(2,1)S(1)} %sent_term.1), channel_id=1, source_target_pairs={{0,2},{2,0},{1,3},{3,1},{4,6},{6,4},{5,7},{7,5},{8,10},{10,8},{9,1... | collective-permute-start | bytes 589832 | tf_op jit(solution)/shard_map/projection/ppermute | solution.py:49
  18.6 1.5 %collective-permute-start.7 = (bf16[352,256]{1,0:T(8,128)(2,1)S(1)}, bf16[352,256]{1,0:T(8,128)(2,1)S(1)}, u32[]{:S(2)}, u32[]{:S(2)}) collective-permute-start(bf16[352,256]{1,0:T(8,128)(2,1)S(1)} %pack.1), channel_id=1, source_target_pairs={{0,1},{1,0},{2,3},{3,2},{4,5},{5,4},{6,7},{7,6},{8,9},{9,8},{10,11... | collective-permute-start | bytes 540680 | tf_op jit(solution)/shard_map/projection/ppermute | solution.py:49

commit v27 on v26

--- a/solution.py
+++ b/solution.py
@@ -50,9 +50,9 @@
 
 
 LINE_OF_FOUR = (
-    ((2, 0, 3, 1), (2, 3, 1, 0)),
-    ((3, 2, 1, 0), (1, 0, 3, 2)),
-    ((1, 3, 0, 2), (3, 2, 0, 1)),
+    ((1, 2, 3, 0), (2, 0, 3, 1)),
+    ((3, 0, 1, 2), (3, 2, 1, 0)),
+    ((2, 3, 0, 1), (1, 3, 0, 2)),
 )
 
 

time: 24.4 us -> 24.6 us (level)
  waiting for transfers between devices: 7.93 us -> 9.18 us
  starting transfers between devices: 11.6 us -> 10.6 us
    ppermute x3, waiting for transfers between devices: 2.79 us -> 4.03 us  [gather(): blocks.append(lax.ppermute(own, ('patch', 'sub'), pairs))]
    ppermute x3, starting transfers between devices: 6.74 us -> 5.72 us  [gather(): blocks.append(lax.ppermute(own, ('patch', 'sub'), pairs))]
where the time goes in v27:
time: 24.6 us; the launch traced here: 24.4 us
  starting transfers between devices  10.6 us (43%)
  waiting for transfers between devices  9.18 us (37%)
  Pallas kernels  4.42 us (18%)
    ppermute x3, starting transfers between devices, gather(): blocks.append(lax.ppermute(own, ('patch', 'sub'), pairs))  5.72 us
    ppermute x6, waiting for transfers between devices, shift(): lax.ppermute(array, axis, [(i, (i + step) % size) for i in range(size)])  5.15 us
    ppermute x6, starting transfers between devices, shift(): lax.ppermute(array, axis, [(i, (i + step) % size) for i in range(size)])  4.84 us
    ppermute x3, waiting for transfers between devices, gather(): blocks.append(lax.ppermute(own, ('patch', 'sub'), pairs))  4.03 us
    pallas_call x1, Pallas kernels, per_device(): call(functools.partial(stage_kernel, patches, subs), [jax.ShapeDtypeStruc...  1.29 us
    pallas_call x1, Pallas kernels, per_device(): call(functools.partial(early_weight_kernel, subs, columns, early), jax.Sh...  0.99 us
    pallas_call x1, Pallas kernels, per_device(): call(functools.partial(final_kernel, early, row_blocks), jax.ShapeDtypeSt...  0.74 us
    pallas_call x1, Pallas kernels, per_device(): call(functools.partial(attention_kernel, 1.0 / math.sqrt(HD)), jax.ShapeD...  0.53 us
  transfers between devices with their start and end apart: 9, of which 5 were waited for; matrix products, arithmetic and copies ran while one was open for 0% of the time, Pallas kernels for 15%

profile of v27, /device:TPU:0, one launch (start us, length us, event | category | flops | bytes accessed | tf_op | source)
XLA Modules:
  0.0 24.4 jit_solution(10960929443451564831)
XLA Ops:
  0.0 0.0 copy-start.2
  0.0 0.0 copy-start.3
  0.0 0.5 %collective-permute-start.4 = (bf16[256,5120]{1,0:T(8,128)(2,1)}, bf16[256,5120]{1,0:T(8,128)(2,1)S(1)}, u32[]{:S(2)}, u32[]{:S(2)}) collective-permute-start(bf16[256,5120]{1,0:T(8,128)(2,1)} %refs_1_.3), channel_id=1, source_target_pairs={{0,1},{1,0},{2,3},{3,2},{4,5},{5,4},{6,7},{7,6},{8,9},{9,8},{10,11... | collective-permute-start | bytes 7864328 | tf_op jit(solution)/shard_map/weight_swap/ppermute | solution.py:49
  0.5 1.0 %early_weight.1 = bf16[256,512]{1,0:T(8,128)(2,1)S(1)} custom-call(bf16[256,5120]{1,0:T(8,128)(2,1)} %refs_1_.3), custom_call_target="tpu_custom_call" | custom-call | bytes 524288 | tf_op jit(solution)/shard_map/early_weight/early_weight/pallas_call | solution.py:250
  1.5 0.0 copy-done.2
  1.5 0.0 copy-done.3
  1.5 3.7 %collective-permute-start.2 = (bf16[96,512]{1,0:T(8,128)(2,1)S(1)}, bf16[96,512]{1,0:T(8,128)(2,1)S(1)}, u32[]{:S(2)}, u32[]{:S(2)}) collective-permute-start(bf16[96,512]{1,0:T(8,128)(2,1)S(1)} %maximum_convert_fusion.refs_0_), channel_id=1, source_target_pairs={{0,8},{1,5},{4,12},{5,13},{8,0},{9,1},{12,4},{13,9},{2,10},{3,7},{... | collective-permute-start | bytes 294920 | tf_op jit(solution)/shard_map/residual_gather/ppermute | solution.py:76
  5.2 1.3 %collective-permute-start.1 = (bf16[96,512]{1,0:T(8,128)(2,1)S(1)}, bf16[96,512]{1,0:T(8,128)(2,1)S(1)}, u32[]{:S(2)}, u32[]{:S(2)}) collective-permute-start(bf16[96,512]{1,0:T(8,128)(2,1)S(1)} %maximum_convert_fusion.refs_0_), channel_id=1, source_target_pairs={{0,12},{1,13},{4,0},{5,9},{8,4},{9,5},{12,8},{13,1},{2,14},{3,15},... | collective-permute-start | bytes 294920 | tf_op jit(solution)/shard_map/residual_gather/ppermute | solution.py:76
  6.5 0.7 %collective-permute-start = (bf16[96,512]{1,0:T(8,128)(2,1)S(1)}, bf16[96,512]{1,0:T(8,128)(2,1)S(1)}, u32[]{:S(2)}, u32[]{:S(2)}) collective-permute-start(bf16[96,512]{1,0:T(8,128)(2,1)S(1)} %maximum_convert_fusion.refs_0_), channel_id=1, source_target_pairs={{0,4},{1,9},{4,8},{5,1},{8,12},{9,13},{12,0},{13,5},{2,6},{3,11},{... | collective-permute-start | bytes 294920 | tf_op jit(solution)/shard_map/residual_gather/ppermute | solution.py:76
  7.2 1.5 %collective-permute-start.6 = (bf16[256,512]{1,0:T(8,128)(2,1)S(1)}, bf16[256,512]{1,0:T(8,128)(2,1)S(1)}, u32[]{:S(2)}, u32[]{:S(2)}) collective-permute-start(bf16[256,512]{1,0:T(8,128)(2,1)S(1)} %early_weight.1), channel_id=1, source_target_pairs={{0,2},{2,0},{1,3},{3,1},{4,6},{6,4},{5,7},{7,5},{8,10},{10,8},{9,1... | collective-permute-start | bytes 786440 | tf_op jit(solution)/shard_map/early_weight/ppermute | solution.py:49
  8.7 1.3 %stage.1 = (bf16[96,256]{1,0:T(8,128)(2,1)S(1)}, f32[2,96,384]{2,1,0:T(8,128)S(1)}, bf16[384,256]{1,0:T(8,128)(2,1)S(1)}) custom-call(bf16[96,256]{1,0:T(8,128)(2,1)} %q_hbm.1, bf16[384,256]{1,0:T(8,128)(2,1)} %held_k_hbm.1, bf16[384,256]{1,0:T(8,128)(2,1)} %held_v_hbm.1), custom_call_target="tpu_custom_call" | custom-call | flops 2000000000 | tf_op jit(solution)/shard_map/attention/stage/pallas_call | solution.py:297
  10.0 0.0 collective-permute-done.2.refs_3_
  10.0 1.9 %collective-permute-done.1.refs_2_ = bf16[96,512]{1,0:T(8,128)(2,1)S(1)} collective-permute-done((bf16[96,512]{1,0:T(8,128)(2,1)S(1)}, bf16[96,512]{1,0:T(8,128)(2,1)S(1)}, u32[]{:S(2)}, u32[]{:S(2)}) %collective-permute-start.1) | collective-permute-done | bytes 98336 | tf_op jit(solution)/shard_map/residual_gather/ppermute | solution.py:76
  11.9 2.1 %collective-permute-done.refs_1_ = bf16[96,512]{1,0:T(8,128)(2,1)S(1)} collective-permute-done((bf16[96,512]{1,0:T(8,128)(2,1)S(1)}, bf16[96,512]{1,0:T(8,128)(2,1)S(1)}, u32[]{:S(2)}, u32[]{:S(2)}) %collective-permute-start) | collective-permute-done | bytes 98336 | tf_op jit(solution)/shard_map/residual_gather/ppermute | solution.py:76
  14.0 0.0 copy-start
  14.0 0.5 %attention.1.refs_0_ = bf16[96,256]{1,0:T(8,128)(2,1)S(1)} custom-call(bf16[96,256]{1,0:T(8,128)(2,1)S(1)} %get-tuple-element.11.q_ref, f32[2,96,384]{2,1,0:T(8,128)S(1)} %get-tuple-element.12.products_ref, bf16[384,256]{1,0:T(8,128)(2,1)S(1)} %get-tuple-element.13.values_ref, bf16[96,512]{1,0:T(8,128)(2,1)S(1)} %maximum_convert_fusion.refs_0_, ...), custom_call_target="tpu_custom_call" | custom-call | flops 2000000000 | tf_op jit(solution)/shard_map/attention/attention/pallas_call | solution.py:313
  14.6 0.0 copy-start.4
  14.6 0.0 copy-start.1
  14.6 0.1 collective-permute-start.3
  14.7 1.6 %collective-permute-start.5 = (bf16[96,256]{1,0:T(8,128)(2,1)S(1)}, bf16[96,256]{1,0:T(8,128)(2,1)S(1)}, u32[]{:S(2)}, u32[]{:S(2)}) collective-permute-start(bf16[96,256]{1,0:T(8,128)(2,1)S(1)} %attention.1.refs_0_), channel_id=1, source_target_pairs={{0,2},{2,0},{1,3},{3,1},{4,6},{6,4},{5,7},{7,5},{8,10},{10,8},{9,1... | collective-permute-start | bytes 147464 | tf_op jit(solution)/shard_map/attended_swap/ppermute | solution.py:49
  16.2 0.0 collective-permute-done.3.refs_2_
  16.2 0.0 collective-permute-done.4.refs_3_
  16.2 0.0 copy-done
  16.3 0.3 %sent_term.1 = bf16[96,1024]{1,0:T(8,128)(2,1)S(1)} custom-call(bf16[96,256]{1,0:T(8,128)(2,1)S(1)} %attention.1.refs_0_, bf16[256,5120]{1,0:T(8,128)(2,1)S(1)} %copy-done, bf16[96,256]{1,0:T(8,128)(2,1)S(1)} %collective-permute-done.3.refs_2_, bf16[256,5120]{1,0:T(8,128)(2,1)S(1)} %collective-permute-done.4.refs_3_), custom_call_target="tpu_custom_call" | custom-call | flops 125829120 | tf_op jit(solution)/shard_map/projection/sent_term/pallas_call | solution.py:336
  16.6 1.2 %collective-permute-start.8 = (bf16[96,1024]{1,0:T(8,128)(2,1)S(1)}, bf16[96,1024]{1,0:T(8,128)(2,1)S(1)}, u32[]{:S(2)}, u32[]{:S(2)}) collective-permute-start(bf16[96,1024]{1,0:T(8,128)(2,1)S(1)} %sent_term.1), channel_id=1, source_target_pairs={{0,2},{2,0},{1,3},{3,1},{4,6},{6,4},{5,7},{7,5},{8,10},{10,8},{9,1... | collective-permute-start | bytes 589832 | tf_op jit(solution)/shard_map/projection/ppermute | solution.py:49
  17.8 1.1 %collective-permute-done.5.attended_ref = bf16[96,256]{1,0:T(8,128)(2,1)S(1)} collective-permute-done((bf16[96,256]{1,0:T(8,128)(2,1)S(1)}, bf16[96,256]{1,0:T(8,128)(2,1)S(1)}, u32[]{:S(2)}, u32[]{:S(2)}) %collective-permute-start.5) | collective-permute-done | bytes 49184 | tf_op jit(solution)/shard_map/attended_swap/ppermute | solution.py:49
  18.8 0.0 collective-permute-done.6.weight_ref
  18.9 0.1 collective-permute-start.7
  18.9 0.0 copy-done.4
  19.0 0.0 copy-done.1
  19.0 0.4 %base.1.base_ref = f32[96,1280]{1,0:T(8,128)S(1)} custom-call(bf16[96,1280]{1,0:T(8,128)(2,1)S(1)} %copy-done.1, f32[1,1280]{1,0:T(1,128)S(1)} %reshape.3.gate_ref, bf16[96,256]{1,0:T(8,128)(2,1)S(1)} %attention.1.refs_0_, bf16[256,5120]{1,0:T(8,128)(2,1)S(1)} %copy-done, bf16[96,256]{1,0:T(8,128)(2,1)S(1)} %collective-permute-done.3.refs_2_, ...), custom_call_target="tpu_custom_call" | custom-call | flops 125829120 | tf_op jit(solution)/shard_map/projection/base/pallas_call | solution.py:347
  19.3 1.0 %collective-permute-done.7.packed_ref = bf16[352,256]{1,0:T(8,128)(2,1)S(1)} collective-permute-done((bf16[352,256]{1,0:T(8,128)(2,1)S(1)}, bf16[352,256]{1,0:T(8,128)(2,1)S(1)}, u32[]{:S(2)}, u32[]{:S(2)}) %collective-permute-start.7) | collective-permute-done | bytes 180256 | tf_op jit(solution)/shard_map/projection/ppermute | solution.py:49
  20.3 0.2 early.1.base_ref
  20.5 3.1 %collective-permute-done.8.refs_0_ = bf16[96,1024]{1,0:T(8,128)(2,1)S(1)} collective-permute-done((bf16[96,1024]{1,0:T(8,128)(2,1)S(1)}, bf16[96,1024]{1,0:T(8,128)(2,1)S(1)}, u32[]{:S(2)}, u32[]{:S(2)}) %collective-permute-start.8) | collective-permute-done | bytes 196640 | tf_op jit(solution)/shard_map/projection/ppermute | solution.py:49
  23.6 0.7 %final.1 = bf16[96,1280]{1,0:T(8,128)(2,1)} custom-call(f32[96,1280]{1,0:T(8,128)S(1)} %early.1.base_ref, f32[1,1280]{1,0:T(1,128)S(1)} %reshape.3.gate_ref, bf16[96,1024]{1,0:T(8,128)(2,1)S(1)} %collective-permute-done.8.refs_0_), custom_call_target="tpu_custom_call" | custom-call | bytes 983040 | tf_op jit(solution)/shard_map/projection/final/pallas_call | solution.py:373
  (3 shorter events, 0.0 us)
Async XLA Ops:
  0.0 1.5 %copy-start.2 = (f32[96,256]{1,0:T(8,128)S(1)}, f32[96,256]{1,0:T(8,128)}, u32[]{:S(2)}) copy-start(f32[96,256]{1,0:T(8,128)} %param.12) | copy-start | bytes 294916
  0.0 1.5 %copy-start.3 = (f32[96,256]{1,0:T(8,128)S(1)}, f32[96,256]{1,0:T(8,128)}, u32[]{:S(2)}) copy-start(f32[96,256]{1,0:T(8,128)} %param.11) | copy-start | bytes 294916
  0.0 16.2 %collective-permute-start.4 = (bf16[256,5120]{1,0:T(8,128)(2,1)}, bf16[256,5120]{1,0:T(8,128)(2,1)S(1)}, u32[]{:S(2)}, u32[]{:S(2)}) collective-permute-start(bf16[256,5120]{1,0:T(8,128)(2,1)} %refs_1_.3), channel_id=1, source_target_pairs={{0,1},{1,0},{2,3},{3,2},{4,5},{5,4},{6,7},{7,6},{8,9},{9,8},{10,11... | collective-permute-start | bytes 7864328 | tf_op jit(solution)/shard_map/weight_swap/ppermute | solution.py:49
  1.5 8.5 %collective-permute-start.2 = (bf16[96,512]{1,0:T(8,128)(2,1)S(1)}, bf16[96,512]{1,0:T(8,128)(2,1)S(1)}, u32[]{:S(2)}, u32[]{:S(2)}) collective-permute-start(bf16[96,512]{1,0:T(8,128)(2,1)S(1)} %maximum_convert_fusion.refs_0_), channel_id=1, source_target_pairs={{0,8},{1,5},{4,12},{5,13},{8,0},{9,1},{12,4},{13,9},{2,10},{3,7},{... | collective-permute-start | bytes 294920 | tf_op jit(solution)/shard_map/residual_gather/ppermute | solution.py:76
  5.2 6.7 %collective-permute-start.1 = (bf16[96,512]{1,0:T(8,128)(2,1)S(1)}, bf16[96,512]{1,0:T(8,128)(2,1)S(1)}, u32[]{:S(2)}, u32[]{:S(2)}) collective-permute-start(bf16[96,512]{1,0:T(8,128)(2,1)S(1)} %maximum_convert_fusion.refs_0_), channel_id=1, source_target_pairs={{0,12},{1,13},{4,0},{5,9},{8,4},{9,5},{12,8},{13,1},{2,14},{3,15},... | collective-permute-start | bytes 294920 | tf_op jit(solution)/shard_map/residual_gather/ppermute | solution.py:76
  6.5 7.5 %collective-permute-start = (bf16[96,512]{1,0:T(8,128)(2,1)S(1)}, bf16[96,512]{1,0:T(8,128)(2,1)S(1)}, u32[]{:S(2)}, u32[]{:S(2)}) collective-permute-start(bf16[96,512]{1,0:T(8,128)(2,1)S(1)} %maximum_convert_fusion.refs_0_), channel_id=1, source_target_pairs={{0,4},{1,9},{4,8},{5,1},{8,12},{9,13},{12,0},{13,5},{2,6},{3,11},{... | collective-permute-start | bytes 294920 | tf_op jit(solution)/shard_map/residual_gather/ppermute | solution.py:76
  7.2 11.6 %collective-permute-start.6 = (bf16[256,512]{1,0:T(8,128)(2,1)S(1)}, bf16[256,512]{1,0:T(8,128)(2,1)S(1)}, u32[]{:S(2)}, u32[]{:S(2)}) collective-permute-start(bf16[256,512]{1,0:T(8,128)(2,1)S(1)} %early_weight.1), channel_id=1, source_target_pairs={{0,2},{2,0},{1,3},{3,1},{4,6},{6,4},{5,7},{7,5},{8,10},{10,8},{9,1... | collective-permute-start | bytes 786440 | tf_op jit(solution)/shard_map/early_weight/ppermute | solution.py:49
  14.0 2.2 %copy-start = (bf16[256,5120]{1,0:T(8,128)(2,1)S(1)}, bf16[256,5120]{1,0:T(8,128)(2,1)}, u32[]{:S(2)}) copy-start(bf16[256,5120]{1,0:T(8,128)(2,1)} %refs_1_.3) | copy-start | bytes 7864324
  14.6 4.4 %copy-start.4 = (f32[1280]{0:T(1024)S(1)}, f32[1280]{0:T(1024)}, u32[]{:S(2)}) copy-start(f32[1280]{0:T(1024)} %param.15) | copy-start | bytes 15364
  14.6 4.4 %copy-start.1 = (bf16[96,1280]{1,0:T(8,128)(2,1)S(1)}, bf16[96,1280]{1,0:T(8,128)(2,1)}, u32[]{:S(2)}) copy-start(bf16[96,1280]{1,0:T(8,128)(2,1)} %hidden_ref.1) | copy-start | bytes 737284
  14.6 1.6 %collective-permute-start.3 = (bf16[96,256]{1,0:T(8,128)(2,1)S(1)}, bf16[96,256]{1,0:T(8,128)(2,1)S(1)}, u32[]{:S(2)}, u32[]{:S(2)}) collective-permute-start(bf16[96,256]{1,0:T(8,128)(2,1)S(1)} %attention.1.refs_0_), channel_id=1, source_target_pairs={{0,1},{1,0},{2,3},{3,2},{4,5},{5,4},{6,7},{7,6},{8,9},{9,8},{10,11... | collective-permute-start | bytes 147464 | tf_op jit(solution)/shard_map/attended_swap/ppermute | solution.py:49
  14.7 4.2 %collective-permute-start.5 = (bf16[96,256]{1,0:T(8,128)(2,1)S(1)}, bf16[96,256]{1,0:T(8,128)(2,1)S(1)}, u32[]{:S(2)}, u32[]{:S(2)}) collective-permute-start(bf16[96,256]{1,0:T(8,128)(2,1)S(1)} %attention.1.refs_0_), channel_id=1, source_target_pairs={{0,2},{2,0},{1,3},{3,1},{4,6},{6,4},{5,7},{7,5},{8,10},{10,8},{9,1... | collective-permute-start | bytes 147464 | tf_op jit(solution)/shard_map/attended_swap/ppermute | solution.py:49
  16.6 7.0 %collective-permute-start.8 = (bf16[96,1024]{1,0:T(8,128)(2,1)S(1)}, bf16[96,1024]{1,0:T(8,128)(2,1)S(1)}, u32[]{:S(2)}, u32[]{:S(2)}) collective-permute-start(bf16[96,1024]{1,0:T(8,128)(2,1)S(1)} %sent_term.1), channel_id=1, source_target_pairs={{0,2},{2,0},{1,3},{3,1},{4,6},{6,4},{5,7},{7,5},{8,10},{10,8},{9,1... | collective-permute-start | bytes 589832 | tf_op jit(solution)/shard_map/projection/ppermute | solution.py:49
  18.9 1.5 %collective-permute-start.7 = (bf16[352,256]{1,0:T(8,128)(2,1)S(1)}, bf16[352,256]{1,0:T(8,128)(2,1)S(1)}, u32[]{:S(2)}, u32[]{:S(2)}) collective-permute-start(bf16[352,256]{1,0:T(8,128)(2,1)S(1)} %pack.1), channel_id=1, source_target_pairs={{0,1},{1,0},{2,3},{3,2},{4,5},{5,4},{6,7},{7,6},{8,9},{9,8},{10,11... | collective-permute-start | bytes 540680 | tf_op jit(solution)/shard_map/projection/ppermute | solution.py:49

commit v28 on v24

--- a/solution.py
+++ b/solution.py
@@ -50,8 +50,8 @@
 
 
 LINE_OF_FOUR = (
-    ((2, 0, 3, 1), (1, 2, 3, 0)),
-    ((3, 2, 1, 0), (3, 0, 1, 2)),
+    ((2, 0, 3, 1), (3, 0, 1, 2)),
+    ((3, 2, 1, 0), (1, 2, 3, 0)),
     ((1, 3, 0, 2), (2, 3, 0, 1)),
 )
 

time: 24.1 us -> 24.4 us (1.012); the launches traced: 23.7 us -> 24.2 us
  waiting for transfers between devices: 7.49 us -> 7.97 us
    ppermute x3, waiting for transfers between devices: 2.34 us -> 2.82 us  [gather(): blocks.append(lax.ppermute(own, ('patch', 'sub'), pairs))]
  transfers between devices with their start and end apart: 9 -> 9, of which waited for: 5 -> 5; matrix products, arithmetic and copies ran while one was open for 0% -> 0% of each run, Pallas kernels for 16% -> 15%
where the time goes in v28:
time: 24.4 us; the launch traced here: 24.2 us
  starting transfers between devices  11.6 us (48%)
  waiting for transfers between devices  7.97 us (33%)
  Pallas kernels  4.43 us (18%)
    ppermute x3, starting transfers between devices, gather(): blocks.append(lax.ppermute(own, ('patch', 'sub'), pairs))  6.74 us
    ppermute x6, waiting for transfers between devices, shift(): lax.ppermute(array, axis, [(i, (i + step) % size) for i in range(size)])  5.15 us
    ppermute x6, starting transfers between devices, shift(): lax.ppermute(array, axis, [(i, (i + step) % size) for i in range(size)])  4.91 us
    ppermute x3, waiting for transfers between devices, gather(): blocks.append(lax.ppermute(own, ('patch', 'sub'), pairs))  2.82 us
    pallas_call x1, Pallas kernels, per_device(): call(functools.partial(stage_kernel, patches, subs), [jax.ShapeDtypeStruc...  1.29 us
    pallas_call x1, Pallas kernels, per_device(): call(functools.partial(early_weight_kernel, subs, columns, early), jax.Sh...  0.99 us
    pallas_call x1, Pallas kernels, per_device(): call(functools.partial(final_kernel, early, row_blocks), jax.ShapeDtypeSt...  0.74 us
    pallas_call x1, Pallas kernels, per_device(): call(functools.partial(attention_kernel, 1.0 / math.sqrt(HD)), jax.ShapeD...  0.53 us
  transfers between devices with their start and end apart: 9, of which 5 were waited for; matrix products, arithmetic and copies ran while one was open for 0% of the time, Pallas kernels for 15%

profile of v28, /device:TPU:0, one launch (start us, length us, event | category | flops | bytes accessed | tf_op | source)
XLA Modules:
  0.0 24.2 jit_solution(13514612653092696109)
XLA Ops:
  0.0 0.0 copy-start.2
  0.0 0.0 copy-start.3
  0.0 0.5 %collective-permute-start.4 = (bf16[256,5120]{1,0:T(8,128)(2,1)}, bf16[256,5120]{1,0:T(8,128)(2,1)S(1)}, u32[]{:S(2)}, u32[]{:S(2)}) collective-permute-start(bf16[256,5120]{1,0:T(8,128)(2,1)} %refs_1_.3), channel_id=1, source_target_pairs={{0,1},{1,0},{2,3},{3,2},{4,5},{5,4},{6,7},{7,6},{8,9},{9,8},{10,11... | collective-permute-start | bytes 7864328 | tf_op jit(solution)/shard_map/weight_swap/ppermute | solution.py:49
  0.5 1.0 %early_weight.1 = bf16[256,512]{1,0:T(8,128)(2,1)S(1)} custom-call(bf16[256,5120]{1,0:T(8,128)(2,1)} %refs_1_.3), custom_call_target="tpu_custom_call" | custom-call | bytes 524288 | tf_op jit(solution)/shard_map/early_weight/early_weight/pallas_call | solution.py:250
  1.5 0.0 copy-done.2
  1.5 0.0 copy-done.3
  1.5 2.7 %collective-permute-start.2 = (bf16[96,512]{1,0:T(8,128)(2,1)S(1)}, bf16[96,512]{1,0:T(8,128)(2,1)S(1)}, u32[]{:S(2)}, u32[]{:S(2)}) collective-permute-start(bf16[96,512]{1,0:T(8,128)(2,1)S(1)} %maximum_convert_fusion.refs_0_), channel_id=1, source_target_pairs={{0,4},{1,9},{4,12},{5,13},{8,0},{9,1},{12,8},{13,5},{2,6},{3,11},{... | collective-permute-start | bytes 294920 | tf_op jit(solution)/shard_map/residual_gather/ppermute | solution.py:76
  4.2 2.5 %collective-permute-start.1 = (bf16[96,512]{1,0:T(8,128)(2,1)S(1)}, bf16[96,512]{1,0:T(8,128)(2,1)S(1)}, u32[]{:S(2)}, u32[]{:S(2)}) collective-permute-start(bf16[96,512]{1,0:T(8,128)(2,1)S(1)} %maximum_convert_fusion.refs_0_), channel_id=1, source_target_pairs={{0,12},{1,5},{4,8},{5,9},{8,4},{9,13},{12,0},{13,1},{2,14},{3,7},{... | collective-permute-start | bytes 294920 | tf_op jit(solution)/shard_map/residual_gather/ppermute | solution.py:76
  6.7 1.6 %collective-permute-start = (bf16[96,512]{1,0:T(8,128)(2,1)S(1)}, bf16[96,512]{1,0:T(8,128)(2,1)S(1)}, u32[]{:S(2)}, u32[]{:S(2)}) collective-permute-start(bf16[96,512]{1,0:T(8,128)(2,1)S(1)} %maximum_convert_fusion.refs_0_), channel_id=1, source_target_pairs={{0,8},{1,13},{4,0},{5,1},{8,12},{9,5},{12,4},{13,9},{2,10},{3,15},... | collective-permute-start | bytes 294920 | tf_op jit(solution)/shard_map/residual_gather/ppermute | solution.py:76
  8.2 1.5 %collective-permute-start.6 = (bf16[256,512]{1,0:T(8,128)(2,1)S(1)}, bf16[256,512]{1,0:T(8,128)(2,1)S(1)}, u32[]{:S(2)}, u32[]{:S(2)}) collective-permute-start(bf16[256,512]{1,0:T(8,128)(2,1)S(1)} %early_weight.1), channel_id=1, source_target_pairs={{0,2},{2,0},{1,3},{3,1},{4,6},{6,4},{5,7},{7,5},{8,10},{10,8},{9,1... | collective-permute-start | bytes 786440 | tf_op jit(solution)/shard_map/early_weight/ppermute | solution.py:49
  9.8 1.3 %stage.1 = (bf16[96,256]{1,0:T(8,128)(2,1)S(1)}, f32[2,96,384]{2,1,0:T(8,128)S(1)}, bf16[384,256]{1,0:T(8,128)(2,1)S(1)}) custom-call(bf16[96,256]{1,0:T(8,128)(2,1)} %q_hbm.1, bf16[384,256]{1,0:T(8,128)(2,1)} %held_k_hbm.1, bf16[384,256]{1,0:T(8,128)(2,1)} %held_v_hbm.1), custom_call_target="tpu_custom_call" | custom-call | flops 2000000000 | tf_op jit(solution)/shard_map/attention/stage/pallas_call | solution.py:297
  11.0 1.3 %collective-permute-done.2.refs_3_ = bf16[96,512]{1,0:T(8,128)(2,1)S(1)} collective-permute-done((bf16[96,512]{1,0:T(8,128)(2,1)S(1)}, bf16[96,512]{1,0:T(8,128)(2,1)S(1)}, u32[]{:S(2)}, u32[]{:S(2)}) %collective-permute-start.2) | collective-permute-done | bytes 98336 | tf_op jit(solution)/shard_map/residual_gather/ppermute | solution.py:76
  12.3 0.0 collective-permute-done.1.refs_2_
  12.3 1.5 %collective-permute-done.refs_1_ = bf16[96,512]{1,0:T(8,128)(2,1)S(1)} collective-permute-done((bf16[96,512]{1,0:T(8,128)(2,1)S(1)}, bf16[96,512]{1,0:T(8,128)(2,1)S(1)}, u32[]{:S(2)}, u32[]{:S(2)}) %collective-permute-start) | collective-permute-done | bytes 98336 | tf_op jit(solution)/shard_map/residual_gather/ppermute | solution.py:76
  13.9 0.0 copy-start
  13.9 0.5 %attention.1.refs_0_ = bf16[96,256]{1,0:T(8,128)(2,1)S(1)} custom-call(bf16[96,256]{1,0:T(8,128)(2,1)S(1)} %get-tuple-element.11.q_ref, f32[2,96,384]{2,1,0:T(8,128)S(1)} %get-tuple-element.12.products_ref, bf16[384,256]{1,0:T(8,128)(2,1)S(1)} %get-tuple-element.13.values_ref, bf16[96,512]{1,0:T(8,128)(2,1)S(1)} %maximum_convert_fusion.refs_0_, ...), custom_call_target="tpu_custom_call" | custom-call | flops 2000000000 | tf_op jit(solution)/shard_map/attention/attention/pallas_call | solution.py:313
  14.4 0.0 copy-start.4
  14.4 0.0 copy-start.1
  14.4 0.1 collective-permute-start.3
  14.5 1.6 %collective-permute-start.5 = (bf16[96,256]{1,0:T(8,128)(2,1)S(1)}, bf16[96,256]{1,0:T(8,128)(2,1)S(1)}, u32[]{:S(2)}, u32[]{:S(2)}) collective-permute-start(bf16[96,256]{1,0:T(8,128)(2,1)S(1)} %attention.1.refs_0_), channel_id=1, source_target_pairs={{0,2},{2,0},{1,3},{3,1},{4,6},{6,4},{5,7},{7,5},{8,10},{10,8},{9,1... | collective-permute-start | bytes 147464 | tf_op jit(solution)/shard_map/attended_swap/ppermute | solution.py:49
  16.1 0.0 collective-permute-done.3.refs_2_
  16.1 0.0 collective-permute-done.4.refs_3_
  16.1 0.0 copy-done
  16.1 0.3 %sent_term.1 = bf16[96,1024]{1,0:T(8,128)(2,1)S(1)} custom-call(bf16[96,256]{1,0:T(8,128)(2,1)S(1)} %attention.1.refs_0_, bf16[256,5120]{1,0:T(8,128)(2,1)S(1)} %copy-done, bf16[96,256]{1,0:T(8,128)(2,1)S(1)} %collective-permute-done.3.refs_2_, bf16[256,5120]{1,0:T(8,128)(2,1)S(1)} %collective-permute-done.4.refs_3_), custom_call_target="tpu_custom_call" | custom-call | flops 125829120 | tf_op jit(solution)/shard_map/projection/sent_term/pallas_call | solution.py:336
  16.5 1.2 %collective-permute-start.8 = (bf16[96,1024]{1,0:T(8,128)(2,1)S(1)}, bf16[96,1024]{1,0:T(8,128)(2,1)S(1)}, u32[]{:S(2)}, u32[]{:S(2)}) collective-permute-start(bf16[96,1024]{1,0:T(8,128)(2,1)S(1)} %sent_term.1), channel_id=1, source_target_pairs={{0,2},{2,0},{1,3},{3,1},{4,6},{6,4},{5,7},{7,5},{8,10},{10,8},{9,1... | collective-permute-start | bytes 589832 | tf_op jit(solution)/shard_map/projection/ppermute | solution.py:49
  17.6 1.0 %collective-permute-done.5.attended_ref = bf16[96,256]{1,0:T(8,128)(2,1)S(1)} collective-permute-done((bf16[96,256]{1,0:T(8,128)(2,1)S(1)}, bf16[96,256]{1,0:T(8,128)(2,1)S(1)}, u32[]{:S(2)}, u32[]{:S(2)}) %collective-permute-start.5) | collective-permute-done | bytes 49184 | tf_op jit(solution)/shard_map/attended_swap/ppermute | solution.py:49
  18.7 0.0 collective-permute-done.6.weight_ref
  18.7 0.1 collective-permute-start.7
  18.8 0.0 copy-done.4
  18.8 0.0 copy-done.1
  18.8 0.4 %base.1.base_ref = f32[96,1280]{1,0:T(8,128)S(1)} custom-call(bf16[96,1280]{1,0:T(8,128)(2,1)S(1)} %copy-done.1, f32[1,1280]{1,0:T(1,128)S(1)} %reshape.3.gate_ref, bf16[96,256]{1,0:T(8,128)(2,1)S(1)} %attention.1.refs_0_, bf16[256,5120]{1,0:T(8,128)(2,1)S(1)} %copy-done, bf16[96,256]{1,0:T(8,128)(2,1)S(1)} %collective-permute-done.3.refs_2_, ...), custom_call_target="tpu_custom_call" | custom-call | flops 125829120 | tf_op jit(solution)/shard_map/projection/base/pallas_call | solution.py:347
  19.2 1.0 %collective-permute-done.7.packed_ref = bf16[352,256]{1,0:T(8,128)(2,1)S(1)} collective-permute-done((bf16[352,256]{1,0:T(8,128)(2,1)S(1)}, bf16[352,256]{1,0:T(8,128)(2,1)S(1)}, u32[]{:S(2)}, u32[]{:S(2)}) %collective-permute-start.7) | collective-permute-done | bytes 180256 | tf_op jit(solution)/shard_map/projection/ppermute | solution.py:49
  20.2 0.2 early.1.base_ref
  20.4 3.1 %collective-permute-done.8.refs_0_ = bf16[96,1024]{1,0:T(8,128)(2,1)S(1)} collective-permute-done((bf16[96,1024]{1,0:T(8,128)(2,1)S(1)}, bf16[96,1024]{1,0:T(8,128)(2,1)S(1)}, u32[]{:S(2)}, u32[]{:S(2)}) %collective-permute-start.8) | collective-permute-done | bytes 196640 | tf_op jit(solution)/shard_map/projection/ppermute | solution.py:49
  23.5 0.7 %final.1 = bf16[96,1280]{1,0:T(8,128)(2,1)} custom-call(f32[96,1280]{1,0:T(8,128)S(1)} %early.1.base_ref, f32[1,1280]{1,0:T(1,128)S(1)} %reshape.3.gate_ref, bf16[96,1024]{1,0:T(8,128)(2,1)S(1)} %collective-permute-done.8.refs_0_), custom_call_target="tpu_custom_call" | custom-call | bytes 983040 | tf_op jit(solution)/shard_map/projection/final/pallas_call | solution.py:373
  (3 shorter events, 0.0 us)
Async XLA Ops:
  0.0 1.5 %copy-start.2 = (f32[96,256]{1,0:T(8,128)S(1)}, f32[96,256]{1,0:T(8,128)}, u32[]{:S(2)}) copy-start(f32[96,256]{1,0:T(8,128)} %param.12) | copy-start | bytes 294916
  0.0 1.5 %copy-start.3 = (f32[96,256]{1,0:T(8,128)S(1)}, f32[96,256]{1,0:T(8,128)}, u32[]{:S(2)}) copy-start(f32[96,256]{1,0:T(8,128)} %param.11) | copy-start | bytes 294916
  0.0 16.1 %collective-permute-start.4 = (bf16[256,5120]{1,0:T(8,128)(2,1)}, bf16[256,5120]{1,0:T(8,128)(2,1)S(1)}, u32[]{:S(2)}, u32[]{:S(2)}) collective-permute-start(bf16[256,5120]{1,0:T(8,128)(2,1)} %refs_1_.3), channel_id=1, source_target_pairs={{0,1},{1,0},{2,3},{3,2},{4,5},{5,4},{6,7},{7,6},{8,9},{9,8},{10,11... | collective-permute-start | bytes 7864328 | tf_op jit(solution)/shard_map/weight_swap/ppermute | solution.py:49
  1.5 10.8 %collective-permute-start.2 = (bf16[96,512]{1,0:T(8,128)(2,1)S(1)}, bf16[96,512]{1,0:T(8,128)(2,1)S(1)}, u32[]{:S(2)}, u32[]{:S(2)}) collective-permute-start(bf16[96,512]{1,0:T(8,128)(2,1)S(1)} %maximum_convert_fusion.refs_0_), channel_id=1, source_target_pairs={{0,4},{1,9},{4,12},{5,13},{8,0},{9,1},{12,8},{13,5},{2,6},{3,11},{... | collective-permute-start | bytes 294920 | tf_op jit(solution)/shard_map/residual_gather/ppermute | solution.py:76
  4.2 8.2 %collective-permute-start.1 = (bf16[96,512]{1,0:T(8,128)(2,1)S(1)}, bf16[96,512]{1,0:T(8,128)(2,1)S(1)}, u32[]{:S(2)}, u32[]{:S(2)}) collective-permute-start(bf16[96,512]{1,0:T(8,128)(2,1)S(1)} %maximum_convert_fusion.refs_0_), channel_id=1, source_target_pairs={{0,12},{1,5},{4,8},{5,9},{8,4},{9,13},{12,0},{13,1},{2,14},{3,7},{... | collective-permute-start | bytes 294920 | tf_op jit(solution)/shard_map/residual_gather/ppermute | solution.py:76
  6.7 7.2 %collective-permute-start = (bf16[96,512]{1,0:T(8,128)(2,1)S(1)}, bf16[96,512]{1,0:T(8,128)(2,1)S(1)}, u32[]{:S(2)}, u32[]{:S(2)}) collective-permute-start(bf16[96,512]{1,0:T(8,128)(2,1)S(1)} %maximum_convert_fusion.refs_0_), channel_id=1, source_target_pairs={{0,8},{1,13},{4,0},{5,1},{8,12},{9,5},{12,4},{13,9},{2,10},{3,15},... | collective-permute-start | bytes 294920 | tf_op jit(solution)/shard_map/residual_gather/ppermute | solution.py:76
  8.2 10.4 %collective-permute-start.6 = (bf16[256,512]{1,0:T(8,128)(2,1)S(1)}, bf16[256,512]{1,0:T(8,128)(2,1)S(1)}, u32[]{:S(2)}, u32[]{:S(2)}) collective-permute-start(bf16[256,512]{1,0:T(8,128)(2,1)S(1)} %early_weight.1), channel_id=1, source_target_pairs={{0,2},{2,0},{1,3},{3,1},{4,6},{6,4},{5,7},{7,5},{8,10},{10,8},{9,1... | collective-permute-start | bytes 786440 | tf_op jit(solution)/shard_map/early_weight/ppermute | solution.py:49
  13.9 2.3 %copy-start = (bf16[256,5120]{1,0:T(8,128)(2,1)S(1)}, bf16[256,5120]{1,0:T(8,128)(2,1)}, u32[]{:S(2)}) copy-start(bf16[256,5120]{1,0:T(8,128)(2,1)} %refs_1_.3) | copy-start | bytes 7864324
  14.4 4.4 %copy-start.4 = (f32[1280]{0:T(1024)S(1)}, f32[1280]{0:T(1024)}, u32[]{:S(2)}) copy-start(f32[1280]{0:T(1024)} %param.15) | copy-start | bytes 15364
  14.4 4.4 %copy-start.1 = (bf16[96,1280]{1,0:T(8,128)(2,1)S(1)}, bf16[96,1280]{1,0:T(8,128)(2,1)}, u32[]{:S(2)}) copy-start(bf16[96,1280]{1,0:T(8,128)(2,1)} %hidden_ref.1) | copy-start | bytes 737284
  14.4 1.7 %collective-permute-start.3 = (bf16[96,256]{1,0:T(8,128)(2,1)S(1)}, bf16[96,256]{1,0:T(8,128)(2,1)S(1)}, u32[]{:S(2)}, u32[]{:S(2)}) collective-permute-start(bf16[96,256]{1,0:T(8,128)(2,1)S(1)} %attention.1.refs_0_), channel_id=1, source_target_pairs={{0,1},{1,0},{2,3},{3,2},{4,5},{5,4},{6,7},{7,6},{8,9},{9,8},{10,11... | collective-permute-start | bytes 147464 | tf_op jit(solution)/shard_map/attended_swap/ppermute | solution.py:49
  14.5 4.2 %collective-permute-start.5 = (bf16[96,256]{1,0:T(8,128)(2,1)S(1)}, bf16[96,256]{1,0:T(8,128)(2,1)S(1)}, u32[]{:S(2)}, u32[]{:S(2)}) collective-permute-start(bf16[96,256]{1,0:T(8,128)(2,1)S(1)} %attention.1.refs_0_), channel_id=1, source_target_pairs={{0,2},{2,0},{1,3},{3,1},{4,6},{6,4},{5,7},{7,5},{8,10},{10,8},{9,1... | collective-permute-start | bytes 147464 | tf_op jit(solution)/shard_map/attended_swap/ppermute | solution.py:49
  16.5 7.0 %collective-permute-start.8 = (bf16[96,1024]{1,0:T(8,128)(2,1)S(1)}, bf16[96,1024]{1,0:T(8,128)(2,1)S(1)}, u32[]{:S(2)}, u32[]{:S(2)}) collective-permute-start(bf16[96,1024]{1,0:T(8,128)(2,1)S(1)} %sent_term.1), channel_id=1, source_target_pairs={{0,2},{2,0},{1,3},{3,1},{4,6},{6,4},{5,7},{7,5},{8,10},{10,8},{9,1... | collective-permute-start | bytes 589832 | tf_op jit(solution)/shard_map/projection/ppermute | solution.py:49
  18.7 1.5 %collective-permute-start.7 = (bf16[352,256]{1,0:T(8,128)(2,1)S(1)}, bf16[352,256]{1,0:T(8,128)(2,1)S(1)}, u32[]{:S(2)}, u32[]{:S(2)}) collective-permute-start(bf16[352,256]{1,0:T(8,128)(2,1)S(1)} %pack.1), channel_id=1, source_target_pairs={{0,1},{1,0},{2,3},{3,2},{4,5},{5,4},{6,7},{7,6},{8,9},{9,8},{10,11... | collective-permute-start | bytes 540680 | tf_op jit(solution)/shard_map/projection/ppermute | solution.py:49

commit v29 on v23

--- a/solution.py
+++ b/solution.py
@@ -50,9 +50,9 @@
 
 
 LINE_OF_FOUR = (
-    ((2, 0, 3, 1), (3, 0, 1, 2)),
+    ((2, 0, 3, 1), (1, 0, 3, 2)),
     ((3, 2, 1, 0), (2, 3, 0, 1)),
-    ((1, 3, 0, 2), (1, 2, 3, 0)),
+    ((1, 3, 0, 2), (3, 2, 1, 0)),
 )
 
 

time: 24 us -> 24.8 us (1.033)
  starting transfers between devices: 11.9 us -> 12.8 us
    ppermute x6, starting transfers between devices: 5.13 us -> 6.1 us  [shift(): lax.ppermute(array, axis, [(i, (i + step) % size) for i in range(size)])]
  transfers between devices with their start and end apart: 9 -> 9, of which waited for: 5 -> 6; matrix products, arithmetic and copies ran while one was open for 0% -> 0% of each run, Pallas kernels for 15% -> 15%
where the time goes in v29:
time: 24.8 us; the launch traced here: 24.6 us
  starting transfers between devices  12.8 us (52%)
  waiting for transfers between devices  7.17 us (29%)
  Pallas kernels  4.43 us (18%)
    ppermute x3, starting transfers between devices, gather(): blocks.append(lax.ppermute(own, ('patch', 'sub'), pairs))  6.74 us
    ppermute x6, starting transfers between devices, shift(): lax.ppermute(array, axis, [(i, (i + step) % size) for i in range(size)])  6.1 us
    ppermute x6, waiting for transfers between devices, shift(): lax.ppermute(array, axis, [(i, (i + step) % size) for i in range(size)])  5.17 us
    ppermute x3, waiting for transfers between devices, gather(): blocks.append(lax.ppermute(own, ('patch', 'sub'), pairs))  2 us
    pallas_call x1, Pallas kernels, per_device(): call(functools.partial(stage_kernel, patches, subs), [jax.ShapeDtypeStruc...  1.28 us
    pallas_call x1, Pallas kernels, per_device(): call(functools.partial(early_weight_kernel, subs, columns, early), jax.Sh...  0.99 us
    pallas_call x1, Pallas kernels, per_device(): call(functools.partial(final_kernel, early, row_blocks), jax.ShapeDtypeSt...  0.74 us
    pallas_call x1, Pallas kernels, per_device(): call(functools.partial(attention_kernel, 1.0 / math.sqrt(HD)), jax.ShapeD...  0.53 us
  transfers between devices with their start and end apart: 9, of which 6 were waited for; matrix products, arithmetic and copies ran while one was open for 0% of the time, Pallas kernels for 15%

profile of v29, /device:TPU:0, one launch (start us, length us, event | category | flops | bytes accessed | tf_op | source)
XLA Modules:
  0.0 24.6 jit_solution(3317316275910150963)
XLA Ops:
  0.0 0.0 copy-start.2
  0.0 0.0 copy-start.3
  0.0 0.5 %collective-permute-start.4 = (bf16[256,5120]{1,0:T(8,128)(2,1)}, bf16[256,5120]{1,0:T(8,128)(2,1)S(1)}, u32[]{:S(2)}, u32[]{:S(2)}) collective-permute-start(bf16[256,5120]{1,0:T(8,128)(2,1)} %refs_1_.3), channel_id=1, source_target_pairs={{0,1},{1,0},{2,3},{3,2},{4,5},{5,4},{6,7},{7,6},{8,9},{9,8},{10,11... | collective-permute-start | bytes 7864328 | tf_op jit(solution)/shard_map/weight_swap/ppermute | solution.py:49
  0.5 1.0 %early_weight.1 = bf16[256,512]{1,0:T(8,128)(2,1)S(1)} custom-call(bf16[256,5120]{1,0:T(8,128)(2,1)} %refs_1_.3), custom_call_target="tpu_custom_call" | custom-call | bytes 524288 | tf_op jit(solution)/shard_map/early_weight/early_weight/pallas_call | solution.py:250
  1.5 0.0 copy-done.2
  1.5 0.0 copy-done.3
  1.5 2.7 %collective-permute-start.2 = (bf16[96,512]{1,0:T(8,128)(2,1)S(1)}, bf16[96,512]{1,0:T(8,128)(2,1)S(1)}, u32[]{:S(2)}, u32[]{:S(2)}) collective-permute-start(bf16[96,512]{1,0:T(8,128)(2,1)S(1)} %maximum_convert_fusion.refs_0_), channel_id=1, source_target_pairs={{0,4},{1,13},{4,12},{5,9},{8,0},{9,5},{12,8},{13,1},{2,6},{3,15},{... | collective-permute-start | bytes 294920 | tf_op jit(solution)/shard_map/residual_gather/ppermute | solution.py:76
  4.2 2.5 %collective-permute-start.1 = (bf16[96,512]{1,0:T(8,128)(2,1)S(1)}, bf16[96,512]{1,0:T(8,128)(2,1)S(1)}, u32[]{:S(2)}, u32[]{:S(2)}) collective-permute-start(bf16[96,512]{1,0:T(8,128)(2,1)S(1)} %maximum_convert_fusion.refs_0_), channel_id=1, source_target_pairs={{0,12},{1,9},{4,8},{5,13},{8,4},{9,1},{12,0},{13,5},{2,14},{3,11},... | collective-permute-start | bytes 294920 | tf_op jit(solution)/shard_map/residual_gather/ppermute | solution.py:76
  6.7 1.6 %collective-permute-start = (bf16[96,512]{1,0:T(8,128)(2,1)S(1)}, bf16[96,512]{1,0:T(8,128)(2,1)S(1)}, u32[]{:S(2)}, u32[]{:S(2)}) collective-permute-start(bf16[96,512]{1,0:T(8,128)(2,1)S(1)} %maximum_convert_fusion.refs_0_), channel_id=1, source_target_pairs={{0,8},{1,5},{4,0},{5,1},{8,12},{9,13},{12,4},{13,9},{2,10},{3,7},{... | collective-permute-start | bytes 294920 | tf_op jit(solution)/shard_map/residual_gather/ppermute | solution.py:76
  8.2 1.5 %collective-permute-start.6 = (bf16[256,512]{1,0:T(8,128)(2,1)S(1)}, bf16[256,512]{1,0:T(8,128)(2,1)S(1)}, u32[]{:S(2)}, u32[]{:S(2)}) collective-permute-start(bf16[256,512]{1,0:T(8,128)(2,1)S(1)} %early_weight.1), channel_id=1, source_target_pairs={{0,2},{2,0},{1,3},{3,1},{4,6},{6,4},{5,7},{7,5},{8,10},{10,8},{9,1... | collective-permute-start | bytes 786440 | tf_op jit(solution)/shard_map/early_weight/ppermute | solution.py:49
  9.7 1.3 %stage.1 = (bf16[96,256]{1,0:T(8,128)(2,1)S(1)}, f32[2,96,384]{2,1,0:T(8,128)S(1)}, bf16[384,256]{1,0:T(8,128)(2,1)S(1)}) custom-call(bf16[96,256]{1,0:T(8,128)(2,1)} %q_hbm.1, bf16[384,256]{1,0:T(8,128)(2,1)} %held_k_hbm.1, bf16[384,256]{1,0:T(8,128)(2,1)} %held_v_hbm.1), custom_call_target="tpu_custom_call" | custom-call | flops 2000000000 | tf_op jit(solution)/shard_map/attention/stage/pallas_call | solution.py:297
  11.0 0.7 %collective-permute-done.2.refs_3_ = bf16[96,512]{1,0:T(8,128)(2,1)S(1)} collective-permute-done((bf16[96,512]{1,0:T(8,128)(2,1)S(1)}, bf16[96,512]{1,0:T(8,128)(2,1)S(1)}, u32[]{:S(2)}, u32[]{:S(2)}) %collective-permute-start.2) | collective-permute-done | bytes 98336 | tf_op jit(solution)/shard_map/residual_gather/ppermute | solution.py:76
  11.7 0.7 %collective-permute-done.1.refs_2_ = bf16[96,512]{1,0:T(8,128)(2,1)S(1)} collective-permute-done((bf16[96,512]{1,0:T(8,128)(2,1)S(1)}, bf16[96,512]{1,0:T(8,128)(2,1)S(1)}, u32[]{:S(2)}, u32[]{:S(2)}) %collective-permute-start.1) | collective-permute-done | bytes 98336 | tf_op jit(solution)/shard_map/residual_gather/ppermute | solution.py:76
  12.4 0.7 %collective-permute-done.refs_1_ = bf16[96,512]{1,0:T(8,128)(2,1)S(1)} collective-permute-done((bf16[96,512]{1,0:T(8,128)(2,1)S(1)}, bf16[96,512]{1,0:T(8,128)(2,1)S(1)}, u32[]{:S(2)}, u32[]{:S(2)}) %collective-permute-start) | collective-permute-done | bytes 98336 | tf_op jit(solution)/shard_map/residual_gather/ppermute | solution.py:76
  13.0 0.0 copy-start
  13.0 0.5 %attention.1.refs_0_ = bf16[96,256]{1,0:T(8,128)(2,1)S(1)} custom-call(bf16[96,256]{1,0:T(8,128)(2,1)S(1)} %get-tuple-element.11.q_ref, f32[2,96,384]{2,1,0:T(8,128)S(1)} %get-tuple-element.12.products_ref, bf16[384,256]{1,0:T(8,128)(2,1)S(1)} %get-tuple-element.13.values_ref, bf16[96,512]{1,0:T(8,128)(2,1)S(1)} %maximum_convert_fusion.refs_0_, ...), custom_call_target="tpu_custom_call" | custom-call | flops 2000000000 | tf_op jit(solution)/shard_map/attention/attention/pallas_call | solution.py:313
  13.6 0.0 copy-start.4
  13.6 0.0 copy-start.1
  13.6 1.9 %collective-permute-start.3 = (bf16[96,256]{1,0:T(8,128)(2,1)S(1)}, bf16[96,256]{1,0:T(8,128)(2,1)S(1)}, u32[]{:S(2)}, u32[]{:S(2)}) collective-permute-start(bf16[96,256]{1,0:T(8,128)(2,1)S(1)} %attention.1.refs_0_), channel_id=1, source_target_pairs={{0,1},{1,0},{2,3},{3,2},{4,5},{5,4},{6,7},{7,6},{8,9},{9,8},{10,11... | collective-permute-start | bytes 147464 | tf_op jit(solution)/shard_map/attended_swap/ppermute | solution.py:49
  15.5 1.3 %collective-permute-start.5 = (bf16[96,256]{1,0:T(8,128)(2,1)S(1)}, bf16[96,256]{1,0:T(8,128)(2,1)S(1)}, u32[]{:S(2)}, u32[]{:S(2)}) collective-permute-start(bf16[96,256]{1,0:T(8,128)(2,1)S(1)} %attention.1.refs_0_), channel_id=1, source_target_pairs={{0,2},{2,0},{1,3},{3,1},{4,6},{6,4},{5,7},{7,5},{8,10},{10,8},{9,1... | collective-permute-start | bytes 147464 | tf_op jit(solution)/shard_map/attended_swap/ppermute | solution.py:49
  16.7 0.0 collective-permute-done.3.refs_2_
  16.7 0.0 collective-permute-done.4.refs_3_
  16.7 0.0 copy-done
  16.8 0.3 %sent_term.1 = bf16[96,1024]{1,0:T(8,128)(2,1)S(1)} custom-call(bf16[96,256]{1,0:T(8,128)(2,1)S(1)} %attention.1.refs_0_, bf16[256,5120]{1,0:T(8,128)(2,1)S(1)} %copy-done, bf16[96,256]{1,0:T(8,128)(2,1)S(1)} %collective-permute-done.3.refs_2_, bf16[256,5120]{1,0:T(8,128)(2,1)S(1)} %collective-permute-done.4.refs_3_), custom_call_target="tpu_custom_call" | custom-call | flops 125829120 | tf_op jit(solution)/shard_map/projection/sent_term/pallas_call | solution.py:336
  17.1 0.9 %collective-permute-start.8 = (bf16[96,1024]{1,0:T(8,128)(2,1)S(1)}, bf16[96,1024]{1,0:T(8,128)(2,1)S(1)}, u32[]{:S(2)}, u32[]{:S(2)}) collective-permute-start(bf16[96,1024]{1,0:T(8,128)(2,1)S(1)} %sent_term.1), channel_id=1, source_target_pairs={{0,2},{2,0},{1,3},{3,1},{4,6},{6,4},{5,7},{7,5},{8,10},{10,8},{9,1... | collective-permute-start | bytes 589832 | tf_op jit(solution)/shard_map/projection/ppermute | solution.py:49
  18.0 1.5 %collective-permute-done.5.attended_ref = bf16[96,256]{1,0:T(8,128)(2,1)S(1)} collective-permute-done((bf16[96,256]{1,0:T(8,128)(2,1)S(1)}, bf16[96,256]{1,0:T(8,128)(2,1)S(1)}, u32[]{:S(2)}, u32[]{:S(2)}) %collective-permute-start.5) | collective-permute-done | bytes 49184 | tf_op jit(solution)/shard_map/attended_swap/ppermute | solution.py:49
  19.5 0.0 collective-permute-done.6.weight_ref
  19.6 0.1 collective-permute-start.7
  19.6 0.0 copy-done.4
  19.7 0.0 copy-done.1
  19.7 0.4 %base.1.base_ref = f32[96,1280]{1,0:T(8,128)S(1)} custom-call(bf16[96,1280]{1,0:T(8,128)(2,1)S(1)} %copy-done.1, f32[1,1280]{1,0:T(1,128)S(1)} %reshape.3.gate_ref, bf16[96,256]{1,0:T(8,128)(2,1)S(1)} %attention.1.refs_0_, bf16[256,5120]{1,0:T(8,128)(2,1)S(1)} %copy-done, bf16[96,256]{1,0:T(8,128)(2,1)S(1)} %collective-permute-done.3.refs_2_, ...), custom_call_target="tpu_custom_call" | custom-call | flops 125829120 | tf_op jit(solution)/shard_map/projection/base/pallas_call | solution.py:347
  20.1 1.0 %collective-permute-done.7.packed_ref = bf16[352,256]{1,0:T(8,128)(2,1)S(1)} collective-permute-done((bf16[352,256]{1,0:T(8,128)(2,1)S(1)}, bf16[352,256]{1,0:T(8,128)(2,1)S(1)}, u32[]{:S(2)}, u32[]{:S(2)}) %collective-permute-start.7) | collective-permute-done | bytes 180256 | tf_op jit(solution)/shard_map/projection/ppermute | solution.py:49
  21.1 0.2 early.1.base_ref
  21.2 2.6 %collective-permute-done.8.refs_0_ = bf16[96,1024]{1,0:T(8,128)(2,1)S(1)} collective-permute-done((bf16[96,1024]{1,0:T(8,128)(2,1)S(1)}, bf16[96,1024]{1,0:T(8,128)(2,1)S(1)}, u32[]{:S(2)}, u32[]{:S(2)}) %collective-permute-start.8) | collective-permute-done | bytes 196640 | tf_op jit(solution)/shard_map/projection/ppermute | solution.py:49
  23.9 0.7 %final.1 = bf16[96,1280]{1,0:T(8,128)(2,1)} custom-call(f32[96,1280]{1,0:T(8,128)S(1)} %early.1.base_ref, f32[1,1280]{1,0:T(1,128)S(1)} %reshape.3.gate_ref, bf16[96,1024]{1,0:T(8,128)(2,1)S(1)} %collective-permute-done.8.refs_0_), custom_call_target="tpu_custom_call" | custom-call | bytes 983040 | tf_op jit(solution)/shard_map/projection/final/pallas_call | solution.py:373
  (3 shorter events, 0.0 us)
Async XLA Ops:
  0.0 1.5 %copy-start.2 = (f32[96,256]{1,0:T(8,128)S(1)}, f32[96,256]{1,0:T(8,128)}, u32[]{:S(2)}) copy-start(f32[96,256]{1,0:T(8,128)} %param.12) | copy-start | bytes 294916
  0.0 1.5 %copy-start.3 = (f32[96,256]{1,0:T(8,128)S(1)}, f32[96,256]{1,0:T(8,128)}, u32[]{:S(2)}) copy-start(f32[96,256]{1,0:T(8,128)} %param.11) | copy-start | bytes 294916
  0.0 16.7 %collective-permute-start.4 = (bf16[256,5120]{1,0:T(8,128)(2,1)}, bf16[256,5120]{1,0:T(8,128)(2,1)S(1)}, u32[]{:S(2)}, u32[]{:S(2)}) collective-permute-start(bf16[256,5120]{1,0:T(8,128)(2,1)} %refs_1_.3), channel_id=1, source_target_pairs={{0,1},{1,0},{2,3},{3,2},{4,5},{5,4},{6,7},{7,6},{8,9},{9,8},{10,11... | collective-permute-start | bytes 7864328 | tf_op jit(solution)/shard_map/weight_swap/ppermute | solution.py:49
  1.5 10.2 %collective-permute-start.2 = (bf16[96,512]{1,0:T(8,128)(2,1)S(1)}, bf16[96,512]{1,0:T(8,128)(2,1)S(1)}, u32[]{:S(2)}, u32[]{:S(2)}) collective-permute-start(bf16[96,512]{1,0:T(8,128)(2,1)S(1)} %maximum_convert_fusion.refs_0_), channel_id=1, source_target_pairs={{0,4},{1,13},{4,12},{5,9},{8,0},{9,5},{12,8},{13,1},{2,6},{3,15},{... | collective-permute-start | bytes 294920 | tf_op jit(solution)/shard_map/residual_gather/ppermute | solution.py:76
  4.2 8.2 %collective-permute-start.1 = (bf16[96,512]{1,0:T(8,128)(2,1)S(1)}, bf16[96,512]{1,0:T(8,128)(2,1)S(1)}, u32[]{:S(2)}, u32[]{:S(2)}) collective-permute-start(bf16[96,512]{1,0:T(8,128)(2,1)S(1)} %maximum_convert_fusion.refs_0_), channel_id=1, source_target_pairs={{0,12},{1,9},{4,8},{5,13},{8,4},{9,1},{12,0},{13,5},{2,14},{3,11},... | collective-permute-start | bytes 294920 | tf_op jit(solution)/shard_map/residual_gather/ppermute | solution.py:76
  6.7 6.4 %collective-permute-start = (bf16[96,512]{1,0:T(8,128)(2,1)S(1)}, bf16[96,512]{1,0:T(8,128)(2,1)S(1)}, u32[]{:S(2)}, u32[]{:S(2)}) collective-permute-start(bf16[96,512]{1,0:T(8,128)(2,1)S(1)} %maximum_convert_fusion.refs_0_), channel_id=1, source_target_pairs={{0,8},{1,5},{4,0},{5,1},{8,12},{9,13},{12,4},{13,9},{2,10},{3,7},{... | collective-permute-start | bytes 294920 | tf_op jit(solution)/shard_map/residual_gather/ppermute | solution.py:76
  8.2 11.3 %collective-permute-start.6 = (bf16[256,512]{1,0:T(8,128)(2,1)S(1)}, bf16[256,512]{1,0:T(8,128)(2,1)S(1)}, u32[]{:S(2)}, u32[]{:S(2)}) collective-permute-start(bf16[256,512]{1,0:T(8,128)(2,1)S(1)} %early_weight.1), channel_id=1, source_target_pairs={{0,2},{2,0},{1,3},{3,1},{4,6},{6,4},{5,7},{7,5},{8,10},{10,8},{9,1... | collective-permute-start | bytes 786440 | tf_op jit(solution)/shard_map/early_weight/ppermute | solution.py:49
  13.0 3.7 %copy-start = (bf16[256,5120]{1,0:T(8,128)(2,1)S(1)}, bf16[256,5120]{1,0:T(8,128)(2,1)}, u32[]{:S(2)}) copy-start(bf16[256,5120]{1,0:T(8,128)(2,1)} %refs_1_.3) | copy-start | bytes 7864324
  13.6 6.1 %copy-start.4 = (f32[1280]{0:T(1024)S(1)}, f32[1280]{0:T(1024)}, u32[]{:S(2)}) copy-start(f32[1280]{0:T(1024)} %param.15) | copy-start | bytes 15364
  13.6 6.1 %copy-start.1 = (bf16[96,1280]{1,0:T(8,128)(2,1)S(1)}, bf16[96,1280]{1,0:T(8,128)(2,1)}, u32[]{:S(2)}) copy-start(bf16[96,1280]{1,0:T(8,128)(2,1)} %hidden_ref.1) | copy-start | bytes 737284
  13.6 3.2 %collective-permute-start.3 = (bf16[96,256]{1,0:T(8,128)(2,1)S(1)}, bf16[96,256]{1,0:T(8,128)(2,1)S(1)}, u32[]{:S(2)}, u32[]{:S(2)}) collective-permute-start(bf16[96,256]{1,0:T(8,128)(2,1)S(1)} %attention.1.refs_0_), channel_id=1, source_target_pairs={{0,1},{1,0},{2,3},{3,2},{4,5},{5,4},{6,7},{7,6},{8,9},{9,8},{10,11... | collective-permute-start | bytes 147464 | tf_op jit(solution)/shard_map/attended_swap/ppermute | solution.py:49
  15.5 4.1 %collective-permute-start.5 = (bf16[96,256]{1,0:T(8,128)(2,1)S(1)}, bf16[96,256]{1,0:T(8,128)(2,1)S(1)}, u32[]{:S(2)}, u32[]{:S(2)}) collective-permute-start(bf16[96,256]{1,0:T(8,128)(2,1)S(1)} %attention.1.refs_0_), channel_id=1, source_target_pairs={{0,2},{2,0},{1,3},{3,1},{4,6},{6,4},{5,7},{7,5},{8,10},{10,8},{9,1... | collective-permute-start | bytes 147464 | tf_op jit(solution)/shard_map/attended_swap/ppermute | solution.py:49
  17.1 6.8 %collective-permute-start.8 = (bf16[96,1024]{1,0:T(8,128)(2,1)S(1)}, bf16[96,1024]{1,0:T(8,128)(2,1)S(1)}, u32[]{:S(2)}, u32[]{:S(2)}) collective-permute-start(bf16[96,1024]{1,0:T(8,128)(2,1)S(1)} %sent_term.1), channel_id=1, source_target_pairs={{0,2},{2,0},{1,3},{3,1},{4,6},{6,4},{5,7},{7,5},{8,10},{10,8},{9,1... | collective-permute-start | bytes 589832 | tf_op jit(solution)/shard_map/projection/ppermute | solution.py:49
  19.6 1.5 %collective-permute-start.7 = (bf16[352,256]{1,0:T(8,128)(2,1)S(1)}, bf16[352,256]{1,0:T(8,128)(2,1)S(1)}, u32[]{:S(2)}, u32[]{:S(2)}) collective-permute-start(bf16[352,256]{1,0:T(8,128)(2,1)S(1)} %pack.1), channel_id=1, source_target_pairs={{0,1},{1,0},{2,3},{3,2},{4,5},{5,4},{6,7},{7,6},{8,9},{9,8},{10,11... | collective-permute-start | bytes 540680 | tf_op jit(solution)/shard_map/projection/ppermute | solution.py:49
